TPU v7x, 32 devices: a whole 2x2x4 slice. The times are simulated.
32 devices in a mesh: section: 2 (over x), expert: 16 (over z, y, core).
Axes of the slice: x: 2, y: 2, z: 4, core: 2. Of those that a mesh axis runs over, the one named last changes fastest.
Arguments:
- forward_tokens: bfloat16 [2, 1024, 2048], P('section', 'expert'), may hold values from -6 to 6
- forward_choice: int32 [2, 1024, 8], P('section', 'expert'), may hold values from 0 to 15, all different within a row; in each aligned block of 64 rows (0 to 63, 64 to 127, ..., all dimensions but the last counted through in order) at most 36 rows name the same one
- forward_gates: float32 [2, 1024, 8], P('section', 'expert'), may hold values from 0.1 to 1
- backward_tokens: bfloat16 [2, 1024, 2048], P('section', 'expert'), may hold values from -6 to 6
- backward_cotangent: bfloat16 [2, 1024, 2048], P('section', 'expert'), may hold values from -6 to 6
- backward_choice: int32 [2, 1024, 8], P('section', 'expert'), may hold values from 0 to 15, all different within a row; in each aligned block of 64 rows (0 to 63, 64 to 127, ..., all dimensions but the last counted through in order) at most 36 rows name the same one
- backward_gates: float32 [2, 1024, 8], P('section', 'expert'), may hold values from 0.1 to 1
- norm_gain: float32 [2, 2048], P('section'), may hold values from 0.1 to 1.9
- gate_weight: bfloat16 [2, 16, 2048, 768], P('section', 'expert'), may hold values from -0.125 to 0.125
- up_weight: bfloat16 [2, 16, 2048, 768], P('section', 'expert'), may hold values from -0.125 to 0.125
- down_weight: bfloat16 [2, 16, 768, 2048], P('section', 'expert'), may hold values from -0.21875 to 0.21875
Outputs:
- section_input: bfloat16 [2, 1024, 2048], P('section', 'expert')
- section_gradient: bfloat16 [2, 1024, 2048], P('section', 'expert')
Inputs may be any that keep to these rules, and one draw needn't show every extreme that they name: `forward_choice`: each token names 8 different experts; among the tokens of one device no expert is named more than 36 times, and in every draw some expert of some device is named exactly 36 times. `backward_choice`: each token names 8 different experts; among the tokens of one device no expert is named more than 36 times, and in every draw some expert of some device is named exactly 36 times.
All inputs are finite; a program needn't handle non-finite values.
Results may differ from a plain program's by a relative error of at most 0.0069.
Values may be sent and summed in bfloat16 or wider, within the bound.
No kernel may reach another device: no remote copies, remote signals or barrier semaphores. Data moves between devices by JAX's collectives and lax.ppermute only.
A program may use at most 128 MiB of HBM per device.

v0:
```python
import jax
import jax.numpy as jnp
from jax import lax
from jax.sharding import PartitionSpec as P

norm_epsilon = 1e-06


def passed_along(block, axis, distance):
    devices = range(lax.axis_size(axis))
    route = [((i - distance) % len(devices), i) for i in devices]
    return lax.ppermute(block, axis, route)


def slot_ranks(choices_flat):
    length = choices_flat.shape[0]
    same_expert = choices_flat[:, None] == choices_flat[None, :]
    earlier = lax.broadcasted_iota(jnp.int32, (length, length), 1) < lax.broadcasted_iota(
        jnp.int32, (length, length), 0
    )
    return jnp.sum((same_expert & earlier).astype(jnp.int32), axis=1)


def slot_index(expert_ids, capacity):
    ids_flat = expert_ids.reshape(-1)
    return ids_flat * capacity + slot_ranks(ids_flat)


def scatter_rows(per_slot, slot_flat, total_rows):
    return jnp.zeros((total_rows, per_slot.shape[1]), jnp.bfloat16).at[slot_flat].set(per_slot)


def normalize(tokens, gain_row):
    tokens_f32 = tokens.astype(jnp.float32)
    inverse = lax.rsqrt(jnp.mean(tokens_f32 * tokens_f32, axis=-1, keepdims=True) + norm_epsilon)
    normed = (tokens_f32 * inverse * gain_row).astype(jnp.bfloat16)
    return (tokens_f32, inverse, normed)


def dot_plain(left, right):
    return jnp.dot(left, right, preferred_element_type=jnp.float32)


def dot_trans(left, right):
    return lax.dot_general(
        left, right, (((1,), (1,)), ((), ())), preferred_element_type=jnp.float32
    )


def expert_forward(normed, gate_w, up_w, down_w):
    gate_act = dot_plain(normed, gate_w)
    up_act = dot_plain(normed, up_w)
    hidden = (jax.nn.silu(gate_act) * up_act).astype(jnp.bfloat16)
    return dot_plain(hidden, down_w).astype(jnp.bfloat16)


def expert_backward(normed, out_grad, gate_w, up_w, down_w):
    gate_act = dot_plain(normed, gate_w)
    up_act = dot_plain(normed, up_w)
    hidden_grad = dot_trans(out_grad, down_w)
    sigmoid_val = jax.nn.sigmoid(gate_act)
    silu_val = gate_act * sigmoid_val
    silu_slope = sigmoid_val * (1.0 + gate_act * (1.0 - sigmoid_val))
    gate_grad = (hidden_grad * up_act * silu_slope).astype(jnp.bfloat16)
    up_grad = (hidden_grad * silu_val).astype(jnp.bfloat16)
    return (dot_trans(gate_grad, gate_w) + dot_trans(up_grad, up_w)).astype(jnp.bfloat16)


def per_device(
    forward_tokens,
    forward_choice,
    forward_gates,
    backward_tokens,
    backward_cotangent,
    backward_choice,
    backward_gates,
    norm_gain,
    gate_weight,
    up_weight,
    down_weight,
):
    groups = lax.axis_size("expert")
    tok_count = forward_choice.shape[1]
    top_count = forward_choice.shape[2]
    model_width = forward_tokens.shape[2]
    capacity = min(tok_count, (9 * tok_count * top_count + 8 * groups - 1) // (8 * groups))
    total_rows = groups * capacity
    gain_row = norm_gain[0]
    gate_w = gate_weight[0, 0]
    up_w = up_weight[0, 0]
    down_w = down_weight[0, 0]
    forward_rows = forward_tokens[0]
    _, _, fwd_normed = normalize(forward_rows, gain_row)
    fwd_slots = slot_index(forward_choice[0], capacity)
    fwd_buffer = scatter_rows(
        jnp.repeat(fwd_normed, top_count, axis=0), fwd_slots, total_rows
    ).reshape(groups, capacity, model_width)
    back_f32, back_inverse, back_normed = normalize(backward_tokens[0], gain_row)
    back_slots = slot_index(backward_choice[0], capacity)
    back_buffer = scatter_rows(
        jnp.repeat(back_normed, top_count, axis=0), back_slots, total_rows
    ).reshape(groups, capacity, model_width)
    cot_f32 = backward_cotangent[0].astype(jnp.float32)
    slot_grads = (
        (backward_gates[0][:, :, None] * cot_f32[:, None, :])
        .astype(jnp.bfloat16)
        .reshape(-1, model_width)
    )
    grad_buffer = scatter_rows(slot_grads, back_slots, total_rows).reshape(
        groups, capacity, model_width
    )
    shard_piece = lax.all_to_all(fwd_buffer, "expert", split_axis=0, concat_axis=0, tiled=True)
    result = expert_forward(shard_piece.reshape(-1, model_width), gate_w, up_w, down_w)
    fwd_result = lax.all_to_all(
        result.reshape(shard_piece.shape), "expert", split_axis=0, concat_axis=0, tiled=True
    )
    normed_piece = lax.all_to_all(back_buffer, "expert", split_axis=0, concat_axis=0, tiled=True)
    result = expert_backward(
        normed_piece.reshape(-1, model_width),
        lax.all_to_all(grad_buffer, "expert", split_axis=0, concat_axis=0, tiled=True).reshape(
            -1, model_width
        ),
        gate_w,
        up_w,
        down_w,
    )
    back_result = lax.all_to_all(
        result.reshape(normed_piece.shape), "expert", split_axis=0, concat_axis=0, tiled=True
    )
    picked = (
        fwd_result.reshape(total_rows, model_width)[fwd_slots]
        .reshape(tok_count, top_count, model_width)
        .astype(jnp.float32)
    )
    mixed_out = forward_rows.astype(jnp.float32) + jnp.sum(
        forward_gates[0][:, :, None] * picked, axis=1
    )
    back_picked = (
        back_result.reshape(total_rows, model_width)[back_slots]
        .reshape(tok_count, top_count, model_width)
        .astype(jnp.float32)
    )
    grad_sum = jnp.sum(back_picked, axis=1)
    scaled = gain_row * grad_sum
    mean_term = jnp.mean(back_f32 * scaled, axis=-1, keepdims=True)
    token_grad = (
        cot_f32
        + back_inverse * scaled
        - back_f32 * back_inverse * back_inverse * back_inverse * mean_term
    )
    section_input = passed_along(mixed_out.astype(jnp.bfloat16)[None], "section", 1)
    section_gradient = passed_along(token_grad.astype(jnp.bfloat16)[None], "section", -1)
    return (section_input, section_gradient)


def solution(mesh):
    placed = (
        P("section", "expert", None),
        P("section", "expert", None),
        P("section", "expert", None),
        P("section", "expert", None),
        P("section", "expert", None),
        P("section", "expert", None),
        P("section", "expert", None),
        P("section", None),
        P("section", "expert", None, None),
        P("section", "expert", None, None),
        P("section", "expert", None, None),
    )
    return jax.shard_map(
        per_device,
        mesh=mesh,
        in_specs=placed,
        out_specs=(P("section", "expert", None), P("section", "expert", None)),
        check_vma=False,
    )
```

profile of v0, /device:TPU:12, one launch (start us, length us, event | category | flops | bytes accessed | tf_op | source)
XLA Modules:
  0.0 438.6 jit_solution(4436530997976247233)
XLA Ops:
  0.6 0.8 broadcast_multiply_fusion
  1.5 0.9 copy.24
  2.4 1.1 fusion.58
  3.8 0.3 convert_reduce_fusion.1
  4.0 1.1 fusion.60
  5.1 5.2 %scatter_custom_fusion.2 = bf16[576,2048]{1,0:T(8,128)(2,1)} fusion(s32[512]{0:T(512)S(1)} %bitcast.100, bf16[]{:T(256)} %constant.8.clone.1, bf16[64,2048]{1,0:T(8,128)(2,1)S(1)} %fusion.60), kind=kCustom, calls=%fused_computation.29 | custom fusion | bytes 2621442 | tf_op jit(solution)/shard_map/scatter | solution.py:30
  10.4 4.1 reshape.233
  14.5 6.4 %all-to-all-start.3 = ((bf16[16,36,2048]{2,1,0:T(8,128)(2,1)}), bf16[16,36,2048]{2,1,0:T(8,128)(2,1)}, u32[]{:S(2)}, u32[]{:S(2)}) async-start(bf16[16,36,2048]{2,1,0:T(8,128)(2,1)} %reshape.233), calls=%async_computation.3 | async-start | bytes 5242880 | tf_op jit(solution)/shard_map/all_to_all | solution.py:117
  21.0 0.8 convert_bitcast_fusion.1
  21.9 5.8 %scatter_custom_fusion.1 = bf16[576,2048]{1,0:T(8,128)(2,1)} fusion(s32[512]{0:T(512)S(1)} %bitcast.101, f32[64,2048]{1,0:T(8,128)} %convert_bitcast_fusion.1, f32[512]{0:T(512)S(1)} %mul.200, bf16[]{:T(256)} %constant.8.clone.1), kind=kCustom, calls=%fused_computation.28 | custom fusion | flops 2097152 | bytes 2885634 | tf_op jit(solution)/shard_map/scatter | solution.py:30
  27.7 4.1 reshape.230
  31.8 47.7 %all-to-all-done.3 = bf16[16,36,2048]{2,1,0:T(8,128)(2,1)} async-done(((bf16[16,36,2048]{2,1,0:T(8,128)(2,1)}), bf16[16,36,2048]{2,1,0:T(8,128)(2,1)}, u32[]{:S(2)}, u32[]{:S(2)}) %all-to-all-start.3) | async-done | bytes 2359328 | tf_op jit(solution)/shard_map/all_to_all | solution.py:117
  79.5 5.4 %all-to-all-start.2 = ((bf16[16,36,2048]{2,1,0:T(8,128)(2,1)}), bf16[16,36,2048]{2,1,0:T(8,128)(2,1)}, u32[]{:S(2)}, u32[]{:S(2)}) async-start(bf16[16,36,2048]{2,1,0:T(8,128)(2,1)} %reshape.230), calls=%async_computation.2 | async-start | bytes 5242880 | tf_op jit(solution)/shard_map/all_to_all | solution.py:120
  84.8 4.1 reshape.234
  88.9 5.8 %fusion.14 = f32[576,768]{1,0:T(8,128)} fusion(bf16[576,2048]{1,0:T(8,128)(2,1)} %reshape.234, bf16[1,1,2048,768]{3,2,1,0:T(8,128)(2,1)} %param.19), kind=kOutput, calls=%fused_computation.23 | convolution fusion | flops 1811939328 | bytes 7274496 | tf_op jit(solution)/shard_map/dot_general | solution.py:41
  94.7 48.6 %all-to-all-done.2 = bf16[16,36,2048]{2,1,0:T(8,128)(2,1)} async-done(((bf16[16,36,2048]{2,1,0:T(8,128)(2,1)}), bf16[16,36,2048]{2,1,0:T(8,128)(2,1)}, u32[]{:S(2)}, u32[]{:S(2)}) %all-to-all-start.2) | async-done | bytes 2359328 | tf_op jit(solution)/shard_map/all_to_all | solution.py:120
  143.3 4.1 reshape.231
  147.4 4.8 %fusion.2 = f32[576,768]{1,0:T(8,128)S(1)} fusion(bf16[576,2048]{1,0:T(8,128)(2,1)} %reshape.231, bf16[1,1,768,2048]{3,2,1,0:T(8,128)(2,1)} %param.21), kind=kOutput, calls=%fused_computation.11 | convolution fusion | flops 1811939328 | bytes 7274496 | tf_op jit(solution)/shard_map/dot_general | solution.py:45
  152.2 1.2 copy-done.12
  153.4 4.3 fusion.6
  157.7 10.8 %add_convert_fusion = bf16[576,2048]{1,0:T(8,128)(2,1)} fusion(f32[576,2048]{1,0:T(8,128)} %fusion.6, bf16[1,1,2048,768]{3,2,1,0:T(8,128)(2,1)} %param.19, f32[576,768]{1,0:T(8,128)} %fusion.14, f32[576,768]{1,0:T(8,128)} %copy-done.12, bf16[576,2048]{1,0:T(8,128)(2,1)} %reshape.234, bf16[1,1,2048,768]{3,2,1,0:T(8,128)(2,1)S(1)} %copy-done), kind=kOutput, calls=%fused_computation.5 | convolution fusion | flops 3630661632 | bytes 19267584 | tf_op jit(solution)/shard_map/dot_general | solution.py:45
  168.5 4.1 reshape.235
  172.7 5.5 %all-to-all-start.4 = ((bf16[16,36,2048]{2,1,0:T(8,128)(2,1)}), bf16[16,36,2048]{2,1,0:T(8,128)(2,1)}, u32[]{:S(2)}, u32[]{:S(2)}) async-start(bf16[16,36,2048]{2,1,0:T(8,128)(2,1)} %reshape.235), calls=%async_computation.4 | async-start | bytes 5242880 | tf_op jit(solution)/shard_map/all_to_all | solution.py:127
  178.7 0.3 convert_reduce_fusion.2
  179.0 57.6 %all-to-all-done.4 = bf16[16,36,2048]{2,1,0:T(8,128)(2,1)} async-done(((bf16[16,36,2048]{2,1,0:T(8,128)(2,1)}), bf16[16,36,2048]{2,1,0:T(8,128)(2,1)}, u32[]{:S(2)}, u32[]{:S(2)}) %all-to-all-start.4) | async-done | bytes 2359328 | tf_op jit(solution)/shard_map/all_to_all | solution.py:127
  236.6 4.1 reshape.236
  240.7 7.3 %gather_fusion.1 = bf16[512,2048]{1,0:T(8,128)(2,1)} fusion(bf16[576,2048]{1,0:T(8,128)(2,1)} %reshape.236, s32[1024]{0:T(1024)S(1)} %pad_clamp_fusion), kind=kCustom, calls=%fused_computation.1 | custom fusion | bytes 4196352 | tf_op jit(solution)/shard_map/gather | solution.py:139
  248.0 3.0 convert_reduce_fusion
  251.1 0.8 copy-done.1
  251.9 1.0 fusion.61
  252.8 5.7 %scatter_custom_fusion = bf16[576,2048]{1,0:T(8,128)(2,1)} fusion(s32[512]{0:T(512)S(1)} %bitcast.103, bf16[]{:T(256)} %constant.8.clone.1, bf16[64,2048]{1,0:T(8,128)(2,1)} %get-tuple-element.3), kind=kCustom, calls=%fused_computation.31 | custom fusion | bytes 2621442 | tf_op jit(solution)/shard_map/scatter | solution.py:30
  258.5 4.1 reshape.226
  262.6 63.8 %all_to_all.25 = bf16[16,36,2048]{2,1,0:T(8,128)(2,1)} all-to-all(bf16[16,36,2048]{2,1,0:T(8,128)(2,1)} %reshape.226), channel_id=1, replica_groups=mesh['section'=2,'expert'=16] {'expert'}, dimensions={0} | all-to-all | bytes 4718592 | tf_op jit(solution)/shard_map/all_to_all | solution.py:112
  326.4 4.1 reshape.227
  330.5 5.8 %fusion.16 = f32[576,768]{1,0:T(8,128)} fusion(bf16[576,2048]{1,0:T(8,128)(2,1)} %reshape.227, bf16[1,1,2048,768]{3,2,1,0:T(8,128)(2,1)} %param.19), kind=kOutput, calls=%fused_computation.25 | convolution fusion | flops 1811939328 | bytes 7274496 | tf_op jit(solution)/shard_map/dot_general | solution.py:41
  336.3 8.9 %fusion.18 = bf16[576,2048]{1,0:T(8,128)(2,1)} fusion(bf16[1,1,768,2048]{3,2,1,0:T(8,128)(2,1)} %param.21, f32[576,768]{1,0:T(8,128)} %fusion.16, bf16[576,2048]{1,0:T(8,128)(2,1)} %reshape.227, bf16[1,1,2048,768]{3,2,1,0:T(8,128)(2,1)S(1)} %copy-done), kind=kOutput, calls=%fused_computation.27 | convolution fusion | flops 3627712512 | bytes 12779520 | tf_op jit(solution)/shard_map/dot_general | solution.py:41
  345.2 4.1 reshape.228
  349.3 5.4 %all-to-all-start.1 = ((bf16[16,36,2048]{2,1,0:T(8,128)(2,1)}), bf16[16,36,2048]{2,1,0:T(8,128)(2,1)}, u32[]{:S(2)}, u32[]{:S(2)}) async-start(bf16[16,36,2048]{2,1,0:T(8,128)(2,1)} %reshape.228), calls=%async_computation.1 | async-start | bytes 5242880 | tf_op jit(solution)/shard_map/all_to_all | solution.py:114
  354.8 2.1 fusion.57
  356.9 1.5 collective-permute-start.1
  358.4 54.9 %all-to-all-done.1 = bf16[16,36,2048]{2,1,0:T(8,128)(2,1)} async-done(((bf16[16,36,2048]{2,1,0:T(8,128)(2,1)}), bf16[16,36,2048]{2,1,0:T(8,128)(2,1)}, u32[]{:S(2)}, u32[]{:S(2)}) %all-to-all-start.1) | async-done | bytes 2359328 | tf_op jit(solution)/shard_map/all_to_all | solution.py:114
  413.3 4.1 reshape.229
  417.4 7.3 %gather_fusion = bf16[512,2048]{1,0:T(8,128)(2,1)} fusion(bf16[576,2048]{1,0:T(8,128)(2,1)} %reshape.229, s32[1024]{0:T(1024)S(1)} %pad_clamp_fusion.1), kind=kCustom, calls=%fused_computation | custom fusion | bytes 4196352 | tf_op jit(solution)/shard_map/gather | solution.py:131
  424.7 3.5 fusion
  428.2 1.6 collective-permute-start
  429.8 7.0 %collective-permute-done = bf16[1,64,2048]{2,1,0:T(8,128)(2,1)S(1)} collective-permute-done((bf16[1,64,2048]{2,1,0:T(8,128)(2,1)S(1)}, bf16[1,64,2048]{2,1,0:T(8,128)(2,1)S(1)}, u32[]{:S(2)}, u32[]{:S(2)}) %collective-permute-start) | collective-permute-done | bytes 262176 | tf_op jit(solution)/shard_map/ppermute | solution.py:12
  436.8 0.7 copy.28
  437.5 0.7 copy.29
  (45 shorter events, 1.2 us)
Async XLA Ops:
  0.6 152.8 %copy-start = (bf16[1,1,2048,768]{3,2,1,0:T(8,128)(2,1)S(1)}, bf16[1,1,2048,768]{3,2,1,0:T(8,128)(2,1)}, u32[]{:S(2)}) copy-start(bf16[1,1,2048,768]{3,2,1,0:T(8,128)(2,1)} %param.20) | copy-start | bytes 9437188
  14.5 6.4 %copy-start.9 = (f32[1,64,8]{1,2,0:T(8,128)S(1)}, f32[1,64,8]{1,2,0:T(8,128)}, u32[]{:S(2)}) copy-start(f32[1,64,8]{1,2,0:T(8,128)} %param.17) | copy-start | bytes 6148
  14.5 6.6 %copy-start.6 = (bf16[1,64,2048]{2,1,0:T(8,128)(2,1)S(1)}, bf16[1,64,2048]{2,1,0:T(8,128)(2,1)}, u32[]{:S(2)}) copy-start(bf16[1,64,2048]{2,1,0:T(8,128)(2,1)} %param.15) | copy-start | bytes 786436
  14.5 65.0 %all-to-all-start.3 = ((bf16[16,36,2048]{2,1,0:T(8,128)(2,1)}), bf16[16,36,2048]{2,1,0:T(8,128)(2,1)}, u32[]{:S(2)}, u32[]{:S(2)}) async-start(bf16[16,36,2048]{2,1,0:T(8,128)(2,1)} %reshape.233), calls=%async_computation.3 | async-start | bytes 5242880 | tf_op jit(solution)/shard_map/all_to_all | solution.py:117
  79.5 63.8 %all-to-all-start.2 = ((bf16[16,36,2048]{2,1,0:T(8,128)(2,1)}), bf16[16,36,2048]{2,1,0:T(8,128)(2,1)}, u32[]{:S(2)}, u32[]{:S(2)}) async-start(bf16[16,36,2048]{2,1,0:T(8,128)(2,1)} %reshape.230), calls=%async_computation.2 | async-start | bytes 5242880 | tf_op jit(solution)/shard_map/all_to_all | solution.py:120
  147.4 6.0 %copy-start.11 = (f32[576,768]{1,0:T(8,128)S(1)}, f32[576,768]{1,0:T(8,128)}, u32[]{:S(2)}) copy-start(f32[576,768]{1,0:T(8,128)} %fusion.14) | copy-start | bytes 5308420
  152.2 1.2 copy-start.12
  172.6 5.5 %copy-start.8 = (s32[1,64,8]{1,2,0:T(8,128)S(1)}, s32[1,64,8]{1,2,0:T(8,128)}, u32[]{:S(2)}) copy-start(s32[1,64,8]{1,2,0:T(8,128)} %param.12) | copy-start | bytes 6148
  172.7 5.9 %copy-start.3 = (bf16[1,64,2048]{2,1,0:T(8,128)(2,1)S(1)}, bf16[1,64,2048]{2,1,0:T(8,128)(2,1)}, u32[]{:S(2)}) copy-start(bf16[1,64,2048]{2,1,0:T(8,128)(2,1)} %param.11) | copy-start | bytes 786436
  172.7 64.0 %all-to-all-start.4 = ((bf16[16,36,2048]{2,1,0:T(8,128)(2,1)}), bf16[16,36,2048]{2,1,0:T(8,128)(2,1)}, u32[]{:S(2)}, u32[]{:S(2)}) async-start(bf16[16,36,2048]{2,1,0:T(8,128)(2,1)} %reshape.235), calls=%async_computation.4 | async-start | bytes 5242880 | tf_op jit(solution)/shard_map/all_to_all | solution.py:127
  248.0 3.9 copy-start.2
  248.0 3.9 copy-start.4
  248.0 3.9 copy-start.7
  251.1 0.8 copy-start.1
  349.3 5.4 %copy-start.10 = (f32[1,64,8]{1,2,0:T(8,128)S(1)}, f32[1,64,8]{1,2,0:T(8,128)}, u32[]{:S(2)}) copy-start(f32[1,64,8]{1,2,0:T(8,128)} %param.13) | copy-start | bytes 6148
  349.3 64.0 %all-to-all-start.1 = ((bf16[16,36,2048]{2,1,0:T(8,128)(2,1)}), bf16[16,36,2048]{2,1,0:T(8,128)(2,1)}, u32[]{:S(2)}, u32[]{:S(2)}) async-start(bf16[16,36,2048]{2,1,0:T(8,128)(2,1)} %reshape.228), calls=%async_computation.1 | async-start | bytes 5242880 | tf_op jit(solution)/shard_map/all_to_all | solution.py:114
  356.9 72.9 %collective-permute-start.1 = (bf16[1,64,2048]{2,1,0:T(8,128)(2,1)}, bf16[1,64,2048]{2,1,0:T(8,128)(2,1)S(1)}, u32[]{:S(2)}, u32[]{:S(2)}) collective-permute-start(bf16[1,64,2048]{2,1,0:T(8,128)(2,1)} %fusion.57), channel_id=1, source_target_pairs={{16,0},{0,16},{17,1},{1,17},{18,2},{2,18},{19,3},{3,19},{20,4},{4,... | collective-permute-start | bytes 786440 | tf_op jit(solution)/shard_map/ppermute | solution.py:12
  424.7 3.5 copy-start.5
  428.2 8.6 %collective-permute-start = (bf16[1,64,2048]{2,1,0:T(8,128)(2,1)S(1)}, bf16[1,64,2048]{2,1,0:T(8,128)(2,1)S(1)}, u32[]{:S(2)}, u32[]{:S(2)}) collective-permute-start(bf16[1,64,2048]{2,1,0:T(8,128)(2,1)S(1)} %fusion.55), channel_id=1, source_target_pairs={{16,0},{0,16},{17,1},{1,17},{18,2},{2,18},{19,3},{3,19},{20,4},{4,... | collective-permute-start | bytes 786440 | tf_op jit(solution)/shard_map/ppermute | solution.py:12
where the time goes:
time: 447 us; the launch traced here: 439 us
  waiting for transfers between devices  216 us (48%)
  local copies, waits for them, and re-layouts  71.6 us (16%)
  blocking collectives  63.8 us (14%)
  matrix products  40.4 us (9%)
  starting transfers between devices  25.7 us (6%)
  other arithmetic  20 us (4%)
    all_to_all x1, blocking collectives, per_device(): lax.all_to_all(fwd_buffer, 'expert', split_axis=0, concat_axis=0, tiled=T...  63.8 us
    all_to_all x1, waiting for transfers between devices, per_device(): lax.all_to_all(result.reshape(normed_piece.shape), 'expert', split_axis=0...  57.6 us
    all_to_all x1, waiting for transfers between devices, per_device(): lax.all_to_all(result.reshape(shard_piece.shape), 'expert', split_axis=0,...  54.9 us
    all_to_all x1, waiting for transfers between devices, per_device(): lax.all_to_all(grad_buffer, 'expert', split_axis=0, concat_axis=0, tiled=...  48.6 us
    all_to_all x1, waiting for transfers between devices, per_device(): lax.all_to_all(back_buffer, 'expert', split_axis=0, concat_axis=0, tiled=...  47.7 us
    dot_general x3, matrix products, dot_plain(): return jnp.dot(left, right, preferred_element_type=jnp.float32)  20.5 us
    dot_general x3, matrix products, dot_trans(): lax.dot_general(left, right, (((1,), (1,)), ((), ())), preferred_element_...  19.9 us
    scatter x2, local copies, waits for them, and re-layouts, scatter_rows(): jnp.zeros((total_rows, per_slot.shape[1]), jnp.bfloat16).at[slot_flat]  10.9 us
  transfers between devices with their start and end apart: 6, of which 5 were waited for; matrix products, arithmetic and copies ran while one was open for 9% of the time, Pallas kernels for 0%

commit v1 on v0

v1 whole, which is shorter than its diff:
```python
import jax
import jax.numpy as jnp
from jax import lax
from jax.sharding import PartitionSpec as P

norm_epsilon = 1e-06
CORES = 2
META = 128


def ring_order(chips):
    return [*range(0, chips, 2), *reversed(range(1, chips, 2))]


def ring_route(devices, distance):
    order = ring_order(devices // CORES)
    chips = len(order)
    return [
        (chip * CORES + core, order[(place + distance) % chips] * CORES + core)
        for place, chip in enumerate(order)
        for core in range(CORES)
    ]


def core_route(devices):
    return [(i, i ^ 1) for i in range(devices)]


def passed_along(block, axis, distance):
    size = lax.axis_size(axis)
    return lax.ppermute(block, axis, [(i, (i + distance) % size) for i in range(size)])


def ring_gather(block):
    devices = lax.axis_size("expert")
    reach = devices // CORES // 2
    up, down = ring_route(devices, 1), ring_route(devices, -1)
    half = block.shape[0] // 2
    gathered, behind, ahead = [block], block, block
    for _ in range(reach - 1):
        behind = lax.ppermute(behind, "expert", up)
        ahead = lax.ppermute(ahead, "expert", down)
        gathered += [behind, ahead]
    low = lax.ppermute(behind[:half], "expert", up)
    high = lax.ppermute(ahead[half:], "expert", down)
    return gathered + [low, high]


def ring_scatter(parts):
    devices = lax.axis_size("expert")
    reach = devices // CORES // 2
    up, down = ring_route(devices, 1), ring_route(devices, -1)
    half = parts[0].shape[0] // 2
    low, high = parts[-2], parts[-1]
    behind = lax.ppermute(low.astype(jnp.bfloat16), "expert", down)
    ahead = lax.ppermute(high.astype(jnp.bfloat16), "expert", up)
    for distance in range(reach - 1, 0, -1):
        to_behind, to_ahead = parts[2 * distance - 1], parts[2 * distance]
        if distance == reach - 1:
            behind = jnp.concatenate(
                [to_behind[:half] + behind.astype(jnp.float32), to_behind[half:]]
            )
            ahead = jnp.concatenate(
                [to_ahead[:half], to_ahead[half:] + ahead.astype(jnp.float32)]
            )
        else:
            behind = to_behind + behind.astype(jnp.float32)
            ahead = to_ahead + ahead.astype(jnp.float32)
        behind = lax.ppermute(behind.astype(jnp.bfloat16), "expert", down)
        ahead = lax.ppermute(ahead.astype(jnp.bfloat16), "expert", up)
    return parts[0] + behind.astype(jnp.float32) + ahead.astype(jnp.float32)


def split_rows(array, rows):
    blocks = array.shape[0] // rows
    half = rows // 2
    parts = [array[i * rows : (i + 1) * rows] for i in range(blocks - 1)]
    last = array[(blocks - 1) * rows :]
    return parts + [last[:half], last[half:]]


def normalize(tokens, gain_row):
    tokens_f32 = tokens.astype(jnp.float32)
    inverse = lax.rsqrt(jnp.mean(tokens_f32 * tokens_f32, axis=-1, keepdims=True) + norm_epsilon)
    normed = (tokens_f32 * inverse * gain_row).astype(jnp.bfloat16)
    return (tokens_f32, inverse, normed)


def routing_columns(choice, gates):
    high = gates.astype(jnp.bfloat16)
    low = (gates - high.astype(jnp.float32)).astype(jnp.bfloat16)
    return [choice.astype(jnp.bfloat16), high, low]


def gate_of(columns, expert):
    top = columns.shape[1] // 3
    columns = columns.astype(jnp.float32)
    choice, gates = columns[:, :top], columns[:, top : 2 * top] + columns[:, 2 * top :]
    return jnp.sum(
        jnp.where(choice == expert.astype(jnp.float32), gates, 0.0), axis=1, keepdims=True
    )


def dot_plain(left, right):
    return jnp.dot(left, right, preferred_element_type=jnp.float32)


def dot_trans(left, right):
    return lax.dot_general(
        left, right, (((1,), (1,)), ((), ())), preferred_element_type=jnp.float32
    )


def expert_forward(normed, gate, gate_w, up_w, down_w):
    gate_act = dot_plain(normed, gate_w)
    up_act = dot_plain(normed, up_w)
    hidden = (jax.nn.silu(gate_act) * up_act * gate).astype(jnp.bfloat16)
    return dot_plain(hidden, down_w)


def expert_backward(normed, cotangent, gate, gate_w, up_w, down_w):
    gate_act = dot_plain(normed, gate_w)
    up_act = dot_plain(normed, up_w)
    hidden_grad = dot_trans(cotangent, down_w) * gate
    sigmoid_val = jax.nn.sigmoid(gate_act)
    silu_val = gate_act * sigmoid_val
    silu_slope = sigmoid_val * (1.0 + gate_act * (1.0 - sigmoid_val))
    gate_grad = (hidden_grad * up_act * silu_slope).astype(jnp.bfloat16)
    up_grad = (hidden_grad * silu_val).astype(jnp.bfloat16)
    return dot_trans(gate_grad, gate_w) + dot_trans(up_grad, up_w)


def per_device(
    forward_tokens,
    forward_choice,
    forward_gates,
    backward_tokens,
    backward_cotangent,
    backward_choice,
    backward_gates,
    norm_gain,
    gate_weight,
    up_weight,
    down_weight,
):
    tok_count, width = forward_tokens.shape[1:]
    top = forward_choice.shape[2]
    gain_row = norm_gain[0]
    swap = core_route(lax.axis_size("expert"))
    mine = (gate_weight[0, 0], up_weight[0, 0], down_weight[0, 0])
    theirs = tuple(lax.ppermute(w, "expert", swap) for w in mine)
    me = lax.axis_index("expert")
    sibling = me + 1 - 2 * lax.rem(me, 2)

    forward_rows = forward_tokens[0]
    _, _, fwd_normed = normalize(forward_rows, gain_row)
    back_f32, back_inverse, back_normed = normalize(backward_tokens[0], gain_row)
    columns = routing_columns(forward_choice[0], forward_gates[0]) + routing_columns(
        backward_choice[0], backward_gates[0]
    )
    used = 6 * top
    pad = -used % META
    columns.append(jnp.zeros((tok_count, pad), jnp.bfloat16))
    fwd_blocks = ring_gather(jnp.concatenate([fwd_normed] + columns, axis=1))
    back_blocks = ring_gather(jnp.concatenate([back_normed, backward_cotangent[0]], axis=1))

    fwd_all = jnp.concatenate(fwd_blocks)
    fwd_x = fwd_all[:, :width]
    fwd_columns = fwd_all[:, width : width + 3 * top]
    back_columns = fwd_all[:, width + 3 * top : width + used]
    out = expert_forward(fwd_x, gate_of(fwd_columns, me), *mine) + expert_forward(
        fwd_x, gate_of(fwd_columns, sibling), *theirs
    )
    mixed_out = forward_rows.astype(jnp.float32) + ring_scatter(split_rows(out, tok_count))

    back_all = jnp.concatenate(back_blocks)
    back_x, back_cot = back_all[:, :width], back_all[:, width:]
    out = expert_backward(back_x, back_cot, gate_of(back_columns, me), *mine) + expert_backward(
        back_x, back_cot, gate_of(back_columns, sibling), *theirs
    )
    grad_sum = ring_scatter(split_rows(out, tok_count))
    scaled = gain_row * grad_sum
    mean_term = jnp.mean(back_f32 * scaled, axis=-1, keepdims=True)
    token_grad = (
        backward_cotangent[0].astype(jnp.float32)
        + back_inverse * scaled
        - back_f32 * back_inverse * back_inverse * back_inverse * mean_term
    )
    section_input = passed_along(mixed_out.astype(jnp.bfloat16)[None], "section", 1)
    section_gradient = passed_along(token_grad.astype(jnp.bfloat16)[None], "section", -1)
    return (section_input, section_gradient)


def solution(mesh):
    rows = P("section", "expert", None)
    weights = P("section", "expert", None, None)
    return jax.shard_map(
        per_device,
        mesh=mesh,
        in_specs=(rows,) * 7 + (P("section", None),) + (weights,) * 3,
        out_specs=(rows, rows),
        check_vma=False,
    )
```

time: 447 us -> 231 us (0.52); the launches traced: 439 us -> 228 us
  waiting for transfers between devices: 216 us -> 88.4 us
  blocking collectives: 63.8 us -> 0 us
  local copies, waits for them, and re-layouts: 71.6 us -> 14 us
  matrix products: 40.4 us -> 76.9 us
  starting transfers between devices: 25.7 us -> 33.6 us
  other arithmetic: 20 us -> 14.3 us
    all_to_all x4 -> x0, waiting for transfers between devices: 209 us -> none  [the longest x1 57.6 us: per_device(): lax.all_to_all(result.reshape(normed_piece.shape), 'expert', split_axis=0...]
    ppermute x2 -> x37, waiting for transfers between devices: 7.01 us -> 88.4 us  [the longest x6 44.4 us: ring_gather(): behind = lax.ppermute(behind, 'expert', up)]
    all_to_all x1 -> x0, blocking collectives: 63.8 us -> none  [per_device(): lax.all_to_all(fwd_buffer, 'expert', split_axis=0, concat_axis=0, tiled=T...]
    reshape x10 -> x0, local copies, waits for them, and re-layouts: 41 us -> none  [the longest x1 4.12 us: per_device(): result.reshape(normed_piece.shape)]
    ppermute x2 -> x37, starting transfers between devices: 3.06 us -> 33.6 us  [the longest x6 6.83 us: ring_scatter(): behind = lax.ppermute(behind.astype(jnp.bfloat16), 'expert', down)]
    all_to_all x4 -> x0, starting transfers between devices: 22.7 us -> none  [the longest x1 6.37 us: per_device(): lax.all_to_all(back_buffer, 'expert', split_axis=0, concat_axis=0, tiled=...]
    dot_general x3 -> x6, matrix products: 19.9 us -> 40.3 us  [dot_trans(): lax.dot_general(left, right, (((1,), (1,)), ((), ())), preferred_element_...]
    dot_general x3 -> x6, matrix products: 20.5 us -> 36.7 us  [dot_plain(): return jnp.dot(left, right, preferred_element_type=jnp.float32)]
  transfers between devices with their start and end apart: 6 -> 37, of which waited for: 5 -> 20; matrix products, arithmetic and copies ran while one was open for 9% -> 36% of each run, Pallas kernels for 0% -> 0%
where the time goes in v1:
time: 231 us; the launch traced here: 228 us
  waiting for transfers between devices  88.4 us (38%)
  matrix products  76.9 us (33%)
  starting transfers between devices  33.6 us (15%)
  other arithmetic  14.3 us (6%)
  local copies, waits for them, and re-layouts  14 us (6%)
    ppermute x6, waiting for transfers between devices, ring_gather(): behind = lax.ppermute(behind, 'expert', up)  44.4 us
    dot_general x6, matrix products, dot_trans(): lax.dot_general(left, right, (((1,), (1,)), ((), ())), preferred_element_...  40.3 us
    dot_general x6, matrix products, dot_plain(): return jnp.dot(left, right, preferred_element_type=jnp.float32)  36.7 us
    unnamed x53, local copies, waits for them, and re-layouts  11.5 us
    ppermute x6, waiting for transfers between devices, ring_scatter(): behind = lax.ppermute(behind.astype(jnp.bfloat16), 'expert', down)  9.75 us
    ppermute x6, waiting for transfers between devices, ring_scatter(): ahead = lax.ppermute(ahead.astype(jnp.bfloat16), 'expert', up)  7.58 us
    ppermute x2, waiting for transfers between devices, ring_gather(): high = lax.ppermute(ahead[half:], 'expert', down)  7.16 us
    ppermute x2, waiting for transfers between devices, ring_gather(): low = lax.ppermute(behind[:half], 'expert', up)  6.92 us
  transfers between devices with their start and end apart: 37, of which 20 were waited for; matrix products, arithmetic and copies ran while one was open for 36% of the time, Pallas kernels for 0%

profile of v1, /device:TPU:12, one launch (start us, length us, event | category | flops | bytes accessed | tf_op | source)
XLA Modules:
  0.0 228.3 jit_solution(14134084843958389334)
XLA Ops:
  0.6 1.1 fusion.55
  1.8 1.1 fusion.59
  6.3 1.2 fusion.50
  7.7 1.6 collective-permute-start.1
  11.1 1.6 collective-permute-start.21
  12.7 6.2 %collective-permute-done = bf16[64,2176]{1,0:T(8,128)(2,1)S(1)} collective-permute-done((bf16[64,2176]{1,0:T(8,128)(2,1)S(1)}, bf16[64,2176]{1,0:T(8,128)(2,1)S(1)}, u32[]{:S(2)}, u32[]{:S(2)}) %collective-permute-start) | collective-permute-done | bytes 278560 | tf_op jit(solution)/shard_map/ppermute | solution.py:41
  19.5 9.1 %collective-permute-done.20 = bf16[64,4096]{1,0:T(8,128)(2,1)S(1)} collective-permute-done((bf16[64,4096]{1,0:T(8,128)(2,1)S(1)}, bf16[64,4096]{1,0:T(8,128)(2,1)S(1)}, u32[]{:S(2)}, u32[]{:S(2)}) %collective-permute-start.20) | collective-permute-done | bytes 524320 | tf_op jit(solution)/shard_map/ppermute | solution.py:41
  28.6 1.6 collective-permute-start.3
  32.4 5.6 %collective-permute-done.2 = bf16[64,2176]{1,0:T(8,128)(2,1)S(1)} collective-permute-done((bf16[64,2176]{1,0:T(8,128)(2,1)S(1)}, bf16[64,2176]{1,0:T(8,128)(2,1)S(1)}, u32[]{:S(2)}, u32[]{:S(2)}) %collective-permute-start.2) | collective-permute-done | bytes 278560 | tf_op jit(solution)/shard_map/ppermute | solution.py:41
  39.0 16.2 %collective-permute-done.4 = bf16[64,2176]{1,0:T(8,128)(2,1)S(1)} collective-permute-done((bf16[64,2176]{1,0:T(8,128)(2,1)S(1)}, bf16[64,2176]{1,0:T(8,128)(2,1)S(1)}, u32[]{:S(2)}, u32[]{:S(2)}) %collective-permute-start.4) | collective-permute-done | bytes 278560 | tf_op jit(solution)/shard_map/ppermute | solution.py:41
  55.8 6.0 %collective-permute-done.5 = bf16[64,2176]{1,0:T(8,128)(2,1)S(1)} collective-permute-done((bf16[64,2176]{1,0:T(8,128)(2,1)S(1)}, bf16[64,2176]{1,0:T(8,128)(2,1)S(1)}, u32[]{:S(2)}, u32[]{:S(2)}) %collective-permute-start.5) | collective-permute-done | bytes 278560 | tf_op jit(solution)/shard_map/ppermute | solution.py:42
  62.3 4.6 %collective-permute-done.6 = bf16[32,2176]{1,0:T(8,128)(2,1)S(1)} collective-permute-done((bf16[32,2176]{1,0:T(8,128)(2,1)S(1)}, bf16[32,2176]{1,0:T(8,128)(2,1)S(1)}, u32[]{:S(2)}, u32[]{:S(2)}) %collective-permute-start.6) | collective-permute-done | bytes 139296 | tf_op jit(solution)/shard_map/ppermute | solution.py:44
  67.4 6.1 %collective-permute-done.7 = bf16[32,2176]{1,0:T(8,128)(2,1)S(1)} collective-permute-done((bf16[32,2176]{1,0:T(8,128)(2,1)S(1)}, bf16[32,2176]{1,0:T(8,128)(2,1)S(1)}, u32[]{:S(2)}, u32[]{:S(2)}) %collective-permute-start.7) | collective-permute-done | bytes 139296 | tf_op jit(solution)/shard_map/ppermute | solution.py:45
  74.1 3.0 %fusion.22 = f32[512,768]{1,0:T(8,128)} fusion(bf16[512,2176]{1,0:T(8,128)(2,1)S(1)} %constant_dynamic-update-slice_fusion, bf16[1,1,2048,768]{3,2,1,0:T(8,128)(2,1)S(1)} %copy-done.9), kind=kOutput, calls=%fused_computation.28 | convolution fusion | flops 1610612736 | bytes 6815744 | tf_op jit(solution)/shard_map/dot_general | solution.py:105
  77.5 9.8 %fusion.29 = f32[512,2048]{1,0:T(8,128)} fusion(f32[512,768]{1,0:T(8,128)} %fusion.22, bf16[512,2176]{1,0:T(8,128)(2,1)} %copy-done.4, f32[512]{0:T(512)S(1)} %get-tuple-element.5, bf16[1,1,768,2048]{3,2,1,0:T(8,128)(2,1)} %param.21, bf16[1,1,2048,768]{3,2,1,0:T(8,128)(2,1)} %param.20), kind=kOutput, calls=%fused_computation.30 | convolution fusion | flops 3223977984 | bytes 14157824 | tf_op jit(solution)/shard_map/dot_general | solution.py:105
  87.7 1.6 collective-permute-start.24
  91.5 7.2 %collective-permute-done.24 = bf16[64,4096]{1,0:T(8,128)(2,1)S(1)} collective-permute-done((bf16[64,4096]{1,0:T(8,128)(2,1)S(1)}, bf16[64,4096]{1,0:T(8,128)(2,1)S(1)}, u32[]{:S(2)}, u32[]{:S(2)}) %collective-permute-start.24) | collective-permute-done | bytes 524320 | tf_op jit(solution)/shard_map/ppermute | solution.py:41
  98.7 1.6 collective-permute-start.26
  102.8 2.4 %collective-permute-done.26 = bf16[32,4096]{1,0:T(8,128)(2,1)S(1)} collective-permute-done((bf16[32,4096]{1,0:T(8,128)(2,1)S(1)}, bf16[32,4096]{1,0:T(8,128)(2,1)S(1)}, u32[]{:S(2)}, u32[]{:S(2)}) %collective-permute-start.26) | collective-permute-done | bytes 262176 | tf_op jit(solution)/shard_map/ppermute | solution.py:44
  107.6 3.6 %fusion.13 = f32[512,768]{1,0:T(8,128)S(1)} fusion(bf16[512,4096]{1,0:T(8,128)(2,1)} %constant_dynamic-update-slice_fusion.9, bf16[1,1,2048,768]{3,2,1,0:T(8,128)(2,1)S(1)} %copy-done.10), kind=kOutput, calls=%fused_computation.19 | convolution fusion | flops 1610612736 | bytes 6815744 | tf_op jit(solution)/shard_map/dot_general | solution.py:105
  111.4 1.8 fusion.4
  113.3 1.1 copy-done.15
  114.4 3.9 %fusion.38 = f32[512,2048]{1,0:T(8,128)} fusion(f32[512,768]{1,0:T(8,128)S(1)} %fusion.4, f32[512,768]{1,0:T(8,128)S(1)} %fusion.13, bf16[1,1,2048,768]{3,2,1,0:T(8,128)(2,1)S(1)} %copy-done.11), kind=kOutput, calls=%fused_computation.32 | convolution fusion | flops 1612972032 | bytes 10485760 | tf_op jit(solution)/shard_map/dot_general | solution.py:109
  118.3 10.5 %fusion.34 = f32[512,2048]{1,0:T(8,128)} fusion(f32[512,768]{1,0:T(8,128)} %copy-done.16, f32[512,768]{1,0:T(8,128)} %copy-done.15, bf16[512,4096]{1,0:T(8,128)(2,1)} %constant_dynamic-update-slice_fusion.9, bf16[1,1,2048,768]{3,2,1,0:T(8,128)(2,1)} %param.20, bf16[1,1,2048,768]{3,2,1,0:T(8,128)(2,1)} %param.19), kind=kOutput, calls=%fused_computation.31 | convolution fusion | flops 3225157632 | bytes 15728640 | tf_op jit(solution)/shard_map/dot_general | solution.py:109
  128.8 4.8 %fusion.18 = f32[512,768]{1,0:T(8,128)} fusion(bf16[2048,768]{1,0:T(8,128)(2,1)} %collective-permute-done.8, bf16[512,2176]{1,0:T(8,128)(2,1)S(1)} %copy-done.5), kind=kOutput, calls=%fused_computation.24 | convolution fusion | flops 1610612736 | bytes 6815744 | tf_op jit(solution)/shard_map/dot_general | solution.py:105
  133.6 11.1 %fusion.98 = (bf16[512,2048]{1,0:T(8,128)(2,1)}, f32[512,2048]{1,0:T(8,128)}) fusion(f32[512,2048]{1,0:T(8,128)} %fusion.29, bf16[768,2048]{1,0:T(8,128)(2,1)} %collective-permute-done.10, f32[512,768]{1,0:T(8,128)} %fusion.18, bf16[2048,768]{1,0:T(8,128)(2,1)} %collective-permute-done.9, bf16[512,2176]{1,0:T(8,128)(2,1)S(1)} %copy-done.5, ...), kind=kOutput, calls=%fused_computation.150 | convolution fusion | flops 3226075136 | bytes 20449280 | tf_op jit(solution)/shard_map/dot_general | solution.py:105
  144.8 1.1 fusion.97
  146.5 1.5 collective-permute-start.15
  148.0 4.3 %fusion.10 = f32[512,768]{1,0:T(8,128)S(1)} fusion(bf16[2048,768]{1,0:T(8,128)(2,1)} %collective-permute-done.8, bf16[512,4096]{1,0:T(8,128)(2,1)} %constant_dynamic-update-slice_fusion.9), kind=kOutput, calls=%fused_computation.16 | convolution fusion | flops 1610612736 | bytes 6815744 | tf_op jit(solution)/shard_map/dot_general | solution.py:105
  152.3 4.4 %fusion.7 = f32[512,768]{1,0:T(8,128)S(1)} fusion(bf16[768,2048]{1,0:T(8,128)(2,1)} %collective-permute-done.10, bf16[512,4096]{1,0:T(8,128)(2,1)S(1)} %copy-done.8, f32[512]{0:T(512)S(1)} %get-tuple-element.3), kind=kOutput, calls=%fused_computation.15 | convolution fusion | flops 1611005952 | bytes 6817792 | tf_op jit(solution)/shard_map/dot_general | solution.py:109
  156.7 1.2 copy-done.14
  157.9 5.7 %fusion.39 = f32[512,2048]{1,0:T(8,128)} fusion(bf16[2048,768]{1,0:T(8,128)(2,1)} %collective-permute-done.9, f32[512,768]{1,0:T(8,128)S(1)} %fusion.7, f32[512,768]{1,0:T(8,128)S(1)} %fusion.10), kind=kOutput, calls=%fused_computation.33 | convolution fusion | flops 1612972032 | bytes 10485760 | tf_op jit(solution)/shard_map/dot_general | solution.py:109
  163.6 14.0 %fusion.101 = (bf16[512,2048]{1,0:T(8,128)(2,1)S(1)}, f32[512,2048]{1,0:T(8,128)}) fusion(f32[512,2048]{1,0:T(8,128)} %fusion.39, bf16[2048,768]{1,0:T(8,128)(2,1)} %collective-permute-done.8, f32[512,768]{1,0:T(8,128)} %copy-done.13, f32[512,768]{1,0:T(8,128)} %copy-done.14, bf16[2048,768]{1,0:T(8,128)(2,1)} %collective-permute-done.9, ...), kind=kOutput, calls=%fused_computation.151 | convolution fusion | flops 3229351936 | bytes 30408704 | tf_op jit(solution)/shard_map/dot_general | solution.py:109
  178.2 1.5 collective-permute-start.32
  181.6 1.4 collective-permute-start.12
  183.0 1.1 collective-permute-done.28
  186.0 1.4 collective-permute-start.29
  187.4 3.5 %collective-permute-done.12 = bf16[64,2048]{1,0:T(8,128)(2,1)S(1)} collective-permute-done((bf16[64,2048]{1,0:T(8,128)(2,1)S(1)}, bf16[64,2048]{1,0:T(8,128)(2,1)S(1)}, u32[]{:S(2)}, u32[]{:S(2)}) %collective-permute-start.12) | collective-permute-done | bytes 262176 | tf_op jit(solution)/shard_map/ppermute | solution.py:69
  192.9 3.6 %collective-permute-done.29 = bf16[64,2048]{1,0:T(8,128)(2,1)S(1)} collective-permute-done((bf16[64,2048]{1,0:T(8,128)(2,1)S(1)}, bf16[64,2048]{1,0:T(8,128)(2,1)S(1)}, u32[]{:S(2)}, u32[]{:S(2)}) %collective-permute-start.29) | collective-permute-done | bytes 262176 | tf_op jit(solution)/shard_map/ppermute | solution.py:69
  197.5 2.7 %collective-permute-done.13 = bf16[64,2048]{1,0:T(8,128)(2,1)S(1)} collective-permute-done((bf16[64,2048]{1,0:T(8,128)(2,1)S(1)}, bf16[64,2048]{1,0:T(8,128)(2,1)S(1)}, u32[]{:S(2)}, u32[]{:S(2)}) %collective-permute-start.13) | collective-permute-done | bytes 262176 | tf_op jit(solution)/shard_map/ppermute | solution.py:69
  200.2 1.3 fusion.70
  205.8 3.2 %collective-permute-done.17 = bf16[64,2048]{1,0:T(8,128)(2,1)S(1)} collective-permute-done((bf16[64,2048]{1,0:T(8,128)(2,1)S(1)}, bf16[64,2048]{1,0:T(8,128)(2,1)S(1)}, u32[]{:S(2)}, u32[]{:S(2)}) %collective-permute-start.17) | collective-permute-done | bytes 262176 | tf_op jit(solution)/shard_map/ppermute | solution.py:70
  212.9 3.6 %collective-permute-done.18 = bf16[64,2048]{1,0:T(8,128)(2,1)S(1)} collective-permute-done((bf16[64,2048]{1,0:T(8,128)(2,1)S(1)}, bf16[64,2048]{1,0:T(8,128)(2,1)S(1)}, u32[]{:S(2)}, u32[]{:S(2)}) %collective-permute-start.18) | collective-permute-done | bytes 262176 | tf_op jit(solution)/shard_map/ppermute | solution.py:70
  216.5 1.2 fusion.72
  217.6 1.6 collective-permute-start.19
  219.8 1.6 collective-permute-start.36
  221.4 2.7 %collective-permute-done.19 = bf16[1,64,2048]{2,1,0:T(8,128)(2,1)S(1)} collective-permute-done((bf16[1,64,2048]{2,1,0:T(8,128)(2,1)S(1)}, bf16[1,64,2048]{2,1,0:T(8,128)(2,1)S(1)}, u32[]{:S(2)}, u32[]{:S(2)}) %collective-permute-start.19) | collective-permute-done | bytes 262176 | tf_op jit(solution)/shard_map/ppermute | solution.py:31
  224.1 2.8 %collective-permute-done.36 = bf16[1,64,2048]{2,1,0:T(8,128)(2,1)S(1)} collective-permute-done((bf16[1,64,2048]{2,1,0:T(8,128)(2,1)S(1)}, bf16[1,64,2048]{2,1,0:T(8,128)(2,1)S(1)}, u32[]{:S(2)}, u32[]{:S(2)}) %collective-permute-start.36) | collective-permute-done | bytes 262176 | tf_op jit(solution)/shard_map/ppermute | solution.py:31
  (133 shorter events, 37.5 us)
Async XLA Ops:
  0.6 9.1 %copy-start.3 = (bf16[1,64,2048]{2,1,0:T(8,128)(2,1)S(1)}, bf16[1,64,2048]{2,1,0:T(8,128)(2,1)}, u32[]{:S(2)}) copy-start(bf16[1,64,2048]{2,1,0:T(8,128)(2,1)} %param.15) | copy-start | bytes 786436
  7.7 11.2 %collective-permute-start.1 = (bf16[64,2176]{1,0:T(8,128)(2,1)S(1)}, bf16[64,2176]{1,0:T(8,128)(2,1)S(1)}, u32[]{:S(2)}, u32[]{:S(2)}) collective-permute-start(bf16[64,2176]{1,0:T(8,128)(2,1)S(1)} %concatenate.28), channel_id=1, source_target_pairs={{0,2},{1,3},{4,0},{5,1},{8,4},{9,5},{12,8},{13,9},{14,12},{15,13},... | collective-permute-start | bytes 835592 | tf_op jit(solution)/shard_map/ppermute | solution.py:42
  9.3 9.6 %collective-permute-start = (bf16[64,2176]{1,0:T(8,128)(2,1)S(1)}, bf16[64,2176]{1,0:T(8,128)(2,1)S(1)}, u32[]{:S(2)}, u32[]{:S(2)}) collective-permute-start(bf16[64,2176]{1,0:T(8,128)(2,1)S(1)} %concatenate.28), channel_id=1, source_target_pairs={{0,4},{1,5},{4,8},{5,9},{8,12},{9,13},{12,14},{13,15},{14,10},{15,... | collective-permute-start | bytes 835592 | tf_op jit(solution)/shard_map/ppermute | solution.py:41
  10.6 18.0 %collective-permute-start.20 = (bf16[64,4096]{1,0:T(8,128)(2,1)S(1)}, bf16[64,4096]{1,0:T(8,128)(2,1)S(1)}, u32[]{:S(2)}, u32[]{:S(2)}) collective-permute-start(bf16[64,4096]{1,0:T(8,128)(2,1)S(1)} %get-tuple-element.28), channel_id=1, source_target_pairs={{0,4},{1,5},{4,8},{5,9},{8,12},{9,13},{12,14},{13,15},{14,10},{15,... | collective-permute-start | bytes 1572872 | tf_op jit(solution)/shard_map/ppermute | solution.py:41
  11.1 20.0 %collective-permute-start.21 = (bf16[64,4096]{1,0:T(8,128)(2,1)S(1)}, bf16[64,4096]{1,0:T(8,128)(2,1)S(1)}, u32[]{:S(2)}, u32[]{:S(2)}) collective-permute-start(bf16[64,4096]{1,0:T(8,128)(2,1)S(1)} %get-tuple-element.28), channel_id=1, source_target_pairs={{0,2},{1,3},{4,0},{5,1},{8,4},{9,5},{12,8},{13,9},{14,12},{15,13},... | collective-permute-start | bytes 1572872 | tf_op jit(solution)/shard_map/ppermute | solution.py:42
  12.7 121.0 %collective-permute-start.9 = (bf16[2048,768]{1,0:T(8,128)(2,1)}, bf16[2048,768]{1,0:T(8,128)(2,1)}, u32[]{:S(2)}, u32[]{:S(2)}) collective-permute-start(bf16[2048,768]{1,0:T(8,128)(2,1)} %bitcast.68), channel_id=1, source_target_pairs={{0,1},{1,0},{2,3},{3,2},{4,5},{5,4},{6,7},{7,6},{8,9},{9,8},{10,11... | collective-permute-start | bytes 9437192 | tf_op jit(solution)/shard_map/ppermute | solution.py:151
  18.9 109.9 %collective-permute-start.8 = (bf16[2048,768]{1,0:T(8,128)(2,1)}, bf16[2048,768]{1,0:T(8,128)(2,1)}, u32[]{:S(2)}, u32[]{:S(2)}) collective-permute-start(bf16[2048,768]{1,0:T(8,128)(2,1)} %bitcast.67), channel_id=1, source_target_pairs={{0,1},{1,0},{2,3},{3,2},{4,5},{5,4},{6,7},{7,6},{8,9},{9,8},{10,11... | collective-permute-start | bytes 9437192 | tf_op jit(solution)/shard_map/ppermute | solution.py:151
  18.9 114.7 %collective-permute-start.10 = (bf16[768,2048]{1,0:T(8,128)(2,1)}, bf16[768,2048]{1,0:T(8,128)(2,1)}, u32[]{:S(2)}, u32[]{:S(2)}) collective-permute-start(bf16[768,2048]{1,0:T(8,128)(2,1)} %bitcast.69), channel_id=1, source_target_pairs={{0,1},{1,0},{2,3},{3,2},{4,5},{5,4},{6,7},{7,6},{8,9},{9,8},{10,11... | collective-permute-start | bytes 9437192 | tf_op jit(solution)/shard_map/ppermute | solution.py:151
  28.6 9.8 %collective-permute-start.3 = (bf16[64,2176]{1,0:T(8,128)(2,1)S(1)}, bf16[64,2176]{1,0:T(8,128)(2,1)S(1)}, u32[]{:S(2)}, u32[]{:S(2)}) collective-permute-start(bf16[64,2176]{1,0:T(8,128)(2,1)S(1)} %collective-permute-done.1), channel_id=1, source_target_pairs={{0,2},{1,3},{4,0},{5,1},{8,4},{9,5},{12,8},{13,9},{14,12},{15,13},... | collective-permute-start | bytes 835592 | tf_op jit(solution)/shard_map/ppermute | solution.py:42
  31.1 6.9 %collective-permute-start.2 = (bf16[64,2176]{1,0:T(8,128)(2,1)S(1)}, bf16[64,2176]{1,0:T(8,128)(2,1)S(1)}, u32[]{:S(2)}, u32[]{:S(2)}) collective-permute-start(bf16[64,2176]{1,0:T(8,128)(2,1)S(1)} %collective-permute-done), channel_id=1, source_target_pairs={{0,4},{1,5},{4,8},{5,9},{8,12},{9,13},{12,14},{13,15},{14,10},{15,... | collective-permute-start | bytes 835592 | tf_op jit(solution)/shard_map/ppermute | solution.py:41
  32.4 41.7 %copy-start.9 = (bf16[1,1,2048,768]{3,2,1,0:T(8,128)(2,1)S(1)}, bf16[1,1,2048,768]{3,2,1,0:T(8,128)(2,1)}, u32[]{:S(2)}) copy-start(bf16[1,1,2048,768]{3,2,1,0:T(8,128)(2,1)} %param.19) | copy-start | bytes 9437188
  38.0 49.7 %collective-permute-start.22 = (bf16[64,4096]{1,0:T(8,128)(2,1)S(1)}, bf16[64,4096]{1,0:T(8,128)(2,1)S(1)}, u32[]{:S(2)}, u32[]{:S(2)}) collective-permute-start(bf16[64,4096]{1,0:T(8,128)(2,1)S(1)} %collective-permute-done.20), channel_id=1, source_target_pairs={{0,4},{1,5},{4,8},{5,9},{8,12},{9,13},{12,14},{13,15},{14,10},{15,... | collective-permute-start | bytes 1572872 | tf_op jit(solution)/shard_map/ppermute | solution.py:41
  38.5 16.8 %collective-permute-start.4 = (bf16[64,2176]{1,0:T(8,128)(2,1)S(1)}, bf16[64,2176]{1,0:T(8,128)(2,1)S(1)}, u32[]{:S(2)}, u32[]{:S(2)}) collective-permute-start(bf16[64,2176]{1,0:T(8,128)(2,1)S(1)} %collective-permute-done.2), channel_id=1, source_target_pairs={{0,4},{1,5},{4,8},{5,9},{8,12},{9,13},{12,14},{13,15},{14,10},{15,... | collective-permute-start | bytes 835592 | tf_op jit(solution)/shard_map/ppermute | solution.py:41
  55.2 6.5 %collective-permute-start.5 = (bf16[64,2176]{1,0:T(8,128)(2,1)S(1)}, bf16[64,2176]{1,0:T(8,128)(2,1)S(1)}, u32[]{:S(2)}, u32[]{:S(2)}) collective-permute-start(bf16[64,2176]{1,0:T(8,128)(2,1)S(1)} %collective-permute-done.3), channel_id=1, source_target_pairs={{0,2},{1,3},{4,0},{5,1},{8,4},{9,5},{12,8},{13,9},{14,12},{15,13},... | collective-permute-start | bytes 835592 | tf_op jit(solution)/shard_map/ppermute | solution.py:42
  61.8 5.1 %collective-permute-start.6 = (bf16[32,2176]{1,0:T(8,128)(2,1)S(1)}, bf16[32,2176]{1,0:T(8,128)(2,1)S(1)}, u32[]{:S(2)}, u32[]{:S(2)}) collective-permute-start(bf16[32,2176]{1,0:T(8,128)(2,1)S(1)} %slice.180), channel_id=1, source_target_pairs={{0,4},{1,5},{4,8},{5,9},{8,12},{9,13},{12,14},{13,15},{14,10},{15,... | collective-permute-start | bytes 417800 | tf_op jit(solution)/shard_map/ppermute | solution.py:44
  66.9 6.6 %collective-permute-start.7 = (bf16[32,2176]{1,0:T(8,128)(2,1)S(1)}, bf16[32,2176]{1,0:T(8,128)(2,1)S(1)}, u32[]{:S(2)}, u32[]{:S(2)}) collective-permute-start(bf16[32,2176]{1,0:T(8,128)(2,1)S(1)} %slice.181), channel_id=1, source_target_pairs={{0,2},{1,3},{4,0},{5,1},{8,4},{9,5},{12,8},{13,9},{14,12},{15,13},... | collective-permute-start | bytes 417800 | tf_op jit(solution)/shard_map/ppermute | solution.py:45
  73.5 15.8 %collective-permute-start.23 = (bf16[64,4096]{1,0:T(8,128)(2,1)S(1)}, bf16[64,4096]{1,0:T(8,128)(2,1)S(1)}, u32[]{:S(2)}, u32[]{:S(2)}) collective-permute-start(bf16[64,4096]{1,0:T(8,128)(2,1)S(1)} %collective-permute-done.21), channel_id=1, source_target_pairs={{0,2},{1,3},{4,0},{5,1},{8,4},{9,5},{12,8},{13,9},{14,12},{15,13},... | collective-permute-start | bytes 1572872 | tf_op jit(solution)/shard_map/ppermute | solution.py:42
  87.7 11.0 %collective-permute-start.24 = (bf16[64,4096]{1,0:T(8,128)(2,1)S(1)}, bf16[64,4096]{1,0:T(8,128)(2,1)S(1)}, u32[]{:S(2)}, u32[]{:S(2)}) collective-permute-start(bf16[64,4096]{1,0:T(8,128)(2,1)S(1)} %collective-permute-done.22), channel_id=1, source_target_pairs={{0,4},{1,5},{4,8},{5,9},{8,12},{9,13},{12,14},{13,15},{14,10},{15,... | collective-permute-start | bytes 1572872 | tf_op jit(solution)/shard_map/ppermute | solution.py:41
  89.3 11.0 %collective-permute-start.25 = (bf16[64,4096]{1,0:T(8,128)(2,1)S(1)}, bf16[64,4096]{1,0:T(8,128)(2,1)S(1)}, u32[]{:S(2)}, u32[]{:S(2)}) collective-permute-start(bf16[64,4096]{1,0:T(8,128)(2,1)S(1)} %collective-permute-done.23), channel_id=1, source_target_pairs={{0,2},{1,3},{4,0},{5,1},{8,4},{9,5},{12,8},{13,9},{14,12},{15,13},... | collective-permute-start | bytes 1572872 | tf_op jit(solution)/shard_map/ppermute | solution.py:42
  91.5 16.2 %copy-start.10 = (bf16[1,1,2048,768]{3,2,1,0:T(8,128)(2,1)S(1)}, bf16[1,1,2048,768]{3,2,1,0:T(8,128)(2,1)}, u32[]{:S(2)}) copy-start(bf16[1,1,2048,768]{3,2,1,0:T(8,128)(2,1)} %param.19) | copy-start | bytes 9437188
  98.7 6.4 %collective-permute-start.26 = (bf16[32,4096]{1,0:T(8,128)(2,1)S(1)}, bf16[32,4096]{1,0:T(8,128)(2,1)S(1)}, u32[]{:S(2)}, u32[]{:S(2)}) collective-permute-start(bf16[32,4096]{1,0:T(8,128)(2,1)S(1)} %slice.198), channel_id=1, source_target_pairs={{0,4},{1,5},{4,8},{5,9},{8,12},{9,13},{12,14},{13,15},{14,10},{15,... | collective-permute-start | bytes 786440 | tf_op jit(solution)/shard_map/ppermute | solution.py:44
  100.3 6.6 %collective-permute-start.27 = (bf16[32,4096]{1,0:T(8,128)(2,1)S(1)}, bf16[32,4096]{1,0:T(8,128)(2,1)S(1)}, u32[]{:S(2)}, u32[]{:S(2)}) collective-permute-start(bf16[32,4096]{1,0:T(8,128)(2,1)S(1)} %slice.199), channel_id=1, source_target_pairs={{0,2},{1,3},{4,0},{5,1},{8,4},{9,5},{12,8},{13,9},{14,12},{15,13},... | collective-permute-start | bytes 786440 | tf_op jit(solution)/shard_map/ppermute | solution.py:45
  107.6 3.8 %copy-start.12 = (bf16[1,1,768,2048]{3,2,1,0:T(8,128)(2,1)S(1)}, bf16[1,1,768,2048]{3,2,1,0:T(8,128)(2,1)}, u32[]{:S(2)}) copy-start(bf16[1,1,768,2048]{3,2,1,0:T(8,128)(2,1)} %param.21) | copy-start | bytes 9437188
  118.3 10.5 %copy-start.5 = (bf16[512,2176]{1,0:T(8,128)(2,1)S(1)}, bf16[512,2176]{1,0:T(8,128)(2,1)}, u32[]{:S(2)}) copy-start(bf16[512,2176]{1,0:T(8,128)(2,1)} %copy-done.4) | copy-start | bytes 6684676
  145.9 33.8 %collective-permute-start.11 = (bf16[32,2048]{1,0:T(8,128)(2,1)S(1)}, bf16[32,2048]{1,0:T(8,128)(2,1)S(1)}, u32[]{:S(2)}, u32[]{:S(2)}) collective-permute-start(bf16[32,2048]{1,0:T(8,128)(2,1)S(1)} %get-tuple-element.24), channel_id=1, source_target_pairs={{0,2},{1,3},{4,0},{5,1},{8,4},{9,5},{12,8},{13,9},{14,12},{15,13},... | collective-permute-start | bytes 393224 | tf_op jit(solution)/shard_map/ppermute | solution.py:55
  146.5 5.8 %copy-start.8 = (bf16[512,4096]{1,0:T(8,128)(2,1)S(1)}, bf16[512,4096]{1,0:T(8,128)(2,1)}, u32[]{:S(2)}) copy-start(bf16[512,4096]{1,0:T(8,128)(2,1)} %constant_dynamic-update-slice_fusion.9) | copy-start | bytes 12582916
  146.5 33.3 %collective-permute-start.15 = (bf16[32,2048]{1,0:T(8,128)(2,1)S(1)}, bf16[32,2048]{1,0:T(8,128)(2,1)S(1)}, u32[]{:S(2)}, u32[]{:S(2)}) collective-permute-start(bf16[32,2048]{1,0:T(8,128)(2,1)S(1)} %get-tuple-element.25), channel_id=1, source_target_pairs={{0,4},{1,5},{4,8},{5,9},{8,12},{9,13},{12,14},{13,15},{14,10},{15,... | collective-permute-start | bytes 393224 | tf_op jit(solution)/shard_map/ppermute | solution.py:56
  152.3 4.4 %copy-start.13 = (f32[512,768]{1,0:T(8,128)}, f32[512,768]{1,0:T(8,128)S(1)}, u32[]{:S(2)}) copy-start(f32[512,768]{1,0:T(8,128)S(1)} %fusion.10) | copy-start | bytes 4718596
  177.7 6.5 %collective-permute-start.28 = (bf16[32,2048]{1,0:T(8,128)(2,1)S(1)}, bf16[32,2048]{1,0:T(8,128)(2,1)S(1)}, u32[]{:S(2)}, u32[]{:S(2)}) collective-permute-start(bf16[32,2048]{1,0:T(8,128)(2,1)S(1)} %get-tuple-element.20), channel_id=1, source_target_pairs={{0,2},{1,3},{4,0},{5,1},{8,4},{9,5},{12,8},{13,9},{14,12},{15,13},... | collective-permute-start | bytes 393224 | tf_op jit(solution)/shard_map/ppermute | solution.py:55
  178.2 5.9 %collective-permute-start.32 = (bf16[32,2048]{1,0:T(8,128)(2,1)S(1)}, bf16[32,2048]{1,0:T(8,128)(2,1)S(1)}, u32[]{:S(2)}, u32[]{:S(2)}) collective-permute-start(bf16[32,2048]{1,0:T(8,128)(2,1)S(1)} %get-tuple-element.21), channel_id=1, source_target_pairs={{0,4},{1,5},{4,8},{5,9},{8,12},{9,13},{12,14},{13,15},{14,10},{15,... | collective-permute-start | bytes 393224 | tf_op jit(solution)/shard_map/ppermute | solution.py:56
  180.8 15.7 %copy-start.1 = (f32[512,2048]{1,0:T(8,128)S(1)}, f32[512,2048]{1,0:T(8,128)}, u32[]{:S(2)}) copy-start(f32[512,2048]{1,0:T(8,128)} %get-tuple-element.35) | copy-start | bytes 12582916
  180.9 16.6 %collective-permute-start.16 = (bf16[64,2048]{1,0:T(8,128)(2,1)S(1)}, bf16[64,2048]{1,0:T(8,128)(2,1)S(1)}, u32[]{:S(2)}, u32[]{:S(2)}) collective-permute-start(bf16[64,2048]{1,0:T(8,128)(2,1)S(1)} %pad_maximum_fusion.2), channel_id=1, source_target_pairs={{0,4},{1,5},{4,8},{5,9},{8,12},{9,13},{12,14},{13,15},{14,10},{15,... | collective-permute-start | bytes 786440 | tf_op jit(solution)/shard_map/ppermute | solution.py:70
  181.6 9.3 %collective-permute-start.12 = (bf16[64,2048]{1,0:T(8,128)(2,1)S(1)}, bf16[64,2048]{1,0:T(8,128)(2,1)S(1)}, u32[]{:S(2)}, u32[]{:S(2)}) collective-permute-start(bf16[64,2048]{1,0:T(8,128)(2,1)S(1)} %pad_maximum_fusion.1), channel_id=1, source_target_pairs={{0,2},{1,3},{4,0},{5,1},{8,4},{9,5},{12,8},{13,9},{14,12},{15,13},... | collective-permute-start | bytes 786440 | tf_op jit(solution)/shard_map/ppermute | solution.py:69
  185.3 18.3 %collective-permute-start.33 = (bf16[64,2048]{1,0:T(8,128)(2,1)S(1)}, bf16[64,2048]{1,0:T(8,128)(2,1)S(1)}, u32[]{:S(2)}, u32[]{:S(2)}) collective-permute-start(bf16[64,2048]{1,0:T(8,128)(2,1)S(1)} %pad_maximum_fusion.4), channel_id=1, source_target_pairs={{0,4},{1,5},{4,8},{5,9},{8,12},{9,13},{12,14},{13,15},{14,10},{15,... | collective-permute-start | bytes 786440 | tf_op jit(solution)/shard_map/ppermute | solution.py:70
  186.0 10.5 %collective-permute-start.29 = (bf16[64,2048]{1,0:T(8,128)(2,1)S(1)}, bf16[64,2048]{1,0:T(8,128)(2,1)S(1)}, u32[]{:S(2)}, u32[]{:S(2)}) collective-permute-start(bf16[64,2048]{1,0:T(8,128)(2,1)S(1)} %pad_maximum_fusion.3), channel_id=1, source_target_pairs={{0,2},{1,3},{4,0},{5,1},{8,4},{9,5},{12,8},{13,9},{14,12},{15,13},... | collective-permute-start | bytes 786440 | tf_op jit(solution)/shard_map/ppermute | solution.py:69
  192.0 8.1 %collective-permute-start.13 = (bf16[64,2048]{1,0:T(8,128)(2,1)S(1)}, bf16[64,2048]{1,0:T(8,128)(2,1)S(1)}, u32[]{:S(2)}, u32[]{:S(2)}) collective-permute-start(bf16[64,2048]{1,0:T(8,128)(2,1)S(1)} %fusion.69), channel_id=1, source_target_pairs={{0,2},{1,3},{4,0},{5,1},{8,4},{9,5},{12,8},{13,9},{14,12},{15,13},... | collective-permute-start | bytes 786440 | tf_op jit(solution)/shard_map/ppermute | solution.py:69
  196.6 7.0 %collective-permute-start.30 = (bf16[64,2048]{1,0:T(8,128)(2,1)S(1)}, bf16[64,2048]{1,0:T(8,128)(2,1)S(1)}, u32[]{:S(2)}, u32[]{:S(2)}) collective-permute-start(bf16[64,2048]{1,0:T(8,128)(2,1)S(1)} %fusion.63), channel_id=1, source_target_pairs={{0,2},{1,3},{4,0},{5,1},{8,4},{9,5},{12,8},{13,9},{14,12},{15,13},... | collective-permute-start | bytes 786440 | tf_op jit(solution)/shard_map/ppermute | solution.py:69
  201.5 15.0 %copy-start.2 = (bf16[1,64,2048]{2,1,0:T(8,128)(2,1)S(1)}, bf16[1,64,2048]{2,1,0:T(8,128)(2,1)}, u32[]{:S(2)}) copy-start(bf16[1,64,2048]{2,1,0:T(8,128)(2,1)} %param.11) | copy-start | bytes 786436
  201.5 11.4 %collective-permute-start.14 = (bf16[64,2048]{1,0:T(8,128)(2,1)S(1)}, bf16[64,2048]{1,0:T(8,128)(2,1)S(1)}, u32[]{:S(2)}, u32[]{:S(2)}) collective-permute-start(bf16[64,2048]{1,0:T(8,128)(2,1)S(1)} %get-tuple-element.14), channel_id=1, source_target_pairs={{0,2},{1,3},{4,0},{5,1},{8,4},{9,5},{12,8},{13,9},{14,12},{15,13},... | collective-permute-start | bytes 786440 | tf_op jit(solution)/shard_map/ppermute | solution.py:69
  202.6 6.4 %collective-permute-start.17 = (bf16[64,2048]{1,0:T(8,128)(2,1)S(1)}, bf16[64,2048]{1,0:T(8,128)(2,1)S(1)}, u32[]{:S(2)}, u32[]{:S(2)}) collective-permute-start(bf16[64,2048]{1,0:T(8,128)(2,1)S(1)} %get-tuple-element.15), channel_id=1, source_target_pairs={{0,4},{1,5},{4,8},{5,9},{8,12},{9,13},{12,14},{13,15},{14,10},{15,... | collective-permute-start | bytes 786440 | tf_op jit(solution)/shard_map/ppermute | solution.py:70
  203.7 15.6 %copy-start = (bf16[1,64,2048]{2,1,0:T(8,128)(2,1)S(1)}, bf16[1,64,2048]{2,1,0:T(8,128)(2,1)}, u32[]{:S(2)}) copy-start(bf16[1,64,2048]{2,1,0:T(8,128)(2,1)} %param.14) | copy-start | bytes 786436
  203.7 15.6 %copy-start.6 = (f32[1,2048]{1,0:T(1,128)S(1)}, f32[1,2048]{1,0:T(1,128)}, u32[]{:S(2)}) copy-start(f32[1,2048]{1,0:T(1,128)} %param.18) | copy-start | bytes 24580
  203.7 15.5 %collective-permute-start.31 = (bf16[64,2048]{1,0:T(8,128)(2,1)S(1)}, bf16[64,2048]{1,0:T(8,128)(2,1)S(1)}, u32[]{:S(2)}, u32[]{:S(2)}) collective-permute-start(bf16[64,2048]{1,0:T(8,128)(2,1)S(1)} %get-tuple-element.10), channel_id=1, source_target_pairs={{0,2},{1,3},{4,0},{5,1},{8,4},{9,5},{12,8},{13,9},{14,12},{15,13},... | collective-permute-start | bytes 786440 | tf_op jit(solution)/shard_map/ppermute | solution.py:69
  204.8 7.0 %collective-permute-start.34 = (bf16[64,2048]{1,0:T(8,128)(2,1)S(1)}, bf16[64,2048]{1,0:T(8,128)(2,1)S(1)}, u32[]{:S(2)}, u32[]{:S(2)}) collective-permute-start(bf16[64,2048]{1,0:T(8,128)(2,1)S(1)} %get-tuple-element.11), channel_id=1, source_target_pairs={{0,4},{1,5},{4,8},{5,9},{8,12},{9,13},{12,14},{13,15},{14,10},{15,... | collective-permute-start | bytes 786440 | tf_op jit(solution)/shard_map/ppermute | solution.py:70
  210.0 6.4 %collective-permute-start.18 = (bf16[64,2048]{1,0:T(8,128)(2,1)S(1)}, bf16[64,2048]{1,0:T(8,128)(2,1)S(1)}, u32[]{:S(2)}, u32[]{:S(2)}) collective-permute-start(bf16[64,2048]{1,0:T(8,128)(2,1)S(1)} %fusion.68), channel_id=1, source_target_pairs={{0,4},{1,5},{4,8},{5,9},{8,12},{9,13},{12,14},{13,15},{14,10},{15,... | collective-permute-start | bytes 786440 | tf_op jit(solution)/shard_map/ppermute | solution.py:70
  211.8 7.5 %collective-permute-start.35 = (bf16[64,2048]{1,0:T(8,128)(2,1)S(1)}, bf16[64,2048]{1,0:T(8,128)(2,1)S(1)}, u32[]{:S(2)}, u32[]{:S(2)}) collective-permute-start(bf16[64,2048]{1,0:T(8,128)(2,1)S(1)} %fusion.62), channel_id=1, source_target_pairs={{0,4},{1,5},{4,8},{5,9},{8,12},{9,13},{12,14},{13,15},{14,10},{15,... | collective-permute-start | bytes 786440 | tf_op jit(solution)/shard_map/ppermute | solution.py:70
  217.6 6.4 %collective-permute-start.19 = (bf16[1,64,2048]{2,1,0:T(8,128)(2,1)S(1)}, bf16[1,64,2048]{2,1,0:T(8,128)(2,1)S(1)}, u32[]{:S(2)}, u32[]{:S(2)}) collective-permute-start(bf16[1,64,2048]{2,1,0:T(8,128)(2,1)S(1)} %fusion.72), channel_id=1, source_target_pairs={{0,16},{16,0},{1,17},{17,1},{2,18},{18,2},{3,19},{19,3},{4,20},{20... | collective-permute-start | bytes 786440 | tf_op jit(solution)/shard_map/ppermute | solution.py:31
  219.8 7.1 %collective-permute-start.36 = (bf16[1,64,2048]{2,1,0:T(8,128)(2,1)S(1)}, bf16[1,64,2048]{2,1,0:T(8,128)(2,1)S(1)}, u32[]{:S(2)}, u32[]{:S(2)}) collective-permute-start(bf16[1,64,2048]{2,1,0:T(8,128)(2,1)S(1)} %fusion.73), channel_id=1, source_target_pairs={{0,16},{16,0},{1,17},{17,1},{2,18},{18,2},{3,19},{19,3},{4,20},{20... | collective-permute-start | bytes 786440 | tf_op jit(solution)/shard_map/ppermute | solution.py:31
  (6 other events, 14.1 us)

commit v2 on v1

v2 whole, which is shorter than its diff:
```python
import functools

import jax
import jax.numpy as jnp
from jax import lax
from jax.experimental import pallas as pl
from jax.experimental.pallas import tpu as pltpu
from jax.sharding import PartitionSpec as P

norm_epsilon = 1e-06
CORES = 2
LANES = 128
TILE = 256
ROWS_AT_ONCE = 256
MIB = 1 << 20
IN_HBM = pl.BlockSpec(memory_space=pl.ANY)
IN_VMEM = pl.BlockSpec(memory_space=pltpu.VMEM)
IN_SMEM = pl.BlockSpec(memory_space=pltpu.SMEM)


def ring_order(chips):
    return [*range(0, chips, 2), *reversed(range(1, chips, 2))]


def ring_route(devices, distance):
    order = ring_order(devices // CORES)
    chips = len(order)
    return [
        (chip * CORES + core, order[(place + distance) % chips] * CORES + core)
        for place, chip in enumerate(order)
        for core in range(CORES)
    ]


def core_route(devices):
    return [(i, i ^ 1) for i in range(devices)]


def passed_along(block, axis, distance):
    size = lax.axis_size(axis)
    return lax.ppermute(block, axis, [(i, (i + distance) % size) for i in range(size)])


def after(arrays, others):
    count = len(arrays)
    return lax.optimization_barrier((*arrays, *others))[:count]


class RingGather:
    def __init__(self, block):
        self.blocks = [block]
        self.newest = (block, block)
        self.left = lax.axis_size("expert") // CORES // 2

    def step(self, others=()):
        devices = lax.axis_size("expert")
        behind, ahead = after(self.newest, others)
        self.left -= 1
        if not self.left:
            half = behind.shape[0] // 2
            behind, ahead = behind[:half], ahead[half:]
        behind = lax.ppermute(behind, "expert", ring_route(devices, 1))
        ahead = lax.ppermute(ahead, "expert", ring_route(devices, -1))
        self.newest = (behind, ahead)
        self.blocks += self.newest


class RingScatter:
    def __init__(self, parts):
        self.parts = parts
        self.newest = ()
        self.reach = self.left = lax.axis_size("expert") // CORES // 2

    def step(self, others=()):
        devices = lax.axis_size("expert")
        to_behind, to_ahead = self.parts[2 * self.left - 1], self.parts[2 * self.left]
        if self.left == self.reach:
            behind, ahead = to_behind, to_ahead
        else:
            behind, ahead = after(self.newest, others)
            half = self.parts[0].shape[0] // 2
            if self.left == self.reach - 1:
                behind = jnp.concatenate([added(to_behind[:half], behind), to_behind[half:]])
                ahead = jnp.concatenate([to_ahead[:half], added(to_ahead[half:], ahead)])
            else:
                behind, ahead = added(to_behind, behind), added(to_ahead, ahead)
        self.left -= 1
        behind = lax.ppermute(behind, "expert", ring_route(devices, -1))
        ahead = lax.ppermute(ahead, "expert", ring_route(devices, 1))
        self.newest = (behind, ahead)

    def total(self):
        behind, ahead = self.newest
        return self.parts[0].astype(jnp.float32) + behind.astype(jnp.float32) + ahead.astype(jnp.float32)


def added(left, right):
    return (left.astype(jnp.float32) + right.astype(jnp.float32)).astype(jnp.bfloat16)


def inverse_norm(rows):
    return lax.rsqrt(jnp.mean(rows * rows, axis=-1, keepdims=True) + norm_epsilon)


def normalize(tokens, gain_row):
    tokens_f32 = tokens.astype(jnp.float32)
    return (tokens_f32 * inverse_norm(tokens_f32) * gain_row).astype(jnp.bfloat16)


def gate_table(choice, gates, experts):
    named = choice[:, :, None] == jnp.arange(experts)
    table = jnp.sum(jnp.where(named, gates[:, :, None], 0.0), axis=1)
    high = table.astype(jnp.bfloat16)
    return [high, (table - high.astype(jnp.float32)).astype(jnp.bfloat16)]


def dot_plain(left, right):
    return jnp.dot(left, right, preferred_element_type=jnp.float32)


def dot_trans(left, right):
    return lax.dot_general(
        left, right, (((1,), (1,)), ((), ())), preferred_element_type=jnp.float32
    )


def weights_body(*refs):
    weights, (gate_up, down, done) = refs[:6], refs[6:]
    hidden = weights[0].shape[1]
    copies = []
    for core in range(CORES):
        gate_w, up_w, down_w = weights[3 * core : 3 * core + 3]
        first = gate_up.at[:, pl.ds(2 * core * hidden, hidden)]
        second = gate_up.at[:, pl.ds((2 * core + 1) * hidden, hidden)]
        copies += [(gate_w, first), (up_w, second), (down_w, down.at[pl.ds(core * hidden, hidden)])]
    copies = [pltpu.make_async_copy(*pair, done.at[i]) for i, pair in enumerate(copies)]
    for copy in copies:
        copy.start()
    for copy in copies:
        copy.wait()


def weights_in_vmem(mine, theirs):
    width, hidden = mine[0].shape
    return pl.pallas_call(
        weights_body,
        in_specs=[IN_HBM] * 6,
        out_specs=(IN_VMEM, IN_VMEM),
        out_shape=(
            pltpu.VMEM((width, 2 * CORES * hidden), jnp.bfloat16),
            pltpu.VMEM((CORES * hidden, width), jnp.bfloat16),
        ),
        scratch_shapes=[pltpu.SemaphoreType.DMA((6,))],
        compiler_params=pltpu.CompilerParams(vmem_limit_bytes=24 * MIB),
    )(*mine, *theirs)


def collect(blocks, rows, arrived):
    copies, first = [], 0
    for i, block in enumerate(blocks):
        to = rows.at[pl.ds(first, block.shape[0])]
        copies.append(pltpu.make_async_copy(block, to, arrived.at[i]))
        first += block.shape[0]
    for copy in copies:
        copy.start()
    for copy in copies:
        copy.wait()


def backward_body(count, devices, *refs):
    blocks = refs[:count]
    experts, gate_up, down, out, forward_gates, rows, grads, arrived = refs[count:]
    width, hidden = gate_up.shape[0], down.shape[0] // CORES
    collect(blocks, rows, arrived)
    table = rows[:, 2 * width :].astype(jnp.float32)
    lane = lax.broadcasted_iota(jnp.int32, table.shape, 1)

    def gate(first, core):
        ours = first * devices + experts[core]
        named = (lane == ours) | (lane == ours + devices)
        return jnp.sum(jnp.where(named, table, 0.0), axis=1, keepdims=True)

    out_lane = lax.broadcasted_iota(jnp.int32, forward_gates.shape, 1)
    forward_gates[...] = jnp.where(out_lane == 0, gate(0, 0), gate(0, 1))
    for core in range(CORES):
        scale = gate(2, core)
        for tile in range(0, hidden, TILE):
            gate_at = pl.ds(2 * core * hidden + tile, TILE)
            up_at = pl.ds((2 * core + 1) * hidden + tile, TILE)
            down_at = pl.ds(core * hidden + tile, TILE)
            gate_act = dot_plain(rows[:, :width], gate_up[:, gate_at])
            up_act = dot_plain(rows[:, :width], gate_up[:, up_at])
            hidden_grad = dot_trans(rows[:, width : 2 * width], down[down_at, :]) * scale
            sigmoid_val = jax.nn.sigmoid(gate_act)
            silu_slope = sigmoid_val * (1.0 + gate_act * (1.0 - sigmoid_val))
            grads[:, gate_at] = (hidden_grad * up_act * silu_slope).astype(jnp.bfloat16)
            grads[:, up_at] = (hidden_grad * (gate_act * sigmoid_val)).astype(jnp.bfloat16)
    for tile in range(0, width, TILE):
        at = pl.ds(tile, TILE)
        out[:, at] = dot_trans(grads[...], gate_up[at, :]).astype(jnp.bfloat16)


def experts_backward(blocks, experts, gate_up, down, devices):
    count, rows = sum(b.shape[0] for b in blocks), blocks[0].shape[1]
    width = gate_up.shape[0]
    return pl.pallas_call(
        functools.partial(backward_body, len(blocks), devices),
        in_specs=[IN_HBM] * len(blocks) + [IN_SMEM, IN_VMEM, IN_VMEM],
        out_specs=(IN_VMEM, IN_VMEM),
        out_shape=(
            jax.ShapeDtypeStruct((count, width), jnp.bfloat16),
            jax.ShapeDtypeStruct((count, LANES), jnp.float32),
        ),
        scratch_shapes=[
            pltpu.VMEM((count, rows), jnp.bfloat16),
            pltpu.VMEM((count, gate_up.shape[1]), jnp.bfloat16),
            pltpu.SemaphoreType.DMA((len(blocks),)),
        ],
        compiler_params=pltpu.CompilerParams(vmem_limit_bytes=20 * MIB),
        cost_estimate=pl.CostEstimate(
            flops=2 * count * width * down.shape[0] * 5,
            bytes_accessed=count * (rows + width) * 2,
            transcendentals=0,
        ),
    )(*blocks, experts, gate_up, down)


def forward_body(count, *refs):
    blocks = refs[:count]
    gates, gate_up, down, out, rows, acts, arrived = refs[count:]
    width, hidden = gate_up.shape[0], down.shape[0] // CORES
    collect(blocks, rows, arrived)
    for core in range(CORES):
        scale = gates[:, core : core + 1]
        for tile in range(0, hidden, TILE):
            gate_at = pl.ds(2 * core * hidden + tile, TILE)
            up_at = pl.ds((2 * core + 1) * hidden + tile, TILE)
            gate_act = dot_plain(rows[...], gate_up[:, gate_at])
            up_act = dot_plain(rows[...], gate_up[:, up_at])
            act = gate_act * jax.nn.sigmoid(gate_act) * up_act * scale
            acts[:, pl.ds(core * hidden + tile, TILE)] = act.astype(jnp.bfloat16)
    for tile in range(0, width, TILE):
        at = pl.ds(tile, TILE)
        out[:, at] = dot_plain(acts[...], down[:, at]).astype(jnp.bfloat16)


def experts_forward(blocks, gates, gate_up, down):
    count, width = sum(b.shape[0] for b in blocks), gate_up.shape[0]
    return pl.pallas_call(
        functools.partial(forward_body, len(blocks)),
        in_specs=[IN_HBM] * len(blocks) + [IN_VMEM, IN_VMEM, IN_VMEM],
        out_specs=IN_VMEM,
        out_shape=jax.ShapeDtypeStruct((count, width), jnp.bfloat16),
        scratch_shapes=[
            pltpu.VMEM((count, width), jnp.bfloat16),
            pltpu.VMEM((count, down.shape[0]), jnp.bfloat16),
            pltpu.SemaphoreType.DMA((len(blocks),)),
        ],
        compiler_params=pltpu.CompilerParams(vmem_limit_bytes=20 * MIB),
        cost_estimate=pl.CostEstimate(
            flops=2 * count * width * down.shape[0] * 3,
            bytes_accessed=count * 2 * width * 2,
            transcendentals=0,
        ),
    )(*blocks, gates, gate_up, down)


def grouped(blocks):
    groups, rows = [[]], 0
    for block in blocks:
        if groups[-1] and rows + block.shape[0] > ROWS_AT_ONCE:
            groups.append([])
            rows = 0
        groups[-1].append(block)
        rows += block.shape[0]
    return groups


def ungrouped(outs, groups):
    parts = []
    for out, group in zip(outs, groups):
        first = 0
        for block in group:
            parts.append(out[first : first + block.shape[0]])
            first += block.shape[0]
    return parts


def per_device(
    forward_tokens,
    forward_choice,
    forward_gates,
    backward_tokens,
    backward_cotangent,
    backward_choice,
    backward_gates,
    norm_gain,
    gate_weight,
    up_weight,
    down_weight,
):
    devices = lax.axis_size("expert")
    gain_row = norm_gain[0]
    cotangent = backward_cotangent[0]
    tables = gate_table(forward_choice[0], forward_gates[0], devices) + gate_table(
        backward_choice[0], backward_gates[0], devices
    )
    pad = jnp.zeros((cotangent.shape[0], -4 * devices % LANES), jnp.bfloat16)
    back = RingGather(
        jnp.concatenate([normalize(backward_tokens[0], gain_row), cotangent, *tables, pad], axis=1)
    )
    fwd = RingGather(normalize(forward_tokens[0], gain_row))
    back.step()
    fwd.step()
    while back.left:
        arrived = back.newest
        back.step(fwd.newest)
        fwd.step(arrived)

    mine = (gate_weight[0, 0], up_weight[0, 0], down_weight[0, 0])
    theirs = tuple(lax.ppermute(w, "expert", core_route(devices)) for w in mine)
    gate_up, down = weights_in_vmem(mine, theirs)
    me = lax.axis_index("expert").astype(jnp.int32)
    experts = jnp.stack([me, me + 1 - 2 * lax.rem(me, 2)])

    back_groups, fwd_groups = grouped(back.blocks), grouped(fwd.blocks)
    back_outs = [experts_backward(g, experts, gate_up, down, devices) for g in back_groups]
    back_sum = RingScatter(ungrouped([out for out, _ in back_outs], back_groups))
    fwd_outs = [
        experts_forward(g, gates, gate_up, down) for g, (_, gates) in zip(fwd_groups, back_outs)
    ]
    fwd_sum = RingScatter(ungrouped(fwd_outs, fwd_groups))
    back_sum.step()
    fwd_sum.step()
    while back_sum.left:
        arrived = back_sum.newest
        back_sum.step(fwd_sum.newest)
        fwd_sum.step(arrived)

    back_f32 = backward_tokens[0].astype(jnp.float32)
    back_inverse = inverse_norm(back_f32)
    scaled = gain_row * back_sum.total()
    mean_term = jnp.mean(back_f32 * scaled, axis=-1, keepdims=True)
    token_grad = (
        cotangent.astype(jnp.float32)
        + back_inverse * scaled
        - back_f32 * back_inverse * back_inverse * back_inverse * mean_term
    )
    mixed_out = forward_tokens[0].astype(jnp.float32) + fwd_sum.total()
    section_input = passed_along(mixed_out.astype(jnp.bfloat16)[None], "section", 1)
    section_gradient = passed_along(token_grad.astype(jnp.bfloat16)[None], "section", -1)
    return (section_input, section_gradient)


def solution(mesh):
    rows = P("section", "expert", None)
    weights = P("section", "expert", None, None)
    return jax.shard_map(
        per_device,
        mesh=mesh,
        in_specs=(rows,) * 7 + (P("section", None),) + (weights,) * 3,
        out_specs=(rows, rows),
        check_vma=False,
    )
```

time: 231 us -> 167 us (0.72)
  matrix products: 76.9 us -> 0 us
  Pallas kernels: 0 us -> 35.4 us
  waiting for transfers between devices: 88.4 us -> 69.7 us
  other arithmetic: 14.3 us -> 6.45 us
  starting transfers between devices: 33.6 us -> 37.2 us
    dot_general x12 -> x0, matrix products: 76.9 us -> none  [the longest x6 40.3 us: dot_trans(): lax.dot_general(left, right, (((1,), (1,)), ((), ())), preferred_element_...]
    pallas_call x0 -> x5, Pallas kernels: none -> 35.4 us  [the longest x2 19.8 us: experts_backward(): pl.pallas_call(functools.partial(backward_body, len(blocks), devices), in...]
    ppermute x35, waiting for transfers between devices: 83 us -> 64.4 us  [the longest x8 36.2 us: step(): behind = lax.ppermute(behind, 'expert', ring_route(devices, 1))]
    convert_element_type x11 -> x12, other arithmetic: 6.44 us -> 1.94 us  [the longest x1 1.24 us: normalize(): (tokens_f32 * inverse_norm(tokens_f32) * gain_row).astype(jnp.bfloat16)]
    ppermute x35, starting transfers between devices: 30.4 us -> 34 us  [the longest x8 13.5 us: step(): ahead = lax.ppermute(ahead, 'expert', ring_route(devices, -1))]
    unnamed x53 -> x60, local copies, waits for them, and re-layouts: 11.5 us -> 12 us
  transfers between devices with their start and end apart: 37 -> 37, of which waited for: 20 -> 19; matrix products, arithmetic and copies ran while one was open for 36% -> 6% of each run, Pallas kernels for 0% -> 18%
where the time goes in v2:
time: 167 us; the launch traced here: 165 us
  waiting for transfers between devices  69.7 us (42%)
  starting transfers between devices  37.2 us (22%)
  Pallas kernels  35.4 us (21%)
  local copies, waits for them, and re-layouts  15 us (9%)
  other arithmetic  6.45 us (4%)
    ppermute x8, waiting for transfers between devices, step(): behind = lax.ppermute(behind, 'expert', ring_route(devices, 1))  36.2 us
    pallas_call x2, Pallas kernels, experts_backward(): pl.pallas_call(functools.partial(backward_body, len(blocks), devices), in...  19.8 us
    ppermute x8, waiting for transfers between devices, step(): ahead = lax.ppermute(ahead, 'expert', ring_route(devices, 1))  15.2 us
    ppermute x8, starting transfers between devices, step(): ahead = lax.ppermute(ahead, 'expert', ring_route(devices, -1))  13.5 us
    ppermute x8, starting transfers between devices, step(): behind = lax.ppermute(behind, 'expert', ring_route(devices, -1))  12.4 us
    unnamed x60, local copies, waits for them, and re-layouts  12 us
    pallas_call x2, Pallas kernels, experts_forward(): pl.pallas_call(functools.partial(forward_body, len(blocks)), in_specs=[IN...  10.7 us
    ppermute x8, waiting for transfers between devices, step(): ahead = lax.ppermute(ahead, 'expert', ring_route(devices, -1))  9 us
  transfers between devices with their start and end apart: 37, of which 19 were waited for; matrix products, arithmetic and copies ran while one was open for 6% of the time, Pallas kernels for 18%

profile of v2, /device:TPU:12, one launch (start us, length us, event | category | flops | bytes accessed | tf_op | source)
XLA Modules:
  0.0 164.9 jit_solution(7943991032814838989)
XLA Ops:
  1.3 1.1 fusion.11
  2.4 1.1 fusion.7
  3.5 1.2 fusion.2
  5.3 1.6 collective-permute-start.1
  8.7 1.1 concatenate.15.refs_0_
  9.8 3.6 %collective-permute-done.refs_1_ = bf16[64,2048]{1,0:T(8,128)(2,1)S(1)} collective-permute-done((bf16[64,2048]{1,0:T(8,128)(2,1)S(1)}, bf16[64,2048]{1,0:T(8,128)(2,1)S(1)}, u32[]{:S(2)}, u32[]{:S(2)}) %collective-permute-start) | collective-permute-done | bytes 262176 | tf_op jit(solution)/shard_map/ppermute | solution.py:62
  13.9 1.6 collective-permute-start.3
  15.5 11.8 %collective-permute-done.2.refs_1_ = bf16[64,4224]{1,0:T(8,128)(2,1)S(1)} collective-permute-done((bf16[64,4224]{1,0:T(8,128)(2,1)S(1)}, bf16[64,4224]{1,0:T(8,128)(2,1)S(1)}, u32[]{:S(2)}, u32[]{:S(2)}) %collective-permute-start.2) | collective-permute-done | bytes 540704 | tf_op jit(solution)/shard_map/ppermute | solution.py:62
  28.0 1.6 collective-permute-start.9
  29.5 4.8 %collective-permute-done.4.refs_3_ = bf16[64,2048]{1,0:T(8,128)(2,1)S(1)} collective-permute-done((bf16[64,2048]{1,0:T(8,128)(2,1)S(1)}, bf16[64,2048]{1,0:T(8,128)(2,1)S(1)}, u32[]{:S(2)}, u32[]{:S(2)}) %collective-permute-start.4) | collective-permute-done | bytes 262176 | tf_op jit(solution)/shard_map/ppermute | solution.py:62
  34.3 1.6 collective-permute-start.10
  37.9 8.2 %collective-permute-done.10.refs_0_ = bf16[64,4224]{1,0:T(8,128)(2,1)S(1)} collective-permute-done((bf16[64,4224]{1,0:T(8,128)(2,1)S(1)}, bf16[64,4224]{1,0:T(8,128)(2,1)S(1)}, u32[]{:S(2)}, u32[]{:S(2)}) %collective-permute-start.10) | collective-permute-done | bytes 540704 | tf_op jit(solution)/shard_map/ppermute | solution.py:63
  46.1 3.0 %collective-permute-done.5.refs_3_ = bf16[64,4224]{1,0:T(8,128)(2,1)S(1)} collective-permute-done((bf16[64,4224]{1,0:T(8,128)(2,1)S(1)}, bf16[64,4224]{1,0:T(8,128)(2,1)S(1)}, u32[]{:S(2)}, u32[]{:S(2)}) %collective-permute-start.5) | collective-permute-done | bytes 540704 | tf_op jit(solution)/shard_map/ppermute | solution.py:62
  49.5 1.6 collective-permute-start.12
  51.1 6.4 %collective-permute-done.11.refs_1_ = bf16[64,2048]{1,0:T(8,128)(2,1)S(1)} collective-permute-done((bf16[64,2048]{1,0:T(8,128)(2,1)S(1)}, bf16[64,2048]{1,0:T(8,128)(2,1)S(1)}, u32[]{:S(2)}, u32[]{:S(2)}) %collective-permute-start.11) | collective-permute-done | bytes 262176 | tf_op jit(solution)/shard_map/ppermute | solution.py:62
  58.8 1.6 collective-permute-start.14
  61.2 6.7 %collective-permute-done.13.refs_1_ = bf16[64,4224]{1,0:T(8,128)(2,1)S(1)} collective-permute-done((bf16[64,4224]{1,0:T(8,128)(2,1)S(1)}, bf16[64,4224]{1,0:T(8,128)(2,1)S(1)}, u32[]{:S(2)}, u32[]{:S(2)}) %collective-permute-start.13) | collective-permute-done | bytes 540704 | tf_op jit(solution)/shard_map/ppermute | solution.py:62
  69.2 0.8 copy-done.13
  71.5 2.0 %collective-permute-start.18 = (bf16[32,4224]{1,0:T(8,128)(2,1)}, bf16[32,4224]{1,0:T(8,128)(2,1)}, u32[]{:S(2)}, u32[]{:S(2)}) collective-permute-start(bf16[32,4224]{1,0:T(8,128)(2,1)} %slice.96), channel_id=1, source_target_pairs={{0,2},{1,3},{4,0},{5,1},{8,4},{9,5},{12,8},{13,9},{14,12},{15,13},... | collective-permute-start | bytes 811016 | tf_op jit(solution)/shard_map/ppermute | solution.py:63
  73.8 2.0 %collective-permute-start.16 = (bf16[32,2048]{1,0:T(8,128)(2,1)S(1)}, bf16[32,2048]{1,0:T(8,128)(2,1)S(1)}, u32[]{:S(2)}, u32[]{:S(2)}) collective-permute-start(bf16[32,2048]{1,0:T(8,128)(2,1)S(1)} %slice.94), channel_id=1, source_target_pairs={{0,2},{1,3},{4,0},{5,1},{8,4},{9,5},{12,8},{13,9},{14,12},{15,13},... | collective-permute-start | bytes 393224 | tf_op jit(solution)/shard_map/ppermute | solution.py:63
  75.8 1.9 %copy-done = bf16[1,1,2048,768]{3,2,1,0:T(8,128)(2,1)S(1)} copy-done((bf16[1,1,2048,768]{3,2,1,0:T(8,128)(2,1)S(1)}, bf16[1,1,2048,768]{3,2,1,0:T(8,128)(2,1)}, u32[]{:S(2)}) %copy-start) | copy-done | bytes 3145752
  77.7 1.9 %copy-done.1 = bf16[1,1,2048,768]{3,2,1,0:T(8,128)(2,1)S(1)} copy-done((bf16[1,1,2048,768]{3,2,1,0:T(8,128)(2,1)S(1)}, bf16[1,1,2048,768]{3,2,1,0:T(8,128)(2,1)}, u32[]{:S(2)}) %copy-start.1) | copy-done | bytes 3145752
  79.6 1.9 %copy-done.2 = bf16[1,1,768,2048]{3,2,1,0:T(8,128)(2,1)S(1)} copy-done((bf16[1,1,768,2048]{3,2,1,0:T(8,128)(2,1)S(1)}, bf16[1,1,768,2048]{3,2,1,0:T(8,128)(2,1)}, u32[]{:S(2)}) %copy-start.2) | copy-done | bytes 3145752
  81.5 4.9 %shard_map.122 = (bf16[2048,3072]{1,0:T(8,128)(2,1)S(1)}, bf16[1536,2048]{1,0:T(8,128)(2,1)S(1)}) custom-call(bf16[2048,768]{1,0:T(8,128)(2,1)S(1)} %bitcast.30, bf16[2048,768]{1,0:T(8,128)(2,1)S(1)} %bitcast.32, bf16[768,2048]{1,0:T(8,128)(2,1)S(1)} %bitcast.34, bf16[2048,768]{1,0:T(8,128)(2,1)} %collective-permute-done.6.refs_3_, ...), custom_call_target="tpu_custom_call" | custom-call | tf_op jit(solution)/shard_map/pallas_call | solution.py:145
  86.5 10.4 %shard_map.125 = (bf16[256,2048]{1,0:T(8,128)(2,1)S(1)}, f32[256,128]{1,0:T(8,128)S(1)}) custom-call(bf16[64,4224]{1,0:T(8,128)(2,1)S(1)} %copy-done.24, bf16[64,4224]{1,0:T(8,128)(2,1)S(1)} %copy-done.14, bf16[64,4224]{1,0:T(8,128)(2,1)S(1)} %copy-done.16, bf16[32,4224]{1,0:T(8,128)(2,1)} %collective-permute-done.17.refs_3_, ...), custom_call_target="tpu_custom_call" | custom-call | flops 8053063680 | bytes 3211264 | tf_op jit(solution)/shard_map/pallas_call | solution.py:206
  96.9 5.5 %shard_map.126 = bf16[256,2048]{1,0:T(8,128)(2,1)S(1)} custom-call(bf16[64,2048]{1,0:T(8,128)(2,1)S(1)} %copy-done.12, bf16[64,2048]{1,0:T(8,128)(2,1)S(1)} %collective-permute-done.11.refs_1_, bf16[64,2048]{1,0:T(8,128)(2,1)S(1)} %collective-permute-done.12.refs_2_, bf16[32,2048]{1,0:T(8,128)(2,1)S(1)} %collective-permute-done.15.refs_3_, ...), custom_call_target="tpu_custom_call" | custom-call | flops 4831838208 | bytes 2097152 | tf_op jit(solution)/shard_map/pallas_call | solution.py:249
  102.5 1.5 collective-permute-start.19
  104.6 1.5 collective-permute-start.21
  106.7 9.4 %shard_map.123 = (bf16[256,2048]{1,0:T(8,128)(2,1)S(1)}, f32[256,128]{1,0:T(8,128)S(1)}) custom-call(bf16[64,4224]{1,0:T(8,128)(2,1)S(1)} %copy-done.4, bf16[64,4224]{1,0:T(8,128)(2,1)S(1)} %copy-done.18, bf16[64,4224]{1,0:T(8,128)(2,1)S(1)} %copy-done.20, bf16[64,4224]{1,0:T(8,128)(2,1)S(1)} %copy-done.22, s32[2]{0:T(128)S(1)} %pad_add_fusion.refs_4_.refs_5_, ...), custom_call_target="tpu_custom_call" | custom-call | flops 8053063680 | bytes 3211264 | tf_op jit(solution)/shard_map/pallas_call | solution.py:206
  116.6 1.8 %collective-permute-start.25 = (bf16[64,2048]{1,0:T(8,128)(2,1)S(1)}, bf16[64,2048]{1,0:T(8,128)(2,1)S(1)}, u32[]{:S(2)}, u32[]{:S(2)}) collective-permute-start(bf16[64,2048]{1,0:T(8,128)(2,1)S(1)} %pad_maximum_fusion.2), channel_id=1, source_target_pairs={{0,2},{1,3},{4,0},{5,1},{8,4},{9,5},{12,8},{13,9},{14,12},{15,13},... | collective-permute-start | bytes 786440 | tf_op jit(solution)/shard_map/ppermute | solution.py:88
  118.9 2.1 %collective-permute-start.23 = (bf16[64,2048]{1,0:T(8,128)(2,1)S(1)}, bf16[64,2048]{1,0:T(8,128)(2,1)S(1)}, u32[]{:S(2)}, u32[]{:S(2)}) collective-permute-start(bf16[64,2048]{1,0:T(8,128)(2,1)S(1)} %pad_maximum_fusion), channel_id=1, source_target_pairs={{0,2},{1,3},{4,0},{5,1},{8,4},{9,5},{12,8},{13,9},{14,12},{15,13},... | collective-permute-start | bytes 786440 | tf_op jit(solution)/shard_map/ppermute | solution.py:88
  121.0 5.2 %shard_map.124 = bf16[256,2048]{1,0:T(8,128)(2,1)S(1)} custom-call(bf16[64,2048]{1,0:T(8,128)(2,1)S(1)} %get-tuple-element.37.refs_0_, bf16[64,2048]{1,0:T(8,128)(2,1)S(1)} %copy-done.6, bf16[64,2048]{1,0:T(8,128)(2,1)S(1)} %copy-done.8, bf16[64,2048]{1,0:T(8,128)(2,1)S(1)} %copy-done.10, f32[256,128]{1,0:T(8,128)S(1)} %get-tuple-element.44.refs_4_, ...), custom_call_target="tpu_custom_call" | custom-call | flops 4831838208 | bytes 2097152 | tf_op jit(solution)/shard_map/pallas_call | solution.py:249
  126.2 4.3 %collective-permute-done.24 = bf16[64,2048]{1,0:T(8,128)(2,1)S(1)} collective-permute-done((bf16[64,2048]{1,0:T(8,128)(2,1)S(1)}, bf16[64,2048]{1,0:T(8,128)(2,1)S(1)}, u32[]{:S(2)}, u32[]{:S(2)}) %collective-permute-start.24) | collective-permute-done | bytes 262176 | tf_op jit(solution)/shard_map/ppermute | solution.py:89
  131.0 1.0 collective-permute-start.30
  132.0 1.2 collective-permute-start.29
  133.3 1.2 collective-permute-start.28
  134.5 0.9 collective-permute-start.27
  135.5 4.7 %collective-permute-done.30 = bf16[64,2048]{1,0:T(8,128)(2,1)S(1)} collective-permute-done((bf16[64,2048]{1,0:T(8,128)(2,1)S(1)}, bf16[64,2048]{1,0:T(8,128)(2,1)S(1)}, u32[]{:S(2)}, u32[]{:S(2)}) %collective-permute-start.30) | collective-permute-done | bytes 262176 | tf_op jit(solution)/shard_map/ppermute | solution.py:89
  140.1 1.4 collective-permute-done.29
  141.5 4.0 %collective-permute-done.28 = bf16[64,2048]{1,0:T(8,128)(2,1)S(1)} collective-permute-done((bf16[64,2048]{1,0:T(8,128)(2,1)S(1)}, bf16[64,2048]{1,0:T(8,128)(2,1)S(1)}, u32[]{:S(2)}, u32[]{:S(2)}) %collective-permute-start.28) | collective-permute-done | bytes 262176 | tf_op jit(solution)/shard_map/ppermute | solution.py:89
  145.6 1.7 %collective-permute-start.34 = (bf16[64,2048]{1,0:T(8,128)(2,1)S(1)}, bf16[64,2048]{1,0:T(8,128)(2,1)S(1)}, u32[]{:S(2)}, u32[]{:S(2)}) collective-permute-start(bf16[64,2048]{1,0:T(8,128)(2,1)S(1)} %get-tuple-element.70), channel_id=1, source_target_pairs={{0,2},{1,3},{4,0},{5,1},{8,4},{9,5},{12,8},{13,9},{14,12},{15,13},... | collective-permute-start | bytes 786440 | tf_op jit(solution)/shard_map/ppermute | solution.py:88
  147.9 1.7 %collective-permute-start.31 = (bf16[64,2048]{1,0:T(8,128)(2,1)S(1)}, bf16[64,2048]{1,0:T(8,128)(2,1)S(1)}, u32[]{:S(2)}, u32[]{:S(2)}) collective-permute-start(bf16[64,2048]{1,0:T(8,128)(2,1)S(1)} %get-tuple-element.72), channel_id=1, source_target_pairs={{0,2},{1,3},{4,0},{5,1},{8,4},{9,5},{12,8},{13,9},{14,12},{15,13},... | collective-permute-start | bytes 786440 | tf_op jit(solution)/shard_map/ppermute | solution.py:88
  149.9 2.1 %collective-permute-done.34 = bf16[64,2048]{1,0:T(8,128)(2,1)S(1)} collective-permute-done((bf16[64,2048]{1,0:T(8,128)(2,1)S(1)}, bf16[64,2048]{1,0:T(8,128)(2,1)S(1)}, u32[]{:S(2)}, u32[]{:S(2)}) %collective-permute-start.34) | collective-permute-done | bytes 262176 | tf_op jit(solution)/shard_map/ppermute | solution.py:88
  152.1 1.6 collective-permute-done.35
  154.3 1.6 collective-permute-start.36
  156.6 1.6 collective-permute-start.33
  158.2 2.5 %collective-permute-done.36 = bf16[1,64,2048]{2,1,0:T(8,128)(2,1)S(1)} collective-permute-done((bf16[1,64,2048]{2,1,0:T(8,128)(2,1)S(1)}, bf16[1,64,2048]{2,1,0:T(8,128)(2,1)S(1)}, u32[]{:S(2)}, u32[]{:S(2)}) %collective-permute-start.36) | collective-permute-done | bytes 262176 | tf_op jit(solution)/shard_map/ppermute | solution.py:41
  160.7 2.8 %collective-permute-done.33 = bf16[1,64,2048]{2,1,0:T(8,128)(2,1)S(1)} collective-permute-done((bf16[1,64,2048]{2,1,0:T(8,128)(2,1)S(1)}, bf16[1,64,2048]{2,1,0:T(8,128)(2,1)S(1)}, u32[]{:S(2)}, u32[]{:S(2)}) %collective-permute-start.33) | collective-permute-done | bytes 262176 | tf_op jit(solution)/shard_map/ppermute | solution.py:41
  (129 shorter events, 18.3 us)
Async XLA Ops:
  0.6 73.1 %collective-permute-start.6 = (bf16[2048,768]{1,0:T(8,128)(2,1)}, bf16[2048,768]{1,0:T(8,128)(2,1)}, u32[]{:S(2)}, u32[]{:S(2)}) collective-permute-start(bf16[2048,768]{1,0:T(8,128)(2,1)} %bitcast.29), channel_id=1, source_target_pairs={{0,1},{1,0},{2,3},{3,2},{4,5},{5,4},{6,7},{7,6},{8,9},{9,8},{10,11... | collective-permute-start | bytes 9437192 | tf_op jit(solution)/shard_map/ppermute | solution.py:321
  0.7 73.0 %collective-permute-start.7 = (bf16[2048,768]{1,0:T(8,128)(2,1)}, bf16[2048,768]{1,0:T(8,128)(2,1)}, u32[]{:S(2)}, u32[]{:S(2)}) collective-permute-start(bf16[2048,768]{1,0:T(8,128)(2,1)} %bitcast.31), channel_id=1, source_target_pairs={{0,1},{1,0},{2,3},{3,2},{4,5},{5,4},{6,7},{7,6},{8,9},{9,8},{10,11... | collective-permute-start | bytes 9437192 | tf_op jit(solution)/shard_map/ppermute | solution.py:321
  1.2 74.6 %collective-permute-start.8 = (bf16[768,2048]{1,0:T(8,128)(2,1)}, bf16[768,2048]{1,0:T(8,128)(2,1)}, u32[]{:S(2)}, u32[]{:S(2)}) collective-permute-start(bf16[768,2048]{1,0:T(8,128)(2,1)} %bitcast.33), channel_id=1, source_target_pairs={{0,1},{1,0},{2,3},{3,2},{4,5},{5,4},{6,7},{7,6},{8,9},{9,8},{10,11... | collective-permute-start | bytes 9437192 | tf_op jit(solution)/shard_map/ppermute | solution.py:321
  4.8 8.7 %collective-permute-start = (bf16[64,2048]{1,0:T(8,128)(2,1)S(1)}, bf16[64,2048]{1,0:T(8,128)(2,1)S(1)}, u32[]{:S(2)}, u32[]{:S(2)}) collective-permute-start(bf16[64,2048]{1,0:T(8,128)(2,1)S(1)} %get-tuple-element.37.refs_0_), channel_id=1, source_target_pairs={{0,4},{1,5},{4,8},{5,9},{8,12},{9,13},{12,14},{13,15},{14,10},{15,... | collective-permute-start | bytes 786440 | tf_op jit(solution)/shard_map/ppermute | solution.py:62
  5.3 8.7 %collective-permute-start.1 = (bf16[64,2048]{1,0:T(8,128)(2,1)S(1)}, bf16[64,2048]{1,0:T(8,128)(2,1)S(1)}, u32[]{:S(2)}, u32[]{:S(2)}) collective-permute-start(bf16[64,2048]{1,0:T(8,128)(2,1)S(1)} %get-tuple-element.37.refs_0_), channel_id=1, source_target_pairs={{0,2},{1,3},{4,0},{5,1},{8,4},{9,5},{12,8},{13,9},{14,12},{15,13},... | collective-permute-start | bytes 786440 | tf_op jit(solution)/shard_map/ppermute | solution.py:63
  9.8 65.9 %copy-start.3 = (bf16[64,4224]{1,0:T(8,128)(2,1)}, bf16[64,4224]{1,0:T(8,128)(2,1)S(1)}, u32[]{:S(2)}) copy-start(bf16[64,4224]{1,0:T(8,128)(2,1)S(1)} %concatenate.15.refs_0_) | copy-start | bytes 1622020
  13.5 62.3 %copy-start.5 = (bf16[64,2048]{1,0:T(8,128)(2,1)}, bf16[64,2048]{1,0:T(8,128)(2,1)S(1)}, u32[]{:S(2)}) copy-start(bf16[64,2048]{1,0:T(8,128)(2,1)S(1)} %collective-permute-done.refs_1_) | copy-start | bytes 786436
  13.5 13.8 %collective-permute-start.2 = (bf16[64,4224]{1,0:T(8,128)(2,1)S(1)}, bf16[64,4224]{1,0:T(8,128)(2,1)S(1)}, u32[]{:S(2)}, u32[]{:S(2)}) collective-permute-start(bf16[64,4224]{1,0:T(8,128)(2,1)S(1)} %concatenate.15.refs_0_), channel_id=1, source_target_pairs={{0,4},{1,5},{4,8},{5,9},{8,12},{9,13},{12,14},{13,15},{14,10},{15,... | collective-permute-start | bytes 1622024 | tf_op jit(solution)/shard_map/ppermute | solution.py:62
  13.9 61.9 %copy-start.7 = (bf16[64,2048]{1,0:T(8,128)(2,1)}, bf16[64,2048]{1,0:T(8,128)(2,1)S(1)}, u32[]{:S(2)}) copy-start(bf16[64,2048]{1,0:T(8,128)(2,1)S(1)} %collective-permute-done.1.refs_2_) | copy-start | bytes 786436
  13.9 13.5 %collective-permute-start.3 = (bf16[64,4224]{1,0:T(8,128)(2,1)S(1)}, bf16[64,4224]{1,0:T(8,128)(2,1)S(1)}, u32[]{:S(2)}, u32[]{:S(2)}) collective-permute-start(bf16[64,4224]{1,0:T(8,128)(2,1)S(1)} %concatenate.15.refs_0_), channel_id=1, source_target_pairs={{0,2},{1,3},{4,0},{5,1},{8,4},{9,5},{12,8},{13,9},{14,12},{15,13},... | collective-permute-start | bytes 1622024 | tf_op jit(solution)/shard_map/ppermute | solution.py:63
  27.5 6.8 %collective-permute-start.4 = (bf16[64,2048]{1,0:T(8,128)(2,1)S(1)}, bf16[64,2048]{1,0:T(8,128)(2,1)S(1)}, u32[]{:S(2)}, u32[]{:S(2)}) collective-permute-start(bf16[64,2048]{1,0:T(8,128)(2,1)S(1)} %collective-permute-done.refs_1_), channel_id=1, source_target_pairs={{0,4},{1,5},{4,8},{5,9},{8,12},{9,13},{12,14},{13,15},{14,10},{15,... | collective-permute-start | bytes 786440 | tf_op jit(solution)/shard_map/ppermute | solution.py:62
  28.0 8.7 %collective-permute-start.9 = (bf16[64,2048]{1,0:T(8,128)(2,1)S(1)}, bf16[64,2048]{1,0:T(8,128)(2,1)S(1)}, u32[]{:S(2)}, u32[]{:S(2)}) collective-permute-start(bf16[64,2048]{1,0:T(8,128)(2,1)S(1)} %collective-permute-done.1.refs_2_), channel_id=1, source_target_pairs={{0,2},{1,3},{4,0},{5,1},{8,4},{9,5},{12,8},{13,9},{14,12},{15,13},... | collective-permute-start | bytes 786440 | tf_op jit(solution)/shard_map/ppermute | solution.py:63
  34.3 41.5 %copy-start.9 = (bf16[64,2048]{1,0:T(8,128)(2,1)}, bf16[64,2048]{1,0:T(8,128)(2,1)S(1)}, u32[]{:S(2)}) copy-start(bf16[64,2048]{1,0:T(8,128)(2,1)S(1)} %collective-permute-done.4.refs_3_) | copy-start | bytes 786436
  34.3 11.9 %collective-permute-start.10 = (bf16[64,4224]{1,0:T(8,128)(2,1)S(1)}, bf16[64,4224]{1,0:T(8,128)(2,1)S(1)}, u32[]{:S(2)}, u32[]{:S(2)}) collective-permute-start(bf16[64,4224]{1,0:T(8,128)(2,1)S(1)} %collective-permute-done.3.refs_2_), channel_id=1, source_target_pairs={{0,2},{1,3},{4,0},{5,1},{8,4},{9,5},{12,8},{13,9},{14,12},{15,13},... | collective-permute-start | bytes 1622024 | tf_op jit(solution)/shard_map/ppermute | solution.py:63
  36.7 39.1 %copy-start.11 = (bf16[64,2048]{1,0:T(8,128)(2,1)}, bf16[64,2048]{1,0:T(8,128)(2,1)S(1)}, u32[]{:S(2)}) copy-start(bf16[64,2048]{1,0:T(8,128)(2,1)S(1)} %collective-permute-done.9.refs_0_) | copy-start | bytes 786436
  36.7 12.4 %collective-permute-start.5 = (bf16[64,4224]{1,0:T(8,128)(2,1)S(1)}, bf16[64,4224]{1,0:T(8,128)(2,1)S(1)}, u32[]{:S(2)}, u32[]{:S(2)}) collective-permute-start(bf16[64,4224]{1,0:T(8,128)(2,1)S(1)} %collective-permute-done.2.refs_1_), channel_id=1, source_target_pairs={{0,4},{1,5},{4,8},{5,9},{8,12},{9,13},{12,14},{13,15},{14,10},{15,... | collective-permute-start | bytes 1622024 | tf_op jit(solution)/shard_map/ppermute | solution.py:62
  49.1 8.4 %collective-permute-start.11 = (bf16[64,2048]{1,0:T(8,128)(2,1)S(1)}, bf16[64,2048]{1,0:T(8,128)(2,1)S(1)}, u32[]{:S(2)}, u32[]{:S(2)}) collective-permute-start(bf16[64,2048]{1,0:T(8,128)(2,1)S(1)} %collective-permute-done.4.refs_3_), channel_id=1, source_target_pairs={{0,4},{1,5},{4,8},{5,9},{8,12},{9,13},{12,14},{13,15},{14,10},{15,... | collective-permute-start | bytes 786440 | tf_op jit(solution)/shard_map/ppermute | solution.py:62
  49.5 9.2 %collective-permute-start.12 = (bf16[64,2048]{1,0:T(8,128)(2,1)S(1)}, bf16[64,2048]{1,0:T(8,128)(2,1)S(1)}, u32[]{:S(2)}, u32[]{:S(2)}) collective-permute-start(bf16[64,2048]{1,0:T(8,128)(2,1)S(1)} %collective-permute-done.9.refs_0_), channel_id=1, source_target_pairs={{0,2},{1,3},{4,0},{5,1},{8,4},{9,5},{12,8},{13,9},{14,12},{15,13},... | collective-permute-start | bytes 786440 | tf_op jit(solution)/shard_map/ppermute | solution.py:63
  57.5 10.3 %collective-permute-start.13 = (bf16[64,4224]{1,0:T(8,128)(2,1)S(1)}, bf16[64,4224]{1,0:T(8,128)(2,1)S(1)}, u32[]{:S(2)}, u32[]{:S(2)}) collective-permute-start(bf16[64,4224]{1,0:T(8,128)(2,1)S(1)} %collective-permute-done.5.refs_3_), channel_id=1, source_target_pairs={{0,4},{1,5},{4,8},{5,9},{8,12},{9,13},{12,14},{13,15},{14,10},{15,... | collective-permute-start | bytes 1622024 | tf_op jit(solution)/shard_map/ppermute | solution.py:62
  58.8 9.7 %collective-permute-start.14 = (bf16[64,4224]{1,0:T(8,128)(2,1)S(1)}, bf16[64,4224]{1,0:T(8,128)(2,1)S(1)}, u32[]{:S(2)}, u32[]{:S(2)}) collective-permute-start(bf16[64,4224]{1,0:T(8,128)(2,1)S(1)} %collective-permute-done.10.refs_0_), channel_id=1, source_target_pairs={{0,2},{1,3},{4,0},{5,1},{8,4},{9,5},{12,8},{13,9},{14,12},{15,13},... | collective-permute-start | bytes 1622024 | tf_op jit(solution)/shard_map/ppermute | solution.py:63
  70.0 16.4 %collective-permute-start.17 = (bf16[32,4224]{1,0:T(8,128)(2,1)}, bf16[32,4224]{1,0:T(8,128)(2,1)}, u32[]{:S(2)}, u32[]{:S(2)}) collective-permute-start(bf16[32,4224]{1,0:T(8,128)(2,1)} %slice.95), channel_id=1, source_target_pairs={{0,4},{1,5},{4,8},{5,9},{8,12},{9,13},{12,14},{13,15},{14,10},{15,... | collective-permute-start | bytes 811016 | tf_op jit(solution)/shard_map/ppermute | solution.py:62
  71.5 14.9 %collective-permute-start.18 = (bf16[32,4224]{1,0:T(8,128)(2,1)}, bf16[32,4224]{1,0:T(8,128)(2,1)}, u32[]{:S(2)}, u32[]{:S(2)}) collective-permute-start(bf16[32,4224]{1,0:T(8,128)(2,1)} %slice.96), channel_id=1, source_target_pairs={{0,2},{1,3},{4,0},{5,1},{8,4},{9,5},{12,8},{13,9},{14,12},{15,13},... | collective-permute-start | bytes 811016 | tf_op jit(solution)/shard_map/ppermute | solution.py:63
  73.7 23.2 %collective-permute-start.15 = (bf16[32,2048]{1,0:T(8,128)(2,1)S(1)}, bf16[32,2048]{1,0:T(8,128)(2,1)S(1)}, u32[]{:S(2)}, u32[]{:S(2)}) collective-permute-start(bf16[32,2048]{1,0:T(8,128)(2,1)S(1)} %slice.93), channel_id=1, source_target_pairs={{0,4},{1,5},{4,8},{5,9},{8,12},{9,13},{12,14},{13,15},{14,10},{15,... | collective-permute-start | bytes 393224 | tf_op jit(solution)/shard_map/ppermute | solution.py:62
  73.8 23.1 %collective-permute-start.16 = (bf16[32,2048]{1,0:T(8,128)(2,1)S(1)}, bf16[32,2048]{1,0:T(8,128)(2,1)S(1)}, u32[]{:S(2)}, u32[]{:S(2)}) collective-permute-start(bf16[32,2048]{1,0:T(8,128)(2,1)S(1)} %slice.94), channel_id=1, source_target_pairs={{0,2},{1,3},{4,0},{5,1},{8,4},{9,5},{12,8},{13,9},{14,12},{15,13},... | collective-permute-start | bytes 393224 | tf_op jit(solution)/shard_map/ppermute | solution.py:63
  86.5 10.4 %copy-start.12 = (bf16[64,2048]{1,0:T(8,128)(2,1)S(1)}, bf16[64,2048]{1,0:T(8,128)(2,1)}, u32[]{:S(2)}) copy-start(bf16[64,2048]{1,0:T(8,128)(2,1)} %copy-done.11) | copy-start | bytes 786436
  96.9 9.8 %copy-start.4 = (bf16[64,4224]{1,0:T(8,128)(2,1)S(1)}, bf16[64,4224]{1,0:T(8,128)(2,1)}, u32[]{:S(2)}) copy-start(bf16[64,4224]{1,0:T(8,128)(2,1)} %copy-done.3) | copy-start | bytes 1622020
  102.5 13.6 %collective-permute-start.19 = (bf16[32,2048]{1,0:T(8,128)(2,1)S(1)}, bf16[32,2048]{1,0:T(8,128)(2,1)S(1)}, u32[]{:S(2)}, u32[]{:S(2)}) collective-permute-start(bf16[32,2048]{1,0:T(8,128)(2,1)S(1)} %get-tuple-element.83), channel_id=1, source_target_pairs={{0,2},{1,3},{4,0},{5,1},{8,4},{9,5},{12,8},{13,9},{14,12},{15,13},... | collective-permute-start | bytes 393224 | tf_op jit(solution)/shard_map/ppermute | solution.py:88
  104.0 12.1 %collective-permute-start.20 = (bf16[32,2048]{1,0:T(8,128)(2,1)S(1)}, bf16[32,2048]{1,0:T(8,128)(2,1)S(1)}, u32[]{:S(2)}, u32[]{:S(2)}) collective-permute-start(bf16[32,2048]{1,0:T(8,128)(2,1)S(1)} %get-tuple-element.82), channel_id=1, source_target_pairs={{0,4},{1,5},{4,8},{5,9},{8,12},{9,13},{12,14},{13,15},{14,10},{15,... | collective-permute-start | bytes 393224 | tf_op jit(solution)/shard_map/ppermute | solution.py:89
  104.6 11.5 %collective-permute-start.21 = (bf16[32,2048]{1,0:T(8,128)(2,1)S(1)}, bf16[32,2048]{1,0:T(8,128)(2,1)S(1)}, u32[]{:S(2)}, u32[]{:S(2)}) collective-permute-start(bf16[32,2048]{1,0:T(8,128)(2,1)S(1)} %get-tuple-element.77), channel_id=1, source_target_pairs={{0,2},{1,3},{4,0},{5,1},{8,4},{9,5},{12,8},{13,9},{14,12},{15,13},... | collective-permute-start | bytes 393224 | tf_op jit(solution)/shard_map/ppermute | solution.py:88
  106.2 10.0 %collective-permute-start.22 = (bf16[32,2048]{1,0:T(8,128)(2,1)S(1)}, bf16[32,2048]{1,0:T(8,128)(2,1)S(1)}, u32[]{:S(2)}, u32[]{:S(2)}) collective-permute-start(bf16[32,2048]{1,0:T(8,128)(2,1)S(1)} %get-tuple-element.76), channel_id=1, source_target_pairs={{0,4},{1,5},{4,8},{5,9},{8,12},{9,13},{12,14},{13,15},{14,10},{15,... | collective-permute-start | bytes 393224 | tf_op jit(solution)/shard_map/ppermute | solution.py:89
  116.3 9.9 %collective-permute-start.26 = (bf16[64,2048]{1,0:T(8,128)(2,1)S(1)}, bf16[64,2048]{1,0:T(8,128)(2,1)S(1)}, u32[]{:S(2)}, u32[]{:S(2)}) collective-permute-start(bf16[64,2048]{1,0:T(8,128)(2,1)S(1)} %pad_maximum_fusion.3), channel_id=1, source_target_pairs={{0,4},{1,5},{4,8},{5,9},{8,12},{9,13},{12,14},{13,15},{14,10},{15,... | collective-permute-start | bytes 786440 | tf_op jit(solution)/shard_map/ppermute | solution.py:89
  116.6 9.6 %collective-permute-start.25 = (bf16[64,2048]{1,0:T(8,128)(2,1)S(1)}, bf16[64,2048]{1,0:T(8,128)(2,1)S(1)}, u32[]{:S(2)}, u32[]{:S(2)}) collective-permute-start(bf16[64,2048]{1,0:T(8,128)(2,1)S(1)} %pad_maximum_fusion.2), channel_id=1, source_target_pairs={{0,2},{1,3},{4,0},{5,1},{8,4},{9,5},{12,8},{13,9},{14,12},{15,13},... | collective-permute-start | bytes 786440 | tf_op jit(solution)/shard_map/ppermute | solution.py:88
  118.5 12.0 %collective-permute-start.24 = (bf16[64,2048]{1,0:T(8,128)(2,1)S(1)}, bf16[64,2048]{1,0:T(8,128)(2,1)S(1)}, u32[]{:S(2)}, u32[]{:S(2)}) collective-permute-start(bf16[64,2048]{1,0:T(8,128)(2,1)S(1)} %pad_maximum_fusion.1), channel_id=1, source_target_pairs={{0,4},{1,5},{4,8},{5,9},{8,12},{9,13},{12,14},{13,15},{14,10},{15,... | collective-permute-start | bytes 786440 | tf_op jit(solution)/shard_map/ppermute | solution.py:89
  118.9 12.1 %collective-permute-start.23 = (bf16[64,2048]{1,0:T(8,128)(2,1)S(1)}, bf16[64,2048]{1,0:T(8,128)(2,1)S(1)}, u32[]{:S(2)}, u32[]{:S(2)}) collective-permute-start(bf16[64,2048]{1,0:T(8,128)(2,1)S(1)} %pad_maximum_fusion), channel_id=1, source_target_pairs={{0,2},{1,3},{4,0},{5,1},{8,4},{9,5},{12,8},{13,9},{14,12},{15,13},... | collective-permute-start | bytes 786440 | tf_op jit(solution)/shard_map/ppermute | solution.py:88
  126.2 27.5 %copy-start.25 = (bf16[1,64,2048]{2,1,0:T(8,128)(2,1)S(1)}, bf16[1,64,2048]{2,1,0:T(8,128)(2,1)}, u32[]{:S(2)}) copy-start(bf16[1,64,2048]{2,1,0:T(8,128)(2,1)} %param.14) | copy-start | bytes 786436
  126.2 27.5 %copy-start.28 = (f32[1,2048]{1,0:T(1,128)S(1)}, f32[1,2048]{1,0:T(1,128)}, u32[]{:S(2)}) copy-start(f32[1,2048]{1,0:T(1,128)} %param.18) | copy-start | bytes 24580
  131.0 9.1 %collective-permute-start.30 = (bf16[64,2048]{1,0:T(8,128)(2,1)S(1)}, bf16[64,2048]{1,0:T(8,128)(2,1)S(1)}, u32[]{:S(2)}, u32[]{:S(2)}) collective-permute-start(bf16[64,2048]{1,0:T(8,128)(2,1)S(1)} %add_convert_fusion.4), channel_id=1, source_target_pairs={{0,4},{1,5},{4,8},{5,9},{8,12},{9,13},{12,14},{13,15},{14,10},{15,... | collective-permute-start | bytes 786440 | tf_op jit(solution)/shard_map/ppermute | solution.py:89
  131.9 22.0 %copy-start.27 = (bf16[1,64,2048]{2,1,0:T(8,128)(2,1)S(1)}, bf16[1,64,2048]{2,1,0:T(8,128)(2,1)}, u32[]{:S(2)}) copy-start(bf16[1,64,2048]{2,1,0:T(8,128)(2,1)} %param.15) | copy-start | bytes 786436
  132.0 9.5 %collective-permute-start.29 = (bf16[64,2048]{1,0:T(8,128)(2,1)S(1)}, bf16[64,2048]{1,0:T(8,128)(2,1)S(1)}, u32[]{:S(2)}, u32[]{:S(2)}) collective-permute-start(bf16[64,2048]{1,0:T(8,128)(2,1)S(1)} %add_convert_fusion.5), channel_id=1, source_target_pairs={{0,2},{1,3},{4,0},{5,1},{8,4},{9,5},{12,8},{13,9},{14,12},{15,13},... | collective-permute-start | bytes 786440 | tf_op jit(solution)/shard_map/ppermute | solution.py:88
  133.3 23.2 %copy-start.26 = (bf16[1,64,2048]{2,1,0:T(8,128)(2,1)S(1)}, bf16[1,64,2048]{2,1,0:T(8,128)(2,1)}, u32[]{:S(2)}) copy-start(bf16[1,64,2048]{2,1,0:T(8,128)(2,1)} %param.11) | copy-start | bytes 786436
  133.3 12.2 %collective-permute-start.28 = (bf16[64,2048]{1,0:T(8,128)(2,1)S(1)}, bf16[64,2048]{1,0:T(8,128)(2,1)S(1)}, u32[]{:S(2)}, u32[]{:S(2)}) collective-permute-start(bf16[64,2048]{1,0:T(8,128)(2,1)S(1)} %add_convert_fusion.6), channel_id=1, source_target_pairs={{0,4},{1,5},{4,8},{5,9},{8,12},{9,13},{12,14},{13,15},{14,10},{15,... | collective-permute-start | bytes 786440 | tf_op jit(solution)/shard_map/ppermute | solution.py:89
  134.5 11.0 %collective-permute-start.27 = (bf16[64,2048]{1,0:T(8,128)(2,1)S(1)}, bf16[64,2048]{1,0:T(8,128)(2,1)S(1)}, u32[]{:S(2)}, u32[]{:S(2)}) collective-permute-start(bf16[64,2048]{1,0:T(8,128)(2,1)S(1)} %add_convert_fusion.7), channel_id=1, source_target_pairs={{0,2},{1,3},{4,0},{5,1},{8,4},{9,5},{12,8},{13,9},{14,12},{15,13},... | collective-permute-start | bytes 786440 | tf_op jit(solution)/shard_map/ppermute | solution.py:88
  145.6 6.4 %collective-permute-start.34 = (bf16[64,2048]{1,0:T(8,128)(2,1)S(1)}, bf16[64,2048]{1,0:T(8,128)(2,1)S(1)}, u32[]{:S(2)}, u32[]{:S(2)}) collective-permute-start(bf16[64,2048]{1,0:T(8,128)(2,1)S(1)} %get-tuple-element.70), channel_id=1, source_target_pairs={{0,2},{1,3},{4,0},{5,1},{8,4},{9,5},{12,8},{13,9},{14,12},{15,13},... | collective-permute-start | bytes 786440 | tf_op jit(solution)/shard_map/ppermute | solution.py:88
  147.3 6.4 %collective-permute-start.35 = (bf16[64,2048]{1,0:T(8,128)(2,1)S(1)}, bf16[64,2048]{1,0:T(8,128)(2,1)S(1)}, u32[]{:S(2)}, u32[]{:S(2)}) collective-permute-start(bf16[64,2048]{1,0:T(8,128)(2,1)S(1)} %get-tuple-element.71), channel_id=1, source_target_pairs={{0,4},{1,5},{4,8},{5,9},{8,12},{9,13},{12,14},{13,15},{14,10},{15,... | collective-permute-start | bytes 786440 | tf_op jit(solution)/shard_map/ppermute | solution.py:89
  147.9 8.0 %collective-permute-start.31 = (bf16[64,2048]{1,0:T(8,128)(2,1)S(1)}, bf16[64,2048]{1,0:T(8,128)(2,1)S(1)}, u32[]{:S(2)}, u32[]{:S(2)}) collective-permute-start(bf16[64,2048]{1,0:T(8,128)(2,1)S(1)} %get-tuple-element.72), channel_id=1, source_target_pairs={{0,2},{1,3},{4,0},{5,1},{8,4},{9,5},{12,8},{13,9},{14,12},{15,13},... | collective-permute-start | bytes 786440 | tf_op jit(solution)/shard_map/ppermute | solution.py:88
  149.5 6.9 %collective-permute-start.32 = (bf16[64,2048]{1,0:T(8,128)(2,1)S(1)}, bf16[64,2048]{1,0:T(8,128)(2,1)S(1)}, u32[]{:S(2)}, u32[]{:S(2)}) collective-permute-start(bf16[64,2048]{1,0:T(8,128)(2,1)S(1)} %get-tuple-element.73), channel_id=1, source_target_pairs={{0,4},{1,5},{4,8},{5,9},{8,12},{9,13},{12,14},{13,15},{14,10},{15,... | collective-permute-start | bytes 786440 | tf_op jit(solution)/shard_map/ppermute | solution.py:89
  154.3 6.4 %collective-permute-start.36 = (bf16[1,64,2048]{2,1,0:T(8,128)(2,1)S(1)}, bf16[1,64,2048]{2,1,0:T(8,128)(2,1)S(1)}, u32[]{:S(2)}, u32[]{:S(2)}) collective-permute-start(bf16[1,64,2048]{2,1,0:T(8,128)(2,1)S(1)} %fusion.14), channel_id=1, source_target_pairs={{0,16},{16,0},{1,17},{17,1},{2,18},{18,2},{3,19},{19,3},{4,20},{20... | collective-permute-start | bytes 786440 | tf_op jit(solution)/shard_map/ppermute | solution.py:41
  156.6 6.9 %collective-permute-start.33 = (bf16[1,64,2048]{2,1,0:T(8,128)(2,1)S(1)}, bf16[1,64,2048]{2,1,0:T(8,128)(2,1)S(1)}, u32[]{:S(2)}, u32[]{:S(2)}) collective-permute-start(bf16[1,64,2048]{2,1,0:T(8,128)(2,1)S(1)} %fusion.13), channel_id=1, source_target_pairs={{0,16},{16,0},{1,17},{17,1},{2,18},{18,2},{3,19},{19,3},{4,20},{20... | collective-permute-start | bytes 786440 | tf_op jit(solution)/shard_map/ppermute | solution.py:41
  (18 other events, 69.3 us)

commit v3 on v2

--- a/solution.py
+++ b/solution.py
@@ -107,11 +107,48 @@
     return (tokens_f32 * inverse_norm(tokens_f32) * gain_row).astype(jnp.bfloat16)
 
 
-def gate_table(choice, gates, experts):
-    named = choice[:, :, None] == jnp.arange(experts)
-    table = jnp.sum(jnp.where(named, gates[:, :, None], 0.0), axis=1)
-    high = table.astype(jnp.bfloat16)
-    return [high, (table - high.astype(jnp.float32)).astype(jnp.bfloat16)]
+def payload_body(devices, *refs):
+    sources, out, held, arrived = refs[:8], refs[8], refs[9:16], refs[16]
+    width = sources[0].shape[1]
+    places = [*held, out.at[:, pl.ds(2 * width, width)]]
+    copies = [
+        pltpu.make_async_copy(source, place, arrived.at[i])
+        for i, (source, place) in enumerate(zip(sources, places))
+    ]
+    for copy in copies:
+        copy.start()
+    for copy in copies:
+        copy.wait()
+    rows, gain, routing = held[:2], held[2], (held[3:5], held[5:7])
+    for i, tokens in enumerate(rows):
+        out[:, i * width : (i + 1) * width] = normalize(tokens[...], gain[...])
+    shape = (out.shape[1] - 3 * width, out.shape[0])
+    row = lax.broadcasted_iota(jnp.int32, shape, 0)
+    part, expert = lax.div(row, devices), lax.rem(row, devices)
+    table = jnp.zeros(shape, jnp.float32)
+    for batch, (choices, gates) in enumerate(routing):
+        for i in range(choices.shape[0]):
+            named = (expert == choices[i : i + 1, :]) & (lax.div(part, 2) == batch)
+            table += jnp.where(named, gates[i : i + 1, :], 0.0)
+    high = table.astype(jnp.bfloat16).astype(jnp.float32)
+    table = jnp.where(lax.rem(part, 2) == 0, high, table - high)
+    out[:, 3 * width :] = table.T.astype(jnp.bfloat16)
+
+
+def payload(forward, backward, cotangent, gain, forward_routing, backward_routing, devices):
+    rows, width = forward.shape
+    table = -(-4 * devices // LANES) * LANES
+    sources = (forward, backward, gain, *forward_routing, *backward_routing, cotangent)
+    return pl.pallas_call(
+        functools.partial(payload_body, devices),
+        in_specs=[IN_HBM] * 8,
+        out_specs=IN_VMEM,
+        out_shape=jax.ShapeDtypeStruct((rows, 3 * width + table), jnp.bfloat16),
+        scratch_shapes=[pltpu.VMEM(source.shape, source.dtype) for source in sources[:7]]
+        + [pltpu.SemaphoreType.DMA((8,))],
+        compiler_params=pltpu.CompilerParams(vmem_limit_bytes=60 * MIB),
+        cost_estimate=pl.CostEstimate(flops=1, bytes_accessed=1, transcendentals=0),
+    )(*sources)
 
 
 def dot_plain(left, right):
@@ -151,15 +188,16 @@
             pltpu.VMEM((CORES * hidden, width), jnp.bfloat16),
         ),
         scratch_shapes=[pltpu.SemaphoreType.DMA((6,))],
-        compiler_params=pltpu.CompilerParams(vmem_limit_bytes=24 * MIB),
+        compiler_params=pltpu.CompilerParams(vmem_limit_bytes=38 * MIB),
     )(*mine, *theirs)
 
 
-def collect(blocks, rows, arrived):
+def collect(blocks, column, rows, arrived):
     copies, first = [], 0
     for i, block in enumerate(blocks):
         to = rows.at[pl.ds(first, block.shape[0])]
-        copies.append(pltpu.make_async_copy(block, to, arrived.at[i]))
+        part = block.at[:, pl.ds(column, rows.shape[1])]
+        copies.append(pltpu.make_async_copy(part, to, arrived.at[i]))
         first += block.shape[0]
     for copy in copies:
         copy.start()
@@ -171,7 +209,7 @@
     blocks = refs[:count]
     experts, gate_up, down, out, forward_gates, rows, grads, arrived = refs[count:]
     width, hidden = gate_up.shape[0], down.shape[0] // CORES
-    collect(blocks, rows, arrived)
+    collect(blocks, width, rows, arrived)
     table = rows[:, 2 * width :].astype(jnp.float32)
     lane = lax.broadcasted_iota(jnp.int32, table.shape, 1)
 
@@ -201,8 +239,8 @@
 
 
 def experts_backward(blocks, experts, gate_up, down, devices):
-    count, rows = sum(b.shape[0] for b in blocks), blocks[0].shape[1]
     width = gate_up.shape[0]
+    count, rows = sum(b.shape[0] for b in blocks), blocks[0].shape[1] - width
     return pl.pallas_call(
         functools.partial(backward_body, len(blocks), devices),
         in_specs=[IN_HBM] * len(blocks) + [IN_SMEM, IN_VMEM, IN_VMEM],
@@ -216,10 +254,10 @@
             pltpu.VMEM((count, gate_up.shape[1]), jnp.bfloat16),
             pltpu.SemaphoreType.DMA((len(blocks),)),
         ],
-        compiler_params=pltpu.CompilerParams(vmem_limit_bytes=20 * MIB),
+        compiler_params=pltpu.CompilerParams(vmem_limit_bytes=14 * MIB),
         cost_estimate=pl.CostEstimate(
-            flops=2 * count * width * down.shape[0] * 5,
-            bytes_accessed=count * (rows + width) * 2,
+            flops=1,
+            bytes_accessed=1,
             transcendentals=0,
         ),
     )(*blocks, experts, gate_up, down)
@@ -229,7 +267,7 @@
     blocks = refs[:count]
     gates, gate_up, down, out, rows, acts, arrived = refs[count:]
     width, hidden = gate_up.shape[0], down.shape[0] // CORES
-    collect(blocks, rows, arrived)
+    collect(blocks, 0, rows, arrived)
     for core in range(CORES):
         scale = gates[:, core : core + 1]
         for tile in range(0, hidden, TILE):
@@ -256,10 +294,10 @@
             pltpu.VMEM((count, down.shape[0]), jnp.bfloat16),
             pltpu.SemaphoreType.DMA((len(blocks),)),
         ],
-        compiler_params=pltpu.CompilerParams(vmem_limit_bytes=20 * MIB),
+        compiler_params=pltpu.CompilerParams(vmem_limit_bytes=14 * MIB),
         cost_estimate=pl.CostEstimate(
-            flops=2 * count * width * down.shape[0] * 3,
-            bytes_accessed=count * 2 * width * 2,
+            flops=1,
+            bytes_accessed=1,
             transcendentals=0,
         ),
     )(*blocks, gates, gate_up, down)
@@ -302,40 +340,53 @@
     devices = lax.axis_size("expert")
     gain_row = norm_gain[0]
     cotangent = backward_cotangent[0]
-    tables = gate_table(forward_choice[0], forward_gates[0], devices) + gate_table(
-        backward_choice[0], backward_gates[0], devices
+    tokens = RingGather(
+        payload(
+            forward_tokens[0],
+            backward_tokens[0],
+            cotangent,
+            norm_gain,
+            (forward_choice[0].T, forward_gates[0].T),
+            (backward_choice[0].T, backward_gates[0].T),
+            devices,
+        )
     )
-    pad = jnp.zeros((cotangent.shape[0], -4 * devices % LANES), jnp.bfloat16)
-    back = RingGather(
-        jnp.concatenate([normalize(backward_tokens[0], gain_row), cotangent, *tables, pad], axis=1)
-    )
-    fwd = RingGather(normalize(forward_tokens[0], gain_row))
-    back.step()
-    fwd.step()
-    while back.left:
-        arrived = back.newest
-        back.step(fwd.newest)
-        fwd.step(arrived)
-
     mine = (gate_weight[0, 0], up_weight[0, 0], down_weight[0, 0])
-    theirs = tuple(lax.ppermute(w, "expert", core_route(devices)) for w in mine)
-    gate_up, down = weights_in_vmem(mine, theirs)
     me = lax.axis_index("expert").astype(jnp.int32)
     experts = jnp.stack([me, me + 1 - 2 * lax.rem(me, 2)])
 
-    back_groups, fwd_groups = grouped(back.blocks), grouped(fwd.blocks)
-    back_outs = [experts_backward(g, experts, gate_up, down, devices) for g in back_groups]
-    back_sum = RingScatter(ungrouped([out for out, _ in back_outs], back_groups))
-    fwd_outs = [
-        experts_forward(g, gates, gate_up, down) for g, (_, gates) in zip(fwd_groups, back_outs)
-    ]
-    fwd_sum = RingScatter(ungrouped(fwd_outs, fwd_groups))
+    tokens.step()
+    theirs = after(mine, tokens.newest)
+    theirs = tuple(lax.ppermute(w, "expert", core_route(devices)) for w in theirs)
+    while tokens.left > 1:
+        tokens.step()
+    early = grouped(tokens.blocks)[:-1]
+    theirs = after(theirs, early[-1][-1:])
+    gate_up, down = weights_in_vmem(mine, theirs)
+
+    def run_back(blocks):
+        return experts_backward(blocks, experts, gate_up, down, devices)
+
+    def run_fwd(blocks, gates):
+        return experts_forward(blocks, gates, gate_up, down)
+
+    back_outs = [run_back(group) for group in early]
+    tokens.step([out for out, _ in back_outs])
+    fwd_outs = [run_fwd(group, gates) for group, (_, gates) in zip(early, back_outs)]
+    groups = grouped(tokens.blocks)
+    back_outs.append(run_back(after(groups[-1], fwd_outs)))
+    back_sum = RingScatter(ungrouped([out for out, _ in back_outs], groups))
+    back_sum.step()
+    fwd_outs.append(run_fwd(groups[-1], back_outs[-1][1]))
+    fwd_sum = RingScatter(ungrouped(fwd_outs, groups))
     back_sum.step()
     fwd_sum.step()
     while back_sum.left:
         arrived = back_sum.newest
         back_sum.step(fwd_sum.newest)
         fwd_sum.step(arrived)
+    while fwd_sum.left:
+        fwd_sum.step()
 
     back_f32 = backward_tokens[0].astype(jnp.float32)
     back_inverse = inverse_norm(back_f32)

time: 167 us -> 142 us (0.85)
  local copies, waits for them, and re-layouts: 15 us -> 2.62 us
  starting transfers between devices: 37.2 us -> 28.9 us
  other arithmetic: 6.45 us -> 1.54 us
  Pallas kernels: 35.4 us -> 39.7 us
  waiting for transfers between devices: 69.7 us -> 65.9 us
    unnamed x60 -> x16, local copies, waits for them, and re-layouts: 12 us -> 2.49 us
    ppermute x8 -> x4, starting transfers between devices: 13.5 us -> 4.31 us  [step(): ahead = lax.ppermute(ahead, 'expert', ring_route(devices, -1))]
    ppermute x8 -> x4, waiting for transfers between devices: 9 us -> 2.07 us  [step(): ahead = lax.ppermute(ahead, 'expert', ring_route(devices, -1))]
    ppermute x8, waiting for transfers between devices: 3.94 us -> 7.43 us  [step(): behind = lax.ppermute(behind, 'expert', ring_route(devices, -1))]
    pallas_call x0 -> x1, Pallas kernels: none -> 2.42 us  [payload(): pl.pallas_call(functools.partial(payload_body, devices), in_specs=[IN_HBM...]
    reduce_sum x2 -> x1, other arithmetic: 2.21 us -> 0.29 us  [inverse_norm(): jnp.mean(rows * rows, axis=-1, keepdims=True) + norm_epsilon]
    reduce_sum x3 -> x0, other arithmetic: 1.7 us -> none  [the longest x2 1.44 us: gate_table(): table = jnp.sum(jnp.where(named, gates[:, :, None], 0.0), axis=1)]
    pallas_call x1, Pallas kernels: 4.91 us -> 6.6 us  [weights_in_vmem(): pl.pallas_call(weights_body, in_specs=[IN_HBM] * 6, out_specs=(IN_VMEM, I...]
  transfers between devices with their start and end apart: 37 -> 29, of which waited for: 19 -> 20; matrix products, arithmetic and copies ran while one was open for 6% -> 1% of each run, Pallas kernels for 18% -> 20%
where the time goes in v3:
time: 142 us; the launch traced here: 140 us
  waiting for transfers between devices  65.9 us (46%)
  Pallas kernels  39.7 us (28%)
  starting transfers between devices  28.9 us (20%)
  local copies, waits for them, and re-layouts  2.62 us (2%)
  other arithmetic  1.54 us (1%)
    ppermute x4, waiting for transfers between devices, step(): behind = lax.ppermute(behind, 'expert', ring_route(devices, 1))  37.2 us
    pallas_call x2, Pallas kernels, experts_backward(): pl.pallas_call(functools.partial(backward_body, len(blocks), devices), in...  19.4 us
    ppermute x8, waiting for transfers between devices, step(): ahead = lax.ppermute(ahead, 'expert', ring_route(devices, 1))  14.3 us
    ppermute x8, starting transfers between devices, step(): behind = lax.ppermute(behind, 'expert', ring_route(devices, -1))  12.3 us
    pallas_call x2, Pallas kernels, experts_forward(): pl.pallas_call(functools.partial(forward_body, len(blocks)), in_specs=[IN...  11.3 us
    ppermute x8, waiting for transfers between devices, step(): behind = lax.ppermute(behind, 'expert', ring_route(devices, -1))  7.43 us
    pallas_call x1, Pallas kernels, weights_in_vmem(): pl.pallas_call(weights_body, in_specs=[IN_HBM] * 6, out_specs=(IN_VMEM, I...  6.6 us
    ppermute x2, waiting for transfers between devices, passed_along(): lax.ppermute(block, axis, [(i, (i + distance) % size) for i in range(size)])  4.88 us
  transfers between devices with their start and end apart: 29, of which 20 were waited for; matrix products, arithmetic and copies ran while one was open for 1% of the time, Pallas kernels for 20%

profile of v3, /device:TPU:12, one launch (start us, length us, event | category | flops | bytes accessed | tf_op | source)
XLA Modules:
  0.0 139.6 jit_solution(7557222995441602888)
XLA Ops:
  0.6 2.4 %shard_map.122.refs_0_ = bf16[64,6272]{1,0:T(8,128)(2,1)} custom-call(bf16[64,2048]{1,0:T(8,128)(2,1)} %bitcast.37, bf16[64,2048]{1,0:T(8,128)(2,1)} %bitcast.36, f32[1,2048]{1,0:T(1,128)} %refs_2_.1, s32[8,64]{1,0:T(8,128)} %bitcast.41, f32[8,64]{1,0:T(8,128)} %bitcast.42, s32[8,64]{1,0:T(8,128)} %bitcast.43, f32[8,64]{1,0:T(8,128)} %bitcast.44, ...), custom_call_target="tpu_custom_call" | custom-call | flops 1 | bytes 1 | tf_op jit(solution)/shard_map/pallas_call | solution.py:142
  3.1 0.5 collective-permute-start
  3.6 1.6 %collective-permute-start.1 = (bf16[64,6272]{1,0:T(8,128)(2,1)}, bf16[64,6272]{1,0:T(8,128)(2,1)S(1)}, u32[]{:S(2)}, u32[]{:S(2)}) collective-permute-start(bf16[64,6272]{1,0:T(8,128)(2,1)} %shard_map.122.refs_0_), channel_id=1, source_target_pairs={{0,2},{1,3},{4,0},{5,1},{8,4},{9,5},{12,8},{13,9},{14,12},{15,13},... | collective-permute-start | bytes 2408456 | tf_op jit(solution)/shard_map/ppermute | solution.py:63
  5.1 17.8 %collective-permute-done.refs_1_ = bf16[64,6272]{1,0:T(8,128)(2,1)S(1)} collective-permute-done((bf16[64,6272]{1,0:T(8,128)(2,1)}, bf16[64,6272]{1,0:T(8,128)(2,1)S(1)}, u32[]{:S(2)}, u32[]{:S(2)}) %collective-permute-start) | collective-permute-done | bytes 802848 | tf_op jit(solution)/shard_map/ppermute | solution.py:62
  23.1 0.5 collective-permute-start.4
  24.0 1.7 %collective-permute-start.6 = (bf16[64,6272]{1,0:T(8,128)(2,1)S(1)}, bf16[64,6272]{1,0:T(8,128)(2,1)S(1)}, u32[]{:S(2)}, u32[]{:S(2)}) collective-permute-start(bf16[64,6272]{1,0:T(8,128)(2,1)S(1)} %collective-permute-done.1.refs_2_), channel_id=1, source_target_pairs={{0,2},{1,3},{4,0},{5,1},{8,4},{9,5},{12,8},{13,9},{14,12},{15,13},... | collective-permute-start | bytes 2408456 | tf_op jit(solution)/shard_map/ppermute | solution.py:63
  25.7 0.9 copy-done.1
  26.6 17.5 %collective-permute-done.2.refs_3_ = bf16[64,6272]{1,0:T(8,128)(2,1)} collective-permute-done((bf16[64,6272]{1,0:T(8,128)(2,1)S(1)}, bf16[64,6272]{1,0:T(8,128)(2,1)}, u32[]{:S(2)}, u32[]{:S(2)}) %collective-permute-start.2) | collective-permute-done | bytes 802848 | tf_op jit(solution)/shard_map/ppermute | solution.py:62
  44.1 1.7 %collective-permute-start.7 = (bf16[64,6272]{1,0:T(8,128)(2,1)}, bf16[64,6272]{1,0:T(8,128)(2,1)S(1)}, u32[]{:S(2)}, u32[]{:S(2)}) collective-permute-start(bf16[64,6272]{1,0:T(8,128)(2,1)} %collective-permute-done.2.refs_3_), channel_id=1, source_target_pairs={{0,4},{1,5},{4,8},{5,9},{8,12},{9,13},{12,14},{13,15},{14,10},{15,... | collective-permute-start | bytes 2408456 | tf_op jit(solution)/shard_map/ppermute | solution.py:62
  46.2 6.6 %shard_map.123 = (bf16[2048,3072]{1,0:T(8,128)(2,1)S(1)}, bf16[1536,2048]{1,0:T(8,128)(2,1)S(1)}) custom-call(bf16[2048,768]{1,0:T(8,128)(2,1)} %bitcast.31, bf16[2048,768]{1,0:T(8,128)(2,1)} %bitcast.33, bf16[768,2048]{1,0:T(8,128)(2,1)} %bitcast.35, bf16[2048,768]{1,0:T(8,128)(2,1)} %collective-permute-done.3.refs_3_, ...), custom_call_target="tpu_custom_call" | custom-call | tf_op jit(solution)/shard_map/pallas_call | solution.py:182
  53.0 10.2 %shard_map.124 = (bf16[256,2048]{1,0:T(8,128)(2,1)S(1)}, f32[256,128]{1,0:T(8,128)S(1)}) custom-call(bf16[64,6272]{1,0:T(8,128)(2,1)S(1)} %copy-done, bf16[64,6272]{1,0:T(8,128)(2,1)S(1)} %collective-permute-done.refs_1_, bf16[64,6272]{1,0:T(8,128)(2,1)S(1)} %copy-done.2, bf16[64,6272]{1,0:T(8,128)(2,1)} %collective-permute-done.2.refs_3_, ...), custom_call_target="tpu_custom_call" | custom-call | flops 1 | bytes 1 | tf_op jit(solution)/shard_map/pallas_call | solution.py:244
  63.2 0.6 collective-permute-done.7.refs_1_
  63.8 0.9 collective-permute-done.8.refs_2_
  64.7 0.7 collective-permute-start.10
  65.5 1.6 %collective-permute-start.9 = (bf16[32,6272]{1,0:T(8,128)(2,1)S(1)}, bf16[32,6272]{1,0:T(8,128)(2,1)S(1)}, u32[]{:S(2)}, u32[]{:S(2)}) collective-permute-start(bf16[32,6272]{1,0:T(8,128)(2,1)S(1)} %slice.87), channel_id=1, source_target_pairs={{0,4},{1,5},{4,8},{5,9},{8,12},{9,13},{12,14},{13,15},{14,10},{15,... | collective-permute-start | bytes 1204232 | tf_op jit(solution)/shard_map/ppermute | solution.py:62
  67.0 6.1 %shard_map.125 = bf16[256,2048]{1,0:T(8,128)(2,1)S(1)} custom-call(bf16[64,6272]{1,0:T(8,128)(2,1)S(1)} %copy-done, bf16[64,6272]{1,0:T(8,128)(2,1)S(1)} %collective-permute-done.refs_1_, bf16[64,6272]{1,0:T(8,128)(2,1)S(1)} %copy-done.2, bf16[64,6272]{1,0:T(8,128)(2,1)} %collective-permute-done.2.refs_3_, f32[256,128]{1,0:T(8,128)S(1)} %get-tuple-element.50.refs_4_, ...), custom_call_target="tpu_custom_call" | custom-call | flops 1 | bytes 1 | tf_op jit(solution)/shard_map/pallas_call | solution.py:287
  73.1 1.0 collective-permute-done.10.refs_4_
  74.2 1.2 collective-permute-done.9.refs_3_
  75.4 9.2 %shard_map.126 = (bf16[256,2048]{1,0:T(8,128)(2,1)S(1)}, f32[256,128]{1,0:T(8,128)S(1)}) custom-call(bf16[64,6272]{1,0:T(8,128)(2,1)S(1)} %collective-permute-done.6.refs_0_, bf16[64,6272]{1,0:T(8,128)(2,1)S(1)} %collective-permute-done.7.refs_1_, bf16[64,6272]{1,0:T(8,128)(2,1)S(1)} %collective-permute-done.8.refs_2_, ...), custom_call_target="tpu_custom_call" | custom-call | flops 1 | bytes 1 | tf_op jit(solution)/shard_map/pallas_call | solution.py:244
  84.7 1.6 %collective-permute-start.13 = (bf16[32,2048]{1,0:T(8,128)(2,1)S(1)}, bf16[32,2048]{1,0:T(8,128)(2,1)S(1)}, u32[]{:S(2)}, u32[]{:S(2)}) collective-permute-start(bf16[32,2048]{1,0:T(8,128)(2,1)S(1)} %get-tuple-element.91), channel_id=1, source_target_pairs={{0,2},{1,3},{4,0},{5,1},{8,4},{9,5},{12,8},{13,9},{14,12},{15,13},... | collective-permute-start | bytes 393224 | tf_op jit(solution)/shard_map/ppermute | solution.py:88
  86.3 0.4 collective-permute-start.14
  86.7 5.2 %shard_map.127 = bf16[256,2048]{1,0:T(8,128)(2,1)S(1)} custom-call(bf16[64,6272]{1,0:T(8,128)(2,1)S(1)} %collective-permute-done.6.refs_0_, bf16[64,6272]{1,0:T(8,128)(2,1)S(1)} %collective-permute-done.7.refs_1_, bf16[64,6272]{1,0:T(8,128)(2,1)S(1)} %collective-permute-done.8.refs_2_, bf16[32,6272]{1,0:T(8,128)(2,1)S(1)} %collective-permute-done.9.refs_3_, ...), custom_call_target="tpu_custom_call" | custom-call | flops 1 | bytes 1 | tf_op jit(solution)/shard_map/pallas_call | solution.py:287
  92.1 0.8 collective-permute-start.16
  92.9 1.3 collective-permute-start.15
  94.3 1.6 %collective-permute-start.11 = (bf16[32,2048]{1,0:T(8,128)(2,1)S(1)}, bf16[32,2048]{1,0:T(8,128)(2,1)S(1)}, u32[]{:S(2)}, u32[]{:S(2)}) collective-permute-start(bf16[32,2048]{1,0:T(8,128)(2,1)S(1)} %get-tuple-element.85), channel_id=1, source_target_pairs={{0,2},{1,3},{4,0},{5,1},{8,4},{9,5},{12,8},{13,9},{14,12},{15,13},... | collective-permute-start | bytes 393224 | tf_op jit(solution)/shard_map/ppermute | solution.py:88
  95.9 0.4 collective-permute-start.12
  96.4 4.7 %collective-permute-done.11 = bf16[32,2048]{1,0:T(8,128)(2,1)S(1)} collective-permute-done((bf16[32,2048]{1,0:T(8,128)(2,1)S(1)}, bf16[32,2048]{1,0:T(8,128)(2,1)S(1)}, u32[]{:S(2)}, u32[]{:S(2)}) %collective-permute-start.11) | collective-permute-done | bytes 131104 | tf_op jit(solution)/shard_map/ppermute | solution.py:88
  101.1 1.2 collective-permute-done.12
  102.4 0.5 collective-permute-start.20
  103.0 1.6 %collective-permute-start.19 = (bf16[64,2048]{1,0:T(8,128)(2,1)S(1)}, bf16[64,2048]{1,0:T(8,128)(2,1)S(1)}, u32[]{:S(2)}, u32[]{:S(2)}) collective-permute-start(bf16[64,2048]{1,0:T(8,128)(2,1)S(1)} %add_convert_fusion.8), channel_id=1, source_target_pairs={{0,2},{1,3},{4,0},{5,1},{8,4},{9,5},{12,8},{13,9},{14,12},{15,13},... | collective-permute-start | bytes 786440 | tf_op jit(solution)/shard_map/ppermute | solution.py:88
  104.7 0.5 collective-permute-start.18
  105.2 1.6 %collective-permute-start.17 = (bf16[64,2048]{1,0:T(8,128)(2,1)S(1)}, bf16[64,2048]{1,0:T(8,128)(2,1)S(1)}, u32[]{:S(2)}, u32[]{:S(2)}) collective-permute-start(bf16[64,2048]{1,0:T(8,128)(2,1)S(1)} %pad_maximum_fusion.2), channel_id=1, source_target_pairs={{0,2},{1,3},{4,0},{5,1},{8,4},{9,5},{12,8},{13,9},{14,12},{15,13},... | collective-permute-start | bytes 786440 | tf_op jit(solution)/shard_map/ppermute | solution.py:88
  106.9 2.3 %collective-permute-done.20 = bf16[64,2048]{1,0:T(8,128)(2,1)S(1)} collective-permute-done((bf16[64,2048]{1,0:T(8,128)(2,1)S(1)}, bf16[64,2048]{1,0:T(8,128)(2,1)S(1)}, u32[]{:S(2)}, u32[]{:S(2)}) %collective-permute-start.20) | collective-permute-done | bytes 262176 | tf_op jit(solution)/shard_map/ppermute | solution.py:89
  109.4 5.0 %collective-permute-done.18 = bf16[64,2048]{1,0:T(8,128)(2,1)S(1)} collective-permute-done((bf16[64,2048]{1,0:T(8,128)(2,1)S(1)}, bf16[64,2048]{1,0:T(8,128)(2,1)S(1)}, u32[]{:S(2)}, u32[]{:S(2)}) %collective-permute-start.18) | collective-permute-done | bytes 262176 | tf_op jit(solution)/shard_map/ppermute | solution.py:89
  114.5 1.1 collective-permute-start.22
  115.7 1.0 collective-permute-start.21
  116.8 1.8 %collective-permute-start.26 = (bf16[64,2048]{1,0:T(8,128)(2,1)S(1)}, bf16[64,2048]{1,0:T(8,128)(2,1)S(1)}, u32[]{:S(2)}, u32[]{:S(2)}) collective-permute-start(bf16[64,2048]{1,0:T(8,128)(2,1)S(1)} %get-tuple-element.78), channel_id=1, source_target_pairs={{0,2},{1,3},{4,0},{5,1},{8,4},{9,5},{12,8},{13,9},{14,12},{15,13},... | collective-permute-start | bytes 786440 | tf_op jit(solution)/shard_map/ppermute | solution.py:88
  118.9 4.0 %collective-permute-done.22 = bf16[64,2048]{1,0:T(8,128)(2,1)S(1)} collective-permute-done((bf16[64,2048]{1,0:T(8,128)(2,1)S(1)}, bf16[64,2048]{1,0:T(8,128)(2,1)S(1)}, u32[]{:S(2)}, u32[]{:S(2)}) %collective-permute-start.22) | collective-permute-done | bytes 262176 | tf_op jit(solution)/shard_map/ppermute | solution.py:89
  122.9 0.5 collective-permute-done.21
  123.6 1.6 %collective-permute-start.23 = (bf16[64,2048]{1,0:T(8,128)(2,1)S(1)}, bf16[64,2048]{1,0:T(8,128)(2,1)S(1)}, u32[]{:S(2)}, u32[]{:S(2)}) collective-permute-start(bf16[64,2048]{1,0:T(8,128)(2,1)S(1)} %get-tuple-element.80), channel_id=1, source_target_pairs={{0,2},{1,3},{4,0},{5,1},{8,4},{9,5},{12,8},{13,9},{14,12},{15,13},... | collective-permute-start | bytes 786440 | tf_op jit(solution)/shard_map/ppermute | solution.py:88
  125.6 0.6 collective-permute-done.26
  127.1 1.6 %collective-permute-start.28 = (bf16[1,64,2048]{2,1,0:T(8,128)(2,1)S(1)}, bf16[1,64,2048]{2,1,0:T(8,128)(2,1)S(1)}, u32[]{:S(2)}, u32[]{:S(2)}) collective-permute-start(bf16[1,64,2048]{2,1,0:T(8,128)(2,1)S(1)} %fusion.8), channel_id=1, source_target_pairs={{0,16},{16,0},{1,17},{17,1},{2,18},{18,2},{3,19},{19,3},{4,20},{20... | collective-permute-start | bytes 786440 | tf_op jit(solution)/shard_map/ppermute | solution.py:41
  128.7 1.3 collective-permute-done.23
  130.0 1.6 %collective-permute-done.24 = bf16[64,2048]{1,0:T(8,128)(2,1)S(1)} collective-permute-done((bf16[64,2048]{1,0:T(8,128)(2,1)S(1)}, bf16[64,2048]{1,0:T(8,128)(2,1)S(1)}, u32[]{:S(2)}, u32[]{:S(2)}) %collective-permute-start.24) | collective-permute-done | bytes 262176 | tf_op jit(solution)/shard_map/ppermute | solution.py:89
  131.7 1.6 %collective-permute-start.25 = (bf16[1,64,2048]{2,1,0:T(8,128)(2,1)S(1)}, bf16[1,64,2048]{2,1,0:T(8,128)(2,1)S(1)}, u32[]{:S(2)}, u32[]{:S(2)}) collective-permute-start(bf16[1,64,2048]{2,1,0:T(8,128)(2,1)S(1)} %fusion.7), channel_id=1, source_target_pairs={{0,16},{16,0},{1,17},{17,1},{2,18},{18,2},{3,19},{19,3},{4,20},{20... | collective-permute-start | bytes 786440 | tf_op jit(solution)/shard_map/ppermute | solution.py:41
  133.6 4.6 %collective-permute-done.25 = bf16[1,64,2048]{2,1,0:T(8,128)(2,1)S(1)} collective-permute-done((bf16[1,64,2048]{2,1,0:T(8,128)(2,1)S(1)}, bf16[1,64,2048]{2,1,0:T(8,128)(2,1)S(1)}, u32[]{:S(2)}, u32[]{:S(2)}) %collective-permute-start.25) | collective-permute-done | bytes 262176 | tf_op jit(solution)/shard_map/ppermute | solution.py:41
  138.2 0.7 copy.15
  138.9 0.7 copy.16
  (53 shorter events, 4.2 us)
Async XLA Ops:
  3.1 19.9 %collective-permute-start = (bf16[64,6272]{1,0:T(8,128)(2,1)}, bf16[64,6272]{1,0:T(8,128)(2,1)S(1)}, u32[]{:S(2)}, u32[]{:S(2)}) collective-permute-start(bf16[64,6272]{1,0:T(8,128)(2,1)} %shard_map.122.refs_0_), channel_id=1, source_target_pairs={{0,4},{1,5},{4,8},{5,9},{8,12},{9,13},{12,14},{13,15},{14,10},{15,... | collective-permute-start | bytes 2408456 | tf_op jit(solution)/shard_map/ppermute | solution.py:62
  3.6 19.6 %collective-permute-start.1 = (bf16[64,6272]{1,0:T(8,128)(2,1)}, bf16[64,6272]{1,0:T(8,128)(2,1)S(1)}, u32[]{:S(2)}, u32[]{:S(2)}) collective-permute-start(bf16[64,6272]{1,0:T(8,128)(2,1)} %shard_map.122.refs_0_), channel_id=1, source_target_pairs={{0,2},{1,3},{4,0},{5,1},{8,4},{9,5},{12,8},{13,9},{14,12},{15,13},... | collective-permute-start | bytes 2408456 | tf_op jit(solution)/shard_map/ppermute | solution.py:63
  23.1 23.0 %collective-permute-start.3 = (bf16[2048,768]{1,0:T(8,128)(2,1)}, bf16[2048,768]{1,0:T(8,128)(2,1)}, u32[]{:S(2)}, u32[]{:S(2)}) collective-permute-start(bf16[2048,768]{1,0:T(8,128)(2,1)} %bitcast.30), channel_id=1, source_target_pairs={{0,1},{1,0},{2,3},{3,2},{4,5},{5,4},{6,7},{7,6},{8,9},{9,8},{10,11... | collective-permute-start | bytes 9437192 | tf_op jit(solution)/shard_map/ppermute | solution.py:360
  23.1 23.0 %collective-permute-start.4 = (bf16[2048,768]{1,0:T(8,128)(2,1)}, bf16[2048,768]{1,0:T(8,128)(2,1)}, u32[]{:S(2)}, u32[]{:S(2)}) collective-permute-start(bf16[2048,768]{1,0:T(8,128)(2,1)} %bitcast.32), channel_id=1, source_target_pairs={{0,1},{1,0},{2,3},{3,2},{4,5},{5,4},{6,7},{7,6},{8,9},{9,8},{10,11... | collective-permute-start | bytes 9437192 | tf_op jit(solution)/shard_map/ppermute | solution.py:360
  23.6 22.5 %collective-permute-start.5 = (bf16[768,2048]{1,0:T(8,128)(2,1)}, bf16[768,2048]{1,0:T(8,128)(2,1)}, u32[]{:S(2)}, u32[]{:S(2)}) collective-permute-start(bf16[768,2048]{1,0:T(8,128)(2,1)} %bitcast.34), channel_id=1, source_target_pairs={{0,1},{1,0},{2,3},{3,2},{4,5},{5,4},{6,7},{7,6},{8,9},{9,8},{10,11... | collective-permute-start | bytes 9437192 | tf_op jit(solution)/shard_map/ppermute | solution.py:360
  23.6 20.4 %collective-permute-start.2 = (bf16[64,6272]{1,0:T(8,128)(2,1)S(1)}, bf16[64,6272]{1,0:T(8,128)(2,1)}, u32[]{:S(2)}, u32[]{:S(2)}) collective-permute-start(bf16[64,6272]{1,0:T(8,128)(2,1)S(1)} %collective-permute-done.refs_1_), channel_id=1, source_target_pairs={{0,4},{1,5},{4,8},{5,9},{8,12},{9,13},{12,14},{13,15},{14,10},{15,... | collective-permute-start | bytes 2408456 | tf_op jit(solution)/shard_map/ppermute | solution.py:62
  24.0 20.0 %collective-permute-start.6 = (bf16[64,6272]{1,0:T(8,128)(2,1)S(1)}, bf16[64,6272]{1,0:T(8,128)(2,1)S(1)}, u32[]{:S(2)}, u32[]{:S(2)}) collective-permute-start(bf16[64,6272]{1,0:T(8,128)(2,1)S(1)} %collective-permute-done.1.refs_2_), channel_id=1, source_target_pairs={{0,2},{1,3},{4,0},{5,1},{8,4},{9,5},{12,8},{13,9},{14,12},{15,13},... | collective-permute-start | bytes 2408456 | tf_op jit(solution)/shard_map/ppermute | solution.py:63
  25.7 0.9 copy-start.1
  44.1 19.7 %collective-permute-start.7 = (bf16[64,6272]{1,0:T(8,128)(2,1)}, bf16[64,6272]{1,0:T(8,128)(2,1)S(1)}, u32[]{:S(2)}, u32[]{:S(2)}) collective-permute-start(bf16[64,6272]{1,0:T(8,128)(2,1)} %collective-permute-done.2.refs_3_), channel_id=1, source_target_pairs={{0,4},{1,5},{4,8},{5,9},{8,12},{9,13},{12,14},{13,15},{14,10},{15,... | collective-permute-start | bytes 2408456 | tf_op jit(solution)/shard_map/ppermute | solution.py:62
  45.7 18.9 %collective-permute-start.8 = (bf16[64,6272]{1,0:T(8,128)(2,1)S(1)}, bf16[64,6272]{1,0:T(8,128)(2,1)S(1)}, u32[]{:S(2)}, u32[]{:S(2)}) collective-permute-start(bf16[64,6272]{1,0:T(8,128)(2,1)S(1)} %collective-permute-done.6.refs_0_), channel_id=1, source_target_pairs={{0,2},{1,3},{4,0},{5,1},{8,4},{9,5},{12,8},{13,9},{14,12},{15,13},... | collective-permute-start | bytes 2408456 | tf_op jit(solution)/shard_map/ppermute | solution.py:63
  46.2 6.6 %copy-start = (bf16[64,6272]{1,0:T(8,128)(2,1)S(1)}, bf16[64,6272]{1,0:T(8,128)(2,1)}, u32[]{:S(2)}) copy-start(bf16[64,6272]{1,0:T(8,128)(2,1)} %shard_map.122.refs_0_) | copy-start | bytes 2408452
  46.2 6.8 %copy-start.2 = (bf16[64,6272]{1,0:T(8,128)(2,1)S(1)}, bf16[64,6272]{1,0:T(8,128)(2,1)}, u32[]{:S(2)}) copy-start(bf16[64,6272]{1,0:T(8,128)(2,1)} %copy-done.1) | copy-start | bytes 2408452
  64.7 9.5 %collective-permute-start.10 = (bf16[32,6272]{1,0:T(8,128)(2,1)S(1)}, bf16[32,6272]{1,0:T(8,128)(2,1)S(1)}, u32[]{:S(2)}, u32[]{:S(2)}) collective-permute-start(bf16[32,6272]{1,0:T(8,128)(2,1)S(1)} %slice.88), channel_id=1, source_target_pairs={{0,2},{1,3},{4,0},{5,1},{8,4},{9,5},{12,8},{13,9},{14,12},{15,13},... | collective-permute-start | bytes 1204232 | tf_op jit(solution)/shard_map/ppermute | solution.py:63
  65.5 9.9 %collective-permute-start.9 = (bf16[32,6272]{1,0:T(8,128)(2,1)S(1)}, bf16[32,6272]{1,0:T(8,128)(2,1)S(1)}, u32[]{:S(2)}, u32[]{:S(2)}) collective-permute-start(bf16[32,6272]{1,0:T(8,128)(2,1)S(1)} %slice.87), channel_id=1, source_target_pairs={{0,4},{1,5},{4,8},{5,9},{8,12},{9,13},{12,14},{13,15},{14,10},{15,... | collective-permute-start | bytes 1204232 | tf_op jit(solution)/shard_map/ppermute | solution.py:62
  84.7 7.3 %collective-permute-start.13 = (bf16[32,2048]{1,0:T(8,128)(2,1)S(1)}, bf16[32,2048]{1,0:T(8,128)(2,1)S(1)}, u32[]{:S(2)}, u32[]{:S(2)}) collective-permute-start(bf16[32,2048]{1,0:T(8,128)(2,1)S(1)} %get-tuple-element.91), channel_id=1, source_target_pairs={{0,2},{1,3},{4,0},{5,1},{8,4},{9,5},{12,8},{13,9},{14,12},{15,13},... | collective-permute-start | bytes 393224 | tf_op jit(solution)/shard_map/ppermute | solution.py:88
  86.3 5.7 %collective-permute-start.14 = (bf16[32,2048]{1,0:T(8,128)(2,1)S(1)}, bf16[32,2048]{1,0:T(8,128)(2,1)S(1)}, u32[]{:S(2)}, u32[]{:S(2)}) collective-permute-start(bf16[32,2048]{1,0:T(8,128)(2,1)S(1)} %get-tuple-element.90), channel_id=1, source_target_pairs={{0,4},{1,5},{4,8},{5,9},{8,12},{9,13},{12,14},{13,15},{14,10},{15,... | collective-permute-start | bytes 393224 | tf_op jit(solution)/shard_map/ppermute | solution.py:89
  92.1 10.2 %collective-permute-start.16 = (bf16[64,2048]{1,0:T(8,128)(2,1)S(1)}, bf16[64,2048]{1,0:T(8,128)(2,1)S(1)}, u32[]{:S(2)}, u32[]{:S(2)}) collective-permute-start(bf16[64,2048]{1,0:T(8,128)(2,1)S(1)} %pad_maximum_fusion.1), channel_id=1, source_target_pairs={{0,4},{1,5},{4,8},{5,9},{8,12},{9,13},{12,14},{13,15},{14,10},{15,... | collective-permute-start | bytes 786440 | tf_op jit(solution)/shard_map/ppermute | solution.py:89
  92.9 9.4 %collective-permute-start.15 = (bf16[64,2048]{1,0:T(8,128)(2,1)S(1)}, bf16[64,2048]{1,0:T(8,128)(2,1)S(1)}, u32[]{:S(2)}, u32[]{:S(2)}) collective-permute-start(bf16[64,2048]{1,0:T(8,128)(2,1)S(1)} %pad_maximum_fusion), channel_id=1, source_target_pairs={{0,2},{1,3},{4,0},{5,1},{8,4},{9,5},{12,8},{13,9},{14,12},{15,13},... | collective-permute-start | bytes 786440 | tf_op jit(solution)/shard_map/ppermute | solution.py:88
  94.3 6.8 %collective-permute-start.11 = (bf16[32,2048]{1,0:T(8,128)(2,1)S(1)}, bf16[32,2048]{1,0:T(8,128)(2,1)S(1)}, u32[]{:S(2)}, u32[]{:S(2)}) collective-permute-start(bf16[32,2048]{1,0:T(8,128)(2,1)S(1)} %get-tuple-element.85), channel_id=1, source_target_pairs={{0,2},{1,3},{4,0},{5,1},{8,4},{9,5},{12,8},{13,9},{14,12},{15,13},... | collective-permute-start | bytes 393224 | tf_op jit(solution)/shard_map/ppermute | solution.py:88
  95.9 6.4 %collective-permute-start.12 = (bf16[32,2048]{1,0:T(8,128)(2,1)S(1)}, bf16[32,2048]{1,0:T(8,128)(2,1)S(1)}, u32[]{:S(2)}, u32[]{:S(2)}) collective-permute-start(bf16[32,2048]{1,0:T(8,128)(2,1)S(1)} %get-tuple-element.84), channel_id=1, source_target_pairs={{0,4},{1,5},{4,8},{5,9},{8,12},{9,13},{12,14},{13,15},{14,10},{15,... | collective-permute-start | bytes 393224 | tf_op jit(solution)/shard_map/ppermute | solution.py:89
  102.4 6.8 %collective-permute-start.20 = (bf16[64,2048]{1,0:T(8,128)(2,1)S(1)}, bf16[64,2048]{1,0:T(8,128)(2,1)S(1)}, u32[]{:S(2)}, u32[]{:S(2)}) collective-permute-start(bf16[64,2048]{1,0:T(8,128)(2,1)S(1)} %add_convert_fusion.7), channel_id=1, source_target_pairs={{0,4},{1,5},{4,8},{5,9},{8,12},{9,13},{12,14},{13,15},{14,10},{15,... | collective-permute-start | bytes 786440 | tf_op jit(solution)/shard_map/ppermute | solution.py:89
  102.9 23.6 %copy-start.3 = (bf16[1,64,2048]{2,1,0:T(8,128)(2,1)S(1)}, bf16[1,64,2048]{2,1,0:T(8,128)(2,1)}, u32[]{:S(2)}) copy-start(bf16[1,64,2048]{2,1,0:T(8,128)(2,1)} %param.14) | copy-start | bytes 786436
  103.0 23.6 %copy-start.6 = (f32[1,2048]{1,0:T(1,128)S(1)}, f32[1,2048]{1,0:T(1,128)}, u32[]{:S(2)}) copy-start(f32[1,2048]{1,0:T(1,128)} %refs_2_.1) | copy-start | bytes 24580
  103.0 6.4 %collective-permute-start.19 = (bf16[64,2048]{1,0:T(8,128)(2,1)S(1)}, bf16[64,2048]{1,0:T(8,128)(2,1)S(1)}, u32[]{:S(2)}, u32[]{:S(2)}) collective-permute-start(bf16[64,2048]{1,0:T(8,128)(2,1)S(1)} %add_convert_fusion.8), channel_id=1, source_target_pairs={{0,2},{1,3},{4,0},{5,1},{8,4},{9,5},{12,8},{13,9},{14,12},{15,13},... | collective-permute-start | bytes 786440 | tf_op jit(solution)/shard_map/ppermute | solution.py:88
  104.7 9.7 %collective-permute-start.18 = (bf16[64,2048]{1,0:T(8,128)(2,1)S(1)}, bf16[64,2048]{1,0:T(8,128)(2,1)S(1)}, u32[]{:S(2)}, u32[]{:S(2)}) collective-permute-start(bf16[64,2048]{1,0:T(8,128)(2,1)S(1)} %pad_maximum_fusion.3), channel_id=1, source_target_pairs={{0,4},{1,5},{4,8},{5,9},{8,12},{9,13},{12,14},{13,15},{14,10},{15,... | collective-permute-start | bytes 786440 | tf_op jit(solution)/shard_map/ppermute | solution.py:89
  105.2 21.6 %copy-start.5 = (bf16[1,64,2048]{2,1,0:T(8,128)(2,1)S(1)}, bf16[1,64,2048]{2,1,0:T(8,128)(2,1)}, u32[]{:S(2)}) copy-start(bf16[1,64,2048]{2,1,0:T(8,128)(2,1)} %param.15) | copy-start | bytes 786436
  105.2 9.2 %collective-permute-start.17 = (bf16[64,2048]{1,0:T(8,128)(2,1)S(1)}, bf16[64,2048]{1,0:T(8,128)(2,1)S(1)}, u32[]{:S(2)}, u32[]{:S(2)}) collective-permute-start(bf16[64,2048]{1,0:T(8,128)(2,1)S(1)} %pad_maximum_fusion.2), channel_id=1, source_target_pairs={{0,2},{1,3},{4,0},{5,1},{8,4},{9,5},{12,8},{13,9},{14,12},{15,13},... | collective-permute-start | bytes 786440 | tf_op jit(solution)/shard_map/ppermute | solution.py:88
  114.5 17.1 %copy-start.4 = (bf16[1,64,2048]{2,1,0:T(8,128)(2,1)S(1)}, bf16[1,64,2048]{2,1,0:T(8,128)(2,1)}, u32[]{:S(2)}) copy-start(bf16[1,64,2048]{2,1,0:T(8,128)(2,1)} %param.11) | copy-start | bytes 786436
  114.5 8.4 %collective-permute-start.22 = (bf16[64,2048]{1,0:T(8,128)(2,1)S(1)}, bf16[64,2048]{1,0:T(8,128)(2,1)S(1)}, u32[]{:S(2)}, u32[]{:S(2)}) collective-permute-start(bf16[64,2048]{1,0:T(8,128)(2,1)S(1)} %add_convert_fusion.5), channel_id=1, source_target_pairs={{0,4},{1,5},{4,8},{5,9},{8,12},{9,13},{12,14},{13,15},{14,10},{15,... | collective-permute-start | bytes 786440 | tf_op jit(solution)/shard_map/ppermute | solution.py:89
  115.7 7.8 %collective-permute-start.21 = (bf16[64,2048]{1,0:T(8,128)(2,1)S(1)}, bf16[64,2048]{1,0:T(8,128)(2,1)S(1)}, u32[]{:S(2)}, u32[]{:S(2)}) collective-permute-start(bf16[64,2048]{1,0:T(8,128)(2,1)S(1)} %add_convert_fusion.6), channel_id=1, source_target_pairs={{0,2},{1,3},{4,0},{5,1},{8,4},{9,5},{12,8},{13,9},{14,12},{15,13},... | collective-permute-start | bytes 786440 | tf_op jit(solution)/shard_map/ppermute | solution.py:88
  116.8 9.4 %collective-permute-start.26 = (bf16[64,2048]{1,0:T(8,128)(2,1)S(1)}, bf16[64,2048]{1,0:T(8,128)(2,1)S(1)}, u32[]{:S(2)}, u32[]{:S(2)}) collective-permute-start(bf16[64,2048]{1,0:T(8,128)(2,1)S(1)} %get-tuple-element.78), channel_id=1, source_target_pairs={{0,2},{1,3},{4,0},{5,1},{8,4},{9,5},{12,8},{13,9},{14,12},{15,13},... | collective-permute-start | bytes 786440 | tf_op jit(solution)/shard_map/ppermute | solution.py:88
  118.6 7.9 %collective-permute-start.27 = (bf16[64,2048]{1,0:T(8,128)(2,1)S(1)}, bf16[64,2048]{1,0:T(8,128)(2,1)S(1)}, u32[]{:S(2)}, u32[]{:S(2)}) collective-permute-start(bf16[64,2048]{1,0:T(8,128)(2,1)S(1)} %get-tuple-element.79), channel_id=1, source_target_pairs={{0,4},{1,5},{4,8},{5,9},{8,12},{9,13},{12,14},{13,15},{14,10},{15,... | collective-permute-start | bytes 786440 | tf_op jit(solution)/shard_map/ppermute | solution.py:89
  123.6 6.4 %collective-permute-start.23 = (bf16[64,2048]{1,0:T(8,128)(2,1)S(1)}, bf16[64,2048]{1,0:T(8,128)(2,1)S(1)}, u32[]{:S(2)}, u32[]{:S(2)}) collective-permute-start(bf16[64,2048]{1,0:T(8,128)(2,1)S(1)} %get-tuple-element.80), channel_id=1, source_target_pairs={{0,2},{1,3},{4,0},{5,1},{8,4},{9,5},{12,8},{13,9},{14,12},{15,13},... | collective-permute-start | bytes 786440 | tf_op jit(solution)/shard_map/ppermute | solution.py:88
  125.2 6.4 %collective-permute-start.24 = (bf16[64,2048]{1,0:T(8,128)(2,1)S(1)}, bf16[64,2048]{1,0:T(8,128)(2,1)S(1)}, u32[]{:S(2)}, u32[]{:S(2)}) collective-permute-start(bf16[64,2048]{1,0:T(8,128)(2,1)S(1)} %get-tuple-element.81), channel_id=1, source_target_pairs={{0,4},{1,5},{4,8},{5,9},{8,12},{9,13},{12,14},{13,15},{14,10},{15,... | collective-permute-start | bytes 786440 | tf_op jit(solution)/shard_map/ppermute | solution.py:89
  127.1 6.4 %collective-permute-start.28 = (bf16[1,64,2048]{2,1,0:T(8,128)(2,1)S(1)}, bf16[1,64,2048]{2,1,0:T(8,128)(2,1)S(1)}, u32[]{:S(2)}, u32[]{:S(2)}) collective-permute-start(bf16[1,64,2048]{2,1,0:T(8,128)(2,1)S(1)} %fusion.8), channel_id=1, source_target_pairs={{0,16},{16,0},{1,17},{17,1},{2,18},{18,2},{3,19},{19,3},{4,20},{20... | collective-permute-start | bytes 786440 | tf_op jit(solution)/shard_map/ppermute | solution.py:41
  131.7 6.4 %collective-permute-start.25 = (bf16[1,64,2048]{2,1,0:T(8,128)(2,1)S(1)}, bf16[1,64,2048]{2,1,0:T(8,128)(2,1)S(1)}, u32[]{:S(2)}, u32[]{:S(2)}) collective-permute-start(bf16[1,64,2048]{2,1,0:T(8,128)(2,1)S(1)} %fusion.7), channel_id=1, source_target_pairs={{0,16},{16,0},{1,17},{17,1},{2,18},{18,2},{3,19},{19,3},{4,20},{20... | collective-permute-start | bytes 786440 | tf_op jit(solution)/shard_map/ppermute | solution.py:41

commit v4 on v3

--- a/solution.py
+++ b/solution.py
@@ -13,6 +13,8 @@
 TILE = 256
 ROWS_AT_ONCE = 256
 MIB = 1 << 20
+COST = 1
+PAUSE = 10**11
 IN_HBM = pl.BlockSpec(memory_space=pl.ANY)
 IN_VMEM = pl.BlockSpec(memory_space=pltpu.VMEM)
 IN_SMEM = pl.BlockSpec(memory_space=pltpu.SMEM)
@@ -41,9 +43,8 @@
     return lax.ppermute(block, axis, [(i, (i + distance) % size) for i in range(size)])
 
 
-def after(arrays, others):
-    count = len(arrays)
-    return lax.optimization_barrier((*arrays, *others))[:count]
+def joined(*groups):
+    return lax.optimization_barrier(groups)
 
 
 class RingGather:
@@ -52,17 +53,21 @@
         self.newest = (block, block)
         self.left = lax.axis_size("expert") // CORES // 2
 
-    def step(self, others=()):
+    def step(self):
+        self.newest = self.moved(*self.newest)
+        self.blocks += self.newest
+        self.left -= 1
+
+    def last_step(self, first, last):
+        behind, ahead = self.newest
+        half = behind.shape[0] // 2
+        return self.moved(behind[:half, first:last], ahead[half:, first:last])
+
+    def moved(self, behind, ahead):
         devices = lax.axis_size("expert")
-        behind, ahead = after(self.newest, others)
-        self.left -= 1
-        if not self.left:
-            half = behind.shape[0] // 2
-            behind, ahead = behind[:half], ahead[half:]
         behind = lax.ppermute(behind, "expert", ring_route(devices, 1))
         ahead = lax.ppermute(ahead, "expert", ring_route(devices, -1))
-        self.newest = (behind, ahead)
-        self.blocks += self.newest
+        return behind, ahead
 
 
 class RingScatter:
@@ -71,13 +76,13 @@
         self.newest = ()
         self.reach = self.left = lax.axis_size("expert") // CORES // 2
 
-    def step(self, others=()):
+    def step(self):
         devices = lax.axis_size("expert")
         to_behind, to_ahead = self.parts[2 * self.left - 1], self.parts[2 * self.left]
         if self.left == self.reach:
             behind, ahead = to_behind, to_ahead
         else:
-            behind, ahead = after(self.newest, others)
+            behind, ahead = self.newest
             half = self.parts[0].shape[0] // 2
             if self.left == self.reach - 1:
                 behind = jnp.concatenate([added(to_behind[:half], behind), to_behind[half:]])
@@ -110,7 +115,9 @@
 def payload_body(devices, *refs):
     sources, out, held, arrived = refs[:8], refs[8], refs[9:16], refs[16]
     width = sources[0].shape[1]
-    places = [*held, out.at[:, pl.ds(2 * width, width)]]
+    table_width = out.shape[1] - 3 * width
+    first = width + table_width
+    places = [*held, out.at[:, pl.ds(first + width, width)]]
     copies = [
         pltpu.make_async_copy(source, place, arrived.at[i])
         for i, (source, place) in enumerate(zip(sources, places))
@@ -120,9 +127,9 @@
     for copy in copies:
         copy.wait()
     rows, gain, routing = held[:2], held[2], (held[3:5], held[5:7])
-    for i, tokens in enumerate(rows):
-        out[:, i * width : (i + 1) * width] = normalize(tokens[...], gain[...])
-    shape = (out.shape[1] - 3 * width, out.shape[0])
+    out[:, :width] = normalize(rows[0][...], gain[...])
+    out[:, first : first + width] = normalize(rows[1][...], gain[...])
+    shape = (table_width, out.shape[0])
     row = lax.broadcasted_iota(jnp.int32, shape, 0)
     part, expert = lax.div(row, devices), lax.rem(row, devices)
     table = jnp.zeros(shape, jnp.float32)
@@ -132,7 +139,7 @@
             table += jnp.where(named, gates[i : i + 1, :], 0.0)
     high = table.astype(jnp.bfloat16).astype(jnp.float32)
     table = jnp.where(lax.rem(part, 2) == 0, high, table - high)
-    out[:, 3 * width :] = table.T.astype(jnp.bfloat16)
+    out[:, width:first] = table.T.astype(jnp.bfloat16)
 
 
 def payload(forward, backward, cotangent, gain, forward_routing, backward_routing, devices):
@@ -192,11 +199,11 @@
     )(*mine, *theirs)
 
 
-def collect(blocks, column, rows, arrived):
-    copies, first = [], 0
+def collect(blocks, rows, arrived):
+    copies, first, columns = [], 0, rows.shape[1]
     for i, block in enumerate(blocks):
         to = rows.at[pl.ds(first, block.shape[0])]
-        part = block.at[:, pl.ds(column, rows.shape[1])]
+        part = block.at[:, pl.ds(block.shape[1] - columns, columns)]
         copies.append(pltpu.make_async_copy(part, to, arrived.at[i]))
         first += block.shape[0]
     for copy in copies:
@@ -205,76 +212,82 @@
         copy.wait()
 
 
-def backward_body(count, devices, *refs):
+def gate_of(table, devices, experts, part, core):
+    lane = lax.broadcasted_iota(jnp.int32, table.shape, 1)
+    ours = part * devices + experts[core]
+    named = (lane == ours) | (lane == ours + devices)
+    return jnp.sum(jnp.where(named, table, 0.0), axis=1, keepdims=True)
+
+
+def grads_body(count, devices, *refs):
     blocks = refs[:count]
-    experts, gate_up, down, out, forward_gates, rows, grads, arrived = refs[count:]
+    experts, gate_up, down, grads, rows, arrived = refs[count:]
     width, hidden = gate_up.shape[0], down.shape[0] // CORES
-    collect(blocks, width, rows, arrived)
-    table = rows[:, 2 * width :].astype(jnp.float32)
-    lane = lax.broadcasted_iota(jnp.int32, table.shape, 1)
-
-    def gate(first, core):
-        ours = first * devices + experts[core]
-        named = (lane == ours) | (lane == ours + devices)
-        return jnp.sum(jnp.where(named, table, 0.0), axis=1, keepdims=True)
-
-    out_lane = lax.broadcasted_iota(jnp.int32, forward_gates.shape, 1)
-    forward_gates[...] = jnp.where(out_lane == 0, gate(0, 0), gate(0, 1))
+    first = rows.shape[1] - 2 * width
+    collect(blocks, rows, arrived)
+    table = rows[:, :first].astype(jnp.float32)
+    normed, cotangent = rows.at[:, pl.ds(first, width)], rows.at[:, pl.ds(first + width, width)]
     for core in range(CORES):
-        scale = gate(2, core)
+        scale = gate_of(table, devices, experts, 2, core)
         for tile in range(0, hidden, TILE):
             gate_at = pl.ds(2 * core * hidden + tile, TILE)
             up_at = pl.ds((2 * core + 1) * hidden + tile, TILE)
             down_at = pl.ds(core * hidden + tile, TILE)
-            gate_act = dot_plain(rows[:, :width], gate_up[:, gate_at])
-            up_act = dot_plain(rows[:, :width], gate_up[:, up_at])
-            hidden_grad = dot_trans(rows[:, width : 2 * width], down[down_at, :]) * scale
+            gate_act = dot_plain(normed[...], gate_up[:, gate_at])
+            up_act = dot_plain(normed[...], gate_up[:, up_at])
+            hidden_grad = dot_trans(cotangent[...], down[down_at, :]) * scale
             sigmoid_val = jax.nn.sigmoid(gate_act)
             silu_slope = sigmoid_val * (1.0 + gate_act * (1.0 - sigmoid_val))
             grads[:, gate_at] = (hidden_grad * up_act * silu_slope).astype(jnp.bfloat16)
             grads[:, up_at] = (hidden_grad * (gate_act * sigmoid_val)).astype(jnp.bfloat16)
-    for tile in range(0, width, TILE):
-        at = pl.ds(tile, TILE)
-        out[:, at] = dot_trans(grads[...], gate_up[at, :]).astype(jnp.bfloat16)
-
-
-def experts_backward(blocks, experts, gate_up, down, devices):
-    width = gate_up.shape[0]
-    count, rows = sum(b.shape[0] for b in blocks), blocks[0].shape[1] - width
+
+
+def hidden_grads(blocks, experts, gate_up, down, devices, table):
+    count, width = sum(b.shape[0] for b in blocks), gate_up.shape[0]
     return pl.pallas_call(
-        functools.partial(backward_body, len(blocks), devices),
+        functools.partial(grads_body, len(blocks), devices),
         in_specs=[IN_HBM] * len(blocks) + [IN_SMEM, IN_VMEM, IN_VMEM],
-        out_specs=(IN_VMEM, IN_VMEM),
-        out_shape=(
-            jax.ShapeDtypeStruct((count, width), jnp.bfloat16),
-            jax.ShapeDtypeStruct((count, LANES), jnp.float32),
-        ),
+        out_specs=IN_VMEM,
+        out_shape=jax.ShapeDtypeStruct((count, gate_up.shape[1]), jnp.bfloat16),
         scratch_shapes=[
-            pltpu.VMEM((count, rows), jnp.bfloat16),
-            pltpu.VMEM((count, gate_up.shape[1]), jnp.bfloat16),
+            pltpu.VMEM((count, table + 2 * width), jnp.bfloat16),
             pltpu.SemaphoreType.DMA((len(blocks),)),
         ],
         compiler_params=pltpu.CompilerParams(vmem_limit_bytes=14 * MIB),
-        cost_estimate=pl.CostEstimate(
-            flops=1,
-            bytes_accessed=1,
-            transcendentals=0,
-        ),
+        cost_estimate=pl.CostEstimate(flops=COST, bytes_accessed=1, transcendentals=0),
     )(*blocks, experts, gate_up, down)
 
 
-def forward_body(count, *refs):
+def token_grads_body(grads, gate_up, out):
+    for tile in range(0, out.shape[1], TILE):
+        at = pl.ds(tile, TILE)
+        out[:, at] = dot_trans(grads[...], gate_up[at, :]).astype(jnp.bfloat16)
+
+
+def token_grads(grads, gate_up, cost=COST):
+    return pl.pallas_call(
+        token_grads_body,
+        in_specs=[IN_VMEM, IN_VMEM],
+        out_specs=IN_VMEM,
+        out_shape=jax.ShapeDtypeStruct((grads.shape[0], gate_up.shape[0]), jnp.bfloat16),
+        compiler_params=pltpu.CompilerParams(vmem_limit_bytes=14 * MIB),
+        cost_estimate=pl.CostEstimate(flops=cost, bytes_accessed=1, transcendentals=0),
+    )(grads, gate_up)
+
+
+def forward_body(count, devices, *refs):
     blocks = refs[:count]
-    gates, gate_up, down, out, rows, acts, arrived = refs[count:]
+    experts, gate_up, down, out, rows, acts, arrived = refs[count:]
     width, hidden = gate_up.shape[0], down.shape[0] // CORES
-    collect(blocks, 0, rows, arrived)
+    collect([block.at[:, pl.ds(0, rows.shape[1])] for block in blocks], rows, arrived)
+    table = rows[:, width:].astype(jnp.float32)
     for core in range(CORES):
-        scale = gates[:, core : core + 1]
+        scale = gate_of(table, devices, experts, 0, core)
         for tile in range(0, hidden, TILE):
             gate_at = pl.ds(2 * core * hidden + tile, TILE)
             up_at = pl.ds((2 * core + 1) * hidden + tile, TILE)
-            gate_act = dot_plain(rows[...], gate_up[:, gate_at])
-            up_act = dot_plain(rows[...], gate_up[:, up_at])
+            gate_act = dot_plain(rows[:, :width], gate_up[:, gate_at])
+            up_act = dot_plain(rows[:, :width], gate_up[:, up_at])
             act = gate_act * jax.nn.sigmoid(gate_act) * up_act * scale
             acts[:, pl.ds(core * hidden + tile, TILE)] = act.astype(jnp.bfloat16)
     for tile in range(0, width, TILE):
@@ -282,25 +295,21 @@
         out[:, at] = dot_plain(acts[...], down[:, at]).astype(jnp.bfloat16)
 
 
-def experts_forward(blocks, gates, gate_up, down):
+def experts_forward(blocks, experts, gate_up, down, devices, table):
     count, width = sum(b.shape[0] for b in blocks), gate_up.shape[0]
     return pl.pallas_call(
-        functools.partial(forward_body, len(blocks)),
-        in_specs=[IN_HBM] * len(blocks) + [IN_VMEM, IN_VMEM, IN_VMEM],
+        functools.partial(forward_body, len(blocks), devices),
+        in_specs=[IN_HBM] * len(blocks) + [IN_SMEM, IN_VMEM, IN_VMEM],
         out_specs=IN_VMEM,
         out_shape=jax.ShapeDtypeStruct((count, width), jnp.bfloat16),
         scratch_shapes=[
-            pltpu.VMEM((count, width), jnp.bfloat16),
+            pltpu.VMEM((count, width + table), jnp.bfloat16),
             pltpu.VMEM((count, down.shape[0]), jnp.bfloat16),
             pltpu.SemaphoreType.DMA((len(blocks),)),
         ],
         compiler_params=pltpu.CompilerParams(vmem_limit_bytes=14 * MIB),
-        cost_estimate=pl.CostEstimate(
-            flops=1,
-            bytes_accessed=1,
-            transcendentals=0,
-        ),
-    )(*blocks, gates, gate_up, down)
+        cost_estimate=pl.CostEstimate(flops=COST, bytes_accessed=1, transcendentals=0),
+    )(*blocks, experts, gate_up, down)
 
 
 def grouped(blocks):
@@ -340,53 +349,65 @@
     devices = lax.axis_size("expert")
     gain_row = norm_gain[0]
     cotangent = backward_cotangent[0]
-    tokens = RingGather(
-        payload(
-            forward_tokens[0],
-            backward_tokens[0],
-            cotangent,
-            norm_gain,
-            (forward_choice[0].T, forward_gates[0].T),
-            (backward_choice[0].T, backward_gates[0].T),
-            devices,
-        )
-    )
-    mine = (gate_weight[0, 0], up_weight[0, 0], down_weight[0, 0])
     me = lax.axis_index("expert").astype(jnp.int32)
     experts = jnp.stack([me, me + 1 - 2 * lax.rem(me, 2)])
-
+    own = payload(
+        forward_tokens[0],
+        backward_tokens[0],
+        cotangent,
+        norm_gain,
+        (forward_choice[0].T, forward_gates[0].T),
+        (backward_choice[0].T, backward_gates[0].T),
+        devices,
+    )
+    width, columns = forward_tokens.shape[2], own.shape[1]
+    table = columns - 3 * width
+    tokens = RingGather(own)
     tokens.step()
-    theirs = after(mine, tokens.newest)
-    theirs = tuple(lax.ppermute(w, "expert", core_route(devices)) for w in theirs)
-    while tokens.left > 1:
+    mine = (gate_weight[0, 0], up_weight[0, 0], down_weight[0, 0])
+    theirs = tuple(lax.ppermute(w, "expert", core_route(devices)) for w in mine)
+
+    def run_back(blocks):
+        return hidden_grads(blocks, experts, gate_up, down, devices, table)
+
+    def run_fwd(blocks):
+        return experts_forward(blocks, experts, gate_up, down, devices, table)
+
+    while tokens.left > 3:
         tokens.step()
-    early = grouped(tokens.blocks)[:-1]
-    theirs = after(theirs, early[-1][-1:])
+    tokens.newest, theirs = joined(tokens.newest, theirs)
+    fwd_groups = grouped(tokens.blocks)
+    tokens.step()
     gate_up, down = weights_in_vmem(mine, theirs)
-
-    def run_back(blocks):
-        return experts_backward(blocks, experts, gate_up, down, devices)
-
-    def run_fwd(blocks, gates):
-        return experts_forward(blocks, gates, gate_up, down)
-
-    back_outs = [run_back(group) for group in early]
-    tokens.step([out for out, _ in back_outs])
-    fwd_outs = [run_fwd(group, gates) for group, (_, gates) in zip(early, back_outs)]
-    groups = grouped(tokens.blocks)
-    back_outs.append(run_back(after(groups[-1], fwd_outs)))
-    back_sum = RingScatter(ungrouped([out for out, _ in back_outs], groups))
-    back_sum.step()
-    fwd_outs.append(run_fwd(groups[-1], back_outs[-1][1]))
-    fwd_sum = RingScatter(ungrouped(fwd_outs, groups))
-    back_sum.step()
+    fwd_outs = [run_fwd(group) for group in fwd_groups]
+    tokens.newest, fwd_outs[-1] = joined(tokens.newest, fwd_outs[-1])
+    back_groups = grouped(tokens.blocks)[:-1]
+    fwd_groups.append(tokens.blocks[-2:])
+    tokens.step()
+    back_outs = [token_grads(run_back(group), gate_up) for group in back_groups]
+    fwd_outs.append(run_fwd(fwd_groups[-1]))
+    tokens.newest, fwd_outs[-1], back_outs[-1] = joined(
+        tokens.newest, fwd_outs[-1], back_outs[-1]
+    )
+    fwd_last = tokens.last_step(0, width + table)
+    back_last = tokens.last_step(width, columns)
+    fwd_groups.append([*tokens.blocks[-2:], *fwd_last])
+    fwd_outs.append(run_fwd(fwd_groups[-1]))
+    fwd_sum = RingScatter(ungrouped(fwd_outs, fwd_groups))
     fwd_sum.step()
+    for group in grouped([*tokens.blocks, *back_last])[len(back_groups) :]:
+        fwd_outs[-1], group[0] = joined(fwd_outs[-1], group[0])
+        grads = run_back(group)
+        if fwd_sum.left == fwd_sum.reach - 1:
+            fwd_sum.newest, grads = joined(fwd_sum.newest, grads)
+            fwd_sum.step()
+        back_groups.append(group)
+        back_outs.append(token_grads(grads, gate_up, PAUSE))
+    back_sum = RingScatter(ungrouped(back_outs, back_groups))
     while back_sum.left:
-        arrived = back_sum.newest
-        back_sum.step(fwd_sum.newest)
-        fwd_sum.step(arrived)
-    while fwd_sum.left:
-        fwd_sum.step()
+        back_sum.step()
+        if fwd_sum.left:
+            fwd_sum.step()
 
     back_f32 = backward_tokens[0].astype(jnp.float32)
     back_inverse = inverse_norm(back_f32)

time: 142 us -> 135 us (0.951)
  waiting for transfers between devices: 65.9 us -> 57 us
  starting transfers between devices: 28.9 us -> 30.9 us
    ppermute x8 -> x10, waiting for transfers between devices: 39.3 us -> 32 us  [the longest x5 28.2 us: moved(): behind = lax.ppermute(behind, 'expert', ring_route(devices, 1))]
    ppermute x8, waiting for transfers between devices: 14.3 us -> 11.2 us  [step(): ahead = lax.ppermute(ahead, 'expert', ring_route(devices, 1))]
    ppermute x8, starting transfers between devices: 12.3 us -> 9.61 us  [step(): behind = lax.ppermute(behind, 'expert', ring_route(devices, -1))]
    ppermute x8, starting transfers between devices: 4.51 us -> 7.17 us  [step(): ahead = lax.ppermute(ahead, 'expert', ring_route(devices, 1))]
    ppermute x8 -> x10, starting transfers between devices: 8.44 us -> 10.4 us  [the longest x5 5.4 us: moved(): behind = lax.ppermute(behind, 'expert', ring_route(devices, 1))]
    ppermute x8, waiting for transfers between devices: 7.43 us -> 8.87 us  [step(): behind = lax.ppermute(behind, 'expert', ring_route(devices, -1))]
    pallas_call x4 -> x7, Pallas kernels: 30.7 us -> 31.2 us  [the longest x3 12.5 us: experts_forward(): pl.pallas_call(functools.partial(forward_body, len(blocks), devices), in_...]
  transfers between devices with their start and end apart: 29 -> 31, of which waited for: 20 -> 19; matrix products, arithmetic and copies ran while one was open for 1% -> 1% of each run, Pallas kernels for 20% -> 28%
where the time goes in v4:
time: 135 us; the launch traced here: 132 us
  waiting for transfers between devices  57 us (42%)
  Pallas kernels  40.2 us (30%)
  starting transfers between devices  30.9 us (23%)
  local copies, waits for them, and re-layouts  1.58 us (1%)
  other arithmetic  1.54 us (1%)
    ppermute x5, waiting for transfers between devices, moved(): behind = lax.ppermute(behind, 'expert', ring_route(devices, 1))  28.2 us
    pallas_call x3, Pallas kernels, experts_forward(): pl.pallas_call(functools.partial(forward_body, len(blocks), devices), in_...  12.5 us
    pallas_call x2, Pallas kernels, hidden_grads(): pl.pallas_call(functools.partial(grads_body, len(blocks), devices), in_sp...  11.8 us
    ppermute x8, waiting for transfers between devices, step(): ahead = lax.ppermute(ahead, 'expert', ring_route(devices, 1))  11.2 us
    ppermute x8, starting transfers between devices, step(): behind = lax.ppermute(behind, 'expert', ring_route(devices, -1))  9.61 us
    ppermute x8, waiting for transfers between devices, step(): behind = lax.ppermute(behind, 'expert', ring_route(devices, -1))  8.87 us
    ppermute x8, starting transfers between devices, step(): ahead = lax.ppermute(ahead, 'expert', ring_route(devices, 1))  7.17 us
    pallas_call x2, Pallas kernels, token_grads(): pl.pallas_call(token_grads_body, in_specs=[IN_VMEM, IN_VMEM], out_specs=I...  6.88 us
  transfers between devices with their start and end apart: 31, of which 19 were waited for; matrix products, arithmetic and copies ran while one was open for 1% of the time, Pallas kernels for 28%

profile of v4, /device:TPU:12, one launch (start us, length us, event | category | flops | bytes accessed | tf_op | source)
XLA Modules:
  0.0 132.1 jit_solution(7764913639435438515)
XLA Ops:
  1.3 2.4 %shard_map.122.refs_0_ = bf16[64,6272]{1,0:T(8,128)(2,1)} custom-call(bf16[64,2048]{1,0:T(8,128)(2,1)} %bitcast.37, bf16[64,2048]{1,0:T(8,128)(2,1)} %bitcast.36, f32[1,2048]{1,0:T(1,128)} %refs_2_.1, s32[8,64]{1,0:T(8,128)} %bitcast.41, f32[8,64]{1,0:T(8,128)} %bitcast.42, s32[8,64]{1,0:T(8,128)} %bitcast.43, f32[8,64]{1,0:T(8,128)} %bitcast.44, ...), custom_call_target="tpu_custom_call" | custom-call | flops 1 | bytes 1 | tf_op jit(solution)/shard_map/pallas_call | solution.py:149
  4.2 1.6 %collective-permute-start.1 = (bf16[64,6272]{1,0:T(8,128)(2,1)}, bf16[64,6272]{1,0:T(8,128)(2,1)S(1)}, u32[]{:S(2)}, u32[]{:S(2)}) collective-permute-start(bf16[64,6272]{1,0:T(8,128)(2,1)} %shard_map.122.refs_0_), channel_id=1, source_target_pairs={{0,2},{1,3},{4,0},{5,1},{8,4},{9,5},{12,8},{13,9},{14,12},{15,13},... | collective-permute-start | bytes 2408456 | tf_op jit(solution)/shard_map/ppermute | solution.py:69
  5.8 18.4 %collective-permute-done.refs_1_ = bf16[64,6272]{1,0:T(8,128)(2,1)S(1)} collective-permute-done((bf16[64,6272]{1,0:T(8,128)(2,1)}, bf16[64,6272]{1,0:T(8,128)(2,1)S(1)}, u32[]{:S(2)}, u32[]{:S(2)}) %collective-permute-start) | collective-permute-done | bytes 802848 | tf_op jit(solution)/shard_map/ppermute | solution.py:68
  24.8 1.7 %collective-permute-start.6 = (bf16[64,6272]{1,0:T(8,128)(2,1)S(1)}, bf16[64,6272]{1,0:T(8,128)(2,1)S(1)}, u32[]{:S(2)}, u32[]{:S(2)}) collective-permute-start(bf16[64,6272]{1,0:T(8,128)(2,1)S(1)} %collective-permute-done.1.refs_2_), channel_id=1, source_target_pairs={{0,2},{1,3},{4,0},{5,1},{8,4},{9,5},{12,8},{13,9},{14,12},{15,13},... | collective-permute-start | bytes 2408456 | tf_op jit(solution)/shard_map/ppermute | solution.py:69
  26.5 6.6 %shard_map.123 = (bf16[2048,3072]{1,0:T(8,128)(2,1)S(1)}, bf16[1536,2048]{1,0:T(8,128)(2,1)S(1)}) custom-call(bf16[2048,768]{1,0:T(8,128)(2,1)} %bitcast.31, bf16[2048,768]{1,0:T(8,128)(2,1)} %bitcast.33, bf16[768,2048]{1,0:T(8,128)(2,1)} %bitcast.35, bf16[2048,768]{1,0:T(8,128)(2,1)} %collective-permute-done.2.refs_3_, ...), custom_call_target="tpu_custom_call" | custom-call | tf_op jit(solution)/shard_map/pallas_call | solution.py:189
  33.1 4.5 %shard_map.124 = bf16[192,2048]{1,0:T(8,128)(2,1)S(1)} custom-call(bf16[64,6272]{1,0:T(8,128)(2,1)S(1)} %copy-done, bf16[64,6272]{1,0:T(8,128)(2,1)S(1)} %collective-permute-done.refs_1_, bf16[64,6272]{1,0:T(8,128)(2,1)S(1)} %collective-permute-done.1.refs_2_, s32[2]{0:T(128)S(1)} %pad_add_fusion.refs_3_.refs_2_.refs_4_.refs_5_, ...), custom_call_target="tpu_custom_call" | custom-call | flops 1 | bytes 1 | tf_op jit(solution)/shard_map/pallas_call | solution.py:300
  37.6 6.1 %collective-permute-done.5.refs_0_.refs_3_ = bf16[64,6272]{1,0:T(8,128)(2,1)S(1)} collective-permute-done((bf16[64,6272]{1,0:T(8,128)(2,1)S(1)}, bf16[64,6272]{1,0:T(8,128)(2,1)S(1)}, u32[]{:S(2)}, u32[]{:S(2)}) %collective-permute-start.5) | collective-permute-done | bytes 802848 | tf_op jit(solution)/shard_map/ppermute | solution.py:68
  44.0 1.4 %collective-permute-start.7 = (bf16[64,6272]{1,0:T(8,128)(2,1)S(1)}, bf16[64,6272]{1,0:T(8,128)(2,1)S(1)}, u32[]{:S(2)}, u32[]{:S(2)}) collective-permute-start(bf16[64,6272]{1,0:T(8,128)(2,1)S(1)} %collective-permute-done.5.refs_0_.refs_3_), channel_id=1, source_target_pairs={{0,4},{1,5},{4,8},{5,9},{8,12},{9,13},{12,14},{13,15},{14,10},{15,... | collective-permute-start | bytes 2408456 | tf_op jit(solution)/shard_map/ppermute | solution.py:68
  45.4 0.6 collective-permute-start.8
  46.0 5.9 %shard_map.126.grads = bf16[256,3072]{1,0:T(8,128)(2,1)S(1)} custom-call(bf16[64,6272]{1,0:T(8,128)(2,1)S(1)} %copy-done, bf16[64,6272]{1,0:T(8,128)(2,1)S(1)} %collective-permute-done.refs_1_, bf16[64,6272]{1,0:T(8,128)(2,1)S(1)} %collective-permute-done.1.refs_2_, bf16[64,6272]{1,0:T(8,128)(2,1)S(1)} %collective-permute-done.5.refs_0_.refs_3_, ...), custom_call_target="tpu_custom_call" | custom-call | flops 1 | bytes 1 | tf_op jit(solution)/shard_map/pallas_call | solution.py:247
  51.9 3.4 %shard_map.127 = bf16[256,2048]{1,0:T(8,128)(2,1)S(1)} custom-call(bf16[256,3072]{1,0:T(8,128)(2,1)S(1)} %shard_map.126.grads, bf16[2048,3072]{1,0:T(8,128)(2,1)S(1)} %get-tuple-element.25.refs_4_.refs_3_.refs_5_.gate_up.refs_6_), custom_call_target="tpu_custom_call" | custom-call | flops 1 | bytes 1 | tf_op jit(solution)/shard_map/pallas_call | solution.py:268
  55.4 3.2 %shard_map.125 = bf16[128,2048]{1,0:T(8,128)(2,1)S(1)} custom-call(bf16[64,6272]{1,0:T(8,128)(2,1)S(1)} %collective-permute-done.5.refs_0_.refs_3_, bf16[64,6272]{1,0:T(8,128)(2,1)S(1)} %collective-permute-done.6.refs_1_.refs_0_, s32[2]{0:T(128)S(1)} %pad_add_fusion.refs_3_.refs_2_.refs_4_.refs_5_, ...), custom_call_target="tpu_custom_call" | custom-call | flops 1 | bytes 1 | tf_op jit(solution)/shard_map/pallas_call | solution.py:300
  58.6 3.6 %collective-permute-done.7.refs_0_.refs_1_ = bf16[64,6272]{1,0:T(8,128)(2,1)S(1)} collective-permute-done((bf16[64,6272]{1,0:T(8,128)(2,1)S(1)}, bf16[64,6272]{1,0:T(8,128)(2,1)S(1)}, u32[]{:S(2)}, u32[]{:S(2)}) %collective-permute-start.7) | collective-permute-done | bytes 802848 | tf_op jit(solution)/shard_map/ppermute | solution.py:68
  62.2 1.1 collective-permute-done.8.refs_1_.refs_2_
  63.4 0.7 collective-permute-start.10
  64.1 1.4 %collective-permute-start.9 = (bf16[32,2176]{1,0:T(8,128)(2,1)S(1)}, bf16[32,2176]{1,0:T(8,128)(2,1)S(1)}, u32[]{:S(2)}, u32[]{:S(2)}) collective-permute-start(bf16[32,2176]{1,0:T(8,128)(2,1)S(1)} %slice.93), channel_id=1, source_target_pairs={{0,4},{1,5},{4,8},{5,9},{8,12},{9,13},{12,14},{13,15},{14,10},{15,... | collective-permute-start | bytes 417800 | tf_op jit(solution)/shard_map/ppermute | solution.py:68
  65.6 1.6 %collective-permute-start.13 = (bf16[32,4224]{1,0:T(8,128)(2,1)S(1)}, bf16[32,4224]{1,0:T(8,128)(2,1)S(1)}, u32[]{:S(2)}, u32[]{:S(2)}) collective-permute-start(bf16[32,4224]{1,0:T(8,128)(2,1)S(1)} %slice.98), channel_id=1, source_target_pairs={{0,4},{1,5},{4,8},{5,9},{8,12},{9,13},{12,14},{13,15},{14,10},{15,... | collective-permute-start | bytes 811016 | tf_op jit(solution)/shard_map/ppermute | solution.py:68
  67.7 2.3 %collective-permute-done.10.refs_3_ = bf16[32,2176]{1,0:T(8,128)(2,1)S(1)} collective-permute-done((bf16[32,2176]{1,0:T(8,128)(2,1)S(1)}, bf16[32,2176]{1,0:T(8,128)(2,1)S(1)}, u32[]{:S(2)}, u32[]{:S(2)}) %collective-permute-start.10) | collective-permute-done | bytes 139296 | tf_op jit(solution)/shard_map/ppermute | solution.py:69
  69.9 4.8 %shard_map.128 = bf16[192,2048]{1,0:T(8,128)(2,1)S(1)} custom-call(bf16[64,6272]{1,0:T(8,128)(2,1)S(1)} %collective-permute-done.7.refs_0_.refs_1_, bf16[64,6272]{1,0:T(8,128)(2,1)S(1)} %collective-permute-done.8.refs_1_.refs_2_, bf16[32,2176]{1,0:T(8,128)(2,1)S(1)} %collective-permute-done.9.refs_2_, bf16[32,2176]{1,0:T(8,128)(2,1)S(1)} %collective-permute-done.10.refs_3_, ...), custom_call_target="tpu_custom_call" | custom-call | flops 1 | bytes 1 | tf_op jit(solution)/shard_map/pallas_call | solution.py:300
  74.8 1.2 collective-permute-start.11
  76.0 0.9 collective-permute-start.12
  76.9 5.9 %shard_map.129.grads = bf16[256,3072]{1,0:T(8,128)(2,1)S(1)} custom-call(bf16[64,6272]{1,0:T(8,128)(2,1)S(1)} %collective-permute-done.6.refs_1_.refs_0_, bf16[64,6272]{1,0:T(8,128)(2,1)S(1)} %collective-permute-done.7.refs_0_.refs_1_, bf16[64,6272]{1,0:T(8,128)(2,1)S(1)} %collective-permute-done.8.refs_1_.refs_2_, ...), custom_call_target="tpu_custom_call" | custom-call | flops 1 | bytes 1 | tf_op jit(solution)/shard_map/pallas_call | solution.py:247
  82.8 3.4 %shard_map.130 = bf16[256,2048]{1,0:T(8,128)(2,1)S(1)} custom-call(bf16[256,3072]{1,0:T(8,128)(2,1)S(1)} %shard_map.129.grads, bf16[2048,3072]{1,0:T(8,128)(2,1)S(1)} %get-tuple-element.25.refs_4_.refs_3_.refs_5_.gate_up.refs_6_), custom_call_target="tpu_custom_call" | custom-call | flops 99999997952 | bytes 1 | tf_op jit(solution)/shard_map/pallas_call | solution.py:268
  86.3 1.2 collective-permute-start.22
  87.6 0.9 collective-permute-start.26
  88.5 1.6 %collective-permute-start.18 = (bf16[64,2048]{1,0:T(8,128)(2,1)S(1)}, bf16[64,2048]{1,0:T(8,128)(2,1)S(1)}, u32[]{:S(2)}, u32[]{:S(2)}) collective-permute-start(bf16[64,2048]{1,0:T(8,128)(2,1)S(1)} %pad_maximum_fusion.1), channel_id=1, source_target_pairs={{0,4},{1,5},{4,8},{5,9},{8,12},{9,13},{12,14},{13,15},{14,10},{15,... | collective-permute-start | bytes 786440 | tf_op jit(solution)/shard_map/ppermute | solution.py:94
  90.7 2.1 %collective-permute-done.22 = bf16[32,2048]{1,0:T(8,128)(2,1)S(1)} collective-permute-done((bf16[32,2048]{1,0:T(8,128)(2,1)S(1)}, bf16[32,2048]{1,0:T(8,128)(2,1)S(1)}, u32[]{:S(2)}, u32[]{:S(2)}) %collective-permute-start.22) | collective-permute-done | bytes 131104 | tf_op jit(solution)/shard_map/ppermute | solution.py:93
  92.8 0.7 collective-permute-done.26
  93.6 1.0 collective-permute-start.27
  94.6 1.2 collective-permute-start.23
  95.7 3.4 %collective-permute-done.18 = bf16[64,2048]{1,0:T(8,128)(2,1)S(1)} collective-permute-done((bf16[64,2048]{1,0:T(8,128)(2,1)S(1)}, bf16[64,2048]{1,0:T(8,128)(2,1)S(1)}, u32[]{:S(2)}, u32[]{:S(2)}) %collective-permute-start.18) | collective-permute-done | bytes 262176 | tf_op jit(solution)/shard_map/ppermute | solution.py:94
  99.6 1.2 collective-permute-start.16
  100.9 0.8 collective-permute-start.19
  101.7 3.0 %collective-permute-done.27 = bf16[64,2048]{1,0:T(8,128)(2,1)S(1)} collective-permute-done((bf16[64,2048]{1,0:T(8,128)(2,1)S(1)}, bf16[64,2048]{1,0:T(8,128)(2,1)S(1)}, u32[]{:S(2)}, u32[]{:S(2)}) %collective-permute-start.27) | collective-permute-done | bytes 262176 | tf_op jit(solution)/shard_map/ppermute | solution.py:94
  105.4 1.6 %collective-permute-start.24 = (bf16[64,2048]{1,0:T(8,128)(2,1)S(1)}, bf16[64,2048]{1,0:T(8,128)(2,1)S(1)}, u32[]{:S(2)}, u32[]{:S(2)}) collective-permute-start(bf16[64,2048]{1,0:T(8,128)(2,1)S(1)} %add_convert_fusion.3), channel_id=1, source_target_pairs={{0,2},{1,3},{4,0},{5,1},{8,4},{9,5},{12,8},{13,9},{14,12},{15,13},... | collective-permute-start | bytes 786440 | tf_op jit(solution)/shard_map/ppermute | solution.py:93
  107.0 3.7 %collective-permute-done.16 = bf16[64,2048]{1,0:T(8,128)(2,1)S(1)} collective-permute-done((bf16[64,2048]{1,0:T(8,128)(2,1)S(1)}, bf16[64,2048]{1,0:T(8,128)(2,1)S(1)}, u32[]{:S(2)}, u32[]{:S(2)}) %collective-permute-start.16) | collective-permute-done | bytes 262176 | tf_op jit(solution)/shard_map/ppermute | solution.py:93
  110.8 1.2 collective-permute-start.17
  112.1 0.9 collective-permute-start.20
  112.9 2.7 %collective-permute-done.28 = bf16[64,2048]{1,0:T(8,128)(2,1)S(1)} collective-permute-done((bf16[64,2048]{1,0:T(8,128)(2,1)S(1)}, bf16[64,2048]{1,0:T(8,128)(2,1)S(1)}, u32[]{:S(2)}, u32[]{:S(2)}) %collective-permute-start.28) | collective-permute-done | bytes 262176 | tf_op jit(solution)/shard_map/ppermute | solution.py:94
  115.8 1.5 %collective-permute-start.25 = (bf16[64,2048]{1,0:T(8,128)(2,1)S(1)}, bf16[64,2048]{1,0:T(8,128)(2,1)S(1)}, u32[]{:S(2)}, u32[]{:S(2)}) collective-permute-start(bf16[64,2048]{1,0:T(8,128)(2,1)S(1)} %get-tuple-element.40), channel_id=1, source_target_pairs={{0,2},{1,3},{4,0},{5,1},{8,4},{9,5},{12,8},{13,9},{14,12},{15,13},... | collective-permute-start | bytes 786440 | tf_op jit(solution)/shard_map/ppermute | solution.py:93
  117.3 0.6 collective-permute-start.29
  118.6 1.5 %collective-permute-start.21 = (bf16[1,64,2048]{2,1,0:T(8,128)(2,1)S(1)}, bf16[1,64,2048]{2,1,0:T(8,128)(2,1)S(1)}, u32[]{:S(2)}, u32[]{:S(2)}) collective-permute-start(bf16[1,64,2048]{2,1,0:T(8,128)(2,1)S(1)} %fusion.7), channel_id=1, source_target_pairs={{0,16},{16,0},{1,17},{17,1},{2,18},{18,2},{3,19},{19,3},{4,20},{20... | collective-permute-start | bytes 786440 | tf_op jit(solution)/shard_map/ppermute | solution.py:43
  120.2 2.1 %collective-permute-done.25 = bf16[64,2048]{1,0:T(8,128)(2,1)S(1)} collective-permute-done((bf16[64,2048]{1,0:T(8,128)(2,1)S(1)}, bf16[64,2048]{1,0:T(8,128)(2,1)S(1)}, u32[]{:S(2)}, u32[]{:S(2)}) %collective-permute-start.25) | collective-permute-done | bytes 262176 | tf_op jit(solution)/shard_map/ppermute | solution.py:93
  122.2 1.4 %collective-permute-done.29 = bf16[64,2048]{1,0:T(8,128)(2,1)S(1)} collective-permute-done((bf16[64,2048]{1,0:T(8,128)(2,1)S(1)}, bf16[64,2048]{1,0:T(8,128)(2,1)S(1)}, u32[]{:S(2)}, u32[]{:S(2)}) %collective-permute-start.29) | collective-permute-done | bytes 262176 | tf_op jit(solution)/shard_map/ppermute | solution.py:94
  124.2 1.6 %collective-permute-start.30 = (bf16[1,64,2048]{2,1,0:T(8,128)(2,1)S(1)}, bf16[1,64,2048]{2,1,0:T(8,128)(2,1)S(1)}, u32[]{:S(2)}, u32[]{:S(2)}) collective-permute-start(bf16[1,64,2048]{2,1,0:T(8,128)(2,1)S(1)} %fusion.8), channel_id=1, source_target_pairs={{0,16},{16,0},{1,17},{17,1},{2,18},{18,2},{3,19},{19,3},{4,20},{20... | collective-permute-start | bytes 786440 | tf_op jit(solution)/shard_map/ppermute | solution.py:43
  125.8 4.9 %collective-permute-done.30 = bf16[1,64,2048]{2,1,0:T(8,128)(2,1)S(1)} collective-permute-done((bf16[1,64,2048]{2,1,0:T(8,128)(2,1)S(1)}, bf16[1,64,2048]{2,1,0:T(8,128)(2,1)S(1)}, u32[]{:S(2)}, u32[]{:S(2)}) %collective-permute-start.30) | collective-permute-done | bytes 262176 | tf_op jit(solution)/shard_map/ppermute | solution.py:43
  130.7 0.7 copy.15
  131.4 0.7 copy.16
  (57 shorter events, 6.2 us)
Async XLA Ops:
  0.6 23.7 %collective-permute-start.2 = (bf16[2048,768]{1,0:T(8,128)(2,1)}, bf16[2048,768]{1,0:T(8,128)(2,1)}, u32[]{:S(2)}, u32[]{:S(2)}) collective-permute-start(bf16[2048,768]{1,0:T(8,128)(2,1)} %bitcast.30), channel_id=1, source_target_pairs={{0,1},{1,0},{2,3},{3,2},{4,5},{5,4},{6,7},{7,6},{8,9},{9,8},{10,11... | collective-permute-start | bytes 9437192 | tf_op jit(solution)/shard_map/ppermute | solution.py:368
  0.7 23.7 %collective-permute-start.3 = (bf16[2048,768]{1,0:T(8,128)(2,1)}, bf16[2048,768]{1,0:T(8,128)(2,1)}, u32[]{:S(2)}, u32[]{:S(2)}) collective-permute-start(bf16[2048,768]{1,0:T(8,128)(2,1)} %bitcast.32), channel_id=1, source_target_pairs={{0,1},{1,0},{2,3},{3,2},{4,5},{5,4},{6,7},{7,6},{8,9},{9,8},{10,11... | collective-permute-start | bytes 9437192 | tf_op jit(solution)/shard_map/ppermute | solution.py:368
  1.2 23.2 %collective-permute-start.4 = (bf16[768,2048]{1,0:T(8,128)(2,1)}, bf16[768,2048]{1,0:T(8,128)(2,1)}, u32[]{:S(2)}, u32[]{:S(2)}) collective-permute-start(bf16[768,2048]{1,0:T(8,128)(2,1)} %bitcast.34), channel_id=1, source_target_pairs={{0,1},{1,0},{2,3},{3,2},{4,5},{5,4},{6,7},{7,6},{8,9},{9,8},{10,11... | collective-permute-start | bytes 9437192 | tf_op jit(solution)/shard_map/ppermute | solution.py:368
  3.7 20.5 %collective-permute-start = (bf16[64,6272]{1,0:T(8,128)(2,1)}, bf16[64,6272]{1,0:T(8,128)(2,1)S(1)}, u32[]{:S(2)}, u32[]{:S(2)}) collective-permute-start(bf16[64,6272]{1,0:T(8,128)(2,1)} %shard_map.122.refs_0_), channel_id=1, source_target_pairs={{0,4},{1,5},{4,8},{5,9},{8,12},{9,13},{12,14},{13,15},{14,10},{15,... | collective-permute-start | bytes 2408456 | tf_op jit(solution)/shard_map/ppermute | solution.py:68
  4.2 20.2 %collective-permute-start.1 = (bf16[64,6272]{1,0:T(8,128)(2,1)}, bf16[64,6272]{1,0:T(8,128)(2,1)S(1)}, u32[]{:S(2)}, u32[]{:S(2)}) collective-permute-start(bf16[64,6272]{1,0:T(8,128)(2,1)} %shard_map.122.refs_0_), channel_id=1, source_target_pairs={{0,2},{1,3},{4,0},{5,1},{8,4},{9,5},{12,8},{13,9},{14,12},{15,13},... | collective-permute-start | bytes 2408456 | tf_op jit(solution)/shard_map/ppermute | solution.py:69
  24.4 19.3 %collective-permute-start.5 = (bf16[64,6272]{1,0:T(8,128)(2,1)S(1)}, bf16[64,6272]{1,0:T(8,128)(2,1)S(1)}, u32[]{:S(2)}, u32[]{:S(2)}) collective-permute-start(bf16[64,6272]{1,0:T(8,128)(2,1)S(1)} %collective-permute-done.refs_1_), channel_id=1, source_target_pairs={{0,4},{1,5},{4,8},{5,9},{8,12},{9,13},{12,14},{13,15},{14,10},{15,... | collective-permute-start | bytes 2408456 | tf_op jit(solution)/shard_map/ppermute | solution.py:68
  24.8 19.2 %collective-permute-start.6 = (bf16[64,6272]{1,0:T(8,128)(2,1)S(1)}, bf16[64,6272]{1,0:T(8,128)(2,1)S(1)}, u32[]{:S(2)}, u32[]{:S(2)}) collective-permute-start(bf16[64,6272]{1,0:T(8,128)(2,1)S(1)} %collective-permute-done.1.refs_2_), channel_id=1, source_target_pairs={{0,2},{1,3},{4,0},{5,1},{8,4},{9,5},{12,8},{13,9},{14,12},{15,13},... | collective-permute-start | bytes 2408456 | tf_op jit(solution)/shard_map/ppermute | solution.py:69
  26.5 6.6 %copy-start = (bf16[64,6272]{1,0:T(8,128)(2,1)S(1)}, bf16[64,6272]{1,0:T(8,128)(2,1)}, u32[]{:S(2)}) copy-start(bf16[64,6272]{1,0:T(8,128)(2,1)} %shard_map.122.refs_0_) | copy-start | bytes 2408452
  44.0 18.2 %collective-permute-start.7 = (bf16[64,6272]{1,0:T(8,128)(2,1)S(1)}, bf16[64,6272]{1,0:T(8,128)(2,1)S(1)}, u32[]{:S(2)}, u32[]{:S(2)}) collective-permute-start(bf16[64,6272]{1,0:T(8,128)(2,1)S(1)} %collective-permute-done.5.refs_0_.refs_3_), channel_id=1, source_target_pairs={{0,4},{1,5},{4,8},{5,9},{8,12},{9,13},{12,14},{13,15},{14,10},{15,... | collective-permute-start | bytes 2408456 | tf_op jit(solution)/shard_map/ppermute | solution.py:68
  45.4 18.0 %collective-permute-start.8 = (bf16[64,6272]{1,0:T(8,128)(2,1)S(1)}, bf16[64,6272]{1,0:T(8,128)(2,1)S(1)}, u32[]{:S(2)}, u32[]{:S(2)}) collective-permute-start(bf16[64,6272]{1,0:T(8,128)(2,1)S(1)} %collective-permute-done.6.refs_1_.refs_0_), channel_id=1, source_target_pairs={{0,2},{1,3},{4,0},{5,1},{8,4},{9,5},{12,8},{13,9},{14,12},{15,13},... | collective-permute-start | bytes 2408456 | tf_op jit(solution)/shard_map/ppermute | solution.py:69
  63.4 6.5 %collective-permute-start.10 = (bf16[32,2176]{1,0:T(8,128)(2,1)S(1)}, bf16[32,2176]{1,0:T(8,128)(2,1)S(1)}, u32[]{:S(2)}, u32[]{:S(2)}) collective-permute-start(bf16[32,2176]{1,0:T(8,128)(2,1)S(1)} %slice.94), channel_id=1, source_target_pairs={{0,2},{1,3},{4,0},{5,1},{8,4},{9,5},{12,8},{13,9},{14,12},{15,13},... | collective-permute-start | bytes 417800 | tf_op jit(solution)/shard_map/ppermute | solution.py:69
  64.1 5.9 %collective-permute-start.9 = (bf16[32,2176]{1,0:T(8,128)(2,1)S(1)}, bf16[32,2176]{1,0:T(8,128)(2,1)S(1)}, u32[]{:S(2)}, u32[]{:S(2)}) collective-permute-start(bf16[32,2176]{1,0:T(8,128)(2,1)S(1)} %slice.93), channel_id=1, source_target_pairs={{0,4},{1,5},{4,8},{5,9},{8,12},{9,13},{12,14},{13,15},{14,10},{15,... | collective-permute-start | bytes 417800 | tf_op jit(solution)/shard_map/ppermute | solution.py:68
  65.6 11.3 %collective-permute-start.13 = (bf16[32,4224]{1,0:T(8,128)(2,1)S(1)}, bf16[32,4224]{1,0:T(8,128)(2,1)S(1)}, u32[]{:S(2)}, u32[]{:S(2)}) collective-permute-start(bf16[32,4224]{1,0:T(8,128)(2,1)S(1)} %slice.98), channel_id=1, source_target_pairs={{0,4},{1,5},{4,8},{5,9},{8,12},{9,13},{12,14},{13,15},{14,10},{15,... | collective-permute-start | bytes 811016 | tf_op jit(solution)/shard_map/ppermute | solution.py:68
  67.2 9.7 %collective-permute-start.14 = (bf16[32,4224]{1,0:T(8,128)(2,1)S(1)}, bf16[32,4224]{1,0:T(8,128)(2,1)S(1)}, u32[]{:S(2)}, u32[]{:S(2)}) collective-permute-start(bf16[32,4224]{1,0:T(8,128)(2,1)S(1)} %slice.99), channel_id=1, source_target_pairs={{0,2},{1,3},{4,0},{5,1},{8,4},{9,5},{12,8},{13,9},{14,12},{15,13},... | collective-permute-start | bytes 811016 | tf_op jit(solution)/shard_map/ppermute | solution.py:69
  74.8 8.0 %collective-permute-start.11 = (bf16[32,2048]{1,0:T(8,128)(2,1)S(1)}, bf16[32,2048]{1,0:T(8,128)(2,1)S(1)}, u32[]{:S(2)}, u32[]{:S(2)}) collective-permute-start(bf16[32,2048]{1,0:T(8,128)(2,1)S(1)} %get-tuple-element.55), channel_id=1, source_target_pairs={{0,2},{1,3},{4,0},{5,1},{8,4},{9,5},{12,8},{13,9},{14,12},{15,13},... | collective-permute-start | bytes 393224 | tf_op jit(solution)/shard_map/ppermute | solution.py:93
  76.0 6.9 %collective-permute-start.12 = (bf16[32,2048]{1,0:T(8,128)(2,1)S(1)}, bf16[32,2048]{1,0:T(8,128)(2,1)S(1)}, u32[]{:S(2)}, u32[]{:S(2)}) collective-permute-start(bf16[32,2048]{1,0:T(8,128)(2,1)S(1)} %get-tuple-element.54), channel_id=1, source_target_pairs={{0,4},{1,5},{4,8},{5,9},{8,12},{9,13},{12,14},{13,15},{14,10},{15,... | collective-permute-start | bytes 393224 | tf_op jit(solution)/shard_map/ppermute | solution.py:94
  86.3 6.4 %collective-permute-start.22 = (bf16[32,2048]{1,0:T(8,128)(2,1)S(1)}, bf16[32,2048]{1,0:T(8,128)(2,1)S(1)}, u32[]{:S(2)}, u32[]{:S(2)}) collective-permute-start(bf16[32,2048]{1,0:T(8,128)(2,1)S(1)} %get-tuple-element.44), channel_id=1, source_target_pairs={{0,2},{1,3},{4,0},{5,1},{8,4},{9,5},{12,8},{13,9},{14,12},{15,13},... | collective-permute-start | bytes 393224 | tf_op jit(solution)/shard_map/ppermute | solution.py:93
  87.6 5.9 %collective-permute-start.26 = (bf16[32,2048]{1,0:T(8,128)(2,1)S(1)}, bf16[32,2048]{1,0:T(8,128)(2,1)S(1)}, u32[]{:S(2)}, u32[]{:S(2)}) collective-permute-start(bf16[32,2048]{1,0:T(8,128)(2,1)S(1)} %get-tuple-element.45), channel_id=1, source_target_pairs={{0,4},{1,5},{4,8},{5,9},{8,12},{9,13},{12,14},{13,15},{14,10},{15,... | collective-permute-start | bytes 393224 | tf_op jit(solution)/shard_map/ppermute | solution.py:94
  88.5 10.6 %collective-permute-start.18 = (bf16[64,2048]{1,0:T(8,128)(2,1)S(1)}, bf16[64,2048]{1,0:T(8,128)(2,1)S(1)}, u32[]{:S(2)}, u32[]{:S(2)}) collective-permute-start(bf16[64,2048]{1,0:T(8,128)(2,1)S(1)} %pad_maximum_fusion.1), channel_id=1, source_target_pairs={{0,4},{1,5},{4,8},{5,9},{8,12},{9,13},{12,14},{13,15},{14,10},{15,... | collective-permute-start | bytes 786440 | tf_op jit(solution)/shard_map/ppermute | solution.py:94
  90.2 9.3 %collective-permute-start.15 = (bf16[64,2048]{1,0:T(8,128)(2,1)S(1)}, bf16[64,2048]{1,0:T(8,128)(2,1)S(1)}, u32[]{:S(2)}, u32[]{:S(2)}) collective-permute-start(bf16[64,2048]{1,0:T(8,128)(2,1)S(1)} %pad_maximum_fusion), channel_id=1, source_target_pairs={{0,2},{1,3},{4,0},{5,1},{8,4},{9,5},{12,8},{13,9},{14,12},{15,13},... | collective-permute-start | bytes 786440 | tf_op jit(solution)/shard_map/ppermute | solution.py:93
  93.6 11.1 %collective-permute-start.27 = (bf16[64,2048]{1,0:T(8,128)(2,1)S(1)}, bf16[64,2048]{1,0:T(8,128)(2,1)S(1)}, u32[]{:S(2)}, u32[]{:S(2)}) collective-permute-start(bf16[64,2048]{1,0:T(8,128)(2,1)S(1)} %pad_maximum_fusion.3), channel_id=1, source_target_pairs={{0,4},{1,5},{4,8},{5,9},{8,12},{9,13},{12,14},{13,15},{14,10},{15,... | collective-permute-start | bytes 786440 | tf_op jit(solution)/shard_map/ppermute | solution.py:94
  94.6 23.9 %copy-start.2 = (bf16[1,64,2048]{2,1,0:T(8,128)(2,1)S(1)}, bf16[1,64,2048]{2,1,0:T(8,128)(2,1)}, u32[]{:S(2)}) copy-start(bf16[1,64,2048]{2,1,0:T(8,128)(2,1)} %param.11) | copy-start | bytes 786436
  94.6 10.7 %collective-permute-start.23 = (bf16[64,2048]{1,0:T(8,128)(2,1)S(1)}, bf16[64,2048]{1,0:T(8,128)(2,1)S(1)}, u32[]{:S(2)}, u32[]{:S(2)}) collective-permute-start(bf16[64,2048]{1,0:T(8,128)(2,1)S(1)} %pad_maximum_fusion.2), channel_id=1, source_target_pairs={{0,2},{1,3},{4,0},{5,1},{8,4},{9,5},{12,8},{13,9},{14,12},{15,13},... | collective-permute-start | bytes 786440 | tf_op jit(solution)/shard_map/ppermute | solution.py:93
  99.6 24.0 %copy-start.1 = (bf16[1,64,2048]{2,1,0:T(8,128)(2,1)S(1)}, bf16[1,64,2048]{2,1,0:T(8,128)(2,1)}, u32[]{:S(2)}) copy-start(bf16[1,64,2048]{2,1,0:T(8,128)(2,1)} %param.14) | copy-start | bytes 786436
  99.6 24.0 %copy-start.4 = (f32[1,2048]{1,0:T(1,128)S(1)}, f32[1,2048]{1,0:T(1,128)}, u32[]{:S(2)}) copy-start(f32[1,2048]{1,0:T(1,128)} %refs_2_.1) | copy-start | bytes 24580
  99.6 11.1 %collective-permute-start.16 = (bf16[64,2048]{1,0:T(8,128)(2,1)S(1)}, bf16[64,2048]{1,0:T(8,128)(2,1)S(1)}, u32[]{:S(2)}, u32[]{:S(2)}) collective-permute-start(bf16[64,2048]{1,0:T(8,128)(2,1)S(1)} %get-tuple-element.56), channel_id=1, source_target_pairs={{0,2},{1,3},{4,0},{5,1},{8,4},{9,5},{12,8},{13,9},{14,12},{15,13},... | collective-permute-start | bytes 786440 | tf_op jit(solution)/shard_map/ppermute | solution.py:93
  100.9 9.8 %collective-permute-start.19 = (bf16[64,2048]{1,0:T(8,128)(2,1)S(1)}, bf16[64,2048]{1,0:T(8,128)(2,1)S(1)}, u32[]{:S(2)}, u32[]{:S(2)}) collective-permute-start(bf16[64,2048]{1,0:T(8,128)(2,1)S(1)} %get-tuple-element.57), channel_id=1, source_target_pairs={{0,4},{1,5},{4,8},{5,9},{8,12},{9,13},{12,14},{13,15},{14,10},{15,... | collective-permute-start | bytes 786440 | tf_op jit(solution)/shard_map/ppermute | solution.py:94
  104.8 19.1 %copy-start.3 = (bf16[1,64,2048]{2,1,0:T(8,128)(2,1)S(1)}, bf16[1,64,2048]{2,1,0:T(8,128)(2,1)}, u32[]{:S(2)}) copy-start(bf16[1,64,2048]{2,1,0:T(8,128)(2,1)} %param.15) | copy-start | bytes 786436
  104.8 10.8 %collective-permute-start.28 = (bf16[64,2048]{1,0:T(8,128)(2,1)S(1)}, bf16[64,2048]{1,0:T(8,128)(2,1)S(1)}, u32[]{:S(2)}, u32[]{:S(2)}) collective-permute-start(bf16[64,2048]{1,0:T(8,128)(2,1)S(1)} %add_convert_fusion.1), channel_id=1, source_target_pairs={{0,4},{1,5},{4,8},{5,9},{8,12},{9,13},{12,14},{13,15},{14,10},{15,... | collective-permute-start | bytes 786440 | tf_op jit(solution)/shard_map/ppermute | solution.py:94
  105.4 10.3 %collective-permute-start.24 = (bf16[64,2048]{1,0:T(8,128)(2,1)S(1)}, bf16[64,2048]{1,0:T(8,128)(2,1)S(1)}, u32[]{:S(2)}, u32[]{:S(2)}) collective-permute-start(bf16[64,2048]{1,0:T(8,128)(2,1)S(1)} %add_convert_fusion.3), channel_id=1, source_target_pairs={{0,2},{1,3},{4,0},{5,1},{8,4},{9,5},{12,8},{13,9},{14,12},{15,13},... | collective-permute-start | bytes 786440 | tf_op jit(solution)/shard_map/ppermute | solution.py:93
  110.8 7.6 %collective-permute-start.17 = (bf16[64,2048]{1,0:T(8,128)(2,1)S(1)}, bf16[64,2048]{1,0:T(8,128)(2,1)S(1)}, u32[]{:S(2)}, u32[]{:S(2)}) collective-permute-start(bf16[64,2048]{1,0:T(8,128)(2,1)S(1)} %get-tuple-element.48), channel_id=1, source_target_pairs={{0,2},{1,3},{4,0},{5,1},{8,4},{9,5},{12,8},{13,9},{14,12},{15,13},... | collective-permute-start | bytes 786440 | tf_op jit(solution)/shard_map/ppermute | solution.py:93
  112.1 6.4 %collective-permute-start.20 = (bf16[64,2048]{1,0:T(8,128)(2,1)S(1)}, bf16[64,2048]{1,0:T(8,128)(2,1)S(1)}, u32[]{:S(2)}, u32[]{:S(2)}) collective-permute-start(bf16[64,2048]{1,0:T(8,128)(2,1)S(1)} %get-tuple-element.49), channel_id=1, source_target_pairs={{0,4},{1,5},{4,8},{5,9},{8,12},{9,13},{12,14},{13,15},{14,10},{15,... | collective-permute-start | bytes 786440 | tf_op jit(solution)/shard_map/ppermute | solution.py:94
  115.8 6.4 %collective-permute-start.25 = (bf16[64,2048]{1,0:T(8,128)(2,1)S(1)}, bf16[64,2048]{1,0:T(8,128)(2,1)S(1)}, u32[]{:S(2)}, u32[]{:S(2)}) collective-permute-start(bf16[64,2048]{1,0:T(8,128)(2,1)S(1)} %get-tuple-element.40), channel_id=1, source_target_pairs={{0,2},{1,3},{4,0},{5,1},{8,4},{9,5},{12,8},{13,9},{14,12},{15,13},... | collective-permute-start | bytes 786440 | tf_op jit(solution)/shard_map/ppermute | solution.py:93
  117.3 6.4 %collective-permute-start.29 = (bf16[64,2048]{1,0:T(8,128)(2,1)S(1)}, bf16[64,2048]{1,0:T(8,128)(2,1)S(1)}, u32[]{:S(2)}, u32[]{:S(2)}) collective-permute-start(bf16[64,2048]{1,0:T(8,128)(2,1)S(1)} %get-tuple-element.41), channel_id=1, source_target_pairs={{0,4},{1,5},{4,8},{5,9},{8,12},{9,13},{12,14},{13,15},{14,10},{15,... | collective-permute-start | bytes 786440 | tf_op jit(solution)/shard_map/ppermute | solution.py:94
  118.6 7.2 %collective-permute-start.21 = (bf16[1,64,2048]{2,1,0:T(8,128)(2,1)S(1)}, bf16[1,64,2048]{2,1,0:T(8,128)(2,1)S(1)}, u32[]{:S(2)}, u32[]{:S(2)}) collective-permute-start(bf16[1,64,2048]{2,1,0:T(8,128)(2,1)S(1)} %fusion.7), channel_id=1, source_target_pairs={{0,16},{16,0},{1,17},{17,1},{2,18},{18,2},{3,19},{19,3},{4,20},{20... | collective-permute-start | bytes 786440 | tf_op jit(solution)/shard_map/ppermute | solution.py:43
  124.2 6.4 %collective-permute-start.30 = (bf16[1,64,2048]{2,1,0:T(8,128)(2,1)S(1)}, bf16[1,64,2048]{2,1,0:T(8,128)(2,1)S(1)}, u32[]{:S(2)}, u32[]{:S(2)}) collective-permute-start(bf16[1,64,2048]{2,1,0:T(8,128)(2,1)S(1)} %fusion.8), channel_id=1, source_target_pairs={{0,16},{16,0},{1,17},{17,1},{2,18},{18,2},{3,19},{19,3},{4,20},{20... | collective-permute-start | bytes 786440 | tf_op jit(solution)/shard_map/ppermute | solution.py:43

commit v5 on v4

--- a/solution.py
+++ b/solution.py
@@ -14,6 +14,7 @@
 ROWS_AT_ONCE = 256
 MIB = 1 << 20
 COST = 1
+IN_TURN = 2
 PAUSE = 10**11
 IN_HBM = pl.BlockSpec(memory_space=pl.ANY)
 IN_VMEM = pl.BlockSpec(memory_space=pltpu.VMEM)
@@ -122,10 +123,17 @@
         pltpu.make_async_copy(source, place, arrived.at[i])
         for i, (source, place) in enumerate(zip(sources, places))
     ]
-    for copy in copies:
-        copy.start()
-    for copy in copies:
-        copy.wait()
+    first_core = lax.rem(lax.axis_index("expert"), CORES) == 0
+    for at_once, core in ((len(copies), jnp.logical_not(first_core)), (IN_TURN, first_core)):
+
+        @pl.when(core)
+        def _():
+            for first in range(0, len(copies), at_once):
+                for copy in copies[first : first + at_once]:
+                    copy.start()
+                for copy in copies[first : first + at_once]:
+                    copy.wait()
+
     rows, gain, routing = held[:2], held[2], (held[3:5], held[5:7])
     out[:, :width] = normalize(rows[0][...], gain[...])
     out[:, first : first + width] = normalize(rows[1][...], gain[...])
@@ -331,6 +339,24 @@
             parts.append(out[first : first + block.shape[0]])
             first += block.shape[0]
     return parts
+
+
+def copied_body(array, copy, done):
+    step = pltpu.make_async_copy(array, copy, done)
+    step.start()
+    step.wait()
+
+
+def copied(array):
+    return pl.pallas_call(
+        copied_body,
+        in_specs=[IN_HBM],
+        out_specs=IN_HBM,
+        out_shape=jax.ShapeDtypeStruct(array.shape, array.dtype),
+        scratch_shapes=[pltpu.SemaphoreType.DMA],
+        compiler_params=pltpu.CompilerParams(vmem_limit_bytes=MIB),
+        cost_estimate=pl.CostEstimate(flops=PAUSE, bytes_accessed=1, transcendentals=0),
+    )(array)
 
 
 def per_device(
@@ -421,7 +447,7 @@
     mixed_out = forward_tokens[0].astype(jnp.float32) + fwd_sum.total()
     section_input = passed_along(mixed_out.astype(jnp.bfloat16)[None], "section", 1)
     section_gradient = passed_along(token_grad.astype(jnp.bfloat16)[None], "section", -1)
-    return (section_input, section_gradient)
+    return (copied(section_input), section_gradient)
 
 
 def solution(mesh):

time: 135 us -> 130 us (0.963)
  waiting for transfers between devices: 57 us -> 50.4 us
  Pallas kernels: 40.2 us -> 43.1 us
    ppermute x8, starting transfers between devices: 9.61 us -> 13.4 us  [step(): behind = lax.ppermute(behind, 'expert', ring_route(devices, -1))]
    ppermute x8, starting transfers between devices: 7.17 us -> 3.39 us  [step(): ahead = lax.ppermute(ahead, 'expert', ring_route(devices, 1))]
    ppermute x8, waiting for transfers between devices: 8.87 us -> 5.41 us  [step(): behind = lax.ppermute(behind, 'expert', ring_route(devices, -1))]
    ppermute x5, waiting for transfers between devices: 28.2 us -> 24.8 us  [moved(): behind = lax.ppermute(behind, 'expert', ring_route(devices, 1))]
    pallas_call x1, Pallas kernels: 2.4 us -> 4.61 us  [payload(): pl.pallas_call(functools.partial(payload_body, devices), in_specs=[IN_HBM...]
    ppermute x8, waiting for transfers between devices: 11.2 us -> 13.3 us  [step(): ahead = lax.ppermute(ahead, 'expert', ring_route(devices, 1))]
  transfers between devices with their start and end apart: 31 -> 31, of which waited for: 19 -> 19; matrix products, arithmetic and copies ran while one was open for 1% -> 1% of each run, Pallas kernels for 28% -> 31%
where the time goes in v5:
time: 130 us; the launch traced here: 128 us
  waiting for transfers between devices  50.4 us (39%)
  Pallas kernels  43.1 us (33%)
  starting transfers between devices  30.9 us (24%)
  other arithmetic  1.52 us (1%)
    ppermute x5, waiting for transfers between devices, moved(): behind = lax.ppermute(behind, 'expert', ring_route(devices, 1))  24.8 us
    ppermute x8, starting transfers between devices, step(): behind = lax.ppermute(behind, 'expert', ring_route(devices, -1))  13.4 us
    ppermute x8, waiting for transfers between devices, step(): ahead = lax.ppermute(ahead, 'expert', ring_route(devices, 1))  13.3 us
    pallas_call x3, Pallas kernels, experts_forward(): pl.pallas_call(functools.partial(forward_body, len(blocks), devices), in_...  12.5 us
    pallas_call x2, Pallas kernels, hidden_grads(): pl.pallas_call(functools.partial(grads_body, len(blocks), devices), in_sp...  11.8 us
    pallas_call x2, Pallas kernels, token_grads(): pl.pallas_call(token_grads_body, in_specs=[IN_VMEM, IN_VMEM], out_specs=I...  6.87 us
    pallas_call x1, Pallas kernels, weights_in_vmem(): pl.pallas_call(weights_body, in_specs=[IN_HBM] * 6, out_specs=(IN_VMEM, I...  6.55 us
    ppermute x5, starting transfers between devices, moved(): ahead = lax.ppermute(ahead, 'expert', ring_route(devices, -1))  6.09 us
  transfers between devices with their start and end apart: 31, of which 19 were waited for; matrix products, arithmetic and copies ran while one was open for 1% of the time, Pallas kernels for 31%

profile of v5, /device:TPU:12, one launch (start us, length us, event | category | flops | bytes accessed | tf_op | source)
XLA Modules:
  0.0 127.7 jit_solution(8460120143595780277)
XLA Ops:
  1.3 4.6 %shard_map.122.refs_0_ = bf16[64,6272]{1,0:T(8,128)(2,1)} custom-call(bf16[64,2048]{1,0:T(8,128)(2,1)} %bitcast.37, bf16[64,2048]{1,0:T(8,128)(2,1)} %bitcast.36, f32[1,2048]{1,0:T(1,128)} %refs_2_.1, s32[8,64]{1,0:T(8,128)} %bitcast.41, f32[8,64]{1,0:T(8,128)} %bitcast.42, s32[8,64]{1,0:T(8,128)} %bitcast.43, f32[8,64]{1,0:T(8,128)} %bitcast.44, ...), custom_call_target="tpu_custom_call" | custom-call | flops 1 | bytes 1 | tf_op jit(solution)/shard_map/pallas_call | solution.py:157
  5.9 0.5 collective-permute-start
  6.4 1.6 %collective-permute-start.1 = (bf16[64,6272]{1,0:T(8,128)(2,1)}, bf16[64,6272]{1,0:T(8,128)(2,1)S(1)}, u32[]{:S(2)}, u32[]{:S(2)}) collective-permute-start(bf16[64,6272]{1,0:T(8,128)(2,1)} %shard_map.122.refs_0_), channel_id=1, source_target_pairs={{0,2},{1,3},{4,0},{5,1},{8,4},{9,5},{12,8},{13,9},{14,12},{15,13},... | collective-permute-start | bytes 2408456 | tf_op jit(solution)/shard_map/ppermute | solution.py:70
  8.0 16.2 %collective-permute-done.refs_1_ = bf16[64,6272]{1,0:T(8,128)(2,1)S(1)} collective-permute-done((bf16[64,6272]{1,0:T(8,128)(2,1)}, bf16[64,6272]{1,0:T(8,128)(2,1)S(1)}, u32[]{:S(2)}, u32[]{:S(2)}) %collective-permute-start) | collective-permute-done | bytes 802848 | tf_op jit(solution)/shard_map/ppermute | solution.py:69
  24.8 1.7 %collective-permute-start.6 = (bf16[64,6272]{1,0:T(8,128)(2,1)S(1)}, bf16[64,6272]{1,0:T(8,128)(2,1)S(1)}, u32[]{:S(2)}, u32[]{:S(2)}) collective-permute-start(bf16[64,6272]{1,0:T(8,128)(2,1)S(1)} %collective-permute-done.1.refs_2_), channel_id=1, source_target_pairs={{0,2},{1,3},{4,0},{5,1},{8,4},{9,5},{12,8},{13,9},{14,12},{15,13},... | collective-permute-start | bytes 2408456 | tf_op jit(solution)/shard_map/ppermute | solution.py:70
  26.5 6.6 %shard_map.123 = (bf16[2048,3072]{1,0:T(8,128)(2,1)S(1)}, bf16[1536,2048]{1,0:T(8,128)(2,1)S(1)}) custom-call(bf16[2048,768]{1,0:T(8,128)(2,1)} %bitcast.31, bf16[2048,768]{1,0:T(8,128)(2,1)} %bitcast.33, bf16[768,2048]{1,0:T(8,128)(2,1)} %bitcast.35, bf16[2048,768]{1,0:T(8,128)(2,1)} %collective-permute-done.2.refs_3_, ...), custom_call_target="tpu_custom_call" | custom-call | tf_op jit(solution)/shard_map/pallas_call | solution.py:197
  33.1 4.5 %shard_map.124 = bf16[192,2048]{1,0:T(8,128)(2,1)S(1)} custom-call(bf16[64,6272]{1,0:T(8,128)(2,1)S(1)} %copy-done, bf16[64,6272]{1,0:T(8,128)(2,1)S(1)} %collective-permute-done.refs_1_, bf16[64,6272]{1,0:T(8,128)(2,1)S(1)} %collective-permute-done.1.refs_2_, s32[2]{0:T(128)S(1)} %pad_add_fusion.refs_3_.refs_2_.refs_4_.refs_5_, ...), custom_call_target="tpu_custom_call" | custom-call | flops 1 | bytes 1 | tf_op jit(solution)/shard_map/pallas_call | solution.py:308
  37.6 4.8 %collective-permute-done.5.refs_0_.refs_3_ = bf16[64,6272]{1,0:T(8,128)(2,1)S(1)} collective-permute-done((bf16[64,6272]{1,0:T(8,128)(2,1)S(1)}, bf16[64,6272]{1,0:T(8,128)(2,1)S(1)}, u32[]{:S(2)}, u32[]{:S(2)}) %collective-permute-start.5) | collective-permute-done | bytes 802848 | tf_op jit(solution)/shard_map/ppermute | solution.py:69
  42.4 0.8 collective-permute-start.7
  43.3 1.2 collective-permute-start.8
  44.4 5.9 %shard_map.126.grads = bf16[256,3072]{1,0:T(8,128)(2,1)S(1)} custom-call(bf16[64,6272]{1,0:T(8,128)(2,1)S(1)} %copy-done, bf16[64,6272]{1,0:T(8,128)(2,1)S(1)} %collective-permute-done.refs_1_, bf16[64,6272]{1,0:T(8,128)(2,1)S(1)} %collective-permute-done.1.refs_2_, bf16[64,6272]{1,0:T(8,128)(2,1)S(1)} %collective-permute-done.5.refs_0_.refs_3_, ...), custom_call_target="tpu_custom_call" | custom-call | flops 1 | bytes 1 | tf_op jit(solution)/shard_map/pallas_call | solution.py:255
  50.4 3.4 %shard_map.127 = bf16[256,2048]{1,0:T(8,128)(2,1)S(1)} custom-call(bf16[256,3072]{1,0:T(8,128)(2,1)S(1)} %shard_map.126.grads, bf16[2048,3072]{1,0:T(8,128)(2,1)S(1)} %get-tuple-element.25.refs_4_.refs_3_.refs_5_.gate_up.refs_6_), custom_call_target="tpu_custom_call" | custom-call | flops 1 | bytes 1 | tf_op jit(solution)/shard_map/pallas_call | solution.py:276
  53.8 3.2 %shard_map.125 = bf16[128,2048]{1,0:T(8,128)(2,1)S(1)} custom-call(bf16[64,6272]{1,0:T(8,128)(2,1)S(1)} %collective-permute-done.5.refs_0_.refs_3_, bf16[64,6272]{1,0:T(8,128)(2,1)S(1)} %collective-permute-done.6.refs_1_.refs_0_, s32[2]{0:T(128)S(1)} %pad_add_fusion.refs_3_.refs_2_.refs_4_.refs_5_, ...), custom_call_target="tpu_custom_call" | custom-call | flops 1 | bytes 1 | tf_op jit(solution)/shard_map/pallas_call | solution.py:308
  57.0 2.1 %collective-permute-done.7.refs_0_.refs_1_ = bf16[64,6272]{1,0:T(8,128)(2,1)S(1)} collective-permute-done((bf16[64,6272]{1,0:T(8,128)(2,1)S(1)}, bf16[64,6272]{1,0:T(8,128)(2,1)S(1)}, u32[]{:S(2)}, u32[]{:S(2)}) %collective-permute-start.7) | collective-permute-done | bytes 802848 | tf_op jit(solution)/shard_map/ppermute | solution.py:69
  59.2 1.7 %collective-permute-done.8.refs_1_.refs_2_ = bf16[64,6272]{1,0:T(8,128)(2,1)S(1)} collective-permute-done((bf16[64,6272]{1,0:T(8,128)(2,1)S(1)}, bf16[64,6272]{1,0:T(8,128)(2,1)S(1)}, u32[]{:S(2)}, u32[]{:S(2)}) %collective-permute-start.8) | collective-permute-done | bytes 802848 | tf_op jit(solution)/shard_map/ppermute | solution.py:70
  60.9 1.6 %collective-permute-start.10 = (bf16[32,2176]{1,0:T(8,128)(2,1)S(1)}, bf16[32,2176]{1,0:T(8,128)(2,1)S(1)}, u32[]{:S(2)}, u32[]{:S(2)}) collective-permute-start(bf16[32,2176]{1,0:T(8,128)(2,1)S(1)} %slice.94), channel_id=1, source_target_pairs={{0,2},{1,3},{4,0},{5,1},{8,4},{9,5},{12,8},{13,9},{14,12},{15,13},... | collective-permute-start | bytes 417800 | tf_op jit(solution)/shard_map/ppermute | solution.py:70
  63.1 2.0 %collective-permute-start.13 = (bf16[32,4224]{1,0:T(8,128)(2,1)S(1)}, bf16[32,4224]{1,0:T(8,128)(2,1)S(1)}, u32[]{:S(2)}, u32[]{:S(2)}) collective-permute-start(bf16[32,4224]{1,0:T(8,128)(2,1)S(1)} %slice.98), channel_id=1, source_target_pairs={{0,4},{1,5},{4,8},{5,9},{8,12},{9,13},{12,14},{13,15},{14,10},{15,... | collective-permute-start | bytes 811016 | tf_op jit(solution)/shard_map/ppermute | solution.py:69
  65.1 0.8 collective-permute-done.10.refs_3_
  66.0 1.7 %collective-permute-done.9.refs_2_ = bf16[32,2176]{1,0:T(8,128)(2,1)S(1)} collective-permute-done((bf16[32,2176]{1,0:T(8,128)(2,1)S(1)}, bf16[32,2176]{1,0:T(8,128)(2,1)S(1)}, u32[]{:S(2)}, u32[]{:S(2)}) %collective-permute-start.9) | collective-permute-done | bytes 139296 | tf_op jit(solution)/shard_map/ppermute | solution.py:69
  67.6 4.8 %shard_map.128 = bf16[192,2048]{1,0:T(8,128)(2,1)S(1)} custom-call(bf16[64,6272]{1,0:T(8,128)(2,1)S(1)} %collective-permute-done.7.refs_0_.refs_1_, bf16[64,6272]{1,0:T(8,128)(2,1)S(1)} %collective-permute-done.8.refs_1_.refs_2_, bf16[32,2176]{1,0:T(8,128)(2,1)S(1)} %collective-permute-done.9.refs_2_, bf16[32,2176]{1,0:T(8,128)(2,1)S(1)} %collective-permute-done.10.refs_3_, ...), custom_call_target="tpu_custom_call" | custom-call | flops 1 | bytes 1 | tf_op jit(solution)/shard_map/pallas_call | solution.py:308
  72.5 1.8 %collective-permute-start.11 = (bf16[32,2048]{1,0:T(8,128)(2,1)S(1)}, bf16[32,2048]{1,0:T(8,128)(2,1)S(1)}, u32[]{:S(2)}, u32[]{:S(2)}) collective-permute-start(bf16[32,2048]{1,0:T(8,128)(2,1)S(1)} %get-tuple-element.55), channel_id=1, source_target_pairs={{0,2},{1,3},{4,0},{5,1},{8,4},{9,5},{12,8},{13,9},{14,12},{15,13},... | collective-permute-start | bytes 393224 | tf_op jit(solution)/shard_map/ppermute | solution.py:94
  74.6 5.9 %shard_map.129.grads = bf16[256,3072]{1,0:T(8,128)(2,1)S(1)} custom-call(bf16[64,6272]{1,0:T(8,128)(2,1)S(1)} %collective-permute-done.6.refs_1_.refs_0_, bf16[64,6272]{1,0:T(8,128)(2,1)S(1)} %collective-permute-done.7.refs_0_.refs_1_, bf16[64,6272]{1,0:T(8,128)(2,1)S(1)} %collective-permute-done.8.refs_1_.refs_2_, ...), custom_call_target="tpu_custom_call" | custom-call | flops 1 | bytes 1 | tf_op jit(solution)/shard_map/pallas_call | solution.py:255
  80.5 3.4 %shard_map.131 = bf16[256,2048]{1,0:T(8,128)(2,1)S(1)} custom-call(bf16[256,3072]{1,0:T(8,128)(2,1)S(1)} %shard_map.129.grads, bf16[2048,3072]{1,0:T(8,128)(2,1)S(1)} %get-tuple-element.25.refs_4_.refs_3_.refs_5_.gate_up.refs_6_), custom_call_target="tpu_custom_call" | custom-call | flops 99999997952 | bytes 1 | tf_op jit(solution)/shard_map/pallas_call | solution.py:276
  84.0 1.8 %collective-permute-start.22 = (bf16[32,2048]{1,0:T(8,128)(2,1)S(1)}, bf16[32,2048]{1,0:T(8,128)(2,1)S(1)}, u32[]{:S(2)}, u32[]{:S(2)}) collective-permute-start(bf16[32,2048]{1,0:T(8,128)(2,1)S(1)} %get-tuple-element.44), channel_id=1, source_target_pairs={{0,2},{1,3},{4,0},{5,1},{8,4},{9,5},{12,8},{13,9},{14,12},{15,13},... | collective-permute-start | bytes 393224 | tf_op jit(solution)/shard_map/ppermute | solution.py:94
  86.2 0.7 collective-permute-start.18
  86.9 1.5 %collective-permute-start.15 = (bf16[64,2048]{1,0:T(8,128)(2,1)S(1)}, bf16[64,2048]{1,0:T(8,128)(2,1)S(1)}, u32[]{:S(2)}, u32[]{:S(2)}) collective-permute-start(bf16[64,2048]{1,0:T(8,128)(2,1)S(1)} %pad_maximum_fusion), channel_id=1, source_target_pairs={{0,2},{1,3},{4,0},{5,1},{8,4},{9,5},{12,8},{13,9},{14,12},{15,13},... | collective-permute-start | bytes 786440 | tf_op jit(solution)/shard_map/ppermute | solution.py:94
  88.4 2.2 %collective-permute-done.22 = bf16[32,2048]{1,0:T(8,128)(2,1)S(1)} collective-permute-done((bf16[32,2048]{1,0:T(8,128)(2,1)S(1)}, bf16[32,2048]{1,0:T(8,128)(2,1)S(1)}, u32[]{:S(2)}, u32[]{:S(2)}) %collective-permute-start.22) | collective-permute-done | bytes 131104 | tf_op jit(solution)/shard_map/ppermute | solution.py:94
  90.5 1.7 %collective-permute-done.26 = bf16[32,2048]{1,0:T(8,128)(2,1)S(1)} collective-permute-done((bf16[32,2048]{1,0:T(8,128)(2,1)S(1)}, bf16[32,2048]{1,0:T(8,128)(2,1)S(1)}, u32[]{:S(2)}, u32[]{:S(2)}) %collective-permute-start.26) | collective-permute-done | bytes 131104 | tf_op jit(solution)/shard_map/ppermute | solution.py:95
  92.7 1.8 %collective-permute-start.23 = (bf16[64,2048]{1,0:T(8,128)(2,1)S(1)}, bf16[64,2048]{1,0:T(8,128)(2,1)S(1)}, u32[]{:S(2)}, u32[]{:S(2)}) collective-permute-start(bf16[64,2048]{1,0:T(8,128)(2,1)S(1)} %pad_maximum_fusion.2), channel_id=1, source_target_pairs={{0,2},{1,3},{4,0},{5,1},{8,4},{9,5},{12,8},{13,9},{14,12},{15,13},... | collective-permute-start | bytes 786440 | tf_op jit(solution)/shard_map/ppermute | solution.py:94
  94.4 3.4 %collective-permute-done.18 = bf16[64,2048]{1,0:T(8,128)(2,1)S(1)} collective-permute-done((bf16[64,2048]{1,0:T(8,128)(2,1)S(1)}, bf16[64,2048]{1,0:T(8,128)(2,1)S(1)}, u32[]{:S(2)}, u32[]{:S(2)}) %collective-permute-start.18) | collective-permute-done | bytes 262176 | tf_op jit(solution)/shard_map/ppermute | solution.py:95
  98.0 1.8 %collective-permute-start.16 = (bf16[64,2048]{1,0:T(8,128)(2,1)S(1)}, bf16[64,2048]{1,0:T(8,128)(2,1)S(1)}, u32[]{:S(2)}, u32[]{:S(2)}) collective-permute-start(bf16[64,2048]{1,0:T(8,128)(2,1)S(1)} %get-tuple-element.56), channel_id=1, source_target_pairs={{0,2},{1,3},{4,0},{5,1},{8,4},{9,5},{12,8},{13,9},{14,12},{15,13},... | collective-permute-start | bytes 786440 | tf_op jit(solution)/shard_map/ppermute | solution.py:94
  100.0 3.4 %collective-permute-done.27 = bf16[64,2048]{1,0:T(8,128)(2,1)S(1)} collective-permute-done((bf16[64,2048]{1,0:T(8,128)(2,1)S(1)}, bf16[64,2048]{1,0:T(8,128)(2,1)S(1)}, u32[]{:S(2)}, u32[]{:S(2)}) %collective-permute-start.27) | collective-permute-done | bytes 262176 | tf_op jit(solution)/shard_map/ppermute | solution.py:95
  103.9 1.8 %collective-permute-start.24 = (bf16[64,2048]{1,0:T(8,128)(2,1)S(1)}, bf16[64,2048]{1,0:T(8,128)(2,1)S(1)}, u32[]{:S(2)}, u32[]{:S(2)}) collective-permute-start(bf16[64,2048]{1,0:T(8,128)(2,1)S(1)} %add_convert_fusion.3), channel_id=1, source_target_pairs={{0,2},{1,3},{4,0},{5,1},{8,4},{9,5},{12,8},{13,9},{14,12},{15,13},... | collective-permute-start | bytes 786440 | tf_op jit(solution)/shard_map/ppermute | solution.py:94
  105.7 1.9 %collective-permute-done.16 = bf16[64,2048]{1,0:T(8,128)(2,1)S(1)} collective-permute-done((bf16[64,2048]{1,0:T(8,128)(2,1)S(1)}, bf16[64,2048]{1,0:T(8,128)(2,1)S(1)}, u32[]{:S(2)}, u32[]{:S(2)}) %collective-permute-start.16) | collective-permute-done | bytes 262176 | tf_op jit(solution)/shard_map/ppermute | solution.py:94
  107.6 1.5 %collective-permute-done.19 = bf16[64,2048]{1,0:T(8,128)(2,1)S(1)} collective-permute-done((bf16[64,2048]{1,0:T(8,128)(2,1)S(1)}, bf16[64,2048]{1,0:T(8,128)(2,1)S(1)}, u32[]{:S(2)}, u32[]{:S(2)}) %collective-permute-start.19) | collective-permute-done | bytes 262176 | tf_op jit(solution)/shard_map/ppermute | solution.py:95
  109.2 1.6 %collective-permute-start.17 = (bf16[64,2048]{1,0:T(8,128)(2,1)S(1)}, bf16[64,2048]{1,0:T(8,128)(2,1)S(1)}, u32[]{:S(2)}, u32[]{:S(2)}) collective-permute-start(bf16[64,2048]{1,0:T(8,128)(2,1)S(1)} %get-tuple-element.48), channel_id=1, source_target_pairs={{0,2},{1,3},{4,0},{5,1},{8,4},{9,5},{12,8},{13,9},{14,12},{15,13},... | collective-permute-start | bytes 786440 | tf_op jit(solution)/shard_map/ppermute | solution.py:94
  111.2 0.8 collective-permute-done.28
  112.2 1.5 %collective-permute-start.25 = (bf16[64,2048]{1,0:T(8,128)(2,1)S(1)}, bf16[64,2048]{1,0:T(8,128)(2,1)S(1)}, u32[]{:S(2)}, u32[]{:S(2)}) collective-permute-start(bf16[64,2048]{1,0:T(8,128)(2,1)S(1)} %get-tuple-element.40), channel_id=1, source_target_pairs={{0,2},{1,3},{4,0},{5,1},{8,4},{9,5},{12,8},{13,9},{14,12},{15,13},... | collective-permute-start | bytes 786440 | tf_op jit(solution)/shard_map/ppermute | solution.py:94
  113.6 0.6 collective-permute-start.29
  114.2 1.4 %collective-permute-done.17 = bf16[64,2048]{1,0:T(8,128)(2,1)S(1)} collective-permute-done((bf16[64,2048]{1,0:T(8,128)(2,1)S(1)}, bf16[64,2048]{1,0:T(8,128)(2,1)S(1)}, u32[]{:S(2)}, u32[]{:S(2)}) %collective-permute-start.17) | collective-permute-done | bytes 262176 | tf_op jit(solution)/shard_map/ppermute | solution.py:94
  115.6 1.6 %collective-permute-done.20 = bf16[64,2048]{1,0:T(8,128)(2,1)S(1)} collective-permute-done((bf16[64,2048]{1,0:T(8,128)(2,1)S(1)}, bf16[64,2048]{1,0:T(8,128)(2,1)S(1)}, u32[]{:S(2)}, u32[]{:S(2)}) %collective-permute-start.20) | collective-permute-done | bytes 262176 | tf_op jit(solution)/shard_map/ppermute | solution.py:95
  117.3 1.6 %collective-permute-start.21 = (bf16[1,64,2048]{2,1,0:T(8,128)(2,1)S(1)}, bf16[1,64,2048]{2,1,0:T(8,128)(2,1)S(1)}, u32[]{:S(2)}, u32[]{:S(2)}) collective-permute-start(bf16[1,64,2048]{2,1,0:T(8,128)(2,1)S(1)} %fusion.7), channel_id=1, source_target_pairs={{0,16},{16,0},{1,17},{17,1},{2,18},{18,2},{3,19},{19,3},{4,20},{20... | collective-permute-start | bytes 786440 | tf_op jit(solution)/shard_map/ppermute | solution.py:44
  118.9 1.1 collective-permute-done.29
  120.6 1.6 %collective-permute-start.30 = (bf16[1,64,2048]{2,1,0:T(8,128)(2,1)S(1)}, bf16[1,64,2048]{2,1,0:T(8,128)(2,1)S(1)}, u32[]{:S(2)}, u32[]{:S(2)}) collective-permute-start(bf16[1,64,2048]{2,1,0:T(8,128)(2,1)S(1)} %fusion.8), channel_id=1, source_target_pairs={{0,16},{16,0},{1,17},{17,1},{2,18},{18,2},{3,19},{19,3},{4,20},{20... | collective-permute-start | bytes 786440 | tf_op jit(solution)/shard_map/ppermute | solution.py:44
  122.2 1.6 %collective-permute-done.21.array = bf16[1,64,2048]{2,1,0:T(8,128)(2,1)S(1)} collective-permute-done((bf16[1,64,2048]{2,1,0:T(8,128)(2,1)S(1)}, bf16[1,64,2048]{2,1,0:T(8,128)(2,1)S(1)}, u32[]{:S(2)}, u32[]{:S(2)}) %collective-permute-start.21) | collective-permute-done | bytes 262176 | tf_op jit(solution)/shard_map/ppermute | solution.py:44
  123.8 0.7 shard_map.130
  124.5 2.6 %collective-permute-done.30 = bf16[1,64,2048]{2,1,0:T(8,128)(2,1)S(1)} collective-permute-done((bf16[1,64,2048]{2,1,0:T(8,128)(2,1)S(1)}, bf16[1,64,2048]{2,1,0:T(8,128)(2,1)S(1)}, u32[]{:S(2)}, u32[]{:S(2)}) %collective-permute-start.30) | collective-permute-done | bytes 262176 | tf_op jit(solution)/shard_map/ppermute | solution.py:44
  127.0 0.7 copy.14
  (57 shorter events, 5.6 us)
Async XLA Ops:
  0.6 23.7 %collective-permute-start.2 = (bf16[2048,768]{1,0:T(8,128)(2,1)}, bf16[2048,768]{1,0:T(8,128)(2,1)}, u32[]{:S(2)}, u32[]{:S(2)}) collective-permute-start(bf16[2048,768]{1,0:T(8,128)(2,1)} %bitcast.30), channel_id=1, source_target_pairs={{0,1},{1,0},{2,3},{3,2},{4,5},{5,4},{6,7},{7,6},{8,9},{9,8},{10,11... | collective-permute-start | bytes 9437192 | tf_op jit(solution)/shard_map/ppermute | solution.py:394
  0.7 23.6 %collective-permute-start.3 = (bf16[2048,768]{1,0:T(8,128)(2,1)}, bf16[2048,768]{1,0:T(8,128)(2,1)}, u32[]{:S(2)}, u32[]{:S(2)}) collective-permute-start(bf16[2048,768]{1,0:T(8,128)(2,1)} %bitcast.32), channel_id=1, source_target_pairs={{0,1},{1,0},{2,3},{3,2},{4,5},{5,4},{6,7},{7,6},{8,9},{9,8},{10,11... | collective-permute-start | bytes 9437192 | tf_op jit(solution)/shard_map/ppermute | solution.py:394
  1.2 23.2 %collective-permute-start.4 = (bf16[768,2048]{1,0:T(8,128)(2,1)}, bf16[768,2048]{1,0:T(8,128)(2,1)}, u32[]{:S(2)}, u32[]{:S(2)}) collective-permute-start(bf16[768,2048]{1,0:T(8,128)(2,1)} %bitcast.34), channel_id=1, source_target_pairs={{0,1},{1,0},{2,3},{3,2},{4,5},{5,4},{6,7},{7,6},{8,9},{9,8},{10,11... | collective-permute-start | bytes 9437192 | tf_op jit(solution)/shard_map/ppermute | solution.py:394
  5.9 18.3 %collective-permute-start = (bf16[64,6272]{1,0:T(8,128)(2,1)}, bf16[64,6272]{1,0:T(8,128)(2,1)S(1)}, u32[]{:S(2)}, u32[]{:S(2)}) collective-permute-start(bf16[64,6272]{1,0:T(8,128)(2,1)} %shard_map.122.refs_0_), channel_id=1, source_target_pairs={{0,4},{1,5},{4,8},{5,9},{8,12},{9,13},{12,14},{13,15},{14,10},{15,... | collective-permute-start | bytes 2408456 | tf_op jit(solution)/shard_map/ppermute | solution.py:69
  6.4 17.9 %collective-permute-start.1 = (bf16[64,6272]{1,0:T(8,128)(2,1)}, bf16[64,6272]{1,0:T(8,128)(2,1)S(1)}, u32[]{:S(2)}, u32[]{:S(2)}) collective-permute-start(bf16[64,6272]{1,0:T(8,128)(2,1)} %shard_map.122.refs_0_), channel_id=1, source_target_pairs={{0,2},{1,3},{4,0},{5,1},{8,4},{9,5},{12,8},{13,9},{14,12},{15,13},... | collective-permute-start | bytes 2408456 | tf_op jit(solution)/shard_map/ppermute | solution.py:70
  24.4 18.0 %collective-permute-start.5 = (bf16[64,6272]{1,0:T(8,128)(2,1)S(1)}, bf16[64,6272]{1,0:T(8,128)(2,1)S(1)}, u32[]{:S(2)}, u32[]{:S(2)}) collective-permute-start(bf16[64,6272]{1,0:T(8,128)(2,1)S(1)} %collective-permute-done.refs_1_), channel_id=1, source_target_pairs={{0,4},{1,5},{4,8},{5,9},{8,12},{9,13},{12,14},{13,15},{14,10},{15,... | collective-permute-start | bytes 2408456 | tf_op jit(solution)/shard_map/ppermute | solution.py:69
  24.8 17.6 %collective-permute-start.6 = (bf16[64,6272]{1,0:T(8,128)(2,1)S(1)}, bf16[64,6272]{1,0:T(8,128)(2,1)S(1)}, u32[]{:S(2)}, u32[]{:S(2)}) collective-permute-start(bf16[64,6272]{1,0:T(8,128)(2,1)S(1)} %collective-permute-done.1.refs_2_), channel_id=1, source_target_pairs={{0,2},{1,3},{4,0},{5,1},{8,4},{9,5},{12,8},{13,9},{14,12},{15,13},... | collective-permute-start | bytes 2408456 | tf_op jit(solution)/shard_map/ppermute | solution.py:70
  26.5 6.6 %copy-start = (bf16[64,6272]{1,0:T(8,128)(2,1)S(1)}, bf16[64,6272]{1,0:T(8,128)(2,1)}, u32[]{:S(2)}) copy-start(bf16[64,6272]{1,0:T(8,128)(2,1)} %shard_map.122.refs_0_) | copy-start | bytes 2408452
  42.4 16.7 %collective-permute-start.7 = (bf16[64,6272]{1,0:T(8,128)(2,1)S(1)}, bf16[64,6272]{1,0:T(8,128)(2,1)S(1)}, u32[]{:S(2)}, u32[]{:S(2)}) collective-permute-start(bf16[64,6272]{1,0:T(8,128)(2,1)S(1)} %collective-permute-done.5.refs_0_.refs_3_), channel_id=1, source_target_pairs={{0,4},{1,5},{4,8},{5,9},{8,12},{9,13},{12,14},{13,15},{14,10},{15,... | collective-permute-start | bytes 2408456 | tf_op jit(solution)/shard_map/ppermute | solution.py:69
  43.3 17.6 %collective-permute-start.8 = (bf16[64,6272]{1,0:T(8,128)(2,1)S(1)}, bf16[64,6272]{1,0:T(8,128)(2,1)S(1)}, u32[]{:S(2)}, u32[]{:S(2)}) collective-permute-start(bf16[64,6272]{1,0:T(8,128)(2,1)S(1)} %collective-permute-done.6.refs_1_.refs_0_), channel_id=1, source_target_pairs={{0,2},{1,3},{4,0},{5,1},{8,4},{9,5},{12,8},{13,9},{14,12},{15,13},... | collective-permute-start | bytes 2408456 | tf_op jit(solution)/shard_map/ppermute | solution.py:70
  60.9 5.1 %collective-permute-start.10 = (bf16[32,2176]{1,0:T(8,128)(2,1)S(1)}, bf16[32,2176]{1,0:T(8,128)(2,1)S(1)}, u32[]{:S(2)}, u32[]{:S(2)}) collective-permute-start(bf16[32,2176]{1,0:T(8,128)(2,1)S(1)} %slice.94), channel_id=1, source_target_pairs={{0,2},{1,3},{4,0},{5,1},{8,4},{9,5},{12,8},{13,9},{14,12},{15,13},... | collective-permute-start | bytes 417800 | tf_op jit(solution)/shard_map/ppermute | solution.py:70
  62.5 5.1 %collective-permute-start.9 = (bf16[32,2176]{1,0:T(8,128)(2,1)S(1)}, bf16[32,2176]{1,0:T(8,128)(2,1)S(1)}, u32[]{:S(2)}, u32[]{:S(2)}) collective-permute-start(bf16[32,2176]{1,0:T(8,128)(2,1)S(1)} %slice.93), channel_id=1, source_target_pairs={{0,4},{1,5},{4,8},{5,9},{8,12},{9,13},{12,14},{13,15},{14,10},{15,... | collective-permute-start | bytes 417800 | tf_op jit(solution)/shard_map/ppermute | solution.py:69
  63.1 11.5 %collective-permute-start.13 = (bf16[32,4224]{1,0:T(8,128)(2,1)S(1)}, bf16[32,4224]{1,0:T(8,128)(2,1)S(1)}, u32[]{:S(2)}, u32[]{:S(2)}) collective-permute-start(bf16[32,4224]{1,0:T(8,128)(2,1)S(1)} %slice.98), channel_id=1, source_target_pairs={{0,4},{1,5},{4,8},{5,9},{8,12},{9,13},{12,14},{13,15},{14,10},{15,... | collective-permute-start | bytes 811016 | tf_op jit(solution)/shard_map/ppermute | solution.py:69
  65.1 9.5 %collective-permute-start.14 = (bf16[32,4224]{1,0:T(8,128)(2,1)S(1)}, bf16[32,4224]{1,0:T(8,128)(2,1)S(1)}, u32[]{:S(2)}, u32[]{:S(2)}) collective-permute-start(bf16[32,4224]{1,0:T(8,128)(2,1)S(1)} %slice.99), channel_id=1, source_target_pairs={{0,2},{1,3},{4,0},{5,1},{8,4},{9,5},{12,8},{13,9},{14,12},{15,13},... | collective-permute-start | bytes 811016 | tf_op jit(solution)/shard_map/ppermute | solution.py:70
  72.5 8.0 %collective-permute-start.11 = (bf16[32,2048]{1,0:T(8,128)(2,1)S(1)}, bf16[32,2048]{1,0:T(8,128)(2,1)S(1)}, u32[]{:S(2)}, u32[]{:S(2)}) collective-permute-start(bf16[32,2048]{1,0:T(8,128)(2,1)S(1)} %get-tuple-element.55), channel_id=1, source_target_pairs={{0,2},{1,3},{4,0},{5,1},{8,4},{9,5},{12,8},{13,9},{14,12},{15,13},... | collective-permute-start | bytes 393224 | tf_op jit(solution)/shard_map/ppermute | solution.py:94
  74.2 6.3 %collective-permute-start.12 = (bf16[32,2048]{1,0:T(8,128)(2,1)S(1)}, bf16[32,2048]{1,0:T(8,128)(2,1)S(1)}, u32[]{:S(2)}, u32[]{:S(2)}) collective-permute-start(bf16[32,2048]{1,0:T(8,128)(2,1)S(1)} %get-tuple-element.54), channel_id=1, source_target_pairs={{0,4},{1,5},{4,8},{5,9},{8,12},{9,13},{12,14},{13,15},{14,10},{15,... | collective-permute-start | bytes 393224 | tf_op jit(solution)/shard_map/ppermute | solution.py:95
  84.0 6.5 %collective-permute-start.22 = (bf16[32,2048]{1,0:T(8,128)(2,1)S(1)}, bf16[32,2048]{1,0:T(8,128)(2,1)S(1)}, u32[]{:S(2)}, u32[]{:S(2)}) collective-permute-start(bf16[32,2048]{1,0:T(8,128)(2,1)S(1)} %get-tuple-element.44), channel_id=1, source_target_pairs={{0,2},{1,3},{4,0},{5,1},{8,4},{9,5},{12,8},{13,9},{14,12},{15,13},... | collective-permute-start | bytes 393224 | tf_op jit(solution)/shard_map/ppermute | solution.py:94
  85.8 6.4 %collective-permute-start.26 = (bf16[32,2048]{1,0:T(8,128)(2,1)S(1)}, bf16[32,2048]{1,0:T(8,128)(2,1)S(1)}, u32[]{:S(2)}, u32[]{:S(2)}) collective-permute-start(bf16[32,2048]{1,0:T(8,128)(2,1)S(1)} %get-tuple-element.45), channel_id=1, source_target_pairs={{0,4},{1,5},{4,8},{5,9},{8,12},{9,13},{12,14},{13,15},{14,10},{15,... | collective-permute-start | bytes 393224 | tf_op jit(solution)/shard_map/ppermute | solution.py:95
  86.2 11.6 %collective-permute-start.18 = (bf16[64,2048]{1,0:T(8,128)(2,1)S(1)}, bf16[64,2048]{1,0:T(8,128)(2,1)S(1)}, u32[]{:S(2)}, u32[]{:S(2)}) collective-permute-start(bf16[64,2048]{1,0:T(8,128)(2,1)S(1)} %pad_maximum_fusion.1), channel_id=1, source_target_pairs={{0,4},{1,5},{4,8},{5,9},{8,12},{9,13},{12,14},{13,15},{14,10},{15,... | collective-permute-start | bytes 786440 | tf_op jit(solution)/shard_map/ppermute | solution.py:95
  86.9 10.9 %collective-permute-start.15 = (bf16[64,2048]{1,0:T(8,128)(2,1)S(1)}, bf16[64,2048]{1,0:T(8,128)(2,1)S(1)}, u32[]{:S(2)}, u32[]{:S(2)}) collective-permute-start(bf16[64,2048]{1,0:T(8,128)(2,1)S(1)} %pad_maximum_fusion), channel_id=1, source_target_pairs={{0,2},{1,3},{4,0},{5,1},{8,4},{9,5},{12,8},{13,9},{14,12},{15,13},... | collective-permute-start | bytes 786440 | tf_op jit(solution)/shard_map/ppermute | solution.py:94
  92.3 11.1 %collective-permute-start.27 = (bf16[64,2048]{1,0:T(8,128)(2,1)S(1)}, bf16[64,2048]{1,0:T(8,128)(2,1)S(1)}, u32[]{:S(2)}, u32[]{:S(2)}) collective-permute-start(bf16[64,2048]{1,0:T(8,128)(2,1)S(1)} %pad_maximum_fusion.3), channel_id=1, source_target_pairs={{0,4},{1,5},{4,8},{5,9},{8,12},{9,13},{12,14},{13,15},{14,10},{15,... | collective-permute-start | bytes 786440 | tf_op jit(solution)/shard_map/ppermute | solution.py:95
  92.7 24.5 %copy-start.2 = (bf16[1,64,2048]{2,1,0:T(8,128)(2,1)S(1)}, bf16[1,64,2048]{2,1,0:T(8,128)(2,1)}, u32[]{:S(2)}) copy-start(bf16[1,64,2048]{2,1,0:T(8,128)(2,1)} %param.11) | copy-start | bytes 786436
  92.7 11.2 %collective-permute-start.23 = (bf16[64,2048]{1,0:T(8,128)(2,1)S(1)}, bf16[64,2048]{1,0:T(8,128)(2,1)S(1)}, u32[]{:S(2)}, u32[]{:S(2)}) collective-permute-start(bf16[64,2048]{1,0:T(8,128)(2,1)S(1)} %pad_maximum_fusion.2), channel_id=1, source_target_pairs={{0,2},{1,3},{4,0},{5,1},{8,4},{9,5},{12,8},{13,9},{14,12},{15,13},... | collective-permute-start | bytes 786440 | tf_op jit(solution)/shard_map/ppermute | solution.py:94
  97.9 22.1 %copy-start.1 = (bf16[1,64,2048]{2,1,0:T(8,128)(2,1)S(1)}, bf16[1,64,2048]{2,1,0:T(8,128)(2,1)}, u32[]{:S(2)}) copy-start(bf16[1,64,2048]{2,1,0:T(8,128)(2,1)} %param.14) | copy-start | bytes 786436
  98.0 22.0 %copy-start.4 = (f32[1,2048]{1,0:T(1,128)S(1)}, f32[1,2048]{1,0:T(1,128)}, u32[]{:S(2)}) copy-start(f32[1,2048]{1,0:T(1,128)} %refs_2_.1) | copy-start | bytes 24580
  98.0 9.6 %collective-permute-start.16 = (bf16[64,2048]{1,0:T(8,128)(2,1)S(1)}, bf16[64,2048]{1,0:T(8,128)(2,1)S(1)}, u32[]{:S(2)}, u32[]{:S(2)}) collective-permute-start(bf16[64,2048]{1,0:T(8,128)(2,1)S(1)} %get-tuple-element.56), channel_id=1, source_target_pairs={{0,2},{1,3},{4,0},{5,1},{8,4},{9,5},{12,8},{13,9},{14,12},{15,13},... | collective-permute-start | bytes 786440 | tf_op jit(solution)/shard_map/ppermute | solution.py:94
  99.7 9.3 %collective-permute-start.19 = (bf16[64,2048]{1,0:T(8,128)(2,1)S(1)}, bf16[64,2048]{1,0:T(8,128)(2,1)S(1)}, u32[]{:S(2)}, u32[]{:S(2)}) collective-permute-start(bf16[64,2048]{1,0:T(8,128)(2,1)S(1)} %get-tuple-element.57), channel_id=1, source_target_pairs={{0,4},{1,5},{4,8},{5,9},{8,12},{9,13},{12,14},{13,15},{14,10},{15,... | collective-permute-start | bytes 786440 | tf_op jit(solution)/shard_map/ppermute | solution.py:95
  103.5 16.8 %copy-start.3 = (bf16[1,64,2048]{2,1,0:T(8,128)(2,1)S(1)}, bf16[1,64,2048]{2,1,0:T(8,128)(2,1)}, u32[]{:S(2)}) copy-start(bf16[1,64,2048]{2,1,0:T(8,128)(2,1)} %param.15) | copy-start | bytes 786436
  103.5 8.5 %collective-permute-start.28 = (bf16[64,2048]{1,0:T(8,128)(2,1)S(1)}, bf16[64,2048]{1,0:T(8,128)(2,1)S(1)}, u32[]{:S(2)}, u32[]{:S(2)}) collective-permute-start(bf16[64,2048]{1,0:T(8,128)(2,1)S(1)} %add_convert_fusion.1), channel_id=1, source_target_pairs={{0,4},{1,5},{4,8},{5,9},{8,12},{9,13},{12,14},{13,15},{14,10},{15,... | collective-permute-start | bytes 786440 | tf_op jit(solution)/shard_map/ppermute | solution.py:95
  103.9 8.1 %collective-permute-start.24 = (bf16[64,2048]{1,0:T(8,128)(2,1)S(1)}, bf16[64,2048]{1,0:T(8,128)(2,1)S(1)}, u32[]{:S(2)}, u32[]{:S(2)}) collective-permute-start(bf16[64,2048]{1,0:T(8,128)(2,1)S(1)} %add_convert_fusion.3), channel_id=1, source_target_pairs={{0,2},{1,3},{4,0},{5,1},{8,4},{9,5},{12,8},{13,9},{14,12},{15,13},... | collective-permute-start | bytes 786440 | tf_op jit(solution)/shard_map/ppermute | solution.py:94
  109.2 6.4 %collective-permute-start.17 = (bf16[64,2048]{1,0:T(8,128)(2,1)S(1)}, bf16[64,2048]{1,0:T(8,128)(2,1)S(1)}, u32[]{:S(2)}, u32[]{:S(2)}) collective-permute-start(bf16[64,2048]{1,0:T(8,128)(2,1)S(1)} %get-tuple-element.48), channel_id=1, source_target_pairs={{0,2},{1,3},{4,0},{5,1},{8,4},{9,5},{12,8},{13,9},{14,12},{15,13},... | collective-permute-start | bytes 786440 | tf_op jit(solution)/shard_map/ppermute | solution.py:94
  110.8 6.4 %collective-permute-start.20 = (bf16[64,2048]{1,0:T(8,128)(2,1)S(1)}, bf16[64,2048]{1,0:T(8,128)(2,1)S(1)}, u32[]{:S(2)}, u32[]{:S(2)}) collective-permute-start(bf16[64,2048]{1,0:T(8,128)(2,1)S(1)} %get-tuple-element.49), channel_id=1, source_target_pairs={{0,4},{1,5},{4,8},{5,9},{8,12},{9,13},{12,14},{13,15},{14,10},{15,... | collective-permute-start | bytes 786440 | tf_op jit(solution)/shard_map/ppermute | solution.py:95
  112.2 6.7 %collective-permute-start.25 = (bf16[64,2048]{1,0:T(8,128)(2,1)S(1)}, bf16[64,2048]{1,0:T(8,128)(2,1)S(1)}, u32[]{:S(2)}, u32[]{:S(2)}) collective-permute-start(bf16[64,2048]{1,0:T(8,128)(2,1)S(1)} %get-tuple-element.40), channel_id=1, source_target_pairs={{0,2},{1,3},{4,0},{5,1},{8,4},{9,5},{12,8},{13,9},{14,12},{15,13},... | collective-permute-start | bytes 786440 | tf_op jit(solution)/shard_map/ppermute | solution.py:94
  113.6 6.4 %collective-permute-start.29 = (bf16[64,2048]{1,0:T(8,128)(2,1)S(1)}, bf16[64,2048]{1,0:T(8,128)(2,1)S(1)}, u32[]{:S(2)}, u32[]{:S(2)}) collective-permute-start(bf16[64,2048]{1,0:T(8,128)(2,1)S(1)} %get-tuple-element.41), channel_id=1, source_target_pairs={{0,4},{1,5},{4,8},{5,9},{8,12},{9,13},{12,14},{13,15},{14,10},{15,... | collective-permute-start | bytes 786440 | tf_op jit(solution)/shard_map/ppermute | solution.py:95
  117.3 6.4 %collective-permute-start.21 = (bf16[1,64,2048]{2,1,0:T(8,128)(2,1)S(1)}, bf16[1,64,2048]{2,1,0:T(8,128)(2,1)S(1)}, u32[]{:S(2)}, u32[]{:S(2)}) collective-permute-start(bf16[1,64,2048]{2,1,0:T(8,128)(2,1)S(1)} %fusion.7), channel_id=1, source_target_pairs={{0,16},{16,0},{1,17},{17,1},{2,18},{18,2},{3,19},{19,3},{4,20},{20... | collective-permute-start | bytes 786440 | tf_op jit(solution)/shard_map/ppermute | solution.py:44
  120.6 6.4 %collective-permute-start.30 = (bf16[1,64,2048]{2,1,0:T(8,128)(2,1)S(1)}, bf16[1,64,2048]{2,1,0:T(8,128)(2,1)S(1)}, u32[]{:S(2)}, u32[]{:S(2)}) collective-permute-start(bf16[1,64,2048]{2,1,0:T(8,128)(2,1)S(1)} %fusion.8), channel_id=1, source_target_pairs={{0,16},{16,0},{1,17},{17,1},{2,18},{18,2},{3,19},{19,3},{4,20},{20... | collective-permute-start | bytes 786440 | tf_op jit(solution)/shard_map/ppermute | solution.py:44

commit v6 on v5

--- a/solution.py
+++ b/solution.py
@@ -124,19 +124,29 @@
         for i, (source, place) in enumerate(zip(sources, places))
     ]
     first_core = lax.rem(lax.axis_index("expert"), CORES) == 0
-    for at_once, core in ((len(copies), jnp.logical_not(first_core)), (IN_TURN, first_core)):
-
-        @pl.when(core)
+    other_core = jnp.logical_not(first_core)
+
+    @pl.when(first_core)
+    def _():
+        for first in range(0, len(copies), IN_TURN):
+            for copy in copies[first : first + IN_TURN]:
+                copy.start()
+            for copy in copies[first : first + IN_TURN]:
+                copy.wait()
+
+    @pl.when(other_core)
+    def _():
+        for copy in copies:
+            copy.start()
+
+    def needed(some):
+        @pl.when(other_core)
         def _():
-            for first in range(0, len(copies), at_once):
-                for copy in copies[first : first + at_once]:
-                    copy.start()
-                for copy in copies[first : first + at_once]:
-                    copy.wait()
-
+            for copy in some:
+                copy.wait()
+
+    needed(copies[2:7])
     rows, gain, routing = held[:2], held[2], (held[3:5], held[5:7])
-    out[:, :width] = normalize(rows[0][...], gain[...])
-    out[:, first : first + width] = normalize(rows[1][...], gain[...])
     shape = (table_width, out.shape[0])
     row = lax.broadcasted_iota(jnp.int32, shape, 0)
     part, expert = lax.div(row, devices), lax.rem(row, devices)
@@ -148,6 +158,11 @@
     high = table.astype(jnp.bfloat16).astype(jnp.float32)
     table = jnp.where(lax.rem(part, 2) == 0, high, table - high)
     out[:, width:first] = table.T.astype(jnp.bfloat16)
+    needed(copies[:1])
+    out[:, :width] = normalize(rows[0][...], gain[...])
+    needed(copies[1:2])
+    out[:, first : first + width] = normalize(rows[1][...], gain[...])
+    needed(copies[7:])
 
 
 def payload(forward, backward, cotangent, gain, forward_routing, backward_routing, devices):

time: 130 us -> 130 us (level)
  no operation moved by 1% of the time
where the time goes in v6:
time: 130 us; the launch traced here: 128 us
  waiting for transfers between devices  50.5 us (39%)
  Pallas kernels  43.3 us (33%)
  starting transfers between devices  30.9 us (24%)
  other arithmetic  1.52 us (1%)
    ppermute x5, waiting for transfers between devices, moved(): behind = lax.ppermute(behind, 'expert', ring_route(devices, 1))  24.9 us
    ppermute x8, starting transfers between devices, step(): behind = lax.ppermute(behind, 'expert', ring_route(devices, -1))  13.9 us
    ppermute x8, waiting for transfers between devices, step(): ahead = lax.ppermute(ahead, 'expert', ring_route(devices, 1))  13.2 us
    pallas_call x3, Pallas kernels, experts_forward(): pl.pallas_call(functools.partial(forward_body, len(blocks), devices), in_...  12.5 us
    pallas_call x2, Pallas kernels, hidden_grads(): pl.pallas_call(functools.partial(grads_body, len(blocks), devices), in_sp...  11.8 us
    pallas_call x2, Pallas kernels, token_grads(): pl.pallas_call(token_grads_body, in_specs=[IN_VMEM, IN_VMEM], out_specs=I...  6.87 us
    pallas_call x1, Pallas kernels, weights_in_vmem(): pl.pallas_call(weights_body, in_specs=[IN_HBM] * 6, out_specs=(IN_VMEM, I...  6.55 us
    ppermute x5, starting transfers between devices, moved(): ahead = lax.ppermute(ahead, 'expert', ring_route(devices, -1))  6.46 us
  transfers between devices with their start and end apart: 31, of which 19 were waited for; matrix products, arithmetic and copies ran while one was open for 1% of the time, Pallas kernels for 31%

profile of v6, /device:TPU:12, one launch (start us, length us, event | category | flops | bytes accessed | tf_op | source)
XLA Modules:
  0.0 128.0 jit_solution(5768801378471598763)
XLA Ops:
  0.7 0.5 collective-permute-start.3
  1.3 4.8 %shard_map.122.refs_0_ = bf16[64,6272]{1,0:T(8,128)(2,1)} custom-call(bf16[64,2048]{1,0:T(8,128)(2,1)} %bitcast.37, bf16[64,2048]{1,0:T(8,128)(2,1)} %bitcast.36, f32[1,2048]{1,0:T(1,128)} %refs_2_.1, s32[8,64]{1,0:T(8,128)} %bitcast.41, f32[8,64]{1,0:T(8,128)} %bitcast.42, s32[8,64]{1,0:T(8,128)} %bitcast.43, f32[8,64]{1,0:T(8,128)} %bitcast.44, ...), custom_call_target="tpu_custom_call" | custom-call | flops 1 | bytes 1 | tf_op jit(solution)/shard_map/pallas_call | solution.py:172
  6.1 0.5 collective-permute-start
  6.6 1.6 %collective-permute-start.1 = (bf16[64,6272]{1,0:T(8,128)(2,1)}, bf16[64,6272]{1,0:T(8,128)(2,1)S(1)}, u32[]{:S(2)}, u32[]{:S(2)}) collective-permute-start(bf16[64,6272]{1,0:T(8,128)(2,1)} %shard_map.122.refs_0_), channel_id=1, source_target_pairs={{0,2},{1,3},{4,0},{5,1},{8,4},{9,5},{12,8},{13,9},{14,12},{15,13},... | collective-permute-start | bytes 2408456 | tf_op jit(solution)/shard_map/ppermute | solution.py:70
  8.2 16.2 %collective-permute-done.refs_1_ = bf16[64,6272]{1,0:T(8,128)(2,1)S(1)} collective-permute-done((bf16[64,6272]{1,0:T(8,128)(2,1)}, bf16[64,6272]{1,0:T(8,128)(2,1)S(1)}, u32[]{:S(2)}, u32[]{:S(2)}) %collective-permute-start) | collective-permute-done | bytes 802848 | tf_op jit(solution)/shard_map/ppermute | solution.py:69
  24.8 1.7 %collective-permute-start.6 = (bf16[64,6272]{1,0:T(8,128)(2,1)S(1)}, bf16[64,6272]{1,0:T(8,128)(2,1)S(1)}, u32[]{:S(2)}, u32[]{:S(2)}) collective-permute-start(bf16[64,6272]{1,0:T(8,128)(2,1)S(1)} %collective-permute-done.1.refs_2_), channel_id=1, source_target_pairs={{0,2},{1,3},{4,0},{5,1},{8,4},{9,5},{12,8},{13,9},{14,12},{15,13},... | collective-permute-start | bytes 2408456 | tf_op jit(solution)/shard_map/ppermute | solution.py:70
  26.6 6.6 %shard_map.123 = (bf16[2048,3072]{1,0:T(8,128)(2,1)S(1)}, bf16[1536,2048]{1,0:T(8,128)(2,1)S(1)}) custom-call(bf16[2048,768]{1,0:T(8,128)(2,1)} %bitcast.31, bf16[2048,768]{1,0:T(8,128)(2,1)} %bitcast.33, bf16[768,2048]{1,0:T(8,128)(2,1)} %bitcast.35, bf16[2048,768]{1,0:T(8,128)(2,1)} %collective-permute-done.2.refs_3_, ...), custom_call_target="tpu_custom_call" | custom-call | tf_op jit(solution)/shard_map/pallas_call | solution.py:212
  33.2 4.5 %shard_map.124 = bf16[192,2048]{1,0:T(8,128)(2,1)S(1)} custom-call(bf16[64,6272]{1,0:T(8,128)(2,1)S(1)} %copy-done, bf16[64,6272]{1,0:T(8,128)(2,1)S(1)} %collective-permute-done.refs_1_, bf16[64,6272]{1,0:T(8,128)(2,1)S(1)} %collective-permute-done.1.refs_2_, s32[2]{0:T(128)S(1)} %pad_add_fusion.refs_3_.refs_2_.refs_4_.refs_5_, ...), custom_call_target="tpu_custom_call" | custom-call | flops 1 | bytes 1 | tf_op jit(solution)/shard_map/pallas_call | solution.py:323
  37.6 4.9 %collective-permute-done.5.refs_0_.refs_3_ = bf16[64,6272]{1,0:T(8,128)(2,1)S(1)} collective-permute-done((bf16[64,6272]{1,0:T(8,128)(2,1)S(1)}, bf16[64,6272]{1,0:T(8,128)(2,1)S(1)}, u32[]{:S(2)}, u32[]{:S(2)}) %collective-permute-start.5) | collective-permute-done | bytes 802848 | tf_op jit(solution)/shard_map/ppermute | solution.py:69
  42.5 0.7 collective-permute-start.7
  43.2 1.3 %collective-permute-start.8 = (bf16[64,6272]{1,0:T(8,128)(2,1)S(1)}, bf16[64,6272]{1,0:T(8,128)(2,1)S(1)}, u32[]{:S(2)}, u32[]{:S(2)}) collective-permute-start(bf16[64,6272]{1,0:T(8,128)(2,1)S(1)} %collective-permute-done.6.refs_1_.refs_0_), channel_id=1, source_target_pairs={{0,2},{1,3},{4,0},{5,1},{8,4},{9,5},{12,8},{13,9},{14,12},{15,13},... | collective-permute-start | bytes 2408456 | tf_op jit(solution)/shard_map/ppermute | solution.py:70
  44.5 5.9 %shard_map.126.grads = bf16[256,3072]{1,0:T(8,128)(2,1)S(1)} custom-call(bf16[64,6272]{1,0:T(8,128)(2,1)S(1)} %copy-done, bf16[64,6272]{1,0:T(8,128)(2,1)S(1)} %collective-permute-done.refs_1_, bf16[64,6272]{1,0:T(8,128)(2,1)S(1)} %collective-permute-done.1.refs_2_, bf16[64,6272]{1,0:T(8,128)(2,1)S(1)} %collective-permute-done.5.refs_0_.refs_3_, ...), custom_call_target="tpu_custom_call" | custom-call | flops 1 | bytes 1 | tf_op jit(solution)/shard_map/pallas_call | solution.py:270
  50.4 3.4 %shard_map.127 = bf16[256,2048]{1,0:T(8,128)(2,1)S(1)} custom-call(bf16[256,3072]{1,0:T(8,128)(2,1)S(1)} %shard_map.126.grads, bf16[2048,3072]{1,0:T(8,128)(2,1)S(1)} %get-tuple-element.25.refs_4_.refs_3_.refs_5_.gate_up.refs_6_), custom_call_target="tpu_custom_call" | custom-call | flops 1 | bytes 1 | tf_op jit(solution)/shard_map/pallas_call | solution.py:291
  53.9 3.2 %shard_map.125 = bf16[128,2048]{1,0:T(8,128)(2,1)S(1)} custom-call(bf16[64,6272]{1,0:T(8,128)(2,1)S(1)} %collective-permute-done.5.refs_0_.refs_3_, bf16[64,6272]{1,0:T(8,128)(2,1)S(1)} %collective-permute-done.6.refs_1_.refs_0_, s32[2]{0:T(128)S(1)} %pad_add_fusion.refs_3_.refs_2_.refs_4_.refs_5_, ...), custom_call_target="tpu_custom_call" | custom-call | flops 1 | bytes 1 | tf_op jit(solution)/shard_map/pallas_call | solution.py:323
  57.1 2.1 %collective-permute-done.7.refs_0_.refs_1_ = bf16[64,6272]{1,0:T(8,128)(2,1)S(1)} collective-permute-done((bf16[64,6272]{1,0:T(8,128)(2,1)S(1)}, bf16[64,6272]{1,0:T(8,128)(2,1)S(1)}, u32[]{:S(2)}, u32[]{:S(2)}) %collective-permute-start.7) | collective-permute-done | bytes 802848 | tf_op jit(solution)/shard_map/ppermute | solution.py:69
  59.2 1.6 %collective-permute-done.8.refs_1_.refs_2_ = bf16[64,6272]{1,0:T(8,128)(2,1)S(1)} collective-permute-done((bf16[64,6272]{1,0:T(8,128)(2,1)S(1)}, bf16[64,6272]{1,0:T(8,128)(2,1)S(1)}, u32[]{:S(2)}, u32[]{:S(2)}) %collective-permute-start.8) | collective-permute-done | bytes 802848 | tf_op jit(solution)/shard_map/ppermute | solution.py:70
  60.9 1.7 %collective-permute-start.10 = (bf16[32,2176]{1,0:T(8,128)(2,1)S(1)}, bf16[32,2176]{1,0:T(8,128)(2,1)S(1)}, u32[]{:S(2)}, u32[]{:S(2)}) collective-permute-start(bf16[32,2176]{1,0:T(8,128)(2,1)S(1)} %slice.94), channel_id=1, source_target_pairs={{0,2},{1,3},{4,0},{5,1},{8,4},{9,5},{12,8},{13,9},{14,12},{15,13},... | collective-permute-start | bytes 417800 | tf_op jit(solution)/shard_map/ppermute | solution.py:70
  63.0 2.0 %collective-permute-start.13 = (bf16[32,4224]{1,0:T(8,128)(2,1)S(1)}, bf16[32,4224]{1,0:T(8,128)(2,1)S(1)}, u32[]{:S(2)}, u32[]{:S(2)}) collective-permute-start(bf16[32,4224]{1,0:T(8,128)(2,1)S(1)} %slice.98), channel_id=1, source_target_pairs={{0,4},{1,5},{4,8},{5,9},{8,12},{9,13},{12,14},{13,15},{14,10},{15,... | collective-permute-start | bytes 811016 | tf_op jit(solution)/shard_map/ppermute | solution.py:69
  65.1 0.8 collective-permute-done.10.refs_3_
  66.0 1.8 %collective-permute-done.9.refs_2_ = bf16[32,2176]{1,0:T(8,128)(2,1)S(1)} collective-permute-done((bf16[32,2176]{1,0:T(8,128)(2,1)S(1)}, bf16[32,2176]{1,0:T(8,128)(2,1)S(1)}, u32[]{:S(2)}, u32[]{:S(2)}) %collective-permute-start.9) | collective-permute-done | bytes 139296 | tf_op jit(solution)/shard_map/ppermute | solution.py:69
  67.7 4.8 %shard_map.128 = bf16[192,2048]{1,0:T(8,128)(2,1)S(1)} custom-call(bf16[64,6272]{1,0:T(8,128)(2,1)S(1)} %collective-permute-done.7.refs_0_.refs_1_, bf16[64,6272]{1,0:T(8,128)(2,1)S(1)} %collective-permute-done.8.refs_1_.refs_2_, bf16[32,2176]{1,0:T(8,128)(2,1)S(1)} %collective-permute-done.9.refs_2_, bf16[32,2176]{1,0:T(8,128)(2,1)S(1)} %collective-permute-done.10.refs_3_, ...), custom_call_target="tpu_custom_call" | custom-call | flops 1 | bytes 1 | tf_op jit(solution)/shard_map/pallas_call | solution.py:323
  72.6 1.8 %collective-permute-start.11 = (bf16[32,2048]{1,0:T(8,128)(2,1)S(1)}, bf16[32,2048]{1,0:T(8,128)(2,1)S(1)}, u32[]{:S(2)}, u32[]{:S(2)}) collective-permute-start(bf16[32,2048]{1,0:T(8,128)(2,1)S(1)} %get-tuple-element.55), channel_id=1, source_target_pairs={{0,2},{1,3},{4,0},{5,1},{8,4},{9,5},{12,8},{13,9},{14,12},{15,13},... | collective-permute-start | bytes 393224 | tf_op jit(solution)/shard_map/ppermute | solution.py:94
  74.7 5.9 %shard_map.129.grads = bf16[256,3072]{1,0:T(8,128)(2,1)S(1)} custom-call(bf16[64,6272]{1,0:T(8,128)(2,1)S(1)} %collective-permute-done.6.refs_1_.refs_0_, bf16[64,6272]{1,0:T(8,128)(2,1)S(1)} %collective-permute-done.7.refs_0_.refs_1_, bf16[64,6272]{1,0:T(8,128)(2,1)S(1)} %collective-permute-done.8.refs_1_.refs_2_, ...), custom_call_target="tpu_custom_call" | custom-call | flops 1 | bytes 1 | tf_op jit(solution)/shard_map/pallas_call | solution.py:270
  80.6 3.4 %shard_map.131 = bf16[256,2048]{1,0:T(8,128)(2,1)S(1)} custom-call(bf16[256,3072]{1,0:T(8,128)(2,1)S(1)} %shard_map.129.grads, bf16[2048,3072]{1,0:T(8,128)(2,1)S(1)} %get-tuple-element.25.refs_4_.refs_3_.refs_5_.gate_up.refs_6_), custom_call_target="tpu_custom_call" | custom-call | flops 99999997952 | bytes 1 | tf_op jit(solution)/shard_map/pallas_call | solution.py:291
  84.1 1.8 %collective-permute-start.22 = (bf16[32,2048]{1,0:T(8,128)(2,1)S(1)}, bf16[32,2048]{1,0:T(8,128)(2,1)S(1)}, u32[]{:S(2)}, u32[]{:S(2)}) collective-permute-start(bf16[32,2048]{1,0:T(8,128)(2,1)S(1)} %get-tuple-element.44), channel_id=1, source_target_pairs={{0,2},{1,3},{4,0},{5,1},{8,4},{9,5},{12,8},{13,9},{14,12},{15,13},... | collective-permute-start | bytes 393224 | tf_op jit(solution)/shard_map/ppermute | solution.py:94
  86.3 1.0 collective-permute-start.18
  87.4 1.1 collective-permute-start.15
  88.5 2.2 %collective-permute-done.22 = bf16[32,2048]{1,0:T(8,128)(2,1)S(1)} collective-permute-done((bf16[32,2048]{1,0:T(8,128)(2,1)S(1)}, bf16[32,2048]{1,0:T(8,128)(2,1)S(1)}, u32[]{:S(2)}, u32[]{:S(2)}) %collective-permute-start.22) | collective-permute-done | bytes 131104 | tf_op jit(solution)/shard_map/ppermute | solution.py:94
  90.6 1.7 %collective-permute-done.26 = bf16[32,2048]{1,0:T(8,128)(2,1)S(1)} collective-permute-done((bf16[32,2048]{1,0:T(8,128)(2,1)S(1)}, bf16[32,2048]{1,0:T(8,128)(2,1)S(1)}, u32[]{:S(2)}, u32[]{:S(2)}) %collective-permute-start.26) | collective-permute-done | bytes 131104 | tf_op jit(solution)/shard_map/ppermute | solution.py:95
  92.8 1.8 %collective-permute-start.23 = (bf16[64,2048]{1,0:T(8,128)(2,1)S(1)}, bf16[64,2048]{1,0:T(8,128)(2,1)S(1)}, u32[]{:S(2)}, u32[]{:S(2)}) collective-permute-start(bf16[64,2048]{1,0:T(8,128)(2,1)S(1)} %pad_maximum_fusion.2), channel_id=1, source_target_pairs={{0,2},{1,3},{4,0},{5,1},{8,4},{9,5},{12,8},{13,9},{14,12},{15,13},... | collective-permute-start | bytes 786440 | tf_op jit(solution)/shard_map/ppermute | solution.py:94
  94.6 3.4 %collective-permute-done.18 = bf16[64,2048]{1,0:T(8,128)(2,1)S(1)} collective-permute-done((bf16[64,2048]{1,0:T(8,128)(2,1)S(1)}, bf16[64,2048]{1,0:T(8,128)(2,1)S(1)}, u32[]{:S(2)}, u32[]{:S(2)}) %collective-permute-start.18) | collective-permute-done | bytes 262176 | tf_op jit(solution)/shard_map/ppermute | solution.py:95
  98.1 2.0 %collective-permute-start.16 = (bf16[64,2048]{1,0:T(8,128)(2,1)S(1)}, bf16[64,2048]{1,0:T(8,128)(2,1)S(1)}, u32[]{:S(2)}, u32[]{:S(2)}) collective-permute-start(bf16[64,2048]{1,0:T(8,128)(2,1)S(1)} %get-tuple-element.56), channel_id=1, source_target_pairs={{0,2},{1,3},{4,0},{5,1},{8,4},{9,5},{12,8},{13,9},{14,12},{15,13},... | collective-permute-start | bytes 786440 | tf_op jit(solution)/shard_map/ppermute | solution.py:94
  100.2 3.4 %collective-permute-done.27 = bf16[64,2048]{1,0:T(8,128)(2,1)S(1)} collective-permute-done((bf16[64,2048]{1,0:T(8,128)(2,1)S(1)}, bf16[64,2048]{1,0:T(8,128)(2,1)S(1)}, u32[]{:S(2)}, u32[]{:S(2)}) %collective-permute-start.27) | collective-permute-done | bytes 262176 | tf_op jit(solution)/shard_map/ppermute | solution.py:95
  104.0 1.8 %collective-permute-start.24 = (bf16[64,2048]{1,0:T(8,128)(2,1)S(1)}, bf16[64,2048]{1,0:T(8,128)(2,1)S(1)}, u32[]{:S(2)}, u32[]{:S(2)}) collective-permute-start(bf16[64,2048]{1,0:T(8,128)(2,1)S(1)} %add_convert_fusion.3), channel_id=1, source_target_pairs={{0,2},{1,3},{4,0},{5,1},{8,4},{9,5},{12,8},{13,9},{14,12},{15,13},... | collective-permute-start | bytes 786440 | tf_op jit(solution)/shard_map/ppermute | solution.py:94
  105.9 2.0 %collective-permute-done.16 = bf16[64,2048]{1,0:T(8,128)(2,1)S(1)} collective-permute-done((bf16[64,2048]{1,0:T(8,128)(2,1)S(1)}, bf16[64,2048]{1,0:T(8,128)(2,1)S(1)}, u32[]{:S(2)}, u32[]{:S(2)}) %collective-permute-start.16) | collective-permute-done | bytes 262176 | tf_op jit(solution)/shard_map/ppermute | solution.py:94
  107.9 1.3 collective-permute-done.19
  109.3 1.8 %collective-permute-start.17 = (bf16[64,2048]{1,0:T(8,128)(2,1)S(1)}, bf16[64,2048]{1,0:T(8,128)(2,1)S(1)}, u32[]{:S(2)}, u32[]{:S(2)}) collective-permute-start(bf16[64,2048]{1,0:T(8,128)(2,1)S(1)} %get-tuple-element.48), channel_id=1, source_target_pairs={{0,2},{1,3},{4,0},{5,1},{8,4},{9,5},{12,8},{13,9},{14,12},{15,13},... | collective-permute-start | bytes 786440 | tf_op jit(solution)/shard_map/ppermute | solution.py:94
  111.4 0.6 collective-permute-done.28
  112.1 1.8 %collective-permute-start.25 = (bf16[64,2048]{1,0:T(8,128)(2,1)S(1)}, bf16[64,2048]{1,0:T(8,128)(2,1)S(1)}, u32[]{:S(2)}, u32[]{:S(2)}) collective-permute-start(bf16[64,2048]{1,0:T(8,128)(2,1)S(1)} %get-tuple-element.40), channel_id=1, source_target_pairs={{0,2},{1,3},{4,0},{5,1},{8,4},{9,5},{12,8},{13,9},{14,12},{15,13},... | collective-permute-start | bytes 786440 | tf_op jit(solution)/shard_map/ppermute | solution.py:94
  114.2 1.5 %collective-permute-done.17 = bf16[64,2048]{1,0:T(8,128)(2,1)S(1)} collective-permute-done((bf16[64,2048]{1,0:T(8,128)(2,1)S(1)}, bf16[64,2048]{1,0:T(8,128)(2,1)S(1)}, u32[]{:S(2)}, u32[]{:S(2)}) %collective-permute-start.17) | collective-permute-done | bytes 262176 | tf_op jit(solution)/shard_map/ppermute | solution.py:94
  115.7 1.7 %collective-permute-done.20 = bf16[64,2048]{1,0:T(8,128)(2,1)S(1)} collective-permute-done((bf16[64,2048]{1,0:T(8,128)(2,1)S(1)}, bf16[64,2048]{1,0:T(8,128)(2,1)S(1)}, u32[]{:S(2)}, u32[]{:S(2)}) %collective-permute-start.20) | collective-permute-done | bytes 262176 | tf_op jit(solution)/shard_map/ppermute | solution.py:95
  117.6 1.6 %collective-permute-start.21 = (bf16[1,64,2048]{2,1,0:T(8,128)(2,1)S(1)}, bf16[1,64,2048]{2,1,0:T(8,128)(2,1)S(1)}, u32[]{:S(2)}, u32[]{:S(2)}) collective-permute-start(bf16[1,64,2048]{2,1,0:T(8,128)(2,1)S(1)} %fusion.7), channel_id=1, source_target_pairs={{0,16},{16,0},{1,17},{17,1},{2,18},{18,2},{3,19},{19,3},{4,20},{20... | collective-permute-start | bytes 786440 | tf_op jit(solution)/shard_map/ppermute | solution.py:44
  119.2 1.1 collective-permute-done.29
  120.9 1.6 %collective-permute-start.30 = (bf16[1,64,2048]{2,1,0:T(8,128)(2,1)S(1)}, bf16[1,64,2048]{2,1,0:T(8,128)(2,1)S(1)}, u32[]{:S(2)}, u32[]{:S(2)}) collective-permute-start(bf16[1,64,2048]{2,1,0:T(8,128)(2,1)S(1)} %fusion.8), channel_id=1, source_target_pairs={{0,16},{16,0},{1,17},{17,1},{2,18},{18,2},{3,19},{19,3},{4,20},{20... | collective-permute-start | bytes 786440 | tf_op jit(solution)/shard_map/ppermute | solution.py:44
  122.4 1.6 %collective-permute-done.21.array = bf16[1,64,2048]{2,1,0:T(8,128)(2,1)S(1)} collective-permute-done((bf16[1,64,2048]{2,1,0:T(8,128)(2,1)S(1)}, bf16[1,64,2048]{2,1,0:T(8,128)(2,1)S(1)}, u32[]{:S(2)}, u32[]{:S(2)}) %collective-permute-start.21) | collective-permute-done | bytes 262176 | tf_op jit(solution)/shard_map/ppermute | solution.py:44
  124.0 0.7 shard_map.130
  124.8 2.6 %collective-permute-done.30 = bf16[1,64,2048]{2,1,0:T(8,128)(2,1)S(1)} collective-permute-done((bf16[1,64,2048]{2,1,0:T(8,128)(2,1)S(1)}, bf16[1,64,2048]{2,1,0:T(8,128)(2,1)S(1)}, u32[]{:S(2)}, u32[]{:S(2)}) %collective-permute-start.30) | collective-permute-done | bytes 262176 | tf_op jit(solution)/shard_map/ppermute | solution.py:44
  127.3 0.7 copy.14
  (57 shorter events, 4.6 us)
Async XLA Ops:
  0.6 23.8 %collective-permute-start.2 = (bf16[2048,768]{1,0:T(8,128)(2,1)}, bf16[2048,768]{1,0:T(8,128)(2,1)}, u32[]{:S(2)}, u32[]{:S(2)}) collective-permute-start(bf16[2048,768]{1,0:T(8,128)(2,1)} %bitcast.30), channel_id=1, source_target_pairs={{0,1},{1,0},{2,3},{3,2},{4,5},{5,4},{6,7},{7,6},{8,9},{9,8},{10,11... | collective-permute-start | bytes 9437192 | tf_op jit(solution)/shard_map/ppermute | solution.py:409
  0.7 23.7 %collective-permute-start.3 = (bf16[2048,768]{1,0:T(8,128)(2,1)}, bf16[2048,768]{1,0:T(8,128)(2,1)}, u32[]{:S(2)}, u32[]{:S(2)}) collective-permute-start(bf16[2048,768]{1,0:T(8,128)(2,1)} %bitcast.32), channel_id=1, source_target_pairs={{0,1},{1,0},{2,3},{3,2},{4,5},{5,4},{6,7},{7,6},{8,9},{9,8},{10,11... | collective-permute-start | bytes 9437192 | tf_op jit(solution)/shard_map/ppermute | solution.py:409
  1.2 23.2 %collective-permute-start.4 = (bf16[768,2048]{1,0:T(8,128)(2,1)}, bf16[768,2048]{1,0:T(8,128)(2,1)}, u32[]{:S(2)}, u32[]{:S(2)}) collective-permute-start(bf16[768,2048]{1,0:T(8,128)(2,1)} %bitcast.34), channel_id=1, source_target_pairs={{0,1},{1,0},{2,3},{3,2},{4,5},{5,4},{6,7},{7,6},{8,9},{9,8},{10,11... | collective-permute-start | bytes 9437192 | tf_op jit(solution)/shard_map/ppermute | solution.py:409
  6.1 18.2 %collective-permute-start = (bf16[64,6272]{1,0:T(8,128)(2,1)}, bf16[64,6272]{1,0:T(8,128)(2,1)S(1)}, u32[]{:S(2)}, u32[]{:S(2)}) collective-permute-start(bf16[64,6272]{1,0:T(8,128)(2,1)} %shard_map.122.refs_0_), channel_id=1, source_target_pairs={{0,4},{1,5},{4,8},{5,9},{8,12},{9,13},{12,14},{13,15},{14,10},{15,... | collective-permute-start | bytes 2408456 | tf_op jit(solution)/shard_map/ppermute | solution.py:69
  6.6 17.8 %collective-permute-start.1 = (bf16[64,6272]{1,0:T(8,128)(2,1)}, bf16[64,6272]{1,0:T(8,128)(2,1)S(1)}, u32[]{:S(2)}, u32[]{:S(2)}) collective-permute-start(bf16[64,6272]{1,0:T(8,128)(2,1)} %shard_map.122.refs_0_), channel_id=1, source_target_pairs={{0,2},{1,3},{4,0},{5,1},{8,4},{9,5},{12,8},{13,9},{14,12},{15,13},... | collective-permute-start | bytes 2408456 | tf_op jit(solution)/shard_map/ppermute | solution.py:70
  24.4 18.1 %collective-permute-start.5 = (bf16[64,6272]{1,0:T(8,128)(2,1)S(1)}, bf16[64,6272]{1,0:T(8,128)(2,1)S(1)}, u32[]{:S(2)}, u32[]{:S(2)}) collective-permute-start(bf16[64,6272]{1,0:T(8,128)(2,1)S(1)} %collective-permute-done.refs_1_), channel_id=1, source_target_pairs={{0,4},{1,5},{4,8},{5,9},{8,12},{9,13},{12,14},{13,15},{14,10},{15,... | collective-permute-start | bytes 2408456 | tf_op jit(solution)/shard_map/ppermute | solution.py:69
  24.8 17.7 %collective-permute-start.6 = (bf16[64,6272]{1,0:T(8,128)(2,1)S(1)}, bf16[64,6272]{1,0:T(8,128)(2,1)S(1)}, u32[]{:S(2)}, u32[]{:S(2)}) collective-permute-start(bf16[64,6272]{1,0:T(8,128)(2,1)S(1)} %collective-permute-done.1.refs_2_), channel_id=1, source_target_pairs={{0,2},{1,3},{4,0},{5,1},{8,4},{9,5},{12,8},{13,9},{14,12},{15,13},... | collective-permute-start | bytes 2408456 | tf_op jit(solution)/shard_map/ppermute | solution.py:70
  26.6 6.6 %copy-start = (bf16[64,6272]{1,0:T(8,128)(2,1)S(1)}, bf16[64,6272]{1,0:T(8,128)(2,1)}, u32[]{:S(2)}) copy-start(bf16[64,6272]{1,0:T(8,128)(2,1)} %shard_map.122.refs_0_) | copy-start | bytes 2408452
  42.5 16.7 %collective-permute-start.7 = (bf16[64,6272]{1,0:T(8,128)(2,1)S(1)}, bf16[64,6272]{1,0:T(8,128)(2,1)S(1)}, u32[]{:S(2)}, u32[]{:S(2)}) collective-permute-start(bf16[64,6272]{1,0:T(8,128)(2,1)S(1)} %collective-permute-done.5.refs_0_.refs_3_), channel_id=1, source_target_pairs={{0,4},{1,5},{4,8},{5,9},{8,12},{9,13},{12,14},{13,15},{14,10},{15,... | collective-permute-start | bytes 2408456 | tf_op jit(solution)/shard_map/ppermute | solution.py:69
  43.2 17.6 %collective-permute-start.8 = (bf16[64,6272]{1,0:T(8,128)(2,1)S(1)}, bf16[64,6272]{1,0:T(8,128)(2,1)S(1)}, u32[]{:S(2)}, u32[]{:S(2)}) collective-permute-start(bf16[64,6272]{1,0:T(8,128)(2,1)S(1)} %collective-permute-done.6.refs_1_.refs_0_), channel_id=1, source_target_pairs={{0,2},{1,3},{4,0},{5,1},{8,4},{9,5},{12,8},{13,9},{14,12},{15,13},... | collective-permute-start | bytes 2408456 | tf_op jit(solution)/shard_map/ppermute | solution.py:70
  60.9 5.1 %collective-permute-start.10 = (bf16[32,2176]{1,0:T(8,128)(2,1)S(1)}, bf16[32,2176]{1,0:T(8,128)(2,1)S(1)}, u32[]{:S(2)}, u32[]{:S(2)}) collective-permute-start(bf16[32,2176]{1,0:T(8,128)(2,1)S(1)} %slice.94), channel_id=1, source_target_pairs={{0,2},{1,3},{4,0},{5,1},{8,4},{9,5},{12,8},{13,9},{14,12},{15,13},... | collective-permute-start | bytes 417800 | tf_op jit(solution)/shard_map/ppermute | solution.py:70
  62.6 5.1 %collective-permute-start.9 = (bf16[32,2176]{1,0:T(8,128)(2,1)S(1)}, bf16[32,2176]{1,0:T(8,128)(2,1)S(1)}, u32[]{:S(2)}, u32[]{:S(2)}) collective-permute-start(bf16[32,2176]{1,0:T(8,128)(2,1)S(1)} %slice.93), channel_id=1, source_target_pairs={{0,4},{1,5},{4,8},{5,9},{8,12},{9,13},{12,14},{13,15},{14,10},{15,... | collective-permute-start | bytes 417800 | tf_op jit(solution)/shard_map/ppermute | solution.py:69
  63.0 11.6 %collective-permute-start.13 = (bf16[32,4224]{1,0:T(8,128)(2,1)S(1)}, bf16[32,4224]{1,0:T(8,128)(2,1)S(1)}, u32[]{:S(2)}, u32[]{:S(2)}) collective-permute-start(bf16[32,4224]{1,0:T(8,128)(2,1)S(1)} %slice.98), channel_id=1, source_target_pairs={{0,4},{1,5},{4,8},{5,9},{8,12},{9,13},{12,14},{13,15},{14,10},{15,... | collective-permute-start | bytes 811016 | tf_op jit(solution)/shard_map/ppermute | solution.py:69
  65.0 9.6 %collective-permute-start.14 = (bf16[32,4224]{1,0:T(8,128)(2,1)S(1)}, bf16[32,4224]{1,0:T(8,128)(2,1)S(1)}, u32[]{:S(2)}, u32[]{:S(2)}) collective-permute-start(bf16[32,4224]{1,0:T(8,128)(2,1)S(1)} %slice.99), channel_id=1, source_target_pairs={{0,2},{1,3},{4,0},{5,1},{8,4},{9,5},{12,8},{13,9},{14,12},{15,13},... | collective-permute-start | bytes 811016 | tf_op jit(solution)/shard_map/ppermute | solution.py:70
  72.6 8.0 %collective-permute-start.11 = (bf16[32,2048]{1,0:T(8,128)(2,1)S(1)}, bf16[32,2048]{1,0:T(8,128)(2,1)S(1)}, u32[]{:S(2)}, u32[]{:S(2)}) collective-permute-start(bf16[32,2048]{1,0:T(8,128)(2,1)S(1)} %get-tuple-element.55), channel_id=1, source_target_pairs={{0,2},{1,3},{4,0},{5,1},{8,4},{9,5},{12,8},{13,9},{14,12},{15,13},... | collective-permute-start | bytes 393224 | tf_op jit(solution)/shard_map/ppermute | solution.py:94
  74.4 6.2 %collective-permute-start.12 = (bf16[32,2048]{1,0:T(8,128)(2,1)S(1)}, bf16[32,2048]{1,0:T(8,128)(2,1)S(1)}, u32[]{:S(2)}, u32[]{:S(2)}) collective-permute-start(bf16[32,2048]{1,0:T(8,128)(2,1)S(1)} %get-tuple-element.54), channel_id=1, source_target_pairs={{0,4},{1,5},{4,8},{5,9},{8,12},{9,13},{12,14},{13,15},{14,10},{15,... | collective-permute-start | bytes 393224 | tf_op jit(solution)/shard_map/ppermute | solution.py:95
  84.1 6.5 %collective-permute-start.22 = (bf16[32,2048]{1,0:T(8,128)(2,1)S(1)}, bf16[32,2048]{1,0:T(8,128)(2,1)S(1)}, u32[]{:S(2)}, u32[]{:S(2)}) collective-permute-start(bf16[32,2048]{1,0:T(8,128)(2,1)S(1)} %get-tuple-element.44), channel_id=1, source_target_pairs={{0,2},{1,3},{4,0},{5,1},{8,4},{9,5},{12,8},{13,9},{14,12},{15,13},... | collective-permute-start | bytes 393224 | tf_op jit(solution)/shard_map/ppermute | solution.py:94
  85.9 6.4 %collective-permute-start.26 = (bf16[32,2048]{1,0:T(8,128)(2,1)S(1)}, bf16[32,2048]{1,0:T(8,128)(2,1)S(1)}, u32[]{:S(2)}, u32[]{:S(2)}) collective-permute-start(bf16[32,2048]{1,0:T(8,128)(2,1)S(1)} %get-tuple-element.45), channel_id=1, source_target_pairs={{0,4},{1,5},{4,8},{5,9},{8,12},{9,13},{12,14},{13,15},{14,10},{15,... | collective-permute-start | bytes 393224 | tf_op jit(solution)/shard_map/ppermute | solution.py:95
  86.3 11.7 %collective-permute-start.18 = (bf16[64,2048]{1,0:T(8,128)(2,1)S(1)}, bf16[64,2048]{1,0:T(8,128)(2,1)S(1)}, u32[]{:S(2)}, u32[]{:S(2)}) collective-permute-start(bf16[64,2048]{1,0:T(8,128)(2,1)S(1)} %pad_maximum_fusion.1), channel_id=1, source_target_pairs={{0,4},{1,5},{4,8},{5,9},{8,12},{9,13},{12,14},{13,15},{14,10},{15,... | collective-permute-start | bytes 786440 | tf_op jit(solution)/shard_map/ppermute | solution.py:95
  87.4 10.6 %collective-permute-start.15 = (bf16[64,2048]{1,0:T(8,128)(2,1)S(1)}, bf16[64,2048]{1,0:T(8,128)(2,1)S(1)}, u32[]{:S(2)}, u32[]{:S(2)}) collective-permute-start(bf16[64,2048]{1,0:T(8,128)(2,1)S(1)} %pad_maximum_fusion), channel_id=1, source_target_pairs={{0,2},{1,3},{4,0},{5,1},{8,4},{9,5},{12,8},{13,9},{14,12},{15,13},... | collective-permute-start | bytes 786440 | tf_op jit(solution)/shard_map/ppermute | solution.py:94
  92.4 11.1 %collective-permute-start.27 = (bf16[64,2048]{1,0:T(8,128)(2,1)S(1)}, bf16[64,2048]{1,0:T(8,128)(2,1)S(1)}, u32[]{:S(2)}, u32[]{:S(2)}) collective-permute-start(bf16[64,2048]{1,0:T(8,128)(2,1)S(1)} %pad_maximum_fusion.3), channel_id=1, source_target_pairs={{0,4},{1,5},{4,8},{5,9},{8,12},{9,13},{12,14},{13,15},{14,10},{15,... | collective-permute-start | bytes 786440 | tf_op jit(solution)/shard_map/ppermute | solution.py:95
  92.8 24.7 %copy-start.2 = (bf16[1,64,2048]{2,1,0:T(8,128)(2,1)S(1)}, bf16[1,64,2048]{2,1,0:T(8,128)(2,1)}, u32[]{:S(2)}) copy-start(bf16[1,64,2048]{2,1,0:T(8,128)(2,1)} %param.11) | copy-start | bytes 786436
  92.8 11.2 %collective-permute-start.23 = (bf16[64,2048]{1,0:T(8,128)(2,1)S(1)}, bf16[64,2048]{1,0:T(8,128)(2,1)S(1)}, u32[]{:S(2)}, u32[]{:S(2)}) collective-permute-start(bf16[64,2048]{1,0:T(8,128)(2,1)S(1)} %pad_maximum_fusion.2), channel_id=1, source_target_pairs={{0,2},{1,3},{4,0},{5,1},{8,4},{9,5},{12,8},{13,9},{14,12},{15,13},... | collective-permute-start | bytes 786440 | tf_op jit(solution)/shard_map/ppermute | solution.py:94
  98.1 22.2 %copy-start.1 = (bf16[1,64,2048]{2,1,0:T(8,128)(2,1)S(1)}, bf16[1,64,2048]{2,1,0:T(8,128)(2,1)}, u32[]{:S(2)}) copy-start(bf16[1,64,2048]{2,1,0:T(8,128)(2,1)} %param.14) | copy-start | bytes 786436
  98.1 22.2 %copy-start.4 = (f32[1,2048]{1,0:T(1,128)S(1)}, f32[1,2048]{1,0:T(1,128)}, u32[]{:S(2)}) copy-start(f32[1,2048]{1,0:T(1,128)} %refs_2_.1) | copy-start | bytes 24580
  98.1 9.8 %collective-permute-start.16 = (bf16[64,2048]{1,0:T(8,128)(2,1)S(1)}, bf16[64,2048]{1,0:T(8,128)(2,1)S(1)}, u32[]{:S(2)}, u32[]{:S(2)}) collective-permute-start(bf16[64,2048]{1,0:T(8,128)(2,1)S(1)} %get-tuple-element.56), channel_id=1, source_target_pairs={{0,2},{1,3},{4,0},{5,1},{8,4},{9,5},{12,8},{13,9},{14,12},{15,13},... | collective-permute-start | bytes 786440 | tf_op jit(solution)/shard_map/ppermute | solution.py:94
  100.1 9.1 %collective-permute-start.19 = (bf16[64,2048]{1,0:T(8,128)(2,1)S(1)}, bf16[64,2048]{1,0:T(8,128)(2,1)S(1)}, u32[]{:S(2)}, u32[]{:S(2)}) collective-permute-start(bf16[64,2048]{1,0:T(8,128)(2,1)S(1)} %get-tuple-element.57), channel_id=1, source_target_pairs={{0,4},{1,5},{4,8},{5,9},{8,12},{9,13},{12,14},{13,15},{14,10},{15,... | collective-permute-start | bytes 786440 | tf_op jit(solution)/shard_map/ppermute | solution.py:95
  103.6 16.9 %copy-start.3 = (bf16[1,64,2048]{2,1,0:T(8,128)(2,1)S(1)}, bf16[1,64,2048]{2,1,0:T(8,128)(2,1)}, u32[]{:S(2)}) copy-start(bf16[1,64,2048]{2,1,0:T(8,128)(2,1)} %param.15) | copy-start | bytes 786436
  103.7 8.3 %collective-permute-start.28 = (bf16[64,2048]{1,0:T(8,128)(2,1)S(1)}, bf16[64,2048]{1,0:T(8,128)(2,1)S(1)}, u32[]{:S(2)}, u32[]{:S(2)}) collective-permute-start(bf16[64,2048]{1,0:T(8,128)(2,1)S(1)} %add_convert_fusion.1), channel_id=1, source_target_pairs={{0,4},{1,5},{4,8},{5,9},{8,12},{9,13},{12,14},{13,15},{14,10},{15,... | collective-permute-start | bytes 786440 | tf_op jit(solution)/shard_map/ppermute | solution.py:95
  104.0 7.9 %collective-permute-start.24 = (bf16[64,2048]{1,0:T(8,128)(2,1)S(1)}, bf16[64,2048]{1,0:T(8,128)(2,1)S(1)}, u32[]{:S(2)}, u32[]{:S(2)}) collective-permute-start(bf16[64,2048]{1,0:T(8,128)(2,1)S(1)} %add_convert_fusion.3), channel_id=1, source_target_pairs={{0,2},{1,3},{4,0},{5,1},{8,4},{9,5},{12,8},{13,9},{14,12},{15,13},... | collective-permute-start | bytes 786440 | tf_op jit(solution)/shard_map/ppermute | solution.py:94
  109.3 6.4 %collective-permute-start.17 = (bf16[64,2048]{1,0:T(8,128)(2,1)S(1)}, bf16[64,2048]{1,0:T(8,128)(2,1)S(1)}, u32[]{:S(2)}, u32[]{:S(2)}) collective-permute-start(bf16[64,2048]{1,0:T(8,128)(2,1)S(1)} %get-tuple-element.48), channel_id=1, source_target_pairs={{0,2},{1,3},{4,0},{5,1},{8,4},{9,5},{12,8},{13,9},{14,12},{15,13},... | collective-permute-start | bytes 786440 | tf_op jit(solution)/shard_map/ppermute | solution.py:94
  111.1 6.4 %collective-permute-start.20 = (bf16[64,2048]{1,0:T(8,128)(2,1)S(1)}, bf16[64,2048]{1,0:T(8,128)(2,1)S(1)}, u32[]{:S(2)}, u32[]{:S(2)}) collective-permute-start(bf16[64,2048]{1,0:T(8,128)(2,1)S(1)} %get-tuple-element.49), channel_id=1, source_target_pairs={{0,4},{1,5},{4,8},{5,9},{8,12},{9,13},{12,14},{13,15},{14,10},{15,... | collective-permute-start | bytes 786440 | tf_op jit(solution)/shard_map/ppermute | solution.py:95
  112.1 7.1 %collective-permute-start.25 = (bf16[64,2048]{1,0:T(8,128)(2,1)S(1)}, bf16[64,2048]{1,0:T(8,128)(2,1)S(1)}, u32[]{:S(2)}, u32[]{:S(2)}) collective-permute-start(bf16[64,2048]{1,0:T(8,128)(2,1)S(1)} %get-tuple-element.40), channel_id=1, source_target_pairs={{0,2},{1,3},{4,0},{5,1},{8,4},{9,5},{12,8},{13,9},{14,12},{15,13},... | collective-permute-start | bytes 786440 | tf_op jit(solution)/shard_map/ppermute | solution.py:94
  113.9 6.4 %collective-permute-start.29 = (bf16[64,2048]{1,0:T(8,128)(2,1)S(1)}, bf16[64,2048]{1,0:T(8,128)(2,1)S(1)}, u32[]{:S(2)}, u32[]{:S(2)}) collective-permute-start(bf16[64,2048]{1,0:T(8,128)(2,1)S(1)} %get-tuple-element.41), channel_id=1, source_target_pairs={{0,4},{1,5},{4,8},{5,9},{8,12},{9,13},{12,14},{13,15},{14,10},{15,... | collective-permute-start | bytes 786440 | tf_op jit(solution)/shard_map/ppermute | solution.py:95
  117.6 6.4 %collective-permute-start.21 = (bf16[1,64,2048]{2,1,0:T(8,128)(2,1)S(1)}, bf16[1,64,2048]{2,1,0:T(8,128)(2,1)S(1)}, u32[]{:S(2)}, u32[]{:S(2)}) collective-permute-start(bf16[1,64,2048]{2,1,0:T(8,128)(2,1)S(1)} %fusion.7), channel_id=1, source_target_pairs={{0,16},{16,0},{1,17},{17,1},{2,18},{18,2},{3,19},{19,3},{4,20},{20... | collective-permute-start | bytes 786440 | tf_op jit(solution)/shard_map/ppermute | solution.py:44
  120.9 6.4 %collective-permute-start.30 = (bf16[1,64,2048]{2,1,0:T(8,128)(2,1)S(1)}, bf16[1,64,2048]{2,1,0:T(8,128)(2,1)S(1)}, u32[]{:S(2)}, u32[]{:S(2)}) collective-permute-start(bf16[1,64,2048]{2,1,0:T(8,128)(2,1)S(1)} %fusion.8), channel_id=1, source_target_pairs={{0,16},{16,0},{1,17},{17,1},{2,18},{18,2},{3,19},{19,3},{4,20},{20... | collective-permute-start | bytes 786440 | tf_op jit(solution)/shard_map/ppermute | solution.py:44

commit v7 on v6

--- a/solution.py
+++ b/solution.py
@@ -218,7 +218,7 @@
             pltpu.VMEM((CORES * hidden, width), jnp.bfloat16),
         ),
         scratch_shapes=[pltpu.SemaphoreType.DMA((6,))],
-        compiler_params=pltpu.CompilerParams(vmem_limit_bytes=38 * MIB),
+        compiler_params=pltpu.CompilerParams(vmem_limit_bytes=42 * MIB),
     )(*mine, *theirs)
 
 
@@ -276,7 +276,7 @@
             pltpu.VMEM((count, table + 2 * width), jnp.bfloat16),
             pltpu.SemaphoreType.DMA((len(blocks),)),
         ],
-        compiler_params=pltpu.CompilerParams(vmem_limit_bytes=14 * MIB),
+        compiler_params=pltpu.CompilerParams(vmem_limit_bytes=10 * MIB),
         cost_estimate=pl.CostEstimate(flops=COST, bytes_accessed=1, transcendentals=0),
     )(*blocks, experts, gate_up, down)
 
@@ -293,7 +293,7 @@
         in_specs=[IN_VMEM, IN_VMEM],
         out_specs=IN_VMEM,
         out_shape=jax.ShapeDtypeStruct((grads.shape[0], gate_up.shape[0]), jnp.bfloat16),
-        compiler_params=pltpu.CompilerParams(vmem_limit_bytes=14 * MIB),
+        compiler_params=pltpu.CompilerParams(vmem_limit_bytes=10 * MIB),
         cost_estimate=pl.CostEstimate(flops=cost, bytes_accessed=1, transcendentals=0),
     )(grads, gate_up)
 
@@ -330,7 +330,7 @@
             pltpu.VMEM((count, down.shape[0]), jnp.bfloat16),
             pltpu.SemaphoreType.DMA((len(blocks),)),
         ],
-        compiler_params=pltpu.CompilerParams(vmem_limit_bytes=14 * MIB),
+        compiler_params=pltpu.CompilerParams(vmem_limit_bytes=10 * MIB),
         cost_estimate=pl.CostEstimate(flops=COST, bytes_accessed=1, transcendentals=0),
     )(*blocks, experts, gate_up, down)
 

time: 130 us -> 130 us (level)
  no operation moved by 1% of the time
where the time goes in v7:
time: 130 us; the launch traced here: 128 us
  waiting for transfers between devices  50.5 us (39%)
  Pallas kernels  43.3 us (33%)
  starting transfers between devices  30.9 us (24%)
  other arithmetic  1.53 us (1%)
    ppermute x5, waiting for transfers between devices, moved(): behind = lax.ppermute(behind, 'expert', ring_route(devices, 1))  24.9 us
    ppermute x8, starting transfers between devices, step(): behind = lax.ppermute(behind, 'expert', ring_route(devices, -1))  13.9 us
    ppermute x8, waiting for transfers between devices, step(): ahead = lax.ppermute(ahead, 'expert', ring_route(devices, 1))  13.2 us
    pallas_call x3, Pallas kernels, experts_forward(): pl.pallas_call(functools.partial(forward_body, len(blocks), devices), in_...  12.5 us
    pallas_call x2, Pallas kernels, hidden_grads(): pl.pallas_call(functools.partial(grads_body, len(blocks), devices), in_sp...  11.8 us
    pallas_call x2, Pallas kernels, token_grads(): pl.pallas_call(token_grads_body, in_specs=[IN_VMEM, IN_VMEM], out_specs=I...  6.87 us
    pallas_call x1, Pallas kernels, weights_in_vmem(): pl.pallas_call(weights_body, in_specs=[IN_HBM] * 6, out_specs=(IN_VMEM, I...  6.55 us
    ppermute x5, starting transfers between devices, moved(): ahead = lax.ppermute(ahead, 'expert', ring_route(devices, -1))  6.46 us
  transfers between devices with their start and end apart: 31, of which 19 were waited for; matrix products, arithmetic and copies ran while one was open for 1% of the time, Pallas kernels for 31%

profile of v7, /device:TPU:12, one launch (start us, length us, event | category | flops | bytes accessed | tf_op | source)
XLA Modules:
  0.0 128.0 jit_solution(675957736051704419)
XLA Ops:
  0.7 0.5 collective-permute-start.3
  1.3 4.8 %shard_map.122.refs_0_ = bf16[64,6272]{1,0:T(8,128)(2,1)} custom-call(bf16[64,2048]{1,0:T(8,128)(2,1)} %bitcast.37, bf16[64,2048]{1,0:T(8,128)(2,1)} %bitcast.36, f32[1,2048]{1,0:T(1,128)} %refs_2_.1, s32[8,64]{1,0:T(8,128)} %bitcast.41, f32[8,64]{1,0:T(8,128)} %bitcast.42, s32[8,64]{1,0:T(8,128)} %bitcast.43, f32[8,64]{1,0:T(8,128)} %bitcast.44, ...), custom_call_target="tpu_custom_call" | custom-call | flops 1 | bytes 1 | tf_op jit(solution)/shard_map/pallas_call | solution.py:172
  6.1 0.5 collective-permute-start
  6.6 1.6 %collective-permute-start.1 = (bf16[64,6272]{1,0:T(8,128)(2,1)}, bf16[64,6272]{1,0:T(8,128)(2,1)S(1)}, u32[]{:S(2)}, u32[]{:S(2)}) collective-permute-start(bf16[64,6272]{1,0:T(8,128)(2,1)} %shard_map.122.refs_0_), channel_id=1, source_target_pairs={{0,2},{1,3},{4,0},{5,1},{8,4},{9,5},{12,8},{13,9},{14,12},{15,13},... | collective-permute-start | bytes 2408456 | tf_op jit(solution)/shard_map/ppermute | solution.py:70
  8.2 16.2 %collective-permute-done.refs_1_ = bf16[64,6272]{1,0:T(8,128)(2,1)S(1)} collective-permute-done((bf16[64,6272]{1,0:T(8,128)(2,1)}, bf16[64,6272]{1,0:T(8,128)(2,1)S(1)}, u32[]{:S(2)}, u32[]{:S(2)}) %collective-permute-start) | collective-permute-done | bytes 802848 | tf_op jit(solution)/shard_map/ppermute | solution.py:69
  24.8 1.7 %collective-permute-start.6 = (bf16[64,6272]{1,0:T(8,128)(2,1)S(1)}, bf16[64,6272]{1,0:T(8,128)(2,1)S(1)}, u32[]{:S(2)}, u32[]{:S(2)}) collective-permute-start(bf16[64,6272]{1,0:T(8,128)(2,1)S(1)} %collective-permute-done.1.refs_2_), channel_id=1, source_target_pairs={{0,2},{1,3},{4,0},{5,1},{8,4},{9,5},{12,8},{13,9},{14,12},{15,13},... | collective-permute-start | bytes 2408456 | tf_op jit(solution)/shard_map/ppermute | solution.py:70
  26.6 6.6 %shard_map.123 = (bf16[2048,3072]{1,0:T(8,128)(2,1)S(1)}, bf16[1536,2048]{1,0:T(8,128)(2,1)S(1)}) custom-call(bf16[2048,768]{1,0:T(8,128)(2,1)} %bitcast.31, bf16[2048,768]{1,0:T(8,128)(2,1)} %bitcast.33, bf16[768,2048]{1,0:T(8,128)(2,1)} %bitcast.35, bf16[2048,768]{1,0:T(8,128)(2,1)} %collective-permute-done.2.refs_3_, ...), custom_call_target="tpu_custom_call" | custom-call | tf_op jit(solution)/shard_map/pallas_call | solution.py:212
  33.2 4.5 %shard_map.124 = bf16[192,2048]{1,0:T(8,128)(2,1)S(1)} custom-call(bf16[64,6272]{1,0:T(8,128)(2,1)S(1)} %copy-done, bf16[64,6272]{1,0:T(8,128)(2,1)S(1)} %collective-permute-done.refs_1_, bf16[64,6272]{1,0:T(8,128)(2,1)S(1)} %collective-permute-done.1.refs_2_, s32[2]{0:T(128)S(1)} %pad_add_fusion.refs_3_.refs_2_.refs_4_.refs_5_, ...), custom_call_target="tpu_custom_call" | custom-call | flops 1 | bytes 1 | tf_op jit(solution)/shard_map/pallas_call | solution.py:323
  37.6 4.9 %collective-permute-done.5.refs_0_.refs_3_ = bf16[64,6272]{1,0:T(8,128)(2,1)S(1)} collective-permute-done((bf16[64,6272]{1,0:T(8,128)(2,1)S(1)}, bf16[64,6272]{1,0:T(8,128)(2,1)S(1)}, u32[]{:S(2)}, u32[]{:S(2)}) %collective-permute-start.5) | collective-permute-done | bytes 802848 | tf_op jit(solution)/shard_map/ppermute | solution.py:69
  42.5 0.7 collective-permute-start.7
  43.2 1.3 %collective-permute-start.8 = (bf16[64,6272]{1,0:T(8,128)(2,1)S(1)}, bf16[64,6272]{1,0:T(8,128)(2,1)S(1)}, u32[]{:S(2)}, u32[]{:S(2)}) collective-permute-start(bf16[64,6272]{1,0:T(8,128)(2,1)S(1)} %collective-permute-done.6.refs_1_.refs_0_), channel_id=1, source_target_pairs={{0,2},{1,3},{4,0},{5,1},{8,4},{9,5},{12,8},{13,9},{14,12},{15,13},... | collective-permute-start | bytes 2408456 | tf_op jit(solution)/shard_map/ppermute | solution.py:70
  44.5 5.9 %shard_map.126.grads = bf16[256,3072]{1,0:T(8,128)(2,1)S(1)} custom-call(bf16[64,6272]{1,0:T(8,128)(2,1)S(1)} %copy-done, bf16[64,6272]{1,0:T(8,128)(2,1)S(1)} %collective-permute-done.refs_1_, bf16[64,6272]{1,0:T(8,128)(2,1)S(1)} %collective-permute-done.1.refs_2_, bf16[64,6272]{1,0:T(8,128)(2,1)S(1)} %collective-permute-done.5.refs_0_.refs_3_, ...), custom_call_target="tpu_custom_call" | custom-call | flops 1 | bytes 1 | tf_op jit(solution)/shard_map/pallas_call | solution.py:270
  50.4 3.4 %shard_map.127 = bf16[256,2048]{1,0:T(8,128)(2,1)S(1)} custom-call(bf16[256,3072]{1,0:T(8,128)(2,1)S(1)} %shard_map.126.grads, bf16[2048,3072]{1,0:T(8,128)(2,1)S(1)} %get-tuple-element.25.refs_4_.refs_3_.refs_5_.gate_up.refs_6_), custom_call_target="tpu_custom_call" | custom-call | flops 1 | bytes 1 | tf_op jit(solution)/shard_map/pallas_call | solution.py:291
  53.9 3.2 %shard_map.125 = bf16[128,2048]{1,0:T(8,128)(2,1)S(1)} custom-call(bf16[64,6272]{1,0:T(8,128)(2,1)S(1)} %collective-permute-done.5.refs_0_.refs_3_, bf16[64,6272]{1,0:T(8,128)(2,1)S(1)} %collective-permute-done.6.refs_1_.refs_0_, s32[2]{0:T(128)S(1)} %pad_add_fusion.refs_3_.refs_2_.refs_4_.refs_5_, ...), custom_call_target="tpu_custom_call" | custom-call | flops 1 | bytes 1 | tf_op jit(solution)/shard_map/pallas_call | solution.py:323
  57.1 2.1 %collective-permute-done.7.refs_0_.refs_1_ = bf16[64,6272]{1,0:T(8,128)(2,1)S(1)} collective-permute-done((bf16[64,6272]{1,0:T(8,128)(2,1)S(1)}, bf16[64,6272]{1,0:T(8,128)(2,1)S(1)}, u32[]{:S(2)}, u32[]{:S(2)}) %collective-permute-start.7) | collective-permute-done | bytes 802848 | tf_op jit(solution)/shard_map/ppermute | solution.py:69
  59.2 1.6 %collective-permute-done.8.refs_1_.refs_2_ = bf16[64,6272]{1,0:T(8,128)(2,1)S(1)} collective-permute-done((bf16[64,6272]{1,0:T(8,128)(2,1)S(1)}, bf16[64,6272]{1,0:T(8,128)(2,1)S(1)}, u32[]{:S(2)}, u32[]{:S(2)}) %collective-permute-start.8) | collective-permute-done | bytes 802848 | tf_op jit(solution)/shard_map/ppermute | solution.py:70
  60.9 1.7 %collective-permute-start.10 = (bf16[32,2176]{1,0:T(8,128)(2,1)S(1)}, bf16[32,2176]{1,0:T(8,128)(2,1)S(1)}, u32[]{:S(2)}, u32[]{:S(2)}) collective-permute-start(bf16[32,2176]{1,0:T(8,128)(2,1)S(1)} %slice.94), channel_id=1, source_target_pairs={{0,2},{1,3},{4,0},{5,1},{8,4},{9,5},{12,8},{13,9},{14,12},{15,13},... | collective-permute-start | bytes 417800 | tf_op jit(solution)/shard_map/ppermute | solution.py:70
  63.0 2.0 %collective-permute-start.13 = (bf16[32,4224]{1,0:T(8,128)(2,1)S(1)}, bf16[32,4224]{1,0:T(8,128)(2,1)S(1)}, u32[]{:S(2)}, u32[]{:S(2)}) collective-permute-start(bf16[32,4224]{1,0:T(8,128)(2,1)S(1)} %slice.98), channel_id=1, source_target_pairs={{0,4},{1,5},{4,8},{5,9},{8,12},{9,13},{12,14},{13,15},{14,10},{15,... | collective-permute-start | bytes 811016 | tf_op jit(solution)/shard_map/ppermute | solution.py:69
  65.1 0.8 collective-permute-done.10.refs_3_
  66.0 1.8 %collective-permute-done.9.refs_2_ = bf16[32,2176]{1,0:T(8,128)(2,1)S(1)} collective-permute-done((bf16[32,2176]{1,0:T(8,128)(2,1)S(1)}, bf16[32,2176]{1,0:T(8,128)(2,1)S(1)}, u32[]{:S(2)}, u32[]{:S(2)}) %collective-permute-start.9) | collective-permute-done | bytes 139296 | tf_op jit(solution)/shard_map/ppermute | solution.py:69
  67.7 4.8 %shard_map.128 = bf16[192,2048]{1,0:T(8,128)(2,1)S(1)} custom-call(bf16[64,6272]{1,0:T(8,128)(2,1)S(1)} %collective-permute-done.7.refs_0_.refs_1_, bf16[64,6272]{1,0:T(8,128)(2,1)S(1)} %collective-permute-done.8.refs_1_.refs_2_, bf16[32,2176]{1,0:T(8,128)(2,1)S(1)} %collective-permute-done.9.refs_2_, bf16[32,2176]{1,0:T(8,128)(2,1)S(1)} %collective-permute-done.10.refs_3_, ...), custom_call_target="tpu_custom_call" | custom-call | flops 1 | bytes 1 | tf_op jit(solution)/shard_map/pallas_call | solution.py:323
  72.6 1.8 %collective-permute-start.11 = (bf16[32,2048]{1,0:T(8,128)(2,1)S(1)}, bf16[32,2048]{1,0:T(8,128)(2,1)S(1)}, u32[]{:S(2)}, u32[]{:S(2)}) collective-permute-start(bf16[32,2048]{1,0:T(8,128)(2,1)S(1)} %get-tuple-element.55), channel_id=1, source_target_pairs={{0,2},{1,3},{4,0},{5,1},{8,4},{9,5},{12,8},{13,9},{14,12},{15,13},... | collective-permute-start | bytes 393224 | tf_op jit(solution)/shard_map/ppermute | solution.py:94
  74.7 5.9 %shard_map.129.grads = bf16[256,3072]{1,0:T(8,128)(2,1)S(1)} custom-call(bf16[64,6272]{1,0:T(8,128)(2,1)S(1)} %collective-permute-done.6.refs_1_.refs_0_, bf16[64,6272]{1,0:T(8,128)(2,1)S(1)} %collective-permute-done.7.refs_0_.refs_1_, bf16[64,6272]{1,0:T(8,128)(2,1)S(1)} %collective-permute-done.8.refs_1_.refs_2_, ...), custom_call_target="tpu_custom_call" | custom-call | flops 1 | bytes 1 | tf_op jit(solution)/shard_map/pallas_call | solution.py:270
  80.6 3.4 %shard_map.131 = bf16[256,2048]{1,0:T(8,128)(2,1)S(1)} custom-call(bf16[256,3072]{1,0:T(8,128)(2,1)S(1)} %shard_map.129.grads, bf16[2048,3072]{1,0:T(8,128)(2,1)S(1)} %get-tuple-element.25.refs_4_.refs_3_.refs_5_.gate_up.refs_6_), custom_call_target="tpu_custom_call" | custom-call | flops 99999997952 | bytes 1 | tf_op jit(solution)/shard_map/pallas_call | solution.py:291
  84.1 1.8 %collective-permute-start.22 = (bf16[32,2048]{1,0:T(8,128)(2,1)S(1)}, bf16[32,2048]{1,0:T(8,128)(2,1)S(1)}, u32[]{:S(2)}, u32[]{:S(2)}) collective-permute-start(bf16[32,2048]{1,0:T(8,128)(2,1)S(1)} %get-tuple-element.44), channel_id=1, source_target_pairs={{0,2},{1,3},{4,0},{5,1},{8,4},{9,5},{12,8},{13,9},{14,12},{15,13},... | collective-permute-start | bytes 393224 | tf_op jit(solution)/shard_map/ppermute | solution.py:94
  86.3 1.1 collective-permute-start.18
  87.4 1.1 collective-permute-start.15
  88.5 2.2 %collective-permute-done.22 = bf16[32,2048]{1,0:T(8,128)(2,1)S(1)} collective-permute-done((bf16[32,2048]{1,0:T(8,128)(2,1)S(1)}, bf16[32,2048]{1,0:T(8,128)(2,1)S(1)}, u32[]{:S(2)}, u32[]{:S(2)}) %collective-permute-start.22) | collective-permute-done | bytes 131104 | tf_op jit(solution)/shard_map/ppermute | solution.py:94
  90.6 1.7 %collective-permute-done.26 = bf16[32,2048]{1,0:T(8,128)(2,1)S(1)} collective-permute-done((bf16[32,2048]{1,0:T(8,128)(2,1)S(1)}, bf16[32,2048]{1,0:T(8,128)(2,1)S(1)}, u32[]{:S(2)}, u32[]{:S(2)}) %collective-permute-start.26) | collective-permute-done | bytes 131104 | tf_op jit(solution)/shard_map/ppermute | solution.py:95
  92.8 1.8 %collective-permute-start.23 = (bf16[64,2048]{1,0:T(8,128)(2,1)S(1)}, bf16[64,2048]{1,0:T(8,128)(2,1)S(1)}, u32[]{:S(2)}, u32[]{:S(2)}) collective-permute-start(bf16[64,2048]{1,0:T(8,128)(2,1)S(1)} %pad_maximum_fusion.2), channel_id=1, source_target_pairs={{0,2},{1,3},{4,0},{5,1},{8,4},{9,5},{12,8},{13,9},{14,12},{15,13},... | collective-permute-start | bytes 786440 | tf_op jit(solution)/shard_map/ppermute | solution.py:94
  94.6 3.4 %collective-permute-done.18 = bf16[64,2048]{1,0:T(8,128)(2,1)S(1)} collective-permute-done((bf16[64,2048]{1,0:T(8,128)(2,1)S(1)}, bf16[64,2048]{1,0:T(8,128)(2,1)S(1)}, u32[]{:S(2)}, u32[]{:S(2)}) %collective-permute-start.18) | collective-permute-done | bytes 262176 | tf_op jit(solution)/shard_map/ppermute | solution.py:95
  98.1 2.0 %collective-permute-start.16 = (bf16[64,2048]{1,0:T(8,128)(2,1)S(1)}, bf16[64,2048]{1,0:T(8,128)(2,1)S(1)}, u32[]{:S(2)}, u32[]{:S(2)}) collective-permute-start(bf16[64,2048]{1,0:T(8,128)(2,1)S(1)} %get-tuple-element.56), channel_id=1, source_target_pairs={{0,2},{1,3},{4,0},{5,1},{8,4},{9,5},{12,8},{13,9},{14,12},{15,13},... | collective-permute-start | bytes 786440 | tf_op jit(solution)/shard_map/ppermute | solution.py:94
  100.2 3.4 %collective-permute-done.27 = bf16[64,2048]{1,0:T(8,128)(2,1)S(1)} collective-permute-done((bf16[64,2048]{1,0:T(8,128)(2,1)S(1)}, bf16[64,2048]{1,0:T(8,128)(2,1)S(1)}, u32[]{:S(2)}, u32[]{:S(2)}) %collective-permute-start.27) | collective-permute-done | bytes 262176 | tf_op jit(solution)/shard_map/ppermute | solution.py:95
  104.0 1.8 %collective-permute-start.24 = (bf16[64,2048]{1,0:T(8,128)(2,1)S(1)}, bf16[64,2048]{1,0:T(8,128)(2,1)S(1)}, u32[]{:S(2)}, u32[]{:S(2)}) collective-permute-start(bf16[64,2048]{1,0:T(8,128)(2,1)S(1)} %add_convert_fusion.3), channel_id=1, source_target_pairs={{0,2},{1,3},{4,0},{5,1},{8,4},{9,5},{12,8},{13,9},{14,12},{15,13},... | collective-permute-start | bytes 786440 | tf_op jit(solution)/shard_map/ppermute | solution.py:94
  105.9 2.0 %collective-permute-done.16 = bf16[64,2048]{1,0:T(8,128)(2,1)S(1)} collective-permute-done((bf16[64,2048]{1,0:T(8,128)(2,1)S(1)}, bf16[64,2048]{1,0:T(8,128)(2,1)S(1)}, u32[]{:S(2)}, u32[]{:S(2)}) %collective-permute-start.16) | collective-permute-done | bytes 262176 | tf_op jit(solution)/shard_map/ppermute | solution.py:94
  107.9 1.3 collective-permute-done.19
  109.3 1.8 %collective-permute-start.17 = (bf16[64,2048]{1,0:T(8,128)(2,1)S(1)}, bf16[64,2048]{1,0:T(8,128)(2,1)S(1)}, u32[]{:S(2)}, u32[]{:S(2)}) collective-permute-start(bf16[64,2048]{1,0:T(8,128)(2,1)S(1)} %get-tuple-element.48), channel_id=1, source_target_pairs={{0,2},{1,3},{4,0},{5,1},{8,4},{9,5},{12,8},{13,9},{14,12},{15,13},... | collective-permute-start | bytes 786440 | tf_op jit(solution)/shard_map/ppermute | solution.py:94
  111.4 0.6 collective-permute-done.28
  112.1 1.8 %collective-permute-start.25 = (bf16[64,2048]{1,0:T(8,128)(2,1)S(1)}, bf16[64,2048]{1,0:T(8,128)(2,1)S(1)}, u32[]{:S(2)}, u32[]{:S(2)}) collective-permute-start(bf16[64,2048]{1,0:T(8,128)(2,1)S(1)} %get-tuple-element.40), channel_id=1, source_target_pairs={{0,2},{1,3},{4,0},{5,1},{8,4},{9,5},{12,8},{13,9},{14,12},{15,13},... | collective-permute-start | bytes 786440 | tf_op jit(solution)/shard_map/ppermute | solution.py:94
  114.2 1.5 %collective-permute-done.17 = bf16[64,2048]{1,0:T(8,128)(2,1)S(1)} collective-permute-done((bf16[64,2048]{1,0:T(8,128)(2,1)S(1)}, bf16[64,2048]{1,0:T(8,128)(2,1)S(1)}, u32[]{:S(2)}, u32[]{:S(2)}) %collective-permute-start.17) | collective-permute-done | bytes 262176 | tf_op jit(solution)/shard_map/ppermute | solution.py:94
  115.7 1.7 %collective-permute-done.20 = bf16[64,2048]{1,0:T(8,128)(2,1)S(1)} collective-permute-done((bf16[64,2048]{1,0:T(8,128)(2,1)S(1)}, bf16[64,2048]{1,0:T(8,128)(2,1)S(1)}, u32[]{:S(2)}, u32[]{:S(2)}) %collective-permute-start.20) | collective-permute-done | bytes 262176 | tf_op jit(solution)/shard_map/ppermute | solution.py:95
  117.6 1.6 %collective-permute-start.21 = (bf16[1,64,2048]{2,1,0:T(8,128)(2,1)S(1)}, bf16[1,64,2048]{2,1,0:T(8,128)(2,1)S(1)}, u32[]{:S(2)}, u32[]{:S(2)}) collective-permute-start(bf16[1,64,2048]{2,1,0:T(8,128)(2,1)S(1)} %fusion.7), channel_id=1, source_target_pairs={{0,16},{16,0},{1,17},{17,1},{2,18},{18,2},{3,19},{19,3},{4,20},{20... | collective-permute-start | bytes 786440 | tf_op jit(solution)/shard_map/ppermute | solution.py:44
  119.2 1.1 collective-permute-done.29
  120.9 1.6 %collective-permute-start.30 = (bf16[1,64,2048]{2,1,0:T(8,128)(2,1)S(1)}, bf16[1,64,2048]{2,1,0:T(8,128)(2,1)S(1)}, u32[]{:S(2)}, u32[]{:S(2)}) collective-permute-start(bf16[1,64,2048]{2,1,0:T(8,128)(2,1)S(1)} %fusion.8), channel_id=1, source_target_pairs={{0,16},{16,0},{1,17},{17,1},{2,18},{18,2},{3,19},{19,3},{4,20},{20... | collective-permute-start | bytes 786440 | tf_op jit(solution)/shard_map/ppermute | solution.py:44
  122.4 1.6 %collective-permute-done.21.array = bf16[1,64,2048]{2,1,0:T(8,128)(2,1)S(1)} collective-permute-done((bf16[1,64,2048]{2,1,0:T(8,128)(2,1)S(1)}, bf16[1,64,2048]{2,1,0:T(8,128)(2,1)S(1)}, u32[]{:S(2)}, u32[]{:S(2)}) %collective-permute-start.21) | collective-permute-done | bytes 262176 | tf_op jit(solution)/shard_map/ppermute | solution.py:44
  124.0 0.7 shard_map.130
  124.8 2.6 %collective-permute-done.30 = bf16[1,64,2048]{2,1,0:T(8,128)(2,1)S(1)} collective-permute-done((bf16[1,64,2048]{2,1,0:T(8,128)(2,1)S(1)}, bf16[1,64,2048]{2,1,0:T(8,128)(2,1)S(1)}, u32[]{:S(2)}, u32[]{:S(2)}) %collective-permute-start.30) | collective-permute-done | bytes 262176 | tf_op jit(solution)/shard_map/ppermute | solution.py:44
  127.3 0.7 copy.14
  (57 shorter events, 4.6 us)
Async XLA Ops:
  0.6 23.8 %collective-permute-start.2 = (bf16[2048,768]{1,0:T(8,128)(2,1)}, bf16[2048,768]{1,0:T(8,128)(2,1)}, u32[]{:S(2)}, u32[]{:S(2)}) collective-permute-start(bf16[2048,768]{1,0:T(8,128)(2,1)} %bitcast.30), channel_id=1, source_target_pairs={{0,1},{1,0},{2,3},{3,2},{4,5},{5,4},{6,7},{7,6},{8,9},{9,8},{10,11... | collective-permute-start | bytes 9437192 | tf_op jit(solution)/shard_map/ppermute | solution.py:409
  0.7 23.7 %collective-permute-start.3 = (bf16[2048,768]{1,0:T(8,128)(2,1)}, bf16[2048,768]{1,0:T(8,128)(2,1)}, u32[]{:S(2)}, u32[]{:S(2)}) collective-permute-start(bf16[2048,768]{1,0:T(8,128)(2,1)} %bitcast.32), channel_id=1, source_target_pairs={{0,1},{1,0},{2,3},{3,2},{4,5},{5,4},{6,7},{7,6},{8,9},{9,8},{10,11... | collective-permute-start | bytes 9437192 | tf_op jit(solution)/shard_map/ppermute | solution.py:409
  1.2 23.2 %collective-permute-start.4 = (bf16[768,2048]{1,0:T(8,128)(2,1)}, bf16[768,2048]{1,0:T(8,128)(2,1)}, u32[]{:S(2)}, u32[]{:S(2)}) collective-permute-start(bf16[768,2048]{1,0:T(8,128)(2,1)} %bitcast.34), channel_id=1, source_target_pairs={{0,1},{1,0},{2,3},{3,2},{4,5},{5,4},{6,7},{7,6},{8,9},{9,8},{10,11... | collective-permute-start | bytes 9437192 | tf_op jit(solution)/shard_map/ppermute | solution.py:409
  6.1 18.2 %collective-permute-start = (bf16[64,6272]{1,0:T(8,128)(2,1)}, bf16[64,6272]{1,0:T(8,128)(2,1)S(1)}, u32[]{:S(2)}, u32[]{:S(2)}) collective-permute-start(bf16[64,6272]{1,0:T(8,128)(2,1)} %shard_map.122.refs_0_), channel_id=1, source_target_pairs={{0,4},{1,5},{4,8},{5,9},{8,12},{9,13},{12,14},{13,15},{14,10},{15,... | collective-permute-start | bytes 2408456 | tf_op jit(solution)/shard_map/ppermute | solution.py:69
  6.6 17.8 %collective-permute-start.1 = (bf16[64,6272]{1,0:T(8,128)(2,1)}, bf16[64,6272]{1,0:T(8,128)(2,1)S(1)}, u32[]{:S(2)}, u32[]{:S(2)}) collective-permute-start(bf16[64,6272]{1,0:T(8,128)(2,1)} %shard_map.122.refs_0_), channel_id=1, source_target_pairs={{0,2},{1,3},{4,0},{5,1},{8,4},{9,5},{12,8},{13,9},{14,12},{15,13},... | collective-permute-start | bytes 2408456 | tf_op jit(solution)/shard_map/ppermute | solution.py:70
  24.4 18.1 %collective-permute-start.5 = (bf16[64,6272]{1,0:T(8,128)(2,1)S(1)}, bf16[64,6272]{1,0:T(8,128)(2,1)S(1)}, u32[]{:S(2)}, u32[]{:S(2)}) collective-permute-start(bf16[64,6272]{1,0:T(8,128)(2,1)S(1)} %collective-permute-done.refs_1_), channel_id=1, source_target_pairs={{0,4},{1,5},{4,8},{5,9},{8,12},{9,13},{12,14},{13,15},{14,10},{15,... | collective-permute-start | bytes 2408456 | tf_op jit(solution)/shard_map/ppermute | solution.py:69
  24.8 17.7 %collective-permute-start.6 = (bf16[64,6272]{1,0:T(8,128)(2,1)S(1)}, bf16[64,6272]{1,0:T(8,128)(2,1)S(1)}, u32[]{:S(2)}, u32[]{:S(2)}) collective-permute-start(bf16[64,6272]{1,0:T(8,128)(2,1)S(1)} %collective-permute-done.1.refs_2_), channel_id=1, source_target_pairs={{0,2},{1,3},{4,0},{5,1},{8,4},{9,5},{12,8},{13,9},{14,12},{15,13},... | collective-permute-start | bytes 2408456 | tf_op jit(solution)/shard_map/ppermute | solution.py:70
  26.6 6.6 %copy-start = (bf16[64,6272]{1,0:T(8,128)(2,1)S(1)}, bf16[64,6272]{1,0:T(8,128)(2,1)}, u32[]{:S(2)}) copy-start(bf16[64,6272]{1,0:T(8,128)(2,1)} %shard_map.122.refs_0_) | copy-start | bytes 2408452
  42.5 16.7 %collective-permute-start.7 = (bf16[64,6272]{1,0:T(8,128)(2,1)S(1)}, bf16[64,6272]{1,0:T(8,128)(2,1)S(1)}, u32[]{:S(2)}, u32[]{:S(2)}) collective-permute-start(bf16[64,6272]{1,0:T(8,128)(2,1)S(1)} %collective-permute-done.5.refs_0_.refs_3_), channel_id=1, source_target_pairs={{0,4},{1,5},{4,8},{5,9},{8,12},{9,13},{12,14},{13,15},{14,10},{15,... | collective-permute-start | bytes 2408456 | tf_op jit(solution)/shard_map/ppermute | solution.py:69
  43.2 17.6 %collective-permute-start.8 = (bf16[64,6272]{1,0:T(8,128)(2,1)S(1)}, bf16[64,6272]{1,0:T(8,128)(2,1)S(1)}, u32[]{:S(2)}, u32[]{:S(2)}) collective-permute-start(bf16[64,6272]{1,0:T(8,128)(2,1)S(1)} %collective-permute-done.6.refs_1_.refs_0_), channel_id=1, source_target_pairs={{0,2},{1,3},{4,0},{5,1},{8,4},{9,5},{12,8},{13,9},{14,12},{15,13},... | collective-permute-start | bytes 2408456 | tf_op jit(solution)/shard_map/ppermute | solution.py:70
  60.9 5.1 %collective-permute-start.10 = (bf16[32,2176]{1,0:T(8,128)(2,1)S(1)}, bf16[32,2176]{1,0:T(8,128)(2,1)S(1)}, u32[]{:S(2)}, u32[]{:S(2)}) collective-permute-start(bf16[32,2176]{1,0:T(8,128)(2,1)S(1)} %slice.94), channel_id=1, source_target_pairs={{0,2},{1,3},{4,0},{5,1},{8,4},{9,5},{12,8},{13,9},{14,12},{15,13},... | collective-permute-start | bytes 417800 | tf_op jit(solution)/shard_map/ppermute | solution.py:70
  62.6 5.1 %collective-permute-start.9 = (bf16[32,2176]{1,0:T(8,128)(2,1)S(1)}, bf16[32,2176]{1,0:T(8,128)(2,1)S(1)}, u32[]{:S(2)}, u32[]{:S(2)}) collective-permute-start(bf16[32,2176]{1,0:T(8,128)(2,1)S(1)} %slice.93), channel_id=1, source_target_pairs={{0,4},{1,5},{4,8},{5,9},{8,12},{9,13},{12,14},{13,15},{14,10},{15,... | collective-permute-start | bytes 417800 | tf_op jit(solution)/shard_map/ppermute | solution.py:69
  63.0 11.6 %collective-permute-start.13 = (bf16[32,4224]{1,0:T(8,128)(2,1)S(1)}, bf16[32,4224]{1,0:T(8,128)(2,1)S(1)}, u32[]{:S(2)}, u32[]{:S(2)}) collective-permute-start(bf16[32,4224]{1,0:T(8,128)(2,1)S(1)} %slice.98), channel_id=1, source_target_pairs={{0,4},{1,5},{4,8},{5,9},{8,12},{9,13},{12,14},{13,15},{14,10},{15,... | collective-permute-start | bytes 811016 | tf_op jit(solution)/shard_map/ppermute | solution.py:69
  65.0 9.6 %collective-permute-start.14 = (bf16[32,4224]{1,0:T(8,128)(2,1)S(1)}, bf16[32,4224]{1,0:T(8,128)(2,1)S(1)}, u32[]{:S(2)}, u32[]{:S(2)}) collective-permute-start(bf16[32,4224]{1,0:T(8,128)(2,1)S(1)} %slice.99), channel_id=1, source_target_pairs={{0,2},{1,3},{4,0},{5,1},{8,4},{9,5},{12,8},{13,9},{14,12},{15,13},... | collective-permute-start | bytes 811016 | tf_op jit(solution)/shard_map/ppermute | solution.py:70
  72.6 8.0 %collective-permute-start.11 = (bf16[32,2048]{1,0:T(8,128)(2,1)S(1)}, bf16[32,2048]{1,0:T(8,128)(2,1)S(1)}, u32[]{:S(2)}, u32[]{:S(2)}) collective-permute-start(bf16[32,2048]{1,0:T(8,128)(2,1)S(1)} %get-tuple-element.55), channel_id=1, source_target_pairs={{0,2},{1,3},{4,0},{5,1},{8,4},{9,5},{12,8},{13,9},{14,12},{15,13},... | collective-permute-start | bytes 393224 | tf_op jit(solution)/shard_map/ppermute | solution.py:94
  74.4 6.2 %collective-permute-start.12 = (bf16[32,2048]{1,0:T(8,128)(2,1)S(1)}, bf16[32,2048]{1,0:T(8,128)(2,1)S(1)}, u32[]{:S(2)}, u32[]{:S(2)}) collective-permute-start(bf16[32,2048]{1,0:T(8,128)(2,1)S(1)} %get-tuple-element.54), channel_id=1, source_target_pairs={{0,4},{1,5},{4,8},{5,9},{8,12},{9,13},{12,14},{13,15},{14,10},{15,... | collective-permute-start | bytes 393224 | tf_op jit(solution)/shard_map/ppermute | solution.py:95
  84.1 6.5 %collective-permute-start.22 = (bf16[32,2048]{1,0:T(8,128)(2,1)S(1)}, bf16[32,2048]{1,0:T(8,128)(2,1)S(1)}, u32[]{:S(2)}, u32[]{:S(2)}) collective-permute-start(bf16[32,2048]{1,0:T(8,128)(2,1)S(1)} %get-tuple-element.44), channel_id=1, source_target_pairs={{0,2},{1,3},{4,0},{5,1},{8,4},{9,5},{12,8},{13,9},{14,12},{15,13},... | collective-permute-start | bytes 393224 | tf_op jit(solution)/shard_map/ppermute | solution.py:94
  85.9 6.4 %collective-permute-start.26 = (bf16[32,2048]{1,0:T(8,128)(2,1)S(1)}, bf16[32,2048]{1,0:T(8,128)(2,1)S(1)}, u32[]{:S(2)}, u32[]{:S(2)}) collective-permute-start(bf16[32,2048]{1,0:T(8,128)(2,1)S(1)} %get-tuple-element.45), channel_id=1, source_target_pairs={{0,4},{1,5},{4,8},{5,9},{8,12},{9,13},{12,14},{13,15},{14,10},{15,... | collective-permute-start | bytes 393224 | tf_op jit(solution)/shard_map/ppermute | solution.py:95
  86.3 11.7 %collective-permute-start.18 = (bf16[64,2048]{1,0:T(8,128)(2,1)S(1)}, bf16[64,2048]{1,0:T(8,128)(2,1)S(1)}, u32[]{:S(2)}, u32[]{:S(2)}) collective-permute-start(bf16[64,2048]{1,0:T(8,128)(2,1)S(1)} %pad_maximum_fusion.1), channel_id=1, source_target_pairs={{0,4},{1,5},{4,8},{5,9},{8,12},{9,13},{12,14},{13,15},{14,10},{15,... | collective-permute-start | bytes 786440 | tf_op jit(solution)/shard_map/ppermute | solution.py:95
  87.4 10.6 %collective-permute-start.15 = (bf16[64,2048]{1,0:T(8,128)(2,1)S(1)}, bf16[64,2048]{1,0:T(8,128)(2,1)S(1)}, u32[]{:S(2)}, u32[]{:S(2)}) collective-permute-start(bf16[64,2048]{1,0:T(8,128)(2,1)S(1)} %pad_maximum_fusion), channel_id=1, source_target_pairs={{0,2},{1,3},{4,0},{5,1},{8,4},{9,5},{12,8},{13,9},{14,12},{15,13},... | collective-permute-start | bytes 786440 | tf_op jit(solution)/shard_map/ppermute | solution.py:94
  92.4 11.1 %collective-permute-start.27 = (bf16[64,2048]{1,0:T(8,128)(2,1)S(1)}, bf16[64,2048]{1,0:T(8,128)(2,1)S(1)}, u32[]{:S(2)}, u32[]{:S(2)}) collective-permute-start(bf16[64,2048]{1,0:T(8,128)(2,1)S(1)} %pad_maximum_fusion.3), channel_id=1, source_target_pairs={{0,4},{1,5},{4,8},{5,9},{8,12},{9,13},{12,14},{13,15},{14,10},{15,... | collective-permute-start | bytes 786440 | tf_op jit(solution)/shard_map/ppermute | solution.py:95
  92.8 24.7 %copy-start.2 = (bf16[1,64,2048]{2,1,0:T(8,128)(2,1)S(1)}, bf16[1,64,2048]{2,1,0:T(8,128)(2,1)}, u32[]{:S(2)}) copy-start(bf16[1,64,2048]{2,1,0:T(8,128)(2,1)} %param.11) | copy-start | bytes 786436
  92.8 11.2 %collective-permute-start.23 = (bf16[64,2048]{1,0:T(8,128)(2,1)S(1)}, bf16[64,2048]{1,0:T(8,128)(2,1)S(1)}, u32[]{:S(2)}, u32[]{:S(2)}) collective-permute-start(bf16[64,2048]{1,0:T(8,128)(2,1)S(1)} %pad_maximum_fusion.2), channel_id=1, source_target_pairs={{0,2},{1,3},{4,0},{5,1},{8,4},{9,5},{12,8},{13,9},{14,12},{15,13},... | collective-permute-start | bytes 786440 | tf_op jit(solution)/shard_map/ppermute | solution.py:94
  98.1 22.2 %copy-start.1 = (bf16[1,64,2048]{2,1,0:T(8,128)(2,1)S(1)}, bf16[1,64,2048]{2,1,0:T(8,128)(2,1)}, u32[]{:S(2)}) copy-start(bf16[1,64,2048]{2,1,0:T(8,128)(2,1)} %param.14) | copy-start | bytes 786436
  98.1 22.2 %copy-start.4 = (f32[1,2048]{1,0:T(1,128)S(1)}, f32[1,2048]{1,0:T(1,128)}, u32[]{:S(2)}) copy-start(f32[1,2048]{1,0:T(1,128)} %refs_2_.1) | copy-start | bytes 24580
  98.1 9.8 %collective-permute-start.16 = (bf16[64,2048]{1,0:T(8,128)(2,1)S(1)}, bf16[64,2048]{1,0:T(8,128)(2,1)S(1)}, u32[]{:S(2)}, u32[]{:S(2)}) collective-permute-start(bf16[64,2048]{1,0:T(8,128)(2,1)S(1)} %get-tuple-element.56), channel_id=1, source_target_pairs={{0,2},{1,3},{4,0},{5,1},{8,4},{9,5},{12,8},{13,9},{14,12},{15,13},... | collective-permute-start | bytes 786440 | tf_op jit(solution)/shard_map/ppermute | solution.py:94
  100.1 9.1 %collective-permute-start.19 = (bf16[64,2048]{1,0:T(8,128)(2,1)S(1)}, bf16[64,2048]{1,0:T(8,128)(2,1)S(1)}, u32[]{:S(2)}, u32[]{:S(2)}) collective-permute-start(bf16[64,2048]{1,0:T(8,128)(2,1)S(1)} %get-tuple-element.57), channel_id=1, source_target_pairs={{0,4},{1,5},{4,8},{5,9},{8,12},{9,13},{12,14},{13,15},{14,10},{15,... | collective-permute-start | bytes 786440 | tf_op jit(solution)/shard_map/ppermute | solution.py:95
  103.6 16.9 %copy-start.3 = (bf16[1,64,2048]{2,1,0:T(8,128)(2,1)S(1)}, bf16[1,64,2048]{2,1,0:T(8,128)(2,1)}, u32[]{:S(2)}) copy-start(bf16[1,64,2048]{2,1,0:T(8,128)(2,1)} %param.15) | copy-start | bytes 786436
  103.7 8.3 %collective-permute-start.28 = (bf16[64,2048]{1,0:T(8,128)(2,1)S(1)}, bf16[64,2048]{1,0:T(8,128)(2,1)S(1)}, u32[]{:S(2)}, u32[]{:S(2)}) collective-permute-start(bf16[64,2048]{1,0:T(8,128)(2,1)S(1)} %add_convert_fusion.1), channel_id=1, source_target_pairs={{0,4},{1,5},{4,8},{5,9},{8,12},{9,13},{12,14},{13,15},{14,10},{15,... | collective-permute-start | bytes 786440 | tf_op jit(solution)/shard_map/ppermute | solution.py:95
  104.0 7.9 %collective-permute-start.24 = (bf16[64,2048]{1,0:T(8,128)(2,1)S(1)}, bf16[64,2048]{1,0:T(8,128)(2,1)S(1)}, u32[]{:S(2)}, u32[]{:S(2)}) collective-permute-start(bf16[64,2048]{1,0:T(8,128)(2,1)S(1)} %add_convert_fusion.3), channel_id=1, source_target_pairs={{0,2},{1,3},{4,0},{5,1},{8,4},{9,5},{12,8},{13,9},{14,12},{15,13},... | collective-permute-start | bytes 786440 | tf_op jit(solution)/shard_map/ppermute | solution.py:94
  109.3 6.4 %collective-permute-start.17 = (bf16[64,2048]{1,0:T(8,128)(2,1)S(1)}, bf16[64,2048]{1,0:T(8,128)(2,1)S(1)}, u32[]{:S(2)}, u32[]{:S(2)}) collective-permute-start(bf16[64,2048]{1,0:T(8,128)(2,1)S(1)} %get-tuple-element.48), channel_id=1, source_target_pairs={{0,2},{1,3},{4,0},{5,1},{8,4},{9,5},{12,8},{13,9},{14,12},{15,13},... | collective-permute-start | bytes 786440 | tf_op jit(solution)/shard_map/ppermute | solution.py:94
  111.1 6.4 %collective-permute-start.20 = (bf16[64,2048]{1,0:T(8,128)(2,1)S(1)}, bf16[64,2048]{1,0:T(8,128)(2,1)S(1)}, u32[]{:S(2)}, u32[]{:S(2)}) collective-permute-start(bf16[64,2048]{1,0:T(8,128)(2,1)S(1)} %get-tuple-element.49), channel_id=1, source_target_pairs={{0,4},{1,5},{4,8},{5,9},{8,12},{9,13},{12,14},{13,15},{14,10},{15,... | collective-permute-start | bytes 786440 | tf_op jit(solution)/shard_map/ppermute | solution.py:95
  112.1 7.1 %collective-permute-start.25 = (bf16[64,2048]{1,0:T(8,128)(2,1)S(1)}, bf16[64,2048]{1,0:T(8,128)(2,1)S(1)}, u32[]{:S(2)}, u32[]{:S(2)}) collective-permute-start(bf16[64,2048]{1,0:T(8,128)(2,1)S(1)} %get-tuple-element.40), channel_id=1, source_target_pairs={{0,2},{1,3},{4,0},{5,1},{8,4},{9,5},{12,8},{13,9},{14,12},{15,13},... | collective-permute-start | bytes 786440 | tf_op jit(solution)/shard_map/ppermute | solution.py:94
  113.9 6.4 %collective-permute-start.29 = (bf16[64,2048]{1,0:T(8,128)(2,1)S(1)}, bf16[64,2048]{1,0:T(8,128)(2,1)S(1)}, u32[]{:S(2)}, u32[]{:S(2)}) collective-permute-start(bf16[64,2048]{1,0:T(8,128)(2,1)S(1)} %get-tuple-element.41), channel_id=1, source_target_pairs={{0,4},{1,5},{4,8},{5,9},{8,12},{9,13},{12,14},{13,15},{14,10},{15,... | collective-permute-start | bytes 786440 | tf_op jit(solution)/shard_map/ppermute | solution.py:95
  117.6 6.4 %collective-permute-start.21 = (bf16[1,64,2048]{2,1,0:T(8,128)(2,1)S(1)}, bf16[1,64,2048]{2,1,0:T(8,128)(2,1)S(1)}, u32[]{:S(2)}, u32[]{:S(2)}) collective-permute-start(bf16[1,64,2048]{2,1,0:T(8,128)(2,1)S(1)} %fusion.7), channel_id=1, source_target_pairs={{0,16},{16,0},{1,17},{17,1},{2,18},{18,2},{3,19},{19,3},{4,20},{20... | collective-permute-start | bytes 786440 | tf_op jit(solution)/shard_map/ppermute | solution.py:44
  120.9 6.4 %collective-permute-start.30 = (bf16[1,64,2048]{2,1,0:T(8,128)(2,1)S(1)}, bf16[1,64,2048]{2,1,0:T(8,128)(2,1)S(1)}, u32[]{:S(2)}, u32[]{:S(2)}) collective-permute-start(bf16[1,64,2048]{2,1,0:T(8,128)(2,1)S(1)} %fusion.8), channel_id=1, source_target_pairs={{0,16},{16,0},{1,17},{17,1},{2,18},{18,2},{3,19},{19,3},{4,20},{20... | collective-permute-start | bytes 786440 | tf_op jit(solution)/shard_map/ppermute | solution.py:44
